TPU v7x, 32 devices: a whole 2x2x4 slice. The times are simulated.
32 devices in a mesh: grp: 2 (over y), row: 4 (over x, core), slab: 4 (over z).
Axes of the slice: x: 2, y: 2, z: 4, core: 2. Of those that a mesh axis runs over, the one named last changes fastest.
Arguments:
- observed: float32 [128, 256, 256], P(('grp', 'slab'), 'row'), parts along dimension 0, may hold values from 0.25 to 4
- band_index: int32 [64], P('slab'), may hold values from 0 to 15
- taps_x: float32 [16, 31], replicated, may hold values from 0.005 to 0.12
- taps_y: float32 [16, 31], replicated, may hold values from 0.005 to 0.12
- taps_z: float32 [31], replicated, may hold values from 0.005 to 0.12
Outputs:
- estimate: float32 [128, 256, 256], P(('grp', 'slab'), 'row'), parts along dimension 0
There are 2 independent parts, one for each index of `grp`. A program takes and returns all parts, laid end to end along the dimension named above; an argument that names none is the same for every part. Nothing has to cross between parts.
All inputs are finite; a program needn't handle non-finite values.
Results may differ from a plain program's by a relative error of at most 0.00015.
Values sent between devices are 32-bit elements; how exact they have to be, the bound alone decides.
No kernel may reach another device: no remote copies, remote signals or barrier semaphores. Data moves between devices by JAX's collectives and lax.ppermute only.
A program may use at most 64 MiB of HBM per device.

v0:
```python
import jax
import jax.numpy as jnp
from jax import lax
from jax.sharding import PartitionSpec as P

ITERS = 2


def padded_2(block, sides, width):
    for axis, dim in sides:
        count = lax.axis_size(axis)
        forward = [(i, i + 1) for i in range(count - 1)]
        backward = [(target, source) for source, target in forward]
        low = lax.ppermute(
            lax.slice_in_dim(block, block.shape[dim] - width, None, axis=dim), axis, forward
        )
        high = lax.ppermute(lax.slice_in_dim(block, 0, width, axis=dim), axis, backward)
        block = jnp.concatenate([low, block, high], axis=dim)
    return block


def correlate(padded, taps, dim, length):
    total = None
    for k in range(taps.shape[-1]):
        piece = lax.slice_in_dim(padded, k, k + length, axis=dim)
        if taps.ndim == 2:
            weight = taps[:, k][:, None, None]
        else:
            weight = taps[k]
        term = weight * piece
        total = term if total is None else total + term
    return total


def pad_along(field, radius, dim):
    widths = [(0, 0), (0, 0), (0, 0)]
    widths[dim] = (radius, radius)
    return jnp.pad(field, widths)


def along_rows(field, plane_taps):
    radius = plane_taps.shape[-1] // 2
    padded = padded_2(field, (("row", 1),), radius)
    return correlate(padded, plane_taps, 1, field.shape[1])


def along_depth(field, depth_taps):
    radius = depth_taps.shape[-1] // 2
    padded = padded_2(field, (("slab", 0),), radius)
    return correlate(padded, depth_taps, 0, field.shape[0])


def along_columns(field, plane_taps):
    radius = plane_taps.shape[-1] // 2
    return correlate(pad_along(field, radius, 2), plane_taps, 2, field.shape[2])


def forward(field, plane_x, plane_y, taps_z):
    field = along_rows(field, plane_x)
    field = along_columns(field, plane_y)
    return along_depth(field, taps_z)


def adjoint(field, plane_x, plane_y, taps_z):
    field = along_depth(field, taps_z[::-1])
    field = along_columns(field, plane_y[:, ::-1])
    return along_rows(field, plane_x[:, ::-1])


def on_device(observed, band_index, taps_x, taps_y, taps_z):
    band_count = taps_x.shape[0]
    one_hot = (band_index[:, None] == jnp.arange(band_count, dtype=jnp.int32)[None, :]).astype(
        jnp.float32
    )
    plane_x = jnp.dot(one_hot, taps_x, precision=lax.Precision.HIGHEST)
    plane_y = jnp.dot(one_hot, taps_y, precision=lax.Precision.HIGHEST)
    norm = adjoint(jnp.ones(observed.shape, jnp.float32), plane_x, plane_y, taps_z)
    estimate = observed
    for step in range(ITERS):
        blurred = forward(estimate, plane_x, plane_y, taps_z)
        ratio = observed / blurred
        estimate = estimate * adjoint(ratio, plane_x, plane_y, taps_z) / norm
    return estimate


def solution(mesh):
    in_specs = (P(("grp", "slab"), "row", None), P("slab"), P(), P(), P())
    out_specs = P(("grp", "slab"), "row", None)
    return jax.shard_map(
        on_device, mesh=mesh, in_specs=in_specs, out_specs=out_specs, check_vma=False
    )
```

profile of v0, /device:TPU:0, one launch (start us, length us, event | category | flops | bytes accessed | tf_op | source)
XLA Modules:
  0.0 353.1 jit_solution(15672718708147314349)
XLA Ops:
  0.0 1.2 fusion.1141
  1.2 1.3 collective-permute-start.1
  2.5 3.0 collective-permute-start
  5.5 0.8 fusion.1129
  6.4 0.4 slice_reduce_fusion.58
  6.9 0.5 slice_reduce_fusion.61
  7.6 0.2 fusion.1128
  7.8 0.5 slice_reduce_fusion.60
  8.3 0.4 slice_reduce_fusion.59
  8.7 0.1 constant_dynamic-update-slice_fusion.1
  8.8 0.0 collective-permute-done.1
  8.8 0.0 collective-permute-done
  9.1 4.6 %fusion.367 = f32[16,64,256]{2,1,0:T(8,128)S(1)} fusion(f32[16,64,256]{2,1,0:T(8,128)S(1)} %copy-done.1, f32[16,15,256]{2,1,0:T(8,128)S(1)} %collective-permute-done, f32[16,79,256]{2,1,0:T(8,128)S(1)} %constant_dynamic-update-slice_fusion, f32[16]{0:T(128)S(1)} %get-tuple-element.6, f32[16]{0:T(128)S(1)} %get-tuple-element.7, f32[16]{0:T(128)S(1)} %get-tuple-element.8, ...), kind=kLoop, calls=%fused_computation.1023 | loop fusion | flops 19922944 | bytes 18073536 | tf_op jit(solution)/shard_map/add | solution.py:31
  13.7 9.1 %fusion.458 = f32[16,64,256]{2,1,0:T(8,128)S(1)} fusion(f32[16,64,256]{2,1,0:T(8,128)S(1)} %fusion.367, f32[16]{0:T(128)S(1)} %get-tuple-element.37, f32[16]{0:T(128)S(1)} %get-tuple-element.38, f32[16]{0:T(128)S(1)} %get-tuple-element.39, f32[16]{0:T(128)S(1)} %get-tuple-element.40, f32[16]{0:T(128)S(1)} %get-tuple-element.41, ...), kind=kLoop, calls=%fused_computation.1114 | loop fusion | flops 15990784 | bytes 2099136 | tf_op jit(solution)/shard_map/add | solution.py:31
  22.8 0.0 copy-start.4
  22.8 0.2 fusion.1140
  23.0 5.0 %collective-permute-start.2 = (f32[15,64,256]{2,1,0:T(8,128)S(1)}, f32[15,64,256]{2,1,0:T(8,128)S(1)}, u32[]{:S(2)}, u32[]{:S(2)}) collective-permute-start(f32[15,64,256]{2,1,0:T(8,128)S(1)} %get-tuple-element.83), channel_id=1, source_target_pairs={{0,1},{1,2},{2,3},{4,5},{5,6},{6,7},{8,9},{9,10},{10,11},{12,13},{... | collective-permute-start | bytes 2949128 | tf_op jit(solution)/shard_map/ppermute | solution.py:14
  28.0 1.3 collective-permute-start.3
  29.3 0.1 broadcast.18
  29.4 1.3 collective-permute-start.9
  30.7 6.2 %collective-permute-start.8 = (f32[15,64,256]{2,1,0:T(8,128)S(1)}, f32[15,64,256]{2,1,0:T(8,128)}, u32[]{:S(2)}, u32[]{:S(2)}) collective-permute-start(f32[15,64,256]{2,1,0:T(8,128)S(1)} %broadcast.18), channel_id=1, source_target_pairs={{0,1},{1,2},{2,3},{4,5},{5,6},{6,7},{8,9},{9,10},{10,11},{12,13},{... | collective-permute-start | bytes 2949128 | tf_op jit(solution)/shard_map/ppermute | solution.py:14
  36.9 0.7 fusion.1143
  37.6 0.7 fusion.1142
  38.3 11.6 %collective-permute-done.2 = f32[15,64,256]{2,1,0:T(8,128)S(1)} collective-permute-done((f32[15,64,256]{2,1,0:T(8,128)S(1)}, f32[15,64,256]{2,1,0:T(8,128)S(1)}, u32[]{:S(2)}, u32[]{:S(2)}) %collective-permute-start.2) | collective-permute-done | bytes 983072 | tf_op jit(solution)/shard_map/ppermute | solution.py:14
  50.0 4.6 %collective-permute-done.3 = f32[15,64,256]{2,1,0:T(8,128)S(1)} collective-permute-done((f32[15,64,256]{2,1,0:T(8,128)S(1)}, f32[15,64,256]{2,1,0:T(8,128)S(1)}, u32[]{:S(2)}, u32[]{:S(2)}) %collective-permute-start.3) | collective-permute-done | bytes 983072 | tf_op jit(solution)/shard_map/ppermute | solution.py:17
  54.5 23.8 %fusion.969 = f32[16,64,256]{2,1,0:T(8,128)S(1)} fusion(f32[16,64,256]{2,1,0:T(8,128)S(1)} %copy-done.1, f32[16,64,256]{2,1,0:T(8,128)S(1)} %fusion.458, f32[15,64,256]{2,1,0:T(8,128)S(1)} %collective-permute-done.3, f32[15,64,256]{2,1,0:T(8,128)S(1)} %collective-permute-done.2, f32[]{:T(128)} %bitcast.30, f32[]{:T(128)} %bitcast.29, f32[]{:T(128)} %bitcast.28, ...), kind=kLoop, calls=%fused_computation.1625 | loop fusion | flops 24117248 | bytes 5111932 | tf_op jit(solution)/shard_map/div | solution.py:81
  78.3 0.2 fusion.1139
  78.6 4.4 %collective-permute-start.4 = (f32[15,64,256]{2,1,0:T(8,128)S(1)}, f32[15,64,256]{2,1,0:T(8,128)}, u32[]{:S(2)}, u32[]{:S(2)}) collective-permute-start(f32[15,64,256]{2,1,0:T(8,128)S(1)} %get-tuple-element.81), channel_id=1, source_target_pairs={{0,1},{1,2},{2,3},{4,5},{5,6},{6,7},{8,9},{9,10},{10,11},{12,13},{... | collective-permute-start | bytes 2949128 | tf_op jit(solution)/shard_map/ppermute | solution.py:14
  83.0 1.3 collective-permute-start.5
  84.3 0.0 collective-permute-done.9
  84.3 27.5 %fusion.1096 = f32[16,64,256]{2,1,0:T(8,128)S(1)} fusion(f32[15,64,256]{2,1,0:T(8,128)} %collective-permute-done.9, f32[15,64,256]{2,1,0:T(8,128)} %collective-permute-done.8, f32[]{:T(128)} %bitcast.30, f32[]{:T(128)} %bitcast.29, f32[]{:T(128)} %bitcast.28, f32[]{:T(128)} %bitcast.27, f32[]{:T(128)} %bitcast.26, f32[]{:T(128)} %bitcast.25, f32[]{:T(128)} %bitcast.24, ...), kind=kLoop, calls=%fused_computation.1752 | loop fusion | flops 15728640 | bytes 3014780 | tf_op jit(solution)/shard_map/add | solution.py:31
  111.8 9.1 %fusion.578 = f32[16,64,256]{2,1,0:T(8,128)S(1)} fusion(f32[16,64,256]{2,1,0:T(8,128)S(1)} %fusion.1096, f32[16]{0:T(128)S(1)} %get-tuple-element.37, f32[16]{0:T(128)S(1)} %get-tuple-element.38, f32[16]{0:T(128)S(1)} %get-tuple-element.39, f32[16]{0:T(128)S(1)} %get-tuple-element.40, f32[16]{0:T(128)S(1)} %get-tuple-element.41, ...), kind=kLoop, calls=%fused_computation.1234 | loop fusion | flops 15990784 | bytes 2099136 | tf_op jit(solution)/shard_map/add | solution.py:31
  120.9 0.9 fusion.1137
  121.8 1.5 collective-permute-start.10
  123.4 1.3 collective-permute-start.11
  124.7 27.8 %fusion.882 = f32[16,64,256]{2,1,0:T(8,128)S(1)} fusion(f32[16,64,256]{2,1,0:T(8,128)S(1)} %fusion.969, f32[15,64,256]{2,1,0:T(8,128)} %collective-permute-done.5, f32[15,64,256]{2,1,0:T(8,128)} %collective-permute-done.4, f32[]{:T(128)} %bitcast.30, f32[]{:T(128)} %bitcast.29, f32[]{:T(128)} %bitcast.28, f32[]{:T(128)} %bitcast.27, f32[]{:T(128)} %bitcast.26, ...), kind=kLoop, calls=%fused_computation.1538 | loop fusion | flops 23855104 | bytes 4063356 | tf_op jit(solution)/shard_map/add | solution.py:31
  152.5 9.1 %fusion.518 = f32[16,64,256]{2,1,0:T(8,128)S(1)} fusion(f32[16,64,256]{2,1,0:T(8,128)S(1)} %fusion.882, f32[16]{0:T(128)S(1)} %get-tuple-element.37, f32[16]{0:T(128)S(1)} %get-tuple-element.38, f32[16]{0:T(128)S(1)} %get-tuple-element.39, f32[16]{0:T(128)S(1)} %get-tuple-element.40, f32[16]{0:T(128)S(1)} %get-tuple-element.41, ...), kind=kLoop, calls=%fused_computation.1174 | loop fusion | flops 15990784 | bytes 2099136 | tf_op jit(solution)/shard_map/add | solution.py:31
  161.6 0.0 copy-start.2
  161.6 7.2 %collective-permute-start.6 = (f32[16,15,256]{2,1,0:T(8,128)S(1)}, f32[16,15,256]{2,1,0:T(8,128)}, u32[]{:S(2)}, u32[]{:S(2)}) collective-permute-start(f32[16,15,256]{2,1,0:T(8,128)S(1)} %get-tuple-element.79), channel_id=1, source_target_pairs={{0,4},{4,8},{8,12},{1,5},{5,9},{9,13},{2,6},{6,10},{10,14},{3,7},{... | collective-permute-start | bytes 737288 | tf_op jit(solution)/shard_map/ppermute | solution.py:14
  168.9 1.3 collective-permute-start.7
  170.2 2.7 collective-permute-done.7
  173.0 28.6 %fusion.265 = (f32[16,64,256]{2,1,0:T(8,128)S(1)}, f32[16,64,256]{2,1,0:T(8,128)}) fusion(f32[16,64,256]{2,1,0:T(8,128)S(1)} %copy-done.1, f32[16,64,256]{2,1,0:T(8,128)} %copy-done.2, f32[16,15,256]{2,1,0:T(8,128)} %collective-permute-done.7, f32[16,15,256]{2,1,0:T(8,128)} %collective-permute-done.6, f32[16]{0:T(128)} %copy-done.25, f32[16]{0:T(128)} %copy-done.27, ...), kind=kLoop, calls=%fused_computation.921 | loop fusion | flops 48234496 | bytes 6227904 | tf_op jit(solution)/shard_map/div | solution.py:82
  201.6 6.7 %collective-permute-start.12 = (f32[16,15,256]{2,1,0:T(8,128)S(1)}, f32[16,15,256]{2,1,0:T(8,128)S(1)}, u32[]{:S(2)}, u32[]{:S(2)}) collective-permute-start(f32[16,15,256]{2,1,0:T(8,128)S(1)} %get-tuple-element.75), channel_id=1, source_target_pairs={{0,4},{4,8},{8,12},{1,5},{5,9},{9,13},{2,6},{6,10},{10,14},{3,7},{... | collective-permute-start | bytes 737288 | tf_op jit(solution)/shard_map/ppermute | solution.py:14
  208.3 1.5 collective-permute-start.13
  209.8 1.9 collective-permute-done.13
  211.7 6.3 %fusion.91 = f32[16,64,256]{2,1,0:T(8,128)S(1)} fusion(f32[16,64,256]{2,1,0:T(8,128)S(1)} %get-tuple-element.67, f32[16,15,256]{2,1,0:T(8,128)S(1)} %collective-permute-done.13, f32[16,15,256]{2,1,0:T(8,128)S(1)} %collective-permute-done.12, f32[16]{0:T(128)} %copy-done.25, f32[16]{0:T(128)} %copy-done.27, f32[16]{0:T(128)} %copy-done.29, f32[16]{0:T(128)} %copy-done.31, ...), kind=kLoop, calls=%fused_computation.747 | loop fusion | flops 23855104 | bytes 2590656 | tf_op jit(solution)/shard_map/add | solution.py:31
  218.1 9.1 %fusion.638 = f32[16,64,256]{2,1,0:T(8,128)S(1)} fusion(f32[16,64,256]{2,1,0:T(8,128)S(1)} %fusion.91, f32[16]{0:T(128)S(1)} %get-tuple-element.37, f32[16]{0:T(128)S(1)} %get-tuple-element.38, f32[16]{0:T(128)S(1)} %get-tuple-element.39, f32[16]{0:T(128)S(1)} %get-tuple-element.40, f32[16]{0:T(128)S(1)} %get-tuple-element.41, ...), kind=kLoop, calls=%fused_computation.1294 | loop fusion | flops 15990784 | bytes 2099136 | tf_op jit(solution)/shard_map/add | solution.py:31
  227.1 0.2 fusion.1135
  227.3 4.6 %collective-permute-start.14 = (f32[15,64,256]{2,1,0:T(8,128)S(1)}, f32[15,64,256]{2,1,0:T(8,128)S(1)}, u32[]{:S(2)}, u32[]{:S(2)}) collective-permute-start(f32[15,64,256]{2,1,0:T(8,128)S(1)} %get-tuple-element.73), channel_id=1, source_target_pairs={{0,1},{1,2},{2,3},{4,5},{5,6},{6,7},{8,9},{9,10},{10,11},{12,13},{... | collective-permute-start | bytes 2949128 | tf_op jit(solution)/shard_map/ppermute | solution.py:14
  231.9 1.3 collective-permute-start.15
  233.2 17.4 %collective-permute-done.14 = f32[15,64,256]{2,1,0:T(8,128)S(1)} collective-permute-done((f32[15,64,256]{2,1,0:T(8,128)S(1)}, f32[15,64,256]{2,1,0:T(8,128)S(1)}, u32[]{:S(2)}, u32[]{:S(2)}) %collective-permute-start.14) | collective-permute-done | bytes 983072 | tf_op jit(solution)/shard_map/ppermute | solution.py:14
  250.6 4.7 %collective-permute-done.15 = f32[15,64,256]{2,1,0:T(8,128)S(1)} collective-permute-done((f32[15,64,256]{2,1,0:T(8,128)S(1)}, f32[15,64,256]{2,1,0:T(8,128)S(1)}, u32[]{:S(2)}, u32[]{:S(2)}) %collective-permute-start.15) | collective-permute-done | bytes 983072 | tf_op jit(solution)/shard_map/ppermute | solution.py:17
  255.4 23.8 %fusion.796 = f32[16,64,256]{2,1,0:T(8,128)S(1)} fusion(f32[16,64,256]{2,1,0:T(8,128)S(1)} %copy-done.1, f32[16,64,256]{2,1,0:T(8,128)S(1)} %fusion.638, f32[15,64,256]{2,1,0:T(8,128)S(1)} %collective-permute-done.15, f32[15,64,256]{2,1,0:T(8,128)S(1)} %collective-permute-done.14, f32[]{:T(128)} %bitcast.30, f32[]{:T(128)} %bitcast.29, f32[]{:T(128)} %bitcast.28, ...), kind=kLoop, calls=%fused_computation.1452 | loop fusion | flops 24117248 | bytes 5111932 | tf_op jit(solution)/shard_map/div | solution.py:81
  279.1 0.2 fusion.1134
  279.4 2.6 collective-permute-start.16
  281.9 1.3 collective-permute-start.17
  283.2 18.8 %collective-permute-done.16 = f32[15,64,256]{2,1,0:T(8,128)S(1)} collective-permute-done((f32[15,64,256]{2,1,0:T(8,128)S(1)}, f32[15,64,256]{2,1,0:T(8,128)S(1)}, u32[]{:S(2)}, u32[]{:S(2)}) %collective-permute-start.16) | collective-permute-done | bytes 983072 | tf_op jit(solution)/shard_map/ppermute | solution.py:14
  302.0 4.7 %collective-permute-done.17 = f32[15,64,256]{2,1,0:T(8,128)S(1)} collective-permute-done((f32[15,64,256]{2,1,0:T(8,128)S(1)}, f32[15,64,256]{2,1,0:T(8,128)S(1)}, u32[]{:S(2)}, u32[]{:S(2)}) %collective-permute-start.17) | collective-permute-done | bytes 983072 | tf_op jit(solution)/shard_map/ppermute | solution.py:17
  306.7 23.7 %fusion.709 = f32[16,64,256]{2,1,0:T(8,128)S(1)} fusion(f32[16,64,256]{2,1,0:T(8,128)S(1)} %fusion.796, f32[15,64,256]{2,1,0:T(8,128)S(1)} %collective-permute-done.17, f32[15,64,256]{2,1,0:T(8,128)S(1)} %collective-permute-done.16, f32[]{:T(128)} %bitcast.30, f32[]{:T(128)} %bitcast.29, f32[]{:T(128)} %bitcast.28, f32[]{:T(128)} %bitcast.27, f32[]{:T(128)} %bitcast.26, ...), kind=kLoop, calls=%fused_computation.1365 | loop fusion | flops 23855104 | bytes 4063356 | tf_op jit(solution)/shard_map/add | solution.py:31
  330.8 9.1 %fusion.698 = f32[16,64,256]{2,1,0:T(8,128)S(1)} fusion(f32[16,64,256]{2,1,0:T(8,128)S(1)} %fusion.709, f32[16]{0:T(128)S(1)} %get-tuple-element.37, f32[16]{0:T(128)S(1)} %get-tuple-element.38, f32[16]{0:T(128)S(1)} %get-tuple-element.39, f32[16]{0:T(128)S(1)} %get-tuple-element.40, f32[16]{0:T(128)S(1)} %get-tuple-element.41, ...), kind=kLoop, calls=%fused_computation.1354 | loop fusion | flops 15990784 | bytes 2099136 | tf_op jit(solution)/shard_map/add | solution.py:31
  339.9 3.5 collective-permute-start.18
  343.3 1.3 collective-permute-start.19
  344.7 2.1 collective-permute-done.19
  347.0 6.0 %fusion.5 = f32[16,64,256]{2,1,0:T(8,128)} fusion(f32[16,64,256]{2,1,0:T(8,128)S(1)} %copy-done.3, f32[16,64,256]{2,1,0:T(8,128)S(1)} %get-tuple-element.67, f32[16,64,256]{2,1,0:T(8,128)S(1)} %fusion.698, f32[16,15,256]{2,1,0:T(8,128)S(1)} %collective-permute-done.19, f32[16,15,256]{2,1,0:T(8,128)S(1)} %collective-permute-done.18, f32[16]{0:T(128)S(1)} %copy-done.26, ...), kind=kLoop, calls=%fused_computation.661 | loop fusion | flops 24379392 | bytes 4687808 | tf_op jit(solution)/shard_map/div | solution.py:82
  (136 shorter events, 0.4 us)
Async XLA Ops:
  0.0 5.5 %copy-start = (f32[16,31]{1,0:T(8,128)S(1)}, f32[16,31]{1,0:T(8,128)}, u32[]{:S(2)}) copy-start(f32[16,31]{1,0:T(8,128)} %param.7) | copy-start | bytes 5956
  0.0 8.7 %copy-start.1 = (f32[16,64,256]{2,1,0:T(8,128)S(1)}, f32[16,64,256]{2,1,0:T(8,128)}, u32[]{:S(2)}) copy-start(f32[16,64,256]{2,1,0:T(8,128)} %param.5) | copy-start | bytes 3145732
  0.0 7.4 %copy-start.62 = (s32[16]{0:T(128)S(1)}, s32[16]{0:T(128)}, u32[]{:S(2)}) copy-start(s32[16]{0:T(128)} %param.6) | copy-start | bytes 196
  0.0 7.4 %copy-start.61 = (f32[16,31]{1,0:T(8,128)S(1)}, f32[16,31]{1,0:T(8,128)}, u32[]{:S(2)}) copy-start(f32[16,31]{1,0:T(8,128)} %param.8) | copy-start | bytes 5956
  1.2 7.6 %collective-permute-start.1 = (f32[16,15,256]{2,1,0:T(8,128)S(1)}, f32[16,15,256]{2,1,0:T(8,128)S(1)}, u32[]{:S(2)}, u32[]{:S(2)}) collective-permute-start(f32[16,15,256]{2,1,0:T(8,128)S(1)} %get-tuple-element.85), channel_id=1, source_target_pairs={{4,0},{8,4},{12,8},{5,1},{9,5},{13,9},{6,2},{10,6},{14,10},{7,3},{... | collective-permute-start | bytes 737288 | tf_op jit(solution)/shard_map/ppermute | solution.py:17
  2.5 6.3 %collective-permute-start = (f32[16,15,256]{2,1,0:T(8,128)S(1)}, f32[16,15,256]{2,1,0:T(8,128)S(1)}, u32[]{:S(2)}, u32[]{:S(2)}) collective-permute-start(f32[16,15,256]{2,1,0:T(8,128)S(1)} %get-tuple-element.86), channel_id=1, source_target_pairs={{0,4},{4,8},{8,12},{1,5},{5,9},{9,13},{2,6},{6,10},{10,14},{3,7},{... | collective-permute-start | bytes 737288 | tf_op jit(solution)/shard_map/ppermute | solution.py:14
  6.8 2.1 copy-start.7
  6.8 2.1 copy-start.9
  6.8 2.1 copy-start.11
  6.8 2.1 copy-start.13
  6.8 2.1 copy-start.15
  6.8 2.1 copy-start.17
  6.8 2.1 copy-start.19
  6.8 2.1 copy-start.21
  6.8 6.9 %copy-start.5 = (f32[16]{0:T(128)}, f32[16]{0:T(128)S(1)}, u32[]{:S(2)}) copy-start(f32[16]{0:T(128)S(1)} %get-tuple-element.27) | copy-start | bytes 196
  22.8 14.1 %copy-start.4 = (f32[31]{0:T(128)S(1)}, f32[31]{0:T(128)}, u32[]{:S(2)}) copy-start(f32[31]{0:T(128)} %param.9) | copy-start | bytes 376
  23.0 26.9 %collective-permute-start.2 = (f32[15,64,256]{2,1,0:T(8,128)S(1)}, f32[15,64,256]{2,1,0:T(8,128)S(1)}, u32[]{:S(2)}, u32[]{:S(2)}) collective-permute-start(f32[15,64,256]{2,1,0:T(8,128)S(1)} %get-tuple-element.83), channel_id=1, source_target_pairs={{0,1},{1,2},{2,3},{4,5},{5,6},{6,7},{8,9},{9,10},{10,11},{12,13},{... | collective-permute-start | bytes 2949128 | tf_op jit(solution)/shard_map/ppermute | solution.py:14
  28.0 26.5 %collective-permute-start.3 = (f32[15,64,256]{2,1,0:T(8,128)S(1)}, f32[15,64,256]{2,1,0:T(8,128)S(1)}, u32[]{:S(2)}, u32[]{:S(2)}) collective-permute-start(f32[15,64,256]{2,1,0:T(8,128)S(1)} %get-tuple-element.84), channel_id=1, source_target_pairs={{1,0},{2,1},{3,2},{5,4},{6,5},{7,6},{9,8},{10,9},{11,10},{13,12},{... | collective-permute-start | bytes 2949128 | tf_op jit(solution)/shard_map/ppermute | solution.py:17
  29.4 54.9 %collective-permute-start.9 = (f32[15,64,256]{2,1,0:T(8,128)S(1)}, f32[15,64,256]{2,1,0:T(8,128)}, u32[]{:S(2)}, u32[]{:S(2)}) collective-permute-start(f32[15,64,256]{2,1,0:T(8,128)S(1)} %broadcast.18), channel_id=1, source_target_pairs={{1,0},{2,1},{3,2},{5,4},{6,5},{7,6},{9,8},{10,9},{11,10},{13,12},{... | collective-permute-start | bytes 2949128 | tf_op jit(solution)/shard_map/ppermute | solution.py:17
  30.7 53.6 %collective-permute-start.8 = (f32[15,64,256]{2,1,0:T(8,128)S(1)}, f32[15,64,256]{2,1,0:T(8,128)}, u32[]{:S(2)}, u32[]{:S(2)}) collective-permute-start(f32[15,64,256]{2,1,0:T(8,128)S(1)} %broadcast.18), channel_id=1, source_target_pairs={{0,1},{1,2},{2,3},{4,5},{5,6},{6,7},{8,9},{9,10},{10,11},{12,13},{... | collective-permute-start | bytes 2949128 | tf_op jit(solution)/shard_map/ppermute | solution.py:14
  78.6 46.1 %collective-permute-start.4 = (f32[15,64,256]{2,1,0:T(8,128)S(1)}, f32[15,64,256]{2,1,0:T(8,128)}, u32[]{:S(2)}, u32[]{:S(2)}) collective-permute-start(f32[15,64,256]{2,1,0:T(8,128)S(1)} %get-tuple-element.81), channel_id=1, source_target_pairs={{0,1},{1,2},{2,3},{4,5},{5,6},{6,7},{8,9},{9,10},{10,11},{12,13},{... | collective-permute-start | bytes 2949128 | tf_op jit(solution)/shard_map/ppermute | solution.py:14
  83.0 41.7 %collective-permute-start.5 = (f32[15,64,256]{2,1,0:T(8,128)S(1)}, f32[15,64,256]{2,1,0:T(8,128)}, u32[]{:S(2)}, u32[]{:S(2)}) collective-permute-start(f32[15,64,256]{2,1,0:T(8,128)S(1)} %get-tuple-element.82), channel_id=1, source_target_pairs={{1,0},{2,1},{3,2},{5,4},{6,5},{7,6},{9,8},{10,9},{11,10},{13,12},{... | collective-permute-start | bytes 2949128 | tf_op jit(solution)/shard_map/ppermute | solution.py:17
  121.8 48.4 %collective-permute-start.10 = (f32[16,15,256]{2,1,0:T(8,128)}, f32[16,15,256]{2,1,0:T(8,128)S(1)}, u32[]{:S(2)}, u32[]{:S(2)}) collective-permute-start(f32[16,15,256]{2,1,0:T(8,128)} %get-tuple-element.77), channel_id=1, source_target_pairs={{0,4},{4,8},{8,12},{1,5},{5,9},{9,13},{2,6},{6,10},{10,14},{3,7},{... | collective-permute-start | bytes 737288 | tf_op jit(solution)/shard_map/ppermute | solution.py:14
  123.4 46.8 %collective-permute-start.11 = (f32[16,15,256]{2,1,0:T(8,128)}, f32[16,15,256]{2,1,0:T(8,128)}, u32[]{:S(2)}, u32[]{:S(2)}) collective-permute-start(f32[16,15,256]{2,1,0:T(8,128)} %get-tuple-element.78), channel_id=1, source_target_pairs={{4,0},{8,4},{12,8},{5,1},{9,5},{13,9},{6,2},{10,6},{14,10},{7,3},{... | collective-permute-start | bytes 737288 | tf_op jit(solution)/shard_map/ppermute | solution.py:17
  161.6 8.6 %copy-start.2 = (f32[16,64,256]{2,1,0:T(8,128)}, f32[16,64,256]{2,1,0:T(8,128)S(1)}, u32[]{:S(2)}) copy-start(f32[16,64,256]{2,1,0:T(8,128)S(1)} %fusion.518) | copy-start | bytes 3145732
  161.6 8.6 %collective-permute-start.6 = (f32[16,15,256]{2,1,0:T(8,128)S(1)}, f32[16,15,256]{2,1,0:T(8,128)}, u32[]{:S(2)}, u32[]{:S(2)}) collective-permute-start(f32[16,15,256]{2,1,0:T(8,128)S(1)} %get-tuple-element.79), channel_id=1, source_target_pairs={{0,4},{4,8},{8,12},{1,5},{5,9},{9,13},{2,6},{6,10},{10,14},{3,7},{... | collective-permute-start | bytes 737288 | tf_op jit(solution)/shard_map/ppermute | solution.py:14
  168.9 4.1 %collective-permute-start.7 = (f32[16,15,256]{2,1,0:T(8,128)S(1)}, f32[16,15,256]{2,1,0:T(8,128)}, u32[]{:S(2)}, u32[]{:S(2)}) collective-permute-start(f32[16,15,256]{2,1,0:T(8,128)S(1)} %get-tuple-element.80), channel_id=1, source_target_pairs={{4,0},{8,4},{12,8},{5,1},{9,5},{13,9},{6,2},{10,6},{14,10},{7,3},{... | collective-permute-start | bytes 737288 | tf_op jit(solution)/shard_map/ppermute | solution.py:17
  201.6 8.2 %collective-permute-start.12 = (f32[16,15,256]{2,1,0:T(8,128)S(1)}, f32[16,15,256]{2,1,0:T(8,128)S(1)}, u32[]{:S(2)}, u32[]{:S(2)}) collective-permute-start(f32[16,15,256]{2,1,0:T(8,128)S(1)} %get-tuple-element.75), channel_id=1, source_target_pairs={{0,4},{4,8},{8,12},{1,5},{5,9},{9,13},{2,6},{6,10},{10,14},{3,7},{... | collective-permute-start | bytes 737288 | tf_op jit(solution)/shard_map/ppermute | solution.py:14
  208.3 3.4 collective-permute-start.13
  227.3 23.3 %collective-permute-start.14 = (f32[15,64,256]{2,1,0:T(8,128)S(1)}, f32[15,64,256]{2,1,0:T(8,128)S(1)}, u32[]{:S(2)}, u32[]{:S(2)}) collective-permute-start(f32[15,64,256]{2,1,0:T(8,128)S(1)} %get-tuple-element.73), channel_id=1, source_target_pairs={{0,1},{1,2},{2,3},{4,5},{5,6},{6,7},{8,9},{9,10},{10,11},{12,13},{... | collective-permute-start | bytes 2949128 | tf_op jit(solution)/shard_map/ppermute | solution.py:14
  231.9 23.4 %collective-permute-start.15 = (f32[15,64,256]{2,1,0:T(8,128)S(1)}, f32[15,64,256]{2,1,0:T(8,128)S(1)}, u32[]{:S(2)}, u32[]{:S(2)}) collective-permute-start(f32[15,64,256]{2,1,0:T(8,128)S(1)} %get-tuple-element.74), channel_id=1, source_target_pairs={{1,0},{2,1},{3,2},{5,4},{6,5},{7,6},{9,8},{10,9},{11,10},{13,12},{... | collective-permute-start | bytes 2949128 | tf_op jit(solution)/shard_map/ppermute | solution.py:17
  279.4 22.6 %collective-permute-start.16 = (f32[15,64,256]{2,1,0:T(8,128)S(1)}, f32[15,64,256]{2,1,0:T(8,128)S(1)}, u32[]{:S(2)}, u32[]{:S(2)}) collective-permute-start(f32[15,64,256]{2,1,0:T(8,128)S(1)} %get-tuple-element.71), channel_id=1, source_target_pairs={{0,1},{1,2},{2,3},{4,5},{5,6},{6,7},{8,9},{9,10},{10,11},{12,13},{... | collective-permute-start | bytes 2949128 | tf_op jit(solution)/shard_map/ppermute | solution.py:14
  281.9 24.8 %collective-permute-start.17 = (f32[15,64,256]{2,1,0:T(8,128)S(1)}, f32[15,64,256]{2,1,0:T(8,128)S(1)}, u32[]{:S(2)}, u32[]{:S(2)}) collective-permute-start(f32[15,64,256]{2,1,0:T(8,128)S(1)} %get-tuple-element.72), channel_id=1, source_target_pairs={{1,0},{2,1},{3,2},{5,4},{6,5},{7,6},{9,8},{10,9},{11,10},{13,12},{... | collective-permute-start | bytes 2949128 | tf_op jit(solution)/shard_map/ppermute | solution.py:17
  330.5 16.3 %copy-start.3 = (f32[16,64,256]{2,1,0:T(8,128)S(1)}, f32[16,64,256]{2,1,0:T(8,128)}, u32[]{:S(2)}) copy-start(f32[16,64,256]{2,1,0:T(8,128)} %get-tuple-element.68) | copy-start | bytes 3145732
  330.5 16.3 %copy-start.6 = (f32[16]{0:T(128)S(1)}, f32[16]{0:T(128)}, u32[]{:S(2)}) copy-start(f32[16]{0:T(128)} %copy-done.5) | copy-start | bytes 196
  330.5 16.3 %copy-start.8 = (f32[16]{0:T(128)S(1)}, f32[16]{0:T(128)}, u32[]{:S(2)}) copy-start(f32[16]{0:T(128)} %copy-done.7) | copy-start | bytes 196
  330.5 16.3 %copy-start.10 = (f32[16]{0:T(128)S(1)}, f32[16]{0:T(128)}, u32[]{:S(2)}) copy-start(f32[16]{0:T(128)} %copy-done.9) | copy-start | bytes 196
  330.5 16.3 %copy-start.12 = (f32[16]{0:T(128)S(1)}, f32[16]{0:T(128)}, u32[]{:S(2)}) copy-start(f32[16]{0:T(128)} %copy-done.11) | copy-start | bytes 196
  330.5 16.3 %copy-start.14 = (f32[16]{0:T(128)S(1)}, f32[16]{0:T(128)}, u32[]{:S(2)}) copy-start(f32[16]{0:T(128)} %copy-done.13) | copy-start | bytes 196
  330.5 16.3 %copy-start.16 = (f32[16]{0:T(128)S(1)}, f32[16]{0:T(128)}, u32[]{:S(2)}) copy-start(f32[16]{0:T(128)} %copy-done.15) | copy-start | bytes 196
  330.5 16.3 %copy-start.18 = (f32[16]{0:T(128)S(1)}, f32[16]{0:T(128)}, u32[]{:S(2)}) copy-start(f32[16]{0:T(128)} %copy-done.17) | copy-start | bytes 196
  330.5 16.3 %copy-start.20 = (f32[16]{0:T(128)S(1)}, f32[16]{0:T(128)}, u32[]{:S(2)}) copy-start(f32[16]{0:T(128)} %copy-done.19) | copy-start | bytes 196
  330.6 16.3 %copy-start.22 = (f32[16]{0:T(128)S(1)}, f32[16]{0:T(128)}, u32[]{:S(2)}) copy-start(f32[16]{0:T(128)} %copy-done.21) | copy-start | bytes 196
  330.6 16.3 %copy-start.24 = (f32[16]{0:T(128)S(1)}, f32[16]{0:T(128)}, u32[]{:S(2)}) copy-start(f32[16]{0:T(128)} %copy-done.23) | copy-start | bytes 196
  330.6 16.3 %copy-start.26 = (f32[16]{0:T(128)S(1)}, f32[16]{0:T(128)}, u32[]{:S(2)}) copy-start(f32[16]{0:T(128)} %copy-done.25) | copy-start | bytes 196
  330.6 16.3 %copy-start.28 = (f32[16]{0:T(128)S(1)}, f32[16]{0:T(128)}, u32[]{:S(2)}) copy-start(f32[16]{0:T(128)} %copy-done.27) | copy-start | bytes 196
  330.6 16.3 %copy-start.30 = (f32[16]{0:T(128)S(1)}, f32[16]{0:T(128)}, u32[]{:S(2)}) copy-start(f32[16]{0:T(128)} %copy-done.29) | copy-start | bytes 196
  330.6 16.3 %copy-start.32 = (f32[16]{0:T(128)S(1)}, f32[16]{0:T(128)}, u32[]{:S(2)}) copy-start(f32[16]{0:T(128)} %copy-done.31) | copy-start | bytes 196
  330.6 16.3 %copy-start.34 = (f32[16]{0:T(128)S(1)}, f32[16]{0:T(128)}, u32[]{:S(2)}) copy-start(f32[16]{0:T(128)} %copy-done.33) | copy-start | bytes 196
  330.6 16.3 %copy-start.36 = (f32[16]{0:T(128)S(1)}, f32[16]{0:T(128)}, u32[]{:S(2)}) copy-start(f32[16]{0:T(128)} %copy-done.35) | copy-start | bytes 196
  330.6 16.3 %copy-start.38 = (f32[16]{0:T(128)S(1)}, f32[16]{0:T(128)}, u32[]{:S(2)}) copy-start(f32[16]{0:T(128)} %copy-done.37) | copy-start | bytes 196
  330.6 16.3 %copy-start.40 = (f32[16]{0:T(128)S(1)}, f32[16]{0:T(128)}, u32[]{:S(2)}) copy-start(f32[16]{0:T(128)} %copy-done.39) | copy-start | bytes 196
  330.7 16.3 %copy-start.42 = (f32[16]{0:T(128)S(1)}, f32[16]{0:T(128)}, u32[]{:S(2)}) copy-start(f32[16]{0:T(128)} %copy-done.41) | copy-start | bytes 196
  330.7 16.3 %copy-start.44 = (f32[16]{0:T(128)S(1)}, f32[16]{0:T(128)}, u32[]{:S(2)}) copy-start(f32[16]{0:T(128)} %copy-done.43) | copy-start | bytes 196
  330.7 16.3 %copy-start.46 = (f32[16]{0:T(128)S(1)}, f32[16]{0:T(128)}, u32[]{:S(2)}) copy-start(f32[16]{0:T(128)} %copy-done.45) | copy-start | bytes 196
  330.7 16.3 %copy-start.48 = (f32[16]{0:T(128)S(1)}, f32[16]{0:T(128)}, u32[]{:S(2)}) copy-start(f32[16]{0:T(128)} %copy-done.47) | copy-start | bytes 196
  330.7 16.3 %copy-start.50 = (f32[16]{0:T(128)S(1)}, f32[16]{0:T(128)}, u32[]{:S(2)}) copy-start(f32[16]{0:T(128)} %copy-done.49) | copy-start | bytes 196
  330.7 16.3 %copy-start.52 = (f32[16]{0:T(128)S(1)}, f32[16]{0:T(128)}, u32[]{:S(2)}) copy-start(f32[16]{0:T(128)} %copy-done.51) | copy-start | bytes 196
  330.7 16.3 %copy-start.54 = (f32[16]{0:T(128)S(1)}, f32[16]{0:T(128)}, u32[]{:S(2)}) copy-start(f32[16]{0:T(128)} %copy-done.53) | copy-start | bytes 196
  330.7 16.3 %copy-start.56 = (f32[16]{0:T(128)S(1)}, f32[16]{0:T(128)}, u32[]{:S(2)}) copy-start(f32[16]{0:T(128)} %copy-done.55) | copy-start | bytes 196
  330.7 16.3 %copy-start.58 = (f32[16]{0:T(128)S(1)}, f32[16]{0:T(128)}, u32[]{:S(2)}) copy-start(f32[16]{0:T(128)} %copy-done.57) | copy-start | bytes 196
  330.7 16.3 %copy-start.60 = (f32[16]{0:T(128)S(1)}, f32[16]{0:T(128)}, u32[]{:S(2)}) copy-start(f32[16]{0:T(128)} %copy-done.59) | copy-start | bytes 196
  339.9 4.8 %collective-permute-start.18 = (f32[16,15,256]{2,1,0:T(8,128)S(1)}, f32[16,15,256]{2,1,0:T(8,128)S(1)}, u32[]{:S(2)}, u32[]{:S(2)}) collective-permute-start(f32[16,15,256]{2,1,0:T(8,128)S(1)} %get-tuple-element.69), channel_id=1, source_target_pairs={{0,4},{4,8},{8,12},{1,5},{5,9},{9,13},{2,6},{6,10},{10,14},{3,7},{... | collective-permute-start | bytes 737288 | tf_op jit(solution)/shard_map/ppermute | solution.py:14
  343.3 3.4 collective-permute-start.19
  (19 other events, 28.8 us)
where the time goes:
time: 359 us; the launch traced here: 353 us
  other arithmetic  218 us (61%)
  waiting for transfers between devices  68.7 us (19%)
  starting transfers between devices  57.8 us (16%)
  local copies, waits for them, and re-layouts  6.71 us (2%)
    add x10, other arithmetic, correlate(): total = term if total is None else total + term  135 us
    ppermute x10, waiting for transfers between devices, padded_2(): lax.ppermute(lax.slice_in_dim(block, block.shape[dim] - width, None, axis...  47.8 us
    div x2, other arithmetic, on_device(): ratio = observed / blurred  47.6 us
    ppermute x10, starting transfers between devices, padded_2(): lax.ppermute(lax.slice_in_dim(block, block.shape[dim] - width, None, axis...  44.7 us
    div x2, other arithmetic, on_device(): estimate = estimate * adjoint(ratio, plane_x, plane_y, taps_z) / norm  34.6 us
    ppermute x10, waiting for transfers between devices, padded_2(): lax.ppermute(lax.slice_in_dim(block, 0, width, axis=dim), axis, backward)  20.8 us
    ppermute x10, starting transfers between devices, padded_2(): lax.ppermute(lax.slice_in_dim(block, 0, width, axis=dim), axis, backward)  13.1 us
  transfers between devices with their start and end apart: 20, of which 9 were waited for; matrix products, arithmetic and copies ran while one was open for 29% of the time, Pallas kernels for 0%

commit v1 on v0

v1 whole, which is shorter than its diff:
```python
import functools

import jax
import jax.numpy as jnp
from jax import lax
from jax.experimental import pallas as pl
from jax.experimental.pallas import tpu as pltpu
from jax.sharding import PartitionSpec as P

ITERS = 2
F32 = jnp.float32
BF16 = jnp.bfloat16
VMEM_LIMIT = 40 * 1024 * 1024
SMEM = pl.BlockSpec(memory_space=pltpu.SMEM)


def up(value, step):
    return -(-value // step) * step


def split(x):
    hi = x.astype(BF16)
    return hi, (x - hi.astype(F32)).astype(BF16)


def mm(a, b, transposed=False):
    dims = (((1,), (1 if transposed else 0,)), ((), ()))
    return lax.dot_general(a, b, dims, preferred_element_type=F32)


def blur_rows(w_hi, w_lo, v_hi, v_lo):
    count = w_hi.shape[0]
    both = mm(jnp.concatenate([w_hi, w_lo], axis=0), v_hi)
    return both[:count] + both[count:] + mm(w_hi, v_lo)


def blur_columns(u, a_hi, a_lo, transposed):
    count = u.shape[0]
    u_hi, u_lo = split(u)
    both = mm(jnp.concatenate([u_hi, u_lo], axis=0), a_hi, transposed)
    return both[:count] + both[count:] + mm(u_hi, a_lo, transposed)


def full(shape):
    return pl.BlockSpec(shape, lambda i: (0,) * len(shape))


def planes(shape, per):
    return pl.BlockSpec((per,) + shape[1:], lambda i: (i,) + (0,) * (len(shape) - 1))


def spread(ref, band, lanes, shape, radius, flip):
    base = jnp.zeros(shape, F32)
    for k in range(2 * radius + 1):
        base = jnp.where(lanes == (2 * radius - k if flip else k), ref[band, k], base)
    return base


def row_matrix(base, rows, radius, width):
    parts = []
    for first in range(0, rows, 16):
        parts.append(
            pltpu.roll(base, (first - radius) % width, 1, stride=1, stride_axis=0)
        )
    return jnp.concatenate(parts, axis=0)


def forward_weights_kernel(per, radius, band_ref, tx_ref, ty_ref, ah_ref, al_ref, wx_ref):
    rows, width = wx_ref.shape[2], wx_ref.shape[3]
    columns = ah_ref.shape[1]
    lanes = lax.broadcasted_iota(jnp.int32, (16, 128), 1)
    offset = lanes - lax.broadcasted_iota(jnp.int32, (16, 128), 0)
    wide = lax.broadcasted_iota(jnp.int32, (16, width), 1)
    for p in range(per):
        band = band_ref[pl.program_id(0) * per + p]
        base = spread(ty_ref, band, lanes, (16, 128), radius, False)
        rolled = {}
        for first in range(0, columns, 16):
            key = first % 128
            if key not in rolled:
                rolled[key] = pltpu.roll(
                    base, (key - radius) % 128, 1, stride=1, stride_axis=0
                )
            for left in range(0, columns, 128):
                here = (p, slice(first, first + 16), slice(left, left + 128))
                if left > first + 15 + radius or left + 127 < first - radius:
                    zero = jnp.zeros((16, 128), BF16)
                    ah_ref[here] = zero
                    al_ref[here] = zero
                else:
                    distance = offset + (left - first)
                    tile = jnp.where(jnp.abs(distance) <= radius, rolled[key], 0.0)
                    hi, lo = split(tile)
                    ah_ref[here] = hi
                    al_ref[here] = lo
        base = spread(tx_ref, band, wide, (16, width), radius, False)
        hi, lo = split(row_matrix(base, rows, radius, width))
        wx_ref[p, 0] = hi
        wx_ref[p, 1] = lo


def forward_weights(band_index, taps_x, taps_y, n, rows, columns, width, per):
    radius = taps_x.shape[1] // 2
    a = jax.ShapeDtypeStruct((n, columns, columns), BF16)
    w = jax.ShapeDtypeStruct((n, 2, rows, width), BF16)
    return pl.pallas_call(
        functools.partial(forward_weights_kernel, per, radius),
        grid=(n // per,),
        in_specs=[SMEM] * 3,
        out_specs=[planes(a.shape, per), planes(a.shape, per), planes(w.shape, per)],
        out_shape=[a, a, w],
        compiler_params=pltpu.CompilerParams(vmem_limit_bytes=VMEM_LIMIT),
    )(band_index, taps_x, taps_y)


def adjoint_weights_kernel(
    per, radius, halo, depth, place_ref, band_ref, tx_ref, tz_ref, ah_ref, al_ref, wx_ref, rn_ref
):
    rows, width = wx_ref.shape[2], wx_ref.shape[3]
    wide = lax.broadcasted_iota(jnp.int32, (16, width), 1)
    at = lax.broadcasted_iota(jnp.int32, (rows, width), 1)
    own = at < rows
    above = (at < width - halo) & (place_ref[2] != 0)
    below = (at >= width - halo) & (place_ref[1] != 0)
    valid = own | above | below
    for p in range(per):
        plane = pl.program_id(0) * per + p
        band = band_ref[plane]
        base = spread(tx_ref, band, wide, (16, width), radius, True)
        matrix = row_matrix(base, rows, radius, width)
        hi, lo = split(matrix)
        wx_ref[p, 0] = hi
        wx_ref[p, 1] = lo
        along_x = jnp.sum(jnp.where(valid, matrix, 0.0), axis=1, keepdims=True)
        columns = ah_ref[p].astype(F32) + al_ref[p].astype(F32)
        along_y = jnp.sum(columns, axis=0, keepdims=True)
        along_z = jnp.float32(0.0)
        z = place_ref[0] + plane
        for k in range(2 * radius + 1):
            source = z - k + radius
            inside = (source >= 0) & (source < depth)
            along_z = along_z + jnp.where(inside, tz_ref[k], 0.0)
        rn_ref[p] = 1.0 / (along_x * (along_y * along_z))


def adjoint_weights(place, band_index, taps_x, taps_z, ah, al, rows, width, halo, depth, per):
    radius = taps_x.shape[1] // 2
    n, columns = ah.shape[:2]
    w = jax.ShapeDtypeStruct((n, 2, rows, width), BF16)
    r = jax.ShapeDtypeStruct((n, rows, columns), F32)
    return pl.pallas_call(
        functools.partial(adjoint_weights_kernel, per, radius, halo, depth),
        grid=(n // per,),
        in_specs=[SMEM] * 4 + [planes(ah.shape, per)] * 2,
        out_specs=[planes(w.shape, per), planes(r.shape, per)],
        out_shape=[w, r],
        compiler_params=pltpu.CompilerParams(vmem_limit_bytes=VMEM_LIMIT),
    )(place, band_index, taps_x, taps_z, ah, al)


def store_sends(v, plane, n, radius, low_ref, high_ref):
    @pl.when(plane < radius)
    def _():
        low_ref[jnp.minimum(plane, radius - 1)] = v

    @pl.when(plane >= n - radius)
    def _():
        high_ref[jnp.maximum(plane - (n - radius), 0)] = v


def interior(est_hi, est_lo, wx_ref, ah_ref, al_ref, p, halo, plane, n, radius, sends):
    rows = est_hi.shape[0]
    w_hi = wx_ref[p, 0, halo : rows - halo, :rows]
    w_lo = wx_ref[p, 1, halo : rows - halo, :rows]
    u = blur_rows(w_hi, w_lo, est_hi, est_lo)
    v = blur_columns(u, ah_ref[p], al_ref[p], True)
    for c in range(0, len(sends), 2):
        part = v[c // 2 * halo : (c // 2 + 1) * halo]
        store_sends(part, plane, n, radius, sends[c], sends[c + 1])


def interior_kernel(per, n, radius, halo, est_ref, wx_ref, ah_ref, al_ref, *sends):
    for p in range(per):
        plane = pl.program_id(0) * per + p
        est_hi, est_lo = split(est_ref[p])
        interior(est_hi, est_lo, wx_ref, ah_ref, al_ref, p, halo, plane, n, radius, sends)


def forward_interior(est, wx, ah, al, halo, radius, per):
    n, rows, columns = est.shape
    send = jax.ShapeDtypeStruct((radius, halo, columns), F32)
    count = 2 * (rows // halo - 2)
    return pl.pallas_call(
        functools.partial(interior_kernel, per, n, radius, halo),
        grid=(n // per,),
        in_specs=[planes(x.shape, per) for x in (est, wx, ah, al)],
        out_specs=[full(send.shape)] * count,
        out_shape=[send] * count,
        compiler_params=pltpu.CompilerParams(vmem_limit_bytes=VMEM_LIMIT),
    )(est, wx, ah, al)


def stacked(own, high, low, width):
    rows, columns = own.shape
    gap = width - rows - high.shape[0] - low.shape[0]
    parts = [own, high]
    if gap:
        parts.append(jnp.zeros((gap, columns), own.dtype))
    return jnp.concatenate(parts + [low], axis=0)


def edge_kernel(
    per, n, radius, halo, est_ref, xlo_ref, xhi_ref, wx_ref, ah_ref, al_ref, low_ref, high_ref
):
    rows = est_ref.shape[1]
    width = wx_ref.shape[3]
    for p in range(per):
        plane = pl.program_id(0) * per + p
        v_hi, v_lo = split(stacked(est_ref[p], xhi_ref[p], xlo_ref[p], width))
        w_hi = jnp.concatenate([wx_ref[p, 0, :halo], wx_ref[p, 0, rows - halo :]], axis=0)
        w_lo = jnp.concatenate([wx_ref[p, 1, :halo], wx_ref[p, 1, rows - halo :]], axis=0)
        u = blur_rows(w_hi, w_lo, v_hi, v_lo)
        v = blur_columns(u, ah_ref[p], al_ref[p], True)
        store_sends(v, plane, n, radius, low_ref, high_ref)


def forward_edge(est, xlo, xhi, wx, ah, al, halo, radius, per):
    n, rows, columns = est.shape
    send = jax.ShapeDtypeStruct((radius, 2 * halo, columns), F32)
    return pl.pallas_call(
        functools.partial(edge_kernel, per, n, radius, halo),
        grid=(n // per,),
        in_specs=[planes(x.shape, per) for x in (est, xlo, xhi, wx, ah, al)],
        out_specs=[full(send.shape)] * 2,
        out_shape=[send] * 2,
        compiler_params=pltpu.CompilerParams(vmem_limit_bytes=VMEM_LIMIT),
    )(est, xlo, xhi, wx, ah, al)


def depth_sum(n, radius, flip, tz_ref, low_ref, high_ref, zlo_ref, zhi_ref, rows, lanes):
    last = 2 * radius
    taps = [tz_ref[last - k if flip else k] for k in range(last + 1)]
    total = [None] * n
    for j in range(-radius, n + radius):
        if j < 0:
            piece = zlo_ref[j + radius, rows, lanes]
        elif j < radius:
            piece = low_ref[j, rows, lanes]
        elif j < n:
            piece = high_ref[j - (n - radius), rows, lanes]
        else:
            piece = zhi_ref[j - n, rows, lanes]
        for i in range(max(0, j - radius), min(n, j + radius + 1)):
            term = taps[j - i + radius] * piece
            total[i] = term if total[i] is None else total[i] + term
    return total


def ratio_kernel(
    n, radius, tz_ref, low_ref, high_ref, zlo_ref, zhi_ref, obs_ref, rlow_ref, rhigh_ref
):
    halo, columns = obs_ref.shape[1:]

    def body(t, carry):
        rows = pl.ds(pl.multiple_of(t * 8, 8), 8)
        for left in range(0, columns, 128):
            lanes = slice(left, left + 128)
            total = depth_sum(
                n, radius, False, tz_ref, low_ref, high_ref, zlo_ref, zhi_ref, rows, lanes
            )
            for i in range(n):
                ratio = obs_ref[i, rows, lanes] / total[i]
                if i < radius:
                    rlow_ref[i, rows, lanes] = ratio
                if i >= n - radius:
                    rhigh_ref[i - (n - radius), rows, lanes] = ratio
        return carry

    lax.fori_loop(0, halo // 8, body, 0)


def depth_ratio(taps_z, low, high, zlo, zhi, obs, first, step, halo):
    n, _, columns = obs.shape
    radius, count = low.shape[:2]
    part = pl.BlockSpec((radius, halo, columns), lambda i: (0, i, 0))
    send = jax.ShapeDtypeStruct(low.shape, F32)
    return pl.pallas_call(
        functools.partial(ratio_kernel, n, radius),
        grid=(count // halo,),
        in_specs=[SMEM]
        + [part] * 4
        + [pl.BlockSpec((n, halo, columns), lambda i: (0, first + step * i, 0))],
        out_specs=[part] * 2,
        out_shape=[send] * 2,
        compiler_params=pltpu.CompilerParams(vmem_limit_bytes=VMEM_LIMIT),
    )(taps_z, low, high, zlo, zhi, obs)


def back_kernel(n, radius, tz_ref, low_ref, high_ref, zlo_ref, zhi_ref, *out_refs):
    halo, columns = out_refs[0].shape[1:]

    def run(out_ref):
        def body(t, carry):
            rows = pl.ds(pl.multiple_of(t * 8, 8), 8)
            for left in range(0, columns, 128):
                lanes = slice(left, left + 128)
                total = depth_sum(
                    n, radius, True, tz_ref, low_ref, high_ref, zlo_ref, zhi_ref, rows, lanes
                )
                for i in range(n):
                    out_ref[i, rows, lanes] = total[i]
            return carry

        lax.fori_loop(0, halo // 8, body, 0)

    if len(out_refs) == 1:
        run(out_refs[0])
    else:
        for s, out_ref in enumerate(out_refs):
            pl.when(pl.program_id(0) == s)(functools.partial(run, out_ref))


def depth_back(taps_z, low, high, zlo, zhi, n, halo):
    radius, count, columns = low.shape
    part = pl.BlockSpec((radius, halo, columns), lambda i: (0, i, 0))
    out = jax.ShapeDtypeStruct((n, halo, columns), F32)
    return pl.pallas_call(
        functools.partial(back_kernel, n, radius),
        grid=(count // halo,),
        in_specs=[SMEM] + [part] * 4,
        out_specs=[full(out.shape)] * (count // halo),
        out_shape=[out] * (count // halo),
        compiler_params=pltpu.CompilerParams(vmem_limit_bytes=VMEM_LIMIT),
    )(taps_z, low, high, zlo, zhi)


def update_kernel(per, n, radius, halo, pieces, last, *refs):
    c_refs, refs = refs[:pieces], refs[pieces:]
    xlo_ref, xhi_ref, est_ref, rn_ref, wa_ref, ah_ref, al_ref = refs[:7]
    refs = refs[7:]
    rows = est_ref.shape[1]
    width = wa_ref.shape[3]
    if last:
        (out_ref,) = refs
    else:
        wx_ref, out_ref, top_ref, bottom_ref = refs[:4]
        sends = refs[4:]
    for p in range(per):
        plane = pl.program_id(0) * per + p
        own = jnp.concatenate([c_ref[p] for c_ref in c_refs], axis=0)
        c_hi, c_lo = split(stacked(own, xhi_ref[p], xlo_ref[p], width))
        u = blur_rows(wa_ref[p, 0], wa_ref[p, 1], c_hi, c_lo)
        u = blur_columns(u, ah_ref[p], al_ref[p], False)
        est = est_ref[p] * u * rn_ref[p]
        out_ref[p] = est
        if not last:
            top_ref[p] = est[:halo]
            bottom_ref[p] = est[rows - halo :]
            est_hi, est_lo = split(est)
            interior(est_hi, est_lo, wx_ref, ah_ref, al_ref, p, halo, plane, n, radius, sends)


def update(pieces, xlo, xhi, est, rn, wa, ah, al, wx, halo, radius, per):
    n, rows, columns = est.shape
    last = wx is None
    args = list(pieces) + [xlo, xhi, est, rn, wa, ah, al] + ([] if last else [wx])
    out = jax.ShapeDtypeStruct(est.shape, F32)
    out_specs, out_shape = [planes(out.shape, per)], [out]
    if not last:
        edge = jax.ShapeDtypeStruct((n, halo, columns), F32)
        send = jax.ShapeDtypeStruct((radius, halo, columns), F32)
        count = 2 * (rows // halo - 2)
        out_specs += [planes(edge.shape, per)] * 2 + [full(send.shape)] * count
        out_shape += [edge] * 2 + [send] * count
    return pl.pallas_call(
        functools.partial(update_kernel, per, n, radius, halo, len(pieces), last),
        grid=(n // per,),
        in_specs=[planes(x.shape, per) for x in args],
        out_specs=out_specs,
        out_shape=out_shape,
        compiler_params=pltpu.CompilerParams(vmem_limit_bytes=VMEM_LIMIT),
    )(*args)


def exchange(first, last, axis):
    count = lax.axis_size(axis)
    forward = [(i, i + 1) for i in range(count - 1)]
    backward = [(i + 1, i) for i in range(count - 1)]
    return lax.ppermute(last, axis, forward), lax.ppermute(first, axis, backward)


def on_device(observed, band_index, taps_x, taps_y, taps_z):
    n, rows, columns = observed.shape
    radius = taps_z.shape[0] // 2
    halo = up(radius, 16)
    width = up(rows + 2 * halo, 128)
    per = 4 if n % 4 == 0 else 1
    depth = n * lax.axis_size("slab")
    row, row_count = lax.axis_index("row"), lax.axis_size("row")
    place = jnp.stack(
        [lax.axis_index("slab") * n, row, row_count - 1 - row]
    ).astype(jnp.int32)
    inner = rows // halo - 2

    top, bottom = observed[:, :halo], observed[:, rows - halo :]
    xlo, xhi = exchange(top, bottom, "row")
    ah, al, wx = forward_weights(
        band_index, taps_x, taps_y, n, rows, columns, width, per
    )
    est = observed
    sends = forward_interior(est, wx, ah, al, halo, radius, per)
    wa = None
    for step in range(ITERS):
        chunks = []
        for c in range(inner):
            low, high = sends[2 * c], sends[2 * c + 1]
            zlo, zhi = exchange(low, high, "slab")
            chunks.append((low, high, zlo, zhi, 1 + c, 1))
        low, high = forward_edge(est, xlo, xhi, wx, ah, al, halo, radius, per)
        zlo, zhi = exchange(low, high, "slab")
        chunks.insert(1, (low, high, zlo, zhi, 0, rows // halo - 1))
        if wa is None:
            wa, rn = adjoint_weights(
                place, band_index, taps_x, taps_z, ah, al, rows, width, halo, depth, per
            )
        ratios = []
        for low, high, zlo, zhi, first, stride in chunks:
            low, high = depth_ratio(
                taps_z, low, high, zlo, zhi, observed, first, stride, halo
            )
            zlo, zhi = exchange(low, high, "slab")
            ratios.append((low, high, zlo, zhi))
        inside = []
        for c, (low, high, zlo, zhi) in enumerate(ratios):
            out = depth_back(taps_z, low, high, zlo, zhi, n, halo)
            if c == 1:
                top, bottom = out
                xlo, xhi = exchange(top, bottom, "row")
            else:
                inside += out
        pieces = [top] + inside + [bottom]
        last = step == ITERS - 1
        out = update(
            pieces, xlo, xhi, est, rn, wa, ah, al, None if last else wx, halo, radius, per
        )
        est = out[0]
        if not last:
            xlo, xhi = exchange(out[1], out[2], "row")
            sends = out[3:]
    return est


def solution(mesh):
    in_specs = (P(("grp", "slab"), "row", None), P("slab"), P(), P(), P())
    out_specs = P(("grp", "slab"), "row", None)
    return jax.shard_map(
        on_device, mesh=mesh, in_specs=in_specs, out_specs=out_specs, check_vma=False
    )
```

time: 359 us -> 192 us (0.53); the launches traced: 353 us -> 191 us
  other arithmetic: 218 us -> 0.08 us
  Pallas kernels: 0 us -> 55.4 us
  starting transfers between devices: 57.8 us -> 91.9 us
  waiting for transfers between devices: 68.7 us -> 35.6 us
    add x10 -> x0, other arithmetic: 135 us -> none  [correlate(): total = term if total is None else total + term]
    div x4 -> x0, other arithmetic: 82.2 us -> none  [the longest x2 47.6 us: on_device(): ratio = observed / blurred]
    pallas_call x0 -> x19, Pallas kernels: none -> 55.4 us  [the longest x2 14.7 us: update(): pl.pallas_call(functools.partial(update_kernel, per, n, radius, halo, len...]
    ppermute x20 -> x32, starting transfers between devices: 57.8 us -> 91.9 us  [the longest x16 71 us: exchange(): lax.ppermute(last, axis, forward)]
    ppermute x20 -> x32, waiting for transfers between devices: 68.7 us -> 35.6 us  [the longest x16 30.5 us: exchange(): lax.ppermute(first, axis, backward)]
    unnamed x127 -> x30, local copies, waits for them, and re-layouts: 0.36 us -> 6.35 us
    slice x15 -> x1, local copies, waits for them, and re-layouts: 6.24 us -> 1.07 us  [on_device(): top, bottom = (observed[:, :halo], observed[:, rows - halo:])]
  transfers between devices with their start and end apart: 20 -> 32, of which waited for: 9 -> 9; matrix products, arithmetic and copies ran while one was open for 29% -> 0% of each run, Pallas kernels for 0% -> 13%
where the time goes in v1:
time: 192 us; the launch traced here: 191 us
  starting transfers between devices  91.9 us (48%)
  Pallas kernels  55.4 us (29%)
  waiting for transfers between devices  35.6 us (19%)
  local copies, waits for them, and re-layouts  7.42 us (4%)
    ppermute x16, starting transfers between devices, exchange(): lax.ppermute(last, axis, forward)  71 us
    ppermute x16, waiting for transfers between devices, exchange(): lax.ppermute(first, axis, backward)  30.5 us
    ppermute x16, starting transfers between devices, exchange(): lax.ppermute(first, axis, backward)  20.9 us
    pallas_call x2, Pallas kernels, update(): pl.pallas_call(functools.partial(update_kernel, per, n, radius, halo, len...  14.7 us
    pallas_call x2, Pallas kernels, forward_edge(): pl.pallas_call(functools.partial(edge_kernel, per, n, radius, halo), grid...  11.1 us
    pallas_call x6, Pallas kernels, depth_ratio(): pl.pallas_call(functools.partial(ratio_kernel, n, radius), grid=(count //...  10.4 us
    pallas_call x6, Pallas kernels, depth_back(): pl.pallas_call(functools.partial(back_kernel, n, radius), grid=(count //...  9.75 us
    unnamed x30, local copies, waits for them, and re-layouts  6.35 us
  transfers between devices with their start and end apart: 32, of which 9 were waited for; matrix products, arithmetic and copies ran while one was open for 0% of the time, Pallas kernels for 13%

profile of v1, /device:TPU:0, one launch (start us, length us, event | category | flops | bytes accessed | tf_op | source)
XLA Modules:
  0.0 190.9 jit_solution(10897723080083869154)
XLA Ops:
  0.0 1.1 fusion
  1.1 1.3 collective-permute-start.1
  2.4 3.0 %collective-permute-start = (f32[16,16,256]{2,1,0:T(8,128)S(1)}, f32[16,16,256]{2,1,0:T(8,128)S(1)}, u32[]{:S(2)}, u32[]{:S(2)}) collective-permute-start(f32[16,16,256]{2,1,0:T(8,128)S(1)} %get-tuple-element.78), channel_id=1, source_target_pairs={{0,4},{4,8},{8,12},{1,5},{5,9},{9,13},{2,6},{6,10},{10,14},{3,7},{... | collective-permute-start | bytes 786440 | tf_op jit(solution)/shard_map/ppermute | solution.py:389
  7.5 2.0 %shard_map.55 = (bf16[16,256,256]{2,1,0:T(8,128)(2,1)S(1)}, bf16[16,256,256]{2,1,0:T(8,128)(2,1)S(1)}, bf16[16,2,64,128]{3,2,1,0:T(8,128)(2,1)S(1)}) custom-call(s32[16]{0:T(128)S(1)} %copy-done.13, f32[16,31]{1,0:T(8,128)S(1)} %copy-done.10, f32[16,31]{1,0:T(8,128)S(1)} %copy-done.12), custom_call_target="tpu_custom_call" | custom-call | tf_op jit(solution)/shard_map/pallas_call | solution.py:106
  9.6 2.0 %copy-done = f32[16,64,256]{2,1,0:T(8,128)S(1)} copy-done((f32[16,64,256]{2,1,0:T(8,128)S(1)}, f32[16,64,256]{2,1,0:T(8,128)}, u32[]{:S(2)}) %copy-start) | copy-done | bytes 1048600
  11.5 5.5 %shard_map.56 = (f32[15,32,256]{2,1,0:T(8,128)S(1)}, f32[15,32,256]{2,1,0:T(8,128)S(1)}) custom-call(f32[16,64,256]{2,1,0:T(8,128)S(1)} %copy-done, f32[16,16,256]{2,1,0:T(8,128)S(1)} %collective-permute-done.xlo_ref, f32[16,16,256]{2,1,0:T(8,128)S(1)} %collective-permute-done.1.xhi_ref, bf16[16,2,64,128]{3,2,1,0:T(8,128)(2,1)S(1)} %get-tuple-element.41.wx_ref.refs_11_, ...), custom_call_target="tpu_custom_call" | custom-call | tf_op jit(solution)/shard_map/pallas_call | solution.py:230
  17.1 1.3 collective-permute-start.3
  18.4 5.6 %collective-permute-start.2 = (f32[15,32,256]{2,1,0:T(8,128)S(1)}, f32[15,32,256]{2,1,0:T(8,128)S(1)}, u32[]{:S(2)}, u32[]{:S(2)}) collective-permute-start(f32[15,32,256]{2,1,0:T(8,128)S(1)} %get-tuple-element.45.high_ref), channel_id=1, source_target_pairs={{0,1},{1,2},{2,3},{4,5},{5,6},{6,7},{8,9},{9,10},{10,11},{12,13},{... | collective-permute-start | bytes 1474568 | tf_op jit(solution)/shard_map/ppermute | solution.py:389
  24.0 9.6 %collective-permute-done.3.zhi_ref = f32[15,32,256]{2,1,0:T(8,128)S(1)} collective-permute-done((f32[15,32,256]{2,1,0:T(8,128)S(1)}, f32[15,32,256]{2,1,0:T(8,128)S(1)}, u32[]{:S(2)}, u32[]{:S(2)}) %collective-permute-start.3) | collective-permute-done | bytes 491552 | tf_op jit(solution)/shard_map/ppermute | solution.py:389
  33.6 1.7 collective-permute-done.2.zlo_ref
  35.3 2.1 %shard_map.57 = (f32[15,32,256]{2,1,0:T(8,128)S(1)}, f32[15,32,256]{2,1,0:T(8,128)S(1)}) custom-call(f32[31]{0:T(128)S(1)} %copy-done.9, f32[15,32,256]{2,1,0:T(8,128)S(1)} %get-tuple-element.44.low_ref, f32[15,32,256]{2,1,0:T(8,128)S(1)} %get-tuple-element.45.high_ref, f32[15,32,256]{2,1,0:T(8,128)S(1)} %collective-permute-done.2.zlo_ref, ...), custom_call_target="tpu_custom_call" | custom-call | tf_op jit(solution)/shard_map/pallas_call | solution.py:287
  37.4 1.3 collective-permute-start.5
  38.7 5.0 %collective-permute-start.4 = (f32[15,32,256]{2,1,0:T(8,128)S(1)}, f32[15,32,256]{2,1,0:T(8,128)S(1)}, u32[]{:S(2)}, u32[]{:S(2)}) collective-permute-start(f32[15,32,256]{2,1,0:T(8,128)S(1)} %get-tuple-element.47.high_ref), channel_id=1, source_target_pairs={{0,1},{1,2},{2,3},{4,5},{5,6},{6,7},{8,9},{9,10},{10,11},{12,13},{... | collective-permute-start | bytes 1474568 | tf_op jit(solution)/shard_map/ppermute | solution.py:389
  43.7 5.3 %shard_map.59 = (f32[15,16,256]{2,1,0:T(8,128)S(1)}, f32[15,16,256]{2,1,0:T(8,128)S(1)}, f32[15,16,256]{2,1,0:T(8,128)S(1)}, f32[15,16,256]{2,1,0:T(8,128)S(1)}) custom-call(f32[16,64,256]{2,1,0:T(8,128)S(1)} %copy-done, bf16[16,2,64,128]{3,2,1,0:T(8,128)(2,1)S(1)} %get-tuple-element.41.wx_ref.refs_11_, ...), custom_call_target="tpu_custom_call" | custom-call | tf_op jit(solution)/shard_map/pallas_call | solution.py:193
  49.0 1.3 collective-permute-start.7
  50.4 4.7 %collective-permute-start.6 = (f32[15,16,256]{2,1,0:T(8,128)S(1)}, f32[15,16,256]{2,1,0:T(8,128)S(1)}, u32[]{:S(2)}, u32[]{:S(2)}) collective-permute-start(f32[15,16,256]{2,1,0:T(8,128)S(1)} %get-tuple-element.50.high_ref), channel_id=1, source_target_pairs={{0,1},{1,2},{2,3},{4,5},{5,6},{6,7},{8,9},{9,10},{10,11},{12,13},{... | collective-permute-start | bytes 737288 | tf_op jit(solution)/shard_map/ppermute | solution.py:389
  55.1 1.3 collective-permute-start.11
  56.4 2.5 %collective-permute-done.7.zhi_ref = f32[15,16,256]{2,1,0:T(8,128)S(1)} collective-permute-done((f32[15,16,256]{2,1,0:T(8,128)S(1)}, f32[15,16,256]{2,1,0:T(8,128)S(1)}, u32[]{:S(2)}, u32[]{:S(2)}) %collective-permute-start.7) | collective-permute-done | bytes 245792 | tf_op jit(solution)/shard_map/ppermute | solution.py:389
  58.9 3.7 %collective-permute-start.10 = (f32[15,16,256]{2,1,0:T(8,128)S(1)}, f32[15,16,256]{2,1,0:T(8,128)S(1)}, u32[]{:S(2)}, u32[]{:S(2)}) collective-permute-start(f32[15,16,256]{2,1,0:T(8,128)S(1)} %get-tuple-element.54.high_ref), channel_id=1, source_target_pairs={{0,1},{1,2},{2,3},{4,5},{5,6},{6,7},{8,9},{9,10},{10,11},{12,13},{... | collective-permute-start | bytes 737288 | tf_op jit(solution)/shard_map/ppermute | solution.py:389
  62.6 1.9 shard_map.60
  64.5 1.4 collective-permute-start.9
  65.9 1.9 shard_map.58
  67.8 1.3 collective-permute-start.15
  69.1 3.8 %collective-permute-start.14 = (f32[16,16,256]{2,1,0:T(8,128)S(1)}, f32[16,16,256]{2,1,0:T(8,128)}, u32[]{:S(2)}, u32[]{:S(2)}) collective-permute-start(f32[16,16,256]{2,1,0:T(8,128)S(1)} %get-tuple-element.57.refs_3_), channel_id=1, source_target_pairs={{0,4},{4,8},{8,12},{1,5},{5,9},{9,13},{2,6},{6,10},{10,14},{3,7},{... | collective-permute-start | bytes 786440 | tf_op jit(solution)/shard_map/ppermute | solution.py:389
  72.9 5.3 %collective-permute-start.8 = (f32[15,16,256]{2,1,0:T(8,128)}, f32[15,16,256]{2,1,0:T(8,128)}, u32[]{:S(2)}, u32[]{:S(2)}) collective-permute-start(f32[15,16,256]{2,1,0:T(8,128)} %get-tuple-element.52.high_ref), channel_id=1, source_target_pairs={{0,1},{1,2},{2,3},{4,5},{5,6},{6,7},{8,9},{9,10},{10,11},{12,13},{... | collective-permute-start | bytes 737288 | tf_op jit(solution)/shard_map/ppermute | solution.py:389
  78.1 2.0 %shard_map.62 = (f32[15,16,256]{2,1,0:T(8,128)}, f32[15,16,256]{2,1,0:T(8,128)}) custom-call(f32[31]{0:T(128)S(1)} %copy-done.9, f32[15,16,256]{2,1,0:T(8,128)S(1)} %get-tuple-element.53.low_ref, f32[15,16,256]{2,1,0:T(8,128)S(1)} %get-tuple-element.54.high_ref, f32[15,16,256]{2,1,0:T(8,128)S(1)} %collective-permute-done.10.zlo_ref, ...), custom_call_target="tpu_custom_call" | custom-call | tf_op jit(solution)/shard_map/pallas_call | solution.py:287
  80.1 1.3 collective-permute-start.13
  81.4 0.7 copy-done.7
  82.1 5.2 %collective-permute-start.12 = (f32[15,16,256]{2,1,0:T(8,128)}, f32[15,16,256]{2,1,0:T(8,128)}, u32[]{:S(2)}, u32[]{:S(2)}) collective-permute-start(f32[15,16,256]{2,1,0:T(8,128)} %get-tuple-element.56.high_ref), channel_id=1, source_target_pairs={{0,1},{1,2},{2,3},{4,5},{5,6},{6,7},{8,9},{9,10},{10,11},{12,13},{... | collective-permute-start | bytes 737288 | tf_op jit(solution)/shard_map/ppermute | solution.py:389
  87.5 1.6 copy-done.3
  89.1 2.1 %shard_map.64 = (bf16[16,2,64,128]{3,2,1,0:T(8,128)(2,1)S(1)}, f32[16,64,256]{2,1,0:T(8,128)S(1)}) custom-call(s32[3]{0:T(128)S(1)} %pad_add_fusion.place_ref, s32[16]{0:T(128)S(1)} %copy-done.14, f32[16,31]{1,0:T(8,128)S(1)} %copy-done.11, f32[31]{0:T(128)S(1)} %copy-done.9, bf16[16,256,256]{2,1,0:T(8,128)(2,1)S(1)} %get-tuple-element.42.ah_ref.refs_9_, ...), custom_call_target="tpu_custom_call" | custom-call | tf_op jit(solution)/shard_map/pallas_call | solution.py:151
  91.2 1.8 shard_map.61.refs_1_
  93.0 1.9 %shard_map.63.refs_2_ = f32[16,16,256]{2,1,0:T(8,128)S(1)} custom-call(f32[31]{0:T(128)S(1)} %copy-done.9, f32[15,16,256]{2,1,0:T(8,128)} %get-tuple-element.55.low_ref, f32[15,16,256]{2,1,0:T(8,128)} %get-tuple-element.56.high_ref, f32[15,16,256]{2,1,0:T(8,128)} %collective-permute-done.12.zlo_ref, f32[15,16,256]{2,1,0:T(8,128)} %collective-permute-done.13.zhi_ref), custom_call_target="tpu_custom_call" | custom-call | tf_op jit(solution)/shard_map/pallas_call | solution.py:327
  95.0 11.3 %shard_map.65 = (f32[16,64,256]{2,1,0:T(8,128)S(1)}, f32[16,16,256]{2,1,0:T(8,128)S(1)}, f32[16,16,256]{2,1,0:T(8,128)S(1)}, f32[15,16,256]{2,1,0:T(8,128)S(1)},...) custom-call(f32[16,16,256]{2,1,0:T(8,128)S(1)} %get-tuple-element.48.refs_0_, ...), custom_call_target="tpu_custom_call" | custom-call | tf_op jit(solution)/shard_map/pallas_call | solution.py:375
  106.3 1.3 collective-permute-start.16
  107.6 1.3 collective-permute-start.17
  109.0 2.1 %collective-permute-done.17.xhi_ref = f32[16,16,256]{2,1,0:T(8,128)S(1)} collective-permute-done((f32[16,16,256]{2,1,0:T(8,128)S(1)}, f32[16,16,256]{2,1,0:T(8,128)S(1)}, u32[]{:S(2)}, u32[]{:S(2)}) %collective-permute-start.17) | collective-permute-done | bytes 262176 | tf_op jit(solution)/shard_map/ppermute | solution.py:389
  111.1 5.5 %shard_map.66 = (f32[15,32,256]{2,1,0:T(8,128)S(1)}, f32[15,32,256]{2,1,0:T(8,128)S(1)}) custom-call(f32[16,64,256]{2,1,0:T(8,128)S(1)} %get-tuple-element.60.est_ref.refs_6_, f32[16,16,256]{2,1,0:T(8,128)S(1)} %collective-permute-done.16.xlo_ref, f32[16,16,256]{2,1,0:T(8,128)S(1)} %collective-permute-done.17.xhi_ref, ...), custom_call_target="tpu_custom_call" | custom-call | tf_op jit(solution)/shard_map/pallas_call | solution.py:230
  116.6 1.3 collective-permute-start.19
  117.9 4.6 %collective-permute-start.18 = (f32[15,32,256]{2,1,0:T(8,128)S(1)}, f32[15,32,256]{2,1,0:T(8,128)S(1)}, u32[]{:S(2)}, u32[]{:S(2)}) collective-permute-start(f32[15,32,256]{2,1,0:T(8,128)S(1)} %get-tuple-element.64.high_ref), channel_id=1, source_target_pairs={{0,1},{1,2},{2,3},{4,5},{5,6},{6,7},{8,9},{9,10},{10,11},{12,13},{... | collective-permute-start | bytes 1474568 | tf_op jit(solution)/shard_map/ppermute | solution.py:389
  122.5 6.9 %collective-permute-done.19.zhi_ref = f32[15,32,256]{2,1,0:T(8,128)S(1)} collective-permute-done((f32[15,32,256]{2,1,0:T(8,128)S(1)}, f32[15,32,256]{2,1,0:T(8,128)S(1)}, u32[]{:S(2)}, u32[]{:S(2)}) %collective-permute-start.19) | collective-permute-done | bytes 491552 | tf_op jit(solution)/shard_map/ppermute | solution.py:389
  129.4 1.7 collective-permute-done.18.zlo_ref
  131.1 2.1 %shard_map.67 = (f32[15,32,256]{2,1,0:T(8,128)S(1)}, f32[15,32,256]{2,1,0:T(8,128)S(1)}) custom-call(f32[31]{0:T(128)S(1)} %copy-done.9, f32[15,32,256]{2,1,0:T(8,128)S(1)} %get-tuple-element.63.low_ref, f32[15,32,256]{2,1,0:T(8,128)S(1)} %get-tuple-element.64.high_ref, f32[15,32,256]{2,1,0:T(8,128)S(1)} %collective-permute-done.18.zlo_ref, ...), custom_call_target="tpu_custom_call" | custom-call | tf_op jit(solution)/shard_map/pallas_call | solution.py:287
  133.2 1.3 collective-permute-start.21
  134.5 5.0 %collective-permute-start.20 = (f32[15,32,256]{2,1,0:T(8,128)S(1)}, f32[15,32,256]{2,1,0:T(8,128)S(1)}, u32[]{:S(2)}, u32[]{:S(2)}) collective-permute-start(f32[15,32,256]{2,1,0:T(8,128)S(1)} %get-tuple-element.66.high_ref), channel_id=1, source_target_pairs={{0,1},{1,2},{2,3},{4,5},{5,6},{6,7},{8,9},{9,10},{10,11},{12,13},{... | collective-permute-start | bytes 1474568 | tf_op jit(solution)/shard_map/ppermute | solution.py:389
  139.5 1.3 collective-permute-start.23
  140.8 4.6 %collective-permute-start.22 = (f32[15,16,256]{2,1,0:T(8,128)S(1)}, f32[15,16,256]{2,1,0:T(8,128)S(1)}, u32[]{:S(2)}, u32[]{:S(2)}) collective-permute-start(f32[15,16,256]{2,1,0:T(8,128)S(1)} %get-tuple-element.69.high_ref), channel_id=1, source_target_pairs={{0,1},{1,2},{2,3},{4,5},{5,6},{6,7},{8,9},{9,10},{10,11},{12,13},{... | collective-permute-start | bytes 737288 | tf_op jit(solution)/shard_map/ppermute | solution.py:389
  145.4 1.3 collective-permute-start.27
  146.7 6.0 %collective-permute-done.23.zhi_ref = f32[15,16,256]{2,1,0:T(8,128)S(1)} collective-permute-done((f32[15,16,256]{2,1,0:T(8,128)S(1)}, f32[15,16,256]{2,1,0:T(8,128)S(1)}, u32[]{:S(2)}, u32[]{:S(2)}) %collective-permute-start.23) | collective-permute-done | bytes 245792 | tf_op jit(solution)/shard_map/ppermute | solution.py:389
  152.8 4.2 %collective-permute-start.26 = (f32[15,16,256]{2,1,0:T(8,128)S(1)}, f32[15,16,256]{2,1,0:T(8,128)S(1)}, u32[]{:S(2)}, u32[]{:S(2)}) collective-permute-start(f32[15,16,256]{2,1,0:T(8,128)S(1)} %get-tuple-element.73.high_ref), channel_id=1, source_target_pairs={{0,1},{1,2},{2,3},{4,5},{5,6},{6,7},{8,9},{9,10},{10,11},{12,13},{... | collective-permute-start | bytes 737288 | tf_op jit(solution)/shard_map/ppermute | solution.py:389
  157.0 1.2 shard_map.69
  158.2 1.3 collective-permute-start.25
  159.5 1.9 shard_map.68
  161.4 1.3 collective-permute-start.31
  162.7 6.2 %collective-permute-start.30 = (f32[16,16,256]{2,1,0:T(8,128)S(1)}, f32[16,16,256]{2,1,0:T(8,128)S(1)}, u32[]{:S(2)}, u32[]{:S(2)}) collective-permute-start(f32[16,16,256]{2,1,0:T(8,128)S(1)} %get-tuple-element.76.refs_3_), channel_id=1, source_target_pairs={{0,4},{4,8},{8,12},{1,5},{5,9},{9,13},{2,6},{6,10},{10,14},{3,7},{... | collective-permute-start | bytes 786440 | tf_op jit(solution)/shard_map/ppermute | solution.py:389
  168.9 4.3 %collective-permute-start.24 = (f32[15,16,256]{2,1,0:T(8,128)S(1)}, f32[15,16,256]{2,1,0:T(8,128)S(1)}, u32[]{:S(2)}, u32[]{:S(2)}) collective-permute-start(f32[15,16,256]{2,1,0:T(8,128)S(1)} %get-tuple-element.71.high_ref), channel_id=1, source_target_pairs={{0,1},{1,2},{2,3},{4,5},{5,6},{6,7},{8,9},{9,10},{10,11},{12,13},{... | collective-permute-start | bytes 737288 | tf_op jit(solution)/shard_map/ppermute | solution.py:389
  173.2 1.2 shard_map.71
  174.3 1.3 collective-permute-start.29
  175.6 4.6 %collective-permute-start.28 = (f32[15,16,256]{2,1,0:T(8,128)S(1)}, f32[15,16,256]{2,1,0:T(8,128)S(1)}, u32[]{:S(2)}, u32[]{:S(2)}) collective-permute-start(f32[15,16,256]{2,1,0:T(8,128)S(1)} %get-tuple-element.75.high_ref), channel_id=1, source_target_pairs={{0,1},{1,2},{2,3},{4,5},{5,6},{6,7},{8,9},{9,10},{10,11},{12,13},{... | collective-permute-start | bytes 737288 | tf_op jit(solution)/shard_map/ppermute | solution.py:389
  180.2 1.1 shard_map.70.refs_1_
  181.4 3.3 %collective-permute-done.29.zhi_ref = f32[15,16,256]{2,1,0:T(8,128)S(1)} collective-permute-done((f32[15,16,256]{2,1,0:T(8,128)S(1)}, f32[15,16,256]{2,1,0:T(8,128)S(1)}, u32[]{:S(2)}, u32[]{:S(2)}) %collective-permute-start.29) | collective-permute-done | bytes 245792 | tf_op jit(solution)/shard_map/ppermute | solution.py:389
  184.7 1.7 collective-permute-done.28.zlo_ref
  186.3 1.1 shard_map.72.refs_2_
  187.5 3.4 %shard_map.73 = f32[16,64,256]{2,1,0:T(8,128)} custom-call(f32[16,16,256]{2,1,0:T(8,128)S(1)} %get-tuple-element.67.refs_0_, f32[16,16,256]{2,1,0:T(8,128)S(1)} %shard_map.70.refs_1_, f32[16,16,256]{2,1,0:T(8,128)S(1)} %shard_map.72.refs_2_, f32[16,16,256]{2,1,0:T(8,128)S(1)} %get-tuple-element.76.refs_3_, ...), custom_call_target="tpu_custom_call" | custom-call | tf_op jit(solution)/shard_map/pallas_call | solution.py:375
  (51 shorter events, 2.2 us)
Async XLA Ops:
  1.1 8.5 %collective-permute-start.1 = (f32[16,16,256]{2,1,0:T(8,128)S(1)}, f32[16,16,256]{2,1,0:T(8,128)S(1)}, u32[]{:S(2)}, u32[]{:S(2)}) collective-permute-start(f32[16,16,256]{2,1,0:T(8,128)S(1)} %get-tuple-element.77), channel_id=1, source_target_pairs={{4,0},{8,4},{12,8},{5,1},{9,5},{13,9},{6,2},{10,6},{14,10},{7,3},{... | collective-permute-start | bytes 786440 | tf_op jit(solution)/shard_map/ppermute | solution.py:389
  2.4 7.2 %collective-permute-start = (f32[16,16,256]{2,1,0:T(8,128)S(1)}, f32[16,16,256]{2,1,0:T(8,128)S(1)}, u32[]{:S(2)}, u32[]{:S(2)}) collective-permute-start(f32[16,16,256]{2,1,0:T(8,128)S(1)} %get-tuple-element.78), channel_id=1, source_target_pairs={{0,4},{4,8},{8,12},{1,5},{5,9},{9,13},{2,6},{6,10},{10,14},{3,7},{... | collective-permute-start | bytes 786440 | tf_op jit(solution)/shard_map/ppermute | solution.py:389
  5.4 0.7 copy-start.10
  6.1 0.7 copy-start.12
  6.8 0.7 copy-start.13
  9.5 34.2 %copy-start.2 = (bf16[16,256,256]{2,1,0:T(8,128)(2,1)}, bf16[16,256,256]{2,1,0:T(8,128)(2,1)S(1)}, u32[]{:S(2)}) copy-start(bf16[16,256,256]{2,1,0:T(8,128)(2,1)S(1)} %get-tuple-element.43.al_ref.refs_10_) | copy-start | bytes 6291460
  9.5 2.0 %copy-start = (f32[16,64,256]{2,1,0:T(8,128)S(1)}, f32[16,64,256]{2,1,0:T(8,128)}, u32[]{:S(2)}) copy-start(f32[16,64,256]{2,1,0:T(8,128)} %obs_ref.11) | copy-start | bytes 3145732
  11.5 23.7 %copy-start.9 = (f32[31]{0:T(128)S(1)}, f32[31]{0:T(128)}, u32[]{:S(2)}) copy-start(f32[31]{0:T(128)} %tz_ref.25) | copy-start | bytes 376
  17.1 16.5 %collective-permute-start.3 = (f32[15,32,256]{2,1,0:T(8,128)S(1)}, f32[15,32,256]{2,1,0:T(8,128)S(1)}, u32[]{:S(2)}, u32[]{:S(2)}) collective-permute-start(f32[15,32,256]{2,1,0:T(8,128)S(1)} %get-tuple-element.44.low_ref), channel_id=1, source_target_pairs={{1,0},{2,1},{3,2},{5,4},{6,5},{7,6},{9,8},{10,9},{11,10},{13,12},{... | collective-permute-start | bytes 1474568 | tf_op jit(solution)/shard_map/ppermute | solution.py:389
  18.4 16.9 %collective-permute-start.2 = (f32[15,32,256]{2,1,0:T(8,128)S(1)}, f32[15,32,256]{2,1,0:T(8,128)S(1)}, u32[]{:S(2)}, u32[]{:S(2)}) collective-permute-start(f32[15,32,256]{2,1,0:T(8,128)S(1)} %get-tuple-element.45.high_ref), channel_id=1, source_target_pairs={{0,1},{1,2},{2,3},{4,5},{5,6},{6,7},{8,9},{9,10},{10,11},{12,13},{... | collective-permute-start | bytes 1474568 | tf_op jit(solution)/shard_map/ppermute | solution.py:389
  37.4 28.5 %collective-permute-start.5 = (f32[15,32,256]{2,1,0:T(8,128)S(1)}, f32[15,32,256]{2,1,0:T(8,128)S(1)}, u32[]{:S(2)}, u32[]{:S(2)}) collective-permute-start(f32[15,32,256]{2,1,0:T(8,128)S(1)} %get-tuple-element.46.low_ref), channel_id=1, source_target_pairs={{1,0},{2,1},{3,2},{5,4},{6,5},{7,6},{9,8},{10,9},{11,10},{13,12},{... | collective-permute-start | bytes 1474568 | tf_op jit(solution)/shard_map/ppermute | solution.py:389
  38.7 27.3 %collective-permute-start.4 = (f32[15,32,256]{2,1,0:T(8,128)S(1)}, f32[15,32,256]{2,1,0:T(8,128)S(1)}, u32[]{:S(2)}, u32[]{:S(2)}) collective-permute-start(f32[15,32,256]{2,1,0:T(8,128)S(1)} %get-tuple-element.47.high_ref), channel_id=1, source_target_pairs={{0,1},{1,2},{2,3},{4,5},{5,6},{6,7},{8,9},{9,10},{10,11},{12,13},{... | collective-permute-start | bytes 1474568 | tf_op jit(solution)/shard_map/ppermute | solution.py:389
  49.0 9.9 %collective-permute-start.7 = (f32[15,16,256]{2,1,0:T(8,128)S(1)}, f32[15,16,256]{2,1,0:T(8,128)S(1)}, u32[]{:S(2)}, u32[]{:S(2)}) collective-permute-start(f32[15,16,256]{2,1,0:T(8,128)S(1)} %get-tuple-element.49.low_ref), channel_id=1, source_target_pairs={{1,0},{2,1},{3,2},{5,4},{6,5},{7,6},{9,8},{10,9},{11,10},{13,12},{... | collective-permute-start | bytes 737288 | tf_op jit(solution)/shard_map/ppermute | solution.py:389
  50.4 12.2 %collective-permute-start.6 = (f32[15,16,256]{2,1,0:T(8,128)S(1)}, f32[15,16,256]{2,1,0:T(8,128)S(1)}, u32[]{:S(2)}, u32[]{:S(2)}) collective-permute-start(f32[15,16,256]{2,1,0:T(8,128)S(1)} %get-tuple-element.50.high_ref), channel_id=1, source_target_pairs={{0,1},{1,2},{2,3},{4,5},{5,6},{6,7},{8,9},{9,10},{10,11},{12,13},{... | collective-permute-start | bytes 737288 | tf_op jit(solution)/shard_map/ppermute | solution.py:389
  55.1 17.8 %collective-permute-start.11 = (f32[15,16,256]{2,1,0:T(8,128)S(1)}, f32[15,16,256]{2,1,0:T(8,128)S(1)}, u32[]{:S(2)}, u32[]{:S(2)}) collective-permute-start(f32[15,16,256]{2,1,0:T(8,128)S(1)} %get-tuple-element.53.low_ref), channel_id=1, source_target_pairs={{1,0},{2,1},{3,2},{5,4},{6,5},{7,6},{9,8},{10,9},{11,10},{13,12},{... | collective-permute-start | bytes 737288 | tf_op jit(solution)/shard_map/ppermute | solution.py:389
  58.9 19.2 %collective-permute-start.10 = (f32[15,16,256]{2,1,0:T(8,128)S(1)}, f32[15,16,256]{2,1,0:T(8,128)S(1)}, u32[]{:S(2)}, u32[]{:S(2)}) collective-permute-start(f32[15,16,256]{2,1,0:T(8,128)S(1)} %get-tuple-element.54.high_ref), channel_id=1, source_target_pairs={{0,1},{1,2},{2,3},{4,5},{5,6},{6,7},{8,9},{9,10},{10,11},{12,13},{... | collective-permute-start | bytes 737288 | tf_op jit(solution)/shard_map/ppermute | solution.py:389
  64.5 15.6 %copy-start.5 = (f32[15,16,256]{2,1,0:T(8,128)}, f32[15,16,256]{2,1,0:T(8,128)S(1)}, u32[]{:S(2)}) copy-start(f32[15,16,256]{2,1,0:T(8,128)S(1)} %get-tuple-element.51.low_ref) | copy-start | bytes 737284
  64.5 23.0 %copy-start.11 = (f32[16,31]{1,0:T(8,128)S(1)}, f32[16,31]{1,0:T(8,128)}, u32[]{:S(2)}) copy-start(f32[16,31]{1,0:T(8,128)} %tx_ref.3) | copy-start | bytes 5956
  64.5 23.0 %copy-start.14 = (s32[16]{0:T(128)S(1)}, s32[16]{0:T(128)}, u32[]{:S(2)}) copy-start(s32[16]{0:T(128)} %band_ref.3) | copy-start | bytes 196
  64.5 16.9 %collective-permute-start.9 = (f32[15,16,256]{2,1,0:T(8,128)S(1)}, f32[15,16,256]{2,1,0:T(8,128)S(1)}, u32[]{:S(2)}, u32[]{:S(2)}) collective-permute-start(f32[15,16,256]{2,1,0:T(8,128)S(1)} %get-tuple-element.51.low_ref), channel_id=1, source_target_pairs={{1,0},{2,1},{3,2},{5,4},{6,5},{7,6},{9,8},{10,9},{11,10},{13,12},{... | collective-permute-start | bytes 737288 | tf_op jit(solution)/shard_map/ppermute | solution.py:389
  67.8 27.1 %collective-permute-start.15 = (f32[16,16,256]{2,1,0:T(8,128)S(1)}, f32[16,16,256]{2,1,0:T(8,128)S(1)}, u32[]{:S(2)}, u32[]{:S(2)}) collective-permute-start(f32[16,16,256]{2,1,0:T(8,128)S(1)} %get-tuple-element.48.refs_0_), channel_id=1, source_target_pairs={{4,0},{8,4},{12,8},{5,1},{9,5},{13,9},{6,2},{10,6},{14,10},{7,3},{... | collective-permute-start | bytes 786440 | tf_op jit(solution)/shard_map/ppermute | solution.py:389
  69.1 25.8 %collective-permute-start.14 = (f32[16,16,256]{2,1,0:T(8,128)S(1)}, f32[16,16,256]{2,1,0:T(8,128)}, u32[]{:S(2)}, u32[]{:S(2)}) collective-permute-start(f32[16,16,256]{2,1,0:T(8,128)S(1)} %get-tuple-element.57.refs_3_), channel_id=1, source_target_pairs={{0,4},{4,8},{8,12},{1,5},{5,9},{9,13},{2,6},{6,10},{10,14},{3,7},{... | collective-permute-start | bytes 786440 | tf_op jit(solution)/shard_map/ppermute | solution.py:389
  72.9 18.3 %collective-permute-start.8 = (f32[15,16,256]{2,1,0:T(8,128)}, f32[15,16,256]{2,1,0:T(8,128)}, u32[]{:S(2)}, u32[]{:S(2)}) collective-permute-start(f32[15,16,256]{2,1,0:T(8,128)} %get-tuple-element.52.high_ref), channel_id=1, source_target_pairs={{0,1},{1,2},{2,3},{4,5},{5,6},{6,7},{8,9},{9,10},{10,11},{12,13},{... | collective-permute-start | bytes 737288 | tf_op jit(solution)/shard_map/ppermute | solution.py:389
  80.1 12.9 %collective-permute-start.13 = (f32[15,16,256]{2,1,0:T(8,128)}, f32[15,16,256]{2,1,0:T(8,128)}, u32[]{:S(2)}, u32[]{:S(2)}) collective-permute-start(f32[15,16,256]{2,1,0:T(8,128)} %get-tuple-element.55.low_ref), channel_id=1, source_target_pairs={{1,0},{2,1},{3,2},{5,4},{6,5},{7,6},{9,8},{10,9},{11,10},{13,12},{... | collective-permute-start | bytes 737288 | tf_op jit(solution)/shard_map/ppermute | solution.py:389
  81.4 0.7 copy-start.7
  82.1 10.9 %collective-permute-start.12 = (f32[15,16,256]{2,1,0:T(8,128)}, f32[15,16,256]{2,1,0:T(8,128)}, u32[]{:S(2)}, u32[]{:S(2)}) collective-permute-start(f32[15,16,256]{2,1,0:T(8,128)} %get-tuple-element.56.high_ref), channel_id=1, source_target_pairs={{0,1},{1,2},{2,3},{4,5},{5,6},{6,7},{8,9},{9,10},{10,11},{12,13},{... | collective-permute-start | bytes 737288 | tf_op jit(solution)/shard_map/ppermute | solution.py:389
  87.5 1.6 copy-start.3
  89.1 2.2 %copy-start.6 = (f32[15,16,256]{2,1,0:T(8,128)S(1)}, f32[15,16,256]{2,1,0:T(8,128)}, u32[]{:S(2)}) copy-start(f32[15,16,256]{2,1,0:T(8,128)} %copy-done.5) | copy-start | bytes 737284
  89.1 2.2 %copy-start.8 = (f32[15,16,256]{2,1,0:T(8,128)S(1)}, f32[15,16,256]{2,1,0:T(8,128)}, u32[]{:S(2)}) copy-start(f32[15,16,256]{2,1,0:T(8,128)} %copy-done.7) | copy-start | bytes 737284
  89.1 5.9 %copy-start.4 = (bf16[16,256,256]{2,1,0:T(8,128)(2,1)S(1)}, bf16[16,256,256]{2,1,0:T(8,128)(2,1)}, u32[]{:S(2)}) copy-start(bf16[16,256,256]{2,1,0:T(8,128)(2,1)} %copy-done.2) | copy-start | bytes 6291460
  91.2 3.8 %copy-start.1 = (f32[16,64,256]{2,1,0:T(8,128)S(1)}, f32[16,64,256]{2,1,0:T(8,128)}, u32[]{:S(2)}) copy-start(f32[16,64,256]{2,1,0:T(8,128)} %obs_ref.11) | copy-start | bytes 3145732
  106.3 2.6 %collective-permute-start.16 = (f32[16,16,256]{2,1,0:T(8,128)S(1)}, f32[16,16,256]{2,1,0:T(8,128)S(1)}, u32[]{:S(2)}, u32[]{:S(2)}) collective-permute-start(f32[16,16,256]{2,1,0:T(8,128)S(1)} %get-tuple-element.61), channel_id=1, source_target_pairs={{0,4},{4,8},{8,12},{1,5},{5,9},{9,13},{2,6},{6,10},{10,14},{3,7},{... | collective-permute-start | bytes 786440 | tf_op jit(solution)/shard_map/ppermute | solution.py:389
  107.6 3.4 %collective-permute-start.17 = (f32[16,16,256]{2,1,0:T(8,128)S(1)}, f32[16,16,256]{2,1,0:T(8,128)S(1)}, u32[]{:S(2)}, u32[]{:S(2)}) collective-permute-start(f32[16,16,256]{2,1,0:T(8,128)S(1)} %get-tuple-element.62), channel_id=1, source_target_pairs={{4,0},{8,4},{12,8},{5,1},{9,5},{13,9},{6,2},{10,6},{14,10},{7,3},{... | collective-permute-start | bytes 786440 | tf_op jit(solution)/shard_map/ppermute | solution.py:389
  116.6 12.8 %collective-permute-start.19 = (f32[15,32,256]{2,1,0:T(8,128)S(1)}, f32[15,32,256]{2,1,0:T(8,128)S(1)}, u32[]{:S(2)}, u32[]{:S(2)}) collective-permute-start(f32[15,32,256]{2,1,0:T(8,128)S(1)} %get-tuple-element.63.low_ref), channel_id=1, source_target_pairs={{1,0},{2,1},{3,2},{5,4},{6,5},{7,6},{9,8},{10,9},{11,10},{13,12},{... | collective-permute-start | bytes 1474568 | tf_op jit(solution)/shard_map/ppermute | solution.py:389
  117.9 13.2 %collective-permute-start.18 = (f32[15,32,256]{2,1,0:T(8,128)S(1)}, f32[15,32,256]{2,1,0:T(8,128)S(1)}, u32[]{:S(2)}, u32[]{:S(2)}) collective-permute-start(f32[15,32,256]{2,1,0:T(8,128)S(1)} %get-tuple-element.64.high_ref), channel_id=1, source_target_pairs={{0,1},{1,2},{2,3},{4,5},{5,6},{6,7},{8,9},{9,10},{10,11},{12,13},{... | collective-permute-start | bytes 1474568 | tf_op jit(solution)/shard_map/ppermute | solution.py:389
  133.2 26.3 %collective-permute-start.21 = (f32[15,32,256]{2,1,0:T(8,128)S(1)}, f32[15,32,256]{2,1,0:T(8,128)S(1)}, u32[]{:S(2)}, u32[]{:S(2)}) collective-permute-start(f32[15,32,256]{2,1,0:T(8,128)S(1)} %get-tuple-element.65.low_ref), channel_id=1, source_target_pairs={{1,0},{2,1},{3,2},{5,4},{6,5},{7,6},{9,8},{10,9},{11,10},{13,12},{... | collective-permute-start | bytes 1474568 | tf_op jit(solution)/shard_map/ppermute | solution.py:389
  134.5 25.0 %collective-permute-start.20 = (f32[15,32,256]{2,1,0:T(8,128)S(1)}, f32[15,32,256]{2,1,0:T(8,128)S(1)}, u32[]{:S(2)}, u32[]{:S(2)}) collective-permute-start(f32[15,32,256]{2,1,0:T(8,128)S(1)} %get-tuple-element.66.high_ref), channel_id=1, source_target_pairs={{0,1},{1,2},{2,3},{4,5},{5,6},{6,7},{8,9},{9,10},{10,11},{12,13},{... | collective-permute-start | bytes 1474568 | tf_op jit(solution)/shard_map/ppermute | solution.py:389
  139.5 13.2 %collective-permute-start.23 = (f32[15,16,256]{2,1,0:T(8,128)S(1)}, f32[15,16,256]{2,1,0:T(8,128)S(1)}, u32[]{:S(2)}, u32[]{:S(2)}) collective-permute-start(f32[15,16,256]{2,1,0:T(8,128)S(1)} %get-tuple-element.68.low_ref), channel_id=1, source_target_pairs={{1,0},{2,1},{3,2},{5,4},{6,5},{7,6},{9,8},{10,9},{11,10},{13,12},{... | collective-permute-start | bytes 737288 | tf_op jit(solution)/shard_map/ppermute | solution.py:389
  140.8 16.1 %collective-permute-start.22 = (f32[15,16,256]{2,1,0:T(8,128)S(1)}, f32[15,16,256]{2,1,0:T(8,128)S(1)}, u32[]{:S(2)}, u32[]{:S(2)}) collective-permute-start(f32[15,16,256]{2,1,0:T(8,128)S(1)} %get-tuple-element.69.high_ref), channel_id=1, source_target_pairs={{0,1},{1,2},{2,3},{4,5},{5,6},{6,7},{8,9},{9,10},{10,11},{12,13},{... | collective-permute-start | bytes 737288 | tf_op jit(solution)/shard_map/ppermute | solution.py:389
  145.4 23.4 %collective-permute-start.27 = (f32[15,16,256]{2,1,0:T(8,128)S(1)}, f32[15,16,256]{2,1,0:T(8,128)S(1)}, u32[]{:S(2)}, u32[]{:S(2)}) collective-permute-start(f32[15,16,256]{2,1,0:T(8,128)S(1)} %get-tuple-element.72.low_ref), channel_id=1, source_target_pairs={{1,0},{2,1},{3,2},{5,4},{6,5},{7,6},{9,8},{10,9},{11,10},{13,12},{... | collective-permute-start | bytes 737288 | tf_op jit(solution)/shard_map/ppermute | solution.py:389
  152.8 20.4 %collective-permute-start.26 = (f32[15,16,256]{2,1,0:T(8,128)S(1)}, f32[15,16,256]{2,1,0:T(8,128)S(1)}, u32[]{:S(2)}, u32[]{:S(2)}) collective-permute-start(f32[15,16,256]{2,1,0:T(8,128)S(1)} %get-tuple-element.73.high_ref), channel_id=1, source_target_pairs={{0,1},{1,2},{2,3},{4,5},{5,6},{6,7},{8,9},{9,10},{10,11},{12,13},{... | collective-permute-start | bytes 737288 | tf_op jit(solution)/shard_map/ppermute | solution.py:389
  158.2 17.5 %collective-permute-start.25 = (f32[15,16,256]{2,1,0:T(8,128)S(1)}, f32[15,16,256]{2,1,0:T(8,128)S(1)}, u32[]{:S(2)}, u32[]{:S(2)}) collective-permute-start(f32[15,16,256]{2,1,0:T(8,128)S(1)} %get-tuple-element.70.low_ref), channel_id=1, source_target_pairs={{1,0},{2,1},{3,2},{5,4},{6,5},{7,6},{9,8},{10,9},{11,10},{13,12},{... | collective-permute-start | bytes 737288 | tf_op jit(solution)/shard_map/ppermute | solution.py:389
  161.4 26.1 %collective-permute-start.31 = (f32[16,16,256]{2,1,0:T(8,128)S(1)}, f32[16,16,256]{2,1,0:T(8,128)S(1)}, u32[]{:S(2)}, u32[]{:S(2)}) collective-permute-start(f32[16,16,256]{2,1,0:T(8,128)S(1)} %get-tuple-element.67.refs_0_), channel_id=1, source_target_pairs={{4,0},{8,4},{12,8},{5,1},{9,5},{13,9},{6,2},{10,6},{14,10},{7,3},{... | collective-permute-start | bytes 786440 | tf_op jit(solution)/shard_map/ppermute | solution.py:389
  162.7 24.8 %collective-permute-start.30 = (f32[16,16,256]{2,1,0:T(8,128)S(1)}, f32[16,16,256]{2,1,0:T(8,128)S(1)}, u32[]{:S(2)}, u32[]{:S(2)}) collective-permute-start(f32[16,16,256]{2,1,0:T(8,128)S(1)} %get-tuple-element.76.refs_3_), channel_id=1, source_target_pairs={{0,4},{4,8},{8,12},{1,5},{5,9},{9,13},{2,6},{6,10},{10,14},{3,7},{... | collective-permute-start | bytes 786440 | tf_op jit(solution)/shard_map/ppermute | solution.py:389
  168.9 11.4 %collective-permute-start.24 = (f32[15,16,256]{2,1,0:T(8,128)S(1)}, f32[15,16,256]{2,1,0:T(8,128)S(1)}, u32[]{:S(2)}, u32[]{:S(2)}) collective-permute-start(f32[15,16,256]{2,1,0:T(8,128)S(1)} %get-tuple-element.71.high_ref), channel_id=1, source_target_pairs={{0,1},{1,2},{2,3},{4,5},{5,6},{6,7},{8,9},{9,10},{10,11},{12,13},{... | collective-permute-start | bytes 737288 | tf_op jit(solution)/shard_map/ppermute | solution.py:389
  174.3 10.3 %collective-permute-start.29 = (f32[15,16,256]{2,1,0:T(8,128)S(1)}, f32[15,16,256]{2,1,0:T(8,128)S(1)}, u32[]{:S(2)}, u32[]{:S(2)}) collective-permute-start(f32[15,16,256]{2,1,0:T(8,128)S(1)} %get-tuple-element.74.low_ref), channel_id=1, source_target_pairs={{1,0},{2,1},{3,2},{5,4},{6,5},{7,6},{9,8},{10,9},{11,10},{13,12},{... | collective-permute-start | bytes 737288 | tf_op jit(solution)/shard_map/ppermute | solution.py:389
  175.6 10.7 %collective-permute-start.28 = (f32[15,16,256]{2,1,0:T(8,128)S(1)}, f32[15,16,256]{2,1,0:T(8,128)S(1)}, u32[]{:S(2)}, u32[]{:S(2)}) collective-permute-start(f32[15,16,256]{2,1,0:T(8,128)S(1)} %get-tuple-element.75.high_ref), channel_id=1, source_target_pairs={{0,1},{1,2},{2,3},{4,5},{5,6},{6,7},{8,9},{9,10},{10,11},{12,13},{... | collective-permute-start | bytes 737288 | tf_op jit(solution)/shard_map/ppermute | solution.py:389

commit v2 on v0

v2 whole, which is shorter than its diff:
```python
import functools

import jax
import jax.numpy as jnp
from jax import lax
from jax.experimental import pallas as pl
from jax.experimental.pallas import tpu as pltpu
from jax.sharding import PartitionSpec as P

ITERS = 2
F32 = jnp.float32
BF16 = jnp.bfloat16
PARAMS = pltpu.CompilerParams(vmem_limit_bytes=40 * 1024 * 1024)
SMEM = pl.BlockSpec(memory_space=pltpu.SMEM)
VMEM = pl.BlockSpec(memory_space=pltpu.VMEM)
ANY = pl.BlockSpec(memory_space=pl.ANY)


def up(value, step):
    return -(-value // step) * step


def split(x):
    hi = x.astype(BF16)
    return hi, (x - hi.astype(F32)).astype(BF16)


def mm(a, b):
    return jnp.dot(a, b, preferred_element_type=F32)


def blur_rows(w_hi, w_lo, v_hi, v_lo):
    count = w_hi.shape[0]
    both = mm(jnp.concatenate([w_hi, w_lo], axis=0), v_hi)
    return both[:count] + both[count:] + mm(w_hi, v_lo)


def blur_columns(u, a_hi, a_lo):
    count = u.shape[0]
    u_hi, u_lo = split(u)
    both = mm(jnp.concatenate([u_hi, u_lo], axis=0), a_hi)
    return both[:count] + both[count:] + mm(u_hi, a_lo)


def full(shape):
    return pl.BlockSpec(shape, lambda i: (0,) * len(shape))


def planes(shape, per):
    return pl.BlockSpec((per,) + shape[1:], lambda i: (i,) + (0,) * (len(shape) - 1))


def shape_of(*dims, dtype=F32):
    return jax.ShapeDtypeStruct(dims, dtype)


def spread(ref, band, lanes, radius, flip):
    base = jnp.zeros(lanes.shape, F32)
    for k in range(2 * radius + 1):
        base = jnp.where(lanes == (2 * radius - k if flip else k), ref[band, k], base)
    return base


def iotas(rows, lanes):
    shape = (rows, lanes)
    return (
        lax.broadcasted_iota(jnp.int32, shape, 0),
        lax.broadcasted_iota(jnp.int32, shape, 1),
    )


def column_matrix(base, radius, h_ref, l_ref, p):
    columns = h_ref.shape[1]
    sub, lane = iotas(16, 128)
    rolled = {}
    sums = [None] * (columns // 128)
    for first in range(0, columns, 16):
        key = first % 128
        if key not in rolled:
            rolled[key] = pltpu.roll(base, (key - radius) % 128, 1, stride=1, stride_axis=0)
        for block in range(columns // 128):
            left = block * 128
            here = (p, slice(first, first + 16), slice(left, left + 128))
            if left > first + 15 + radius or left + 127 < first - radius:
                zero = jnp.zeros((16, 128), BF16)
                h_ref[here] = zero
                l_ref[here] = zero
                continue
            inside = jnp.abs(lane - sub + (left - first)) <= radius
            tile = jnp.where(inside, rolled[key], 0.0)
            h_ref[here], l_ref[here] = split(tile)
            sums[block] = tile if sums[block] is None else sums[block] + tile
    return [jnp.sum(s, axis=0, keepdims=True) for s in sums]


def row_matrix(base, rows, shift, width):
    return jnp.concatenate(
        [
            pltpu.roll(base, (first + shift) % width, 1, stride=1, stride_axis=0)
            for first in range(0, rows, 16)
        ],
        axis=0,
    )


def store_sends(v, plane, n, radius, low_ref, high_ref):
    @pl.when(plane < radius)
    def _():
        low_ref[jnp.minimum(plane, radius - 1)] = v

    @pl.when(plane >= n - radius)
    def _():
        high_ref[jnp.maximum(plane - (n - radius), 0)] = v


def own_rows(est, wx_ref, ah_ref, al_ref, p, inner):
    rows = est.shape[0]
    est_hi, est_lo = split(est)
    u = blur_rows(wx_ref[p, 0, :inner, :rows], wx_ref[p, 1, :inner, :rows], est_hi, est_lo)
    return blur_columns(u, ah_ref[p], al_ref[p])


def first_kernel(
    per, n, radius, halo, place_ref, band_ref, tx_ref, ty_ref, est_ref,
    ah_ref, al_ref, wx_ref, low_ref, high_ref,
):
    rows, width = wx_ref.shape[2], wx_ref.shape[3]
    _, lane = iotas(16, 128)
    _, wide = iotas(16, width)
    row, lanes = iotas(rows, width)
    keep = (place_ref[2] == 0) | ((row < rows - radius) == (lanes < rows))
    for p in range(per):
        plane = pl.program_id(0) * per + p
        band = band_ref[plane]
        column_matrix(spread(ty_ref, band, lane, radius, True), radius, ah_ref, al_ref, p)
        matrix = row_matrix(spread(tx_ref, band, wide, radius, False), rows, 0, width)
        wx_ref[p, 0], wx_ref[p, 1] = split(jnp.where(keep, matrix, 0.0))
        v = own_rows(est_ref[p], wx_ref, ah_ref, al_ref, p, rows - halo)
        store_sends(v, plane, n, radius, low_ref, high_ref)


def first_blur(place, band_index, taps_x, taps_y, est, halo, width, per):
    n, rows, columns = est.shape
    radius = taps_x.shape[1] // 2
    a = shape_of(n, columns, columns, dtype=BF16)
    w = shape_of(n, 2, rows, width, dtype=BF16)
    send = shape_of(radius, rows - halo, columns)
    return pl.pallas_call(
        functools.partial(first_kernel, per, n, radius, halo),
        grid=(n // per,),
        in_specs=[SMEM] * 4 + [planes(est.shape, per)],
        out_specs=[planes(x.shape, per) for x in (a, a, w)] + [full(send.shape)] * 2,
        out_shape=[a, a, w, send, send],
        compiler_params=PARAMS,
    )(place, band_index, taps_x, taps_y, est)


def second_kernel(
    per, n, radius, halo, depth, place_ref, band_ref, tx_ref, ty_ref, tz_ref, after_ref,
    obs_ref, next_ref, ah_ref, al_ref, wx_ref, rn_ref, shifted_ref,
):
    rows, width = wx_ref.shape[2], wx_ref.shape[3]
    _, lane = iotas(16, 128)
    _, wide = iotas(16, width)
    _, lanes = iotas(rows, width)
    lower = (place_ref[1] == 0) | (lanes >= rows - radius - (rows - halo))
    upper = (place_ref[2] == 0) | (lanes < rows - radius + halo)
    keep = ((lanes < halo) & lower) | ((lanes >= halo) & upper)
    for p in range(per):
        plane = pl.program_id(0) * per + p
        band = band_ref[plane]
        sums = column_matrix(
            spread(ty_ref, band, lane, radius, False), radius, ah_ref, al_ref, p
        )
        matrix = row_matrix(
            spread(tx_ref, band, wide, radius, True), rows, halo - 2 * radius, width
        )
        matrix = jnp.where(keep, matrix, 0.0)
        wx_ref[p, 0], wx_ref[p, 1] = split(matrix)
        along_x = jnp.sum(matrix, axis=1, keepdims=True)
        along_z = jnp.float32(0.0)
        z = place_ref[0] + plane
        for k in range(2 * radius + 1):
            source = z - k + radius
            inside = (source >= 0) & (source < depth)
            along_z = along_z + jnp.where(inside, tz_ref[k], 0.0)
        for block, along_y in enumerate(sums):
            rn_ref[p, :, block * 128 : block * 128 + 128] = 1.0 / (
                along_x * (along_y * along_z)
            )
        shifted_ref[p, : rows - radius] = obs_ref[p, radius:]
        shifted_ref[p, rows - radius :] = next_ref[p, :radius]


def second_weights(
    place, band_index, taps_x, taps_y, taps_z, after, obs, beyond, halo, width, depth, per
):
    n, rows, columns = obs.shape
    radius = taps_x.shape[1] // 2
    a = shape_of(n, columns, columns, dtype=BF16)
    w = shape_of(n, 2, rows, width, dtype=BF16)
    field = shape_of(*obs.shape)
    return pl.pallas_call(
        functools.partial(second_kernel, per, n, radius, halo, depth),
        grid=(n // per,),
        in_specs=[SMEM] * 5 + [ANY] + [planes(x.shape, per) for x in (obs, beyond)],
        out_specs=[planes(x.shape, per) for x in (a, a, w, field, field)],
        out_shape=[a, a, w, field, field],
        compiler_params=PARAMS,
    )(place, band_index, taps_x, taps_y, taps_z, after, obs, beyond)


def edge_kernel(
    per, n, radius, halo, est_ref, next_ref, wx_ref, ah_ref, al_ref, low_ref, high_ref
):
    rows = est_ref.shape[1]
    inner, used = rows - halo, rows + halo
    for p in range(per):
        plane = pl.program_id(0) * per + p
        v_hi, v_lo = split(jnp.concatenate([est_ref[p], next_ref[p]], axis=0))
        u = blur_rows(wx_ref[p, 0, inner:, :used], wx_ref[p, 1, inner:, :used], v_hi, v_lo)
        v = blur_columns(u, ah_ref[p], al_ref[p])
        store_sends(v, plane, n, radius, low_ref, high_ref)


def edge_blur(est, beyond, wx, ah, al, radius, per):
    n, _, columns = est.shape
    halo = beyond.shape[1]
    send = shape_of(radius, halo, columns)
    args = (est, beyond, wx, ah, al)
    return pl.pallas_call(
        functools.partial(edge_kernel, per, n, radius, halo),
        grid=(n // per,),
        in_specs=[planes(x.shape, per) for x in args],
        out_specs=[full(send.shape)] * 2,
        out_shape=[send] * 2,
        compiler_params=PARAMS,
    )(*args)


def depth_sum(n, radius, flip, tz_ref, refs, rows, lanes):
    low_ref, high_ref, zlo_ref, zhi_ref = refs
    last = 2 * radius
    taps = [tz_ref[last - k if flip else k] for k in range(last + 1)]
    total = [None] * n
    for j in range(-radius, n + radius):
        if j < 0:
            piece = zlo_ref[j + radius, rows, lanes]
        elif j < radius:
            piece = low_ref[j, rows, lanes]
        elif j < n:
            piece = high_ref[j - (n - radius), rows, lanes]
        else:
            piece = zhi_ref[j - n, rows, lanes]
        for i in range(max(0, j - radius), min(n, j + radius + 1)):
            term = taps[j - i + radius] * piece
            total[i] = term if total[i] is None else total[i] + term
    return total


def tiles(count, columns, body):
    def step(t, carry):
        for left in range(0, columns, 128):
            body(t * 8, slice(left, left + 128))
        return carry

    lax.fori_loop(0, count // 8, step, 0)


def at(start, offset):
    return pl.ds(pl.multiple_of(start + offset, 8), 8)


def ratio_kernel(n, radius, skip, obs_skip, tz_ref, obs_ref, *refs):
    rlow_ref, rhigh_ref = refs[-2:]
    _, count, columns = rlow_ref.shape

    def body(start, lanes):
        total = depth_sum(n, radius, False, tz_ref, refs[:4], at(start, skip), lanes)
        rows = at(start, 0)
        for i in range(n):
            ratio = obs_ref[i, at(start, obs_skip), lanes] / total[i]
            if i < radius:
                rlow_ref[i, rows, lanes] = ratio
            if i >= n - radius:
                rhigh_ref[i - (n - radius), rows, lanes] = ratio

    tiles(count, columns, body)


def depth_ratio(taps_z, obs, chunk, skip, obs_skip, count, after=None):
    n, _, columns = obs.shape
    radius = taps_z.shape[0] // 2
    send = shape_of(radius, count, columns)
    extra = [] if after is None else [after]
    return pl.pallas_call(
        functools.partial(ratio_kernel, n, radius, skip, obs_skip),
        in_specs=[SMEM] + [VMEM] * 5 + [ANY] * len(extra),
        out_specs=[VMEM] * 2,
        out_shape=[send] * 2,
        compiler_params=PARAMS,
    )(taps_z, obs, *chunk, *extra)


def back_kernel(n, radius, groups, tz_ref, *refs):
    out_ref = refs[-1]
    columns = out_ref.shape[2]
    first = 0
    for g in range(groups):
        own = refs[4 * g : 4 * g + 4]
        count = own[0].shape[1]

        def body(start, lanes):
            total = depth_sum(n, radius, True, tz_ref, own, at(start, 0), lanes)
            for i in range(n):
                out_ref[i, at(start, first), lanes] = total[i]

        tiles(count, columns, body)
        first += count


def depth_back(taps_z, chunks, n, after=None):
    radius, _, columns = chunks[0][0].shape
    count = sum(chunk[0].shape[1] for chunk in chunks)
    extra = [] if after is None else [after]
    return pl.pallas_call(
        functools.partial(back_kernel, n, radius, len(chunks)),
        in_specs=[SMEM] + [VMEM] * (4 * len(chunks)) + [ANY] * len(extra),
        out_specs=VMEM,
        out_shape=shape_of(n, count, columns),
        compiler_params=PARAMS,
    )(taps_z, *(x for chunk in chunks for x in chunk), *extra)


def update_kernel(per, n, radius, last, *refs):
    before_ref, inner_ref, edge_ref, est_ref, rn_ref, wa_ref, bh_ref, bl_ref = refs[:8]
    refs = refs[8:]
    rows = est_ref.shape[1]
    halo = edge_ref.shape[1]
    if last:
        (out_ref,) = refs
    else:
        wx_ref, ah_ref, al_ref, out_ref, top_ref, low_ref, high_ref = refs
    for p in range(per):
        plane = pl.program_id(0) * per + p
        c = jnp.concatenate([before_ref[p], inner_ref[p], edge_ref[p]], axis=0)
        c_hi, c_lo = split(c)
        used = rows + halo
        u = blur_rows(wa_ref[p, 0, :, :used], wa_ref[p, 1, :, :used], c_hi, c_lo)
        u = blur_columns(u, bh_ref[p], bl_ref[p])
        est = est_ref[p] * u * rn_ref[p]
        out_ref[p] = est
        if not last:
            top_ref[p] = est[:halo]
            v = own_rows(est, wx_ref, ah_ref, al_ref, p, rows - halo)
            store_sends(v, plane, n, radius, low_ref, high_ref)


def update(before, inner, edge, est, rn, adjoint, forward, radius, per):
    n, rows, columns = est.shape
    halo = edge.shape[1]
    last = forward is None
    args = [before, inner, edge, est, rn, *adjoint] + ([] if last else [*forward])
    out_specs, out_shape = [planes(est.shape, per)], [shape_of(*est.shape)]
    if not last:
        top = shape_of(n, halo, columns)
        send = shape_of(radius, rows - halo, columns)
        out_specs += [planes(top.shape, per)] + [full(send.shape)] * 2
        out_shape += [top, send, send]
    return pl.pallas_call(
        functools.partial(update_kernel, per, n, radius, last),
        grid=(n // per,),
        in_specs=[planes(x.shape, per) for x in args],
        out_specs=out_specs,
        out_shape=out_shape,
        compiler_params=PARAMS,
    )(*args)


def depth_exchange(low, high):
    count = lax.axis_size("slab")
    forward = [(i, i + 1) for i in range(count - 1)]
    backward = [(i + 1, i) for i in range(count - 1)]
    zlo = lax.ppermute(high, "slab", forward)
    zhi = lax.ppermute(low, "slab", backward)
    return low, high, zlo, zhi


def ring(x, step):
    count = lax.axis_size("row")
    return lax.ppermute(x, "row", [(i, (i + step) % count) for i in range(count)])


def on_device(observed, band_index, taps_x, taps_y, taps_z):
    n, rows, columns = observed.shape
    radius = taps_z.shape[0] // 2
    halo = up(2 * radius, 16)
    inner = rows - halo
    half = up(inner // 2, 16)
    width = up(rows + halo, 128)
    per = 4 if n % 4 == 0 else 1
    depth = n * lax.axis_size("slab")
    row = lax.axis_index("row")
    last_row = row == lax.axis_size("row") - 1
    place = jnp.stack([lax.axis_index("slab") * n, row == 0, last_row]).astype(jnp.int32)

    beyond = ring(observed[:, :halo], -1)
    ah, al, wx, low, high = first_blur(
        place, band_index, taps_x, taps_y, observed, halo, width, per
    )
    est, adjoint = observed, None
    for step in range(ITERS):
        v_inner = depth_exchange(low, high)
        low, high = edge_blur(est, beyond, wx, ah, al, radius, per)
        v_edge = depth_exchange(low, high)
        if adjoint is None:
            bh, bl, wa, rn, shifted = second_weights(
                place, band_index, taps_x, taps_y, taps_z, low, observed, beyond, halo,
                width, depth, per,
            )
            adjoint = (wa, bh, bl)
        r_first = depth_exchange(
            *depth_ratio(taps_z, shifted, v_inner, 0, 0, half, after=low)
        )
        r_edge = depth_exchange(*depth_ratio(taps_z, shifted, v_edge, 0, inner, halo))
        r_second = depth_exchange(
            *depth_ratio(
                taps_z, shifted, v_inner, half, half, inner - half, after=r_edge[0]
            )
        )
        c_edge = depth_back(taps_z, [r_edge], n)
        before = ring(c_edge, 1)
        c_inner = depth_back(taps_z, [r_first, r_second], n, after=c_edge)
        last = step == ITERS - 1
        out = update(
            before, c_inner, c_edge, est, rn, adjoint, None if last else (wx, ah, al),
            radius, per,
        )
        est = out[0]
        if not last:
            top, low, high = out[1:]
            beyond = ring(top, -1)
    return est


def solution(mesh):
    in_specs = (P(("grp", "slab"), "row", None), P("slab"), P(), P(), P())
    out_specs = P(("grp", "slab"), "row", None)
    return jax.shard_map(
        on_device, mesh=mesh, in_specs=in_specs, out_specs=out_specs, check_vma=False
    )
```

time: 359 us -> 184 us (0.51); the launches traced: 353 us -> 183 us
  other arithmetic: 218 us -> 0.08 us
  Pallas kernels: 0 us -> 50.2 us
    add x10 -> x0, other arithmetic: 135 us -> none  [correlate(): total = term if total is None else total + term]
    div x4 -> x0, other arithmetic: 82.2 us -> none  [the longest x2 47.6 us: on_device(): ratio = observed / blurred]
    pallas_call x0 -> x16, Pallas kernels: none -> 50.2 us  [the longest x2 14.7 us: update(): pl.pallas_call(functools.partial(update_kernel, per, n, radius, last), gr...]
    slice x15 -> x1, local copies, waits for them, and re-layouts: 6.24 us -> 1.17 us  [on_device(): beyond = ring(observed[:, :halo], -1)]
    ppermute x20 -> x24, starting transfers between devices: 57.8 us -> 59.5 us  [the longest x10 43.5 us: depth_exchange(): zlo = lax.ppermute(high, 'slab', forward)]
    ppermute x20 -> x24, waiting for transfers between devices: 68.7 us -> 68.4 us  [the longest x10 37.6 us: depth_exchange(): zhi = lax.ppermute(low, 'slab', backward)]
  transfers between devices with their start and end apart: 20 -> 24, of which waited for: 9 -> 15; matrix products, arithmetic and copies ran while one was open for 29% -> 0% of each run, Pallas kernels for 0% -> 12%
where the time goes in v2:
time: 184 us; the launch traced here: 183 us
  waiting for transfers between devices  68.4 us (37%)
  starting transfers between devices  59.5 us (32%)
  Pallas kernels  50.2 us (27%)
  local copies, waits for them, and re-layouts  4.47 us (2%)
    ppermute x10, starting transfers between devices, depth_exchange(): zlo = lax.ppermute(high, 'slab', forward)  43.5 us
    ppermute x10, waiting for transfers between devices, depth_exchange(): zhi = lax.ppermute(low, 'slab', backward)  37.6 us
    ppermute x10, waiting for transfers between devices, depth_exchange(): zlo = lax.ppermute(high, 'slab', forward)  24.2 us
    pallas_call x2, Pallas kernels, update(): pl.pallas_call(functools.partial(update_kernel, per, n, radius, last), gr...  14.7 us
    ppermute x10, starting transfers between devices, depth_exchange(): zhi = lax.ppermute(low, 'slab', backward)  12.9 us
    pallas_call x2, Pallas kernels, edge_blur(): pl.pallas_call(functools.partial(edge_kernel, per, n, radius, halo), grid...  9.72 us
    pallas_call x6, Pallas kernels, depth_ratio(): pl.pallas_call(functools.partial(ratio_kernel, n, radius, skip, obs_skip)...  8.39 us
    pallas_call x1, Pallas kernels, first_blur(): pl.pallas_call(functools.partial(first_kernel, per, n, radius, halo), gri...  7.47 us
  transfers between devices with their start and end apart: 24, of which 15 were waited for; matrix products, arithmetic and copies ran while one was open for 0% of the time, Pallas kernels for 12%

profile of v2, /device:TPU:0, one launch (start us, length us, event | category | flops | bytes accessed | tf_op | source)
XLA Modules:
  0.0 183.0 jit_solution(7043631901883367999)
XLA Ops:
  0.0 1.2 slice.3
  1.2 2.4 %collective-permute-start = (f32[16,32,256]{2,1,0:T(8,128)S(1)}, f32[16,32,256]{2,1,0:T(8,128)S(1)}, u32[]{:S(2)}, u32[]{:S(2)}) collective-permute-start(f32[16,32,256]{2,1,0:T(8,128)S(1)} %slice.3), channel_id=1, source_target_pairs={{0,12},{4,0},{8,4},{12,8},{1,13},{5,1},{9,5},{13,9},{2,14},{6,2},{... | collective-permute-start | bytes 1572872 | tf_op jit(solution)/shard_map/ppermute | solution.py:391
  3.6 0.1 pad_add_fusion.place_ref
  3.7 1.2 copy-done
  4.9 0.7 copy-done.5
  5.6 0.7 copy-done.6
  6.3 0.7 copy-done.7
  7.0 7.5 %shard_map.55 = (bf16[16,256,256]{2,1,0:T(8,128)(2,1)S(1)}, bf16[16,256,256]{2,1,0:T(8,128)(2,1)S(1)}, bf16[16,2,64,128]{3,2,1,0:T(8,128)(2,1)S(1)}, f32[15,32,256]{2,1,0:T(8,128)S(1)}, f32[15,32,256]{2,1,0:T(8,128)S(1)}) custom-call(s32[3]{0:T(128)S(1)} %pad_add_fusion.place_ref, s32[16]{0:T(128)S(1)} %copy-done.7, f32[16,31]{1,0:T(8,128)S(1)} %copy-done.5, ...), custom_call_target="tpu_custom_call" | custom-call | tf_op jit(solution)/shard_map/pallas_call | solution.py:148
  14.4 0.0 copy-start.2
  14.5 0.0 collective-permute-done.next_ref
  14.5 0.0 copy-start.4
  14.5 4.9 %shard_map.56 = (f32[15,32,256]{2,1,0:T(8,128)S(1)}, f32[15,32,256]{2,1,0:T(8,128)S(1)}) custom-call(f32[16,64,256]{2,1,0:T(8,128)S(1)} %copy-done.1, f32[16,32,256]{2,1,0:T(8,128)S(1)} %collective-permute-done.next_ref, bf16[16,2,64,128]{3,2,1,0:T(8,128)(2,1)S(1)} %get-tuple-element.35.wx_ref.refs_8_, ...), custom_call_target="tpu_custom_call" | custom-call | tf_op jit(solution)/shard_map/pallas_call | solution.py:231
  19.4 3.5 %collective-permute-start.1 = (f32[15,32,256]{2,1,0:T(8,128)S(1)}, f32[15,32,256]{2,1,0:T(8,128)S(1)}, u32[]{:S(2)}, u32[]{:S(2)}) collective-permute-start(f32[15,32,256]{2,1,0:T(8,128)S(1)} %get-tuple-element.40.refs_1_), channel_id=1, source_target_pairs={{0,1},{1,2},{2,3},{4,5},{5,6},{6,7},{8,9},{9,10},{10,11},{12,13},{... | collective-permute-start | bytes 1474568 | tf_op jit(solution)/shard_map/ppermute | solution.py:384
  22.9 1.3 collective-permute-start.2
  24.2 2.9 %shard_map.57 = (bf16[16,256,256]{2,1,0:T(8,128)(2,1)S(1)}, bf16[16,256,256]{2,1,0:T(8,128)(2,1)S(1)}, bf16[16,2,64,128]{3,2,1,0:T(8,128)(2,1)S(1)}, f32[16,64,256]{2,1,0:T(8,128)S(1)}, f32[16,64,256]{2,1,0:T(8,128)S(1)}) custom-call(s32[3]{0:T(128)S(1)} %pad_add_fusion.place_ref, s32[16]{0:T(128)S(1)} %copy-done.7, f32[16,31]{1,0:T(8,128)S(1)} %copy-done.5, ...), custom_call_target="tpu_custom_call" | custom-call | tf_op jit(solution)/shard_map/pallas_call | solution.py:203
  27.2 5.9 %collective-permute-done.1.refs_2_ = f32[15,32,256]{2,1,0:T(8,128)S(1)} collective-permute-done((f32[15,32,256]{2,1,0:T(8,128)S(1)}, f32[15,32,256]{2,1,0:T(8,128)S(1)}, u32[]{:S(2)}, u32[]{:S(2)}) %collective-permute-start.1) | collective-permute-done | bytes 491552 | tf_op jit(solution)/shard_map/ppermute | solution.py:384
  33.1 4.1 %collective-permute-done.2.refs_3_ = f32[15,32,256]{2,1,0:T(8,128)S(1)} collective-permute-done((f32[15,32,256]{2,1,0:T(8,128)S(1)}, f32[15,32,256]{2,1,0:T(8,128)S(1)}, u32[]{:S(2)}, u32[]{:S(2)}) %collective-permute-start.2) | collective-permute-done | bytes 491552 | tf_op jit(solution)/shard_map/ppermute | solution.py:385
  37.2 1.8 %shard_map.58 = (f32[15,32,256]{2,1,0:T(8,128)S(1)}, f32[15,32,256]{2,1,0:T(8,128)S(1)}) custom-call(f32[31]{0:T(128)S(1)} %copy-done.4, f32[16,64,256]{2,1,0:T(8,128)S(1)} %get-tuple-element.39.obs_ref, f32[15,32,256]{2,1,0:T(8,128)S(1)} %get-tuple-element.38.after_ref.refs_0_.refs_4_, f32[15,32,256]{2,1,0:T(8,128)S(1)} %get-tuple-element.40.refs_1_, ...), custom_call_target="tpu_custom_call" | custom-call | tf_op jit(solution)/shard_map/pallas_call | solution.py:296
  39.1 3.5 %collective-permute-start.3 = (f32[15,32,256]{2,1,0:T(8,128)S(1)}, f32[15,32,256]{2,1,0:T(8,128)S(1)}, u32[]{:S(2)}, u32[]{:S(2)}) collective-permute-start(f32[15,32,256]{2,1,0:T(8,128)S(1)} %get-tuple-element.42.refs_1_), channel_id=1, source_target_pairs={{0,1},{1,2},{2,3},{4,5},{5,6},{6,7},{8,9},{9,10},{10,11},{12,13},{... | collective-permute-start | bytes 1474568 | tf_op jit(solution)/shard_map/ppermute | solution.py:384
  42.6 1.3 collective-permute-start.4
  43.9 1.3 collective-permute-start.7
  45.2 5.2 %collective-permute-start.6 = (f32[15,32,256]{2,1,0:T(8,128)S(1)}, f32[15,32,256]{2,1,0:T(8,128)S(1)}, u32[]{:S(2)}, u32[]{:S(2)}) collective-permute-start(f32[15,32,256]{2,1,0:T(8,128)S(1)} %get-tuple-element.44.refs_1_), channel_id=1, source_target_pairs={{0,1},{1,2},{2,3},{4,5},{5,6},{6,7},{8,9},{9,10},{10,11},{12,13},{... | collective-permute-start | bytes 1474568 | tf_op jit(solution)/shard_map/ppermute | solution.py:384
  50.4 3.8 %collective-permute-done.3.refs_2_ = f32[15,32,256]{2,1,0:T(8,128)S(1)} collective-permute-done((f32[15,32,256]{2,1,0:T(8,128)S(1)}, f32[15,32,256]{2,1,0:T(8,128)S(1)}, u32[]{:S(2)}, u32[]{:S(2)}) %collective-permute-start.3) | collective-permute-done | bytes 491552 | tf_op jit(solution)/shard_map/ppermute | solution.py:384
  54.2 4.4 %collective-permute-done.4.refs_3_ = f32[15,32,256]{2,1,0:T(8,128)S(1)} collective-permute-done((f32[15,32,256]{2,1,0:T(8,128)S(1)}, f32[15,32,256]{2,1,0:T(8,128)S(1)}, u32[]{:S(2)}, u32[]{:S(2)}) %collective-permute-start.4) | collective-permute-done | bytes 491552 | tf_op jit(solution)/shard_map/ppermute | solution.py:385
  58.6 1.8 shard_map.59.refs_8_.refs_2_
  60.4 0.1 collective-permute-start.5
  60.4 5.8 %collective-permute-done.7.refs_3_ = f32[15,32,256]{2,1,0:T(8,128)S(1)} collective-permute-done((f32[15,32,256]{2,1,0:T(8,128)S(1)}, f32[15,32,256]{2,1,0:T(8,128)S(1)}, u32[]{:S(2)}, u32[]{:S(2)}) %collective-permute-start.7) | collective-permute-done | bytes 491552 | tf_op jit(solution)/shard_map/ppermute | solution.py:385
  66.2 1.2 shard_map.60
  67.4 1.3 collective-permute-start.9
  68.7 4.6 %collective-permute-start.8 = (f32[15,16,256]{2,1,0:T(8,128)S(1)}, f32[15,16,256]{2,1,0:T(8,128)S(1)}, u32[]{:S(2)}, u32[]{:S(2)}) collective-permute-start(f32[15,16,256]{2,1,0:T(8,128)S(1)} %get-tuple-element.46.refs_1_), channel_id=1, source_target_pairs={{0,1},{1,2},{2,3},{4,5},{5,6},{6,7},{8,9},{9,10},{10,11},{12,13},{... | collective-permute-start | bytes 737288 | tf_op jit(solution)/shard_map/ppermute | solution.py:384
  73.3 1.2 shard_map.61
  74.5 1.3 collective-permute-start.11
  75.8 4.6 %collective-permute-start.10 = (f32[15,16,256]{2,1,0:T(8,128)S(1)}, f32[15,16,256]{2,1,0:T(8,128)S(1)}, u32[]{:S(2)}, u32[]{:S(2)}) collective-permute-start(f32[15,16,256]{2,1,0:T(8,128)S(1)} %get-tuple-element.48.refs_5_), channel_id=1, source_target_pairs={{0,1},{1,2},{2,3},{4,5},{5,6},{6,7},{8,9},{9,10},{10,11},{12,13},{... | collective-permute-start | bytes 737288 | tf_op jit(solution)/shard_map/ppermute | solution.py:384
  80.4 2.2 %collective-permute-done.11.refs_7_ = f32[15,16,256]{2,1,0:T(8,128)S(1)} collective-permute-done((f32[15,16,256]{2,1,0:T(8,128)S(1)}, f32[15,16,256]{2,1,0:T(8,128)S(1)}, u32[]{:S(2)}, u32[]{:S(2)}) %collective-permute-start.11) | collective-permute-done | bytes 245792 | tf_op jit(solution)/shard_map/ppermute | solution.py:385
  82.6 1.5 collective-permute-done.10.refs_6_
  84.0 1.8 shard_map.62.refs_1_
  85.8 11.3 %shard_map.63 = (f32[16,64,256]{2,1,0:T(8,128)S(1)}, f32[16,32,256]{2,1,0:T(8,128)S(1)}, f32[15,32,256]{2,1,0:T(8,128)S(1)}, f32[15,32,256]{2,1,0:T(8,128)S(1)}) custom-call(f32[16,32,256]{2,1,0:T(8,128)S(1)} %collective-permute-done.5.refs_0_, f32[16,32,256]{2,1,0:T(8,128)S(1)} %shard_map.62.refs_1_, f32[16,32,256]{2,1,0:T(8,128)S(1)} %shard_map.59.refs_8_.refs_2_, ...), custom_call_target="tpu_custom_call" | custom-call | tf_op jit(solution)/shard_map/pallas_call | solution.py:370
  97.1 0.0 collective-permute-start.12
  97.1 6.7 %collective-permute-done.12.next_ref = f32[16,32,256]{2,1,0:T(8,128)S(1)} collective-permute-done((f32[16,32,256]{2,1,0:T(8,128)S(1)}, f32[16,32,256]{2,1,0:T(8,128)S(1)}, u32[]{:S(2)}, u32[]{:S(2)}) %collective-permute-start.12) | collective-permute-done | bytes 524320 | tf_op jit(solution)/shard_map/ppermute | solution.py:391
  103.8 4.9 %shard_map.64 = (f32[15,32,256]{2,1,0:T(8,128)S(1)}, f32[15,32,256]{2,1,0:T(8,128)S(1)}) custom-call(f32[16,64,256]{2,1,0:T(8,128)S(1)} %get-tuple-element.53.est_ref.refs_3_, f32[16,32,256]{2,1,0:T(8,128)S(1)} %collective-permute-done.12.next_ref, bf16[16,2,64,128]{3,2,1,0:T(8,128)(2,1)S(1)} %get-tuple-element.35.wx_ref.refs_8_, ...), custom_call_target="tpu_custom_call" | custom-call | tf_op jit(solution)/shard_map/pallas_call | solution.py:231
  108.7 4.4 %collective-permute-start.13 = (f32[15,32,256]{2,1,0:T(8,128)S(1)}, f32[15,32,256]{2,1,0:T(8,128)S(1)}, u32[]{:S(2)}, u32[]{:S(2)}) collective-permute-start(f32[15,32,256]{2,1,0:T(8,128)S(1)} %get-tuple-element.56.refs_1_), channel_id=1, source_target_pairs={{0,1},{1,2},{2,3},{4,5},{5,6},{6,7},{8,9},{9,10},{10,11},{12,13},{... | collective-permute-start | bytes 1474568 | tf_op jit(solution)/shard_map/ppermute | solution.py:384
  113.1 1.3 collective-permute-start.14
  114.4 8.4 %collective-permute-done.13.refs_2_ = f32[15,32,256]{2,1,0:T(8,128)S(1)} collective-permute-done((f32[15,32,256]{2,1,0:T(8,128)S(1)}, f32[15,32,256]{2,1,0:T(8,128)S(1)}, u32[]{:S(2)}, u32[]{:S(2)}) %collective-permute-start.13) | collective-permute-done | bytes 491552 | tf_op jit(solution)/shard_map/ppermute | solution.py:384
  122.8 4.7 %collective-permute-done.14.refs_3_ = f32[15,32,256]{2,1,0:T(8,128)S(1)} collective-permute-done((f32[15,32,256]{2,1,0:T(8,128)S(1)}, f32[15,32,256]{2,1,0:T(8,128)S(1)}, u32[]{:S(2)}, u32[]{:S(2)}) %collective-permute-start.14) | collective-permute-done | bytes 491552 | tf_op jit(solution)/shard_map/ppermute | solution.py:385
  127.5 1.8 shard_map.65
  129.3 3.4 %collective-permute-start.15 = (f32[15,32,256]{2,1,0:T(8,128)S(1)}, f32[15,32,256]{2,1,0:T(8,128)S(1)}, u32[]{:S(2)}, u32[]{:S(2)}) collective-permute-start(f32[15,32,256]{2,1,0:T(8,128)S(1)} %get-tuple-element.58.refs_1_), channel_id=1, source_target_pairs={{0,1},{1,2},{2,3},{4,5},{5,6},{6,7},{8,9},{9,10},{10,11},{12,13},{... | collective-permute-start | bytes 1474568 | tf_op jit(solution)/shard_map/ppermute | solution.py:384
  132.7 1.3 collective-permute-start.16
  134.0 1.3 collective-permute-start.19
  135.3 5.2 %collective-permute-start.18 = (f32[15,32,256]{2,1,0:T(8,128)S(1)}, f32[15,32,256]{2,1,0:T(8,128)S(1)}, u32[]{:S(2)}, u32[]{:S(2)}) collective-permute-start(f32[15,32,256]{2,1,0:T(8,128)S(1)} %get-tuple-element.60.refs_1_), channel_id=1, source_target_pairs={{0,1},{1,2},{2,3},{4,5},{5,6},{6,7},{8,9},{9,10},{10,11},{12,13},{... | collective-permute-start | bytes 1474568 | tf_op jit(solution)/shard_map/ppermute | solution.py:384
  140.5 3.4 %collective-permute-done.15.refs_2_ = f32[15,32,256]{2,1,0:T(8,128)S(1)} collective-permute-done((f32[15,32,256]{2,1,0:T(8,128)S(1)}, f32[15,32,256]{2,1,0:T(8,128)S(1)}, u32[]{:S(2)}, u32[]{:S(2)}) %collective-permute-start.15) | collective-permute-done | bytes 491552 | tf_op jit(solution)/shard_map/ppermute | solution.py:384
  143.9 4.6 %collective-permute-done.16.refs_3_ = f32[15,32,256]{2,1,0:T(8,128)S(1)} collective-permute-done((f32[15,32,256]{2,1,0:T(8,128)S(1)}, f32[15,32,256]{2,1,0:T(8,128)S(1)}, u32[]{:S(2)}, u32[]{:S(2)}) %collective-permute-start.16) | collective-permute-done | bytes 491552 | tf_op jit(solution)/shard_map/ppermute | solution.py:385
  148.5 1.7 shard_map.66.refs_8_.refs_2_
  150.3 0.5 collective-permute-start.17
  150.8 8.3 %collective-permute-done.19.refs_3_ = f32[15,32,256]{2,1,0:T(8,128)S(1)} collective-permute-done((f32[15,32,256]{2,1,0:T(8,128)S(1)}, f32[15,32,256]{2,1,0:T(8,128)S(1)}, u32[]{:S(2)}, u32[]{:S(2)}) %collective-permute-start.19) | collective-permute-done | bytes 491552 | tf_op jit(solution)/shard_map/ppermute | solution.py:385
  159.1 1.2 shard_map.67
  160.3 1.3 collective-permute-start.21
  161.6 4.6 %collective-permute-start.20 = (f32[15,16,256]{2,1,0:T(8,128)S(1)}, f32[15,16,256]{2,1,0:T(8,128)S(1)}, u32[]{:S(2)}, u32[]{:S(2)}) collective-permute-start(f32[15,16,256]{2,1,0:T(8,128)S(1)} %get-tuple-element.62.refs_1_), channel_id=1, source_target_pairs={{0,1},{1,2},{2,3},{4,5},{5,6},{6,7},{8,9},{9,10},{10,11},{12,13},{... | collective-permute-start | bytes 737288 | tf_op jit(solution)/shard_map/ppermute | solution.py:384
  166.1 1.2 shard_map.68
  167.3 1.3 collective-permute-start.23
  168.6 4.6 %collective-permute-start.22 = (f32[15,16,256]{2,1,0:T(8,128)S(1)}, f32[15,16,256]{2,1,0:T(8,128)S(1)}, u32[]{:S(2)}, u32[]{:S(2)}) collective-permute-start(f32[15,16,256]{2,1,0:T(8,128)S(1)} %get-tuple-element.64.refs_5_), channel_id=1, source_target_pairs={{0,1},{1,2},{2,3},{4,5},{5,6},{6,7},{8,9},{9,10},{10,11},{12,13},{... | collective-permute-start | bytes 737288 | tf_op jit(solution)/shard_map/ppermute | solution.py:384
  173.2 3.4 %collective-permute-done.23.refs_7_ = f32[15,16,256]{2,1,0:T(8,128)S(1)} collective-permute-done((f32[15,16,256]{2,1,0:T(8,128)S(1)}, f32[15,16,256]{2,1,0:T(8,128)S(1)}, u32[]{:S(2)}, u32[]{:S(2)}) %collective-permute-start.23) | collective-permute-done | bytes 245792 | tf_op jit(solution)/shard_map/ppermute | solution.py:385
  176.6 1.2 collective-permute-done.22.refs_6_
  177.8 1.8 shard_map.69.refs_1_
  179.6 3.4 %shard_map.70 = f32[16,64,256]{2,1,0:T(8,128)} custom-call(f32[16,32,256]{2,1,0:T(8,128)S(1)} %collective-permute-done.17.refs_0_, f32[16,32,256]{2,1,0:T(8,128)S(1)} %shard_map.69.refs_1_, f32[16,32,256]{2,1,0:T(8,128)S(1)} %shard_map.66.refs_8_.refs_2_, f32[16,64,256]{2,1,0:T(8,128)S(1)} %get-tuple-element.53.est_ref.refs_3_, ...), custom_call_target="tpu_custom_call" | custom-call | tf_op jit(solution)/shard_map/pallas_call | solution.py:370
  (18 shorter events, 0.0 us)
Async XLA Ops:
  0.0 14.5 %copy-start.1 = (f32[16,64,256]{2,1,0:T(8,128)S(1)}, f32[16,64,256]{2,1,0:T(8,128)}, u32[]{:S(2)}) copy-start(f32[16,64,256]{2,1,0:T(8,128)} %refs_3_.1) | copy-start | bytes 3145732
  1.2 13.3 %collective-permute-start = (f32[16,32,256]{2,1,0:T(8,128)S(1)}, f32[16,32,256]{2,1,0:T(8,128)S(1)}, u32[]{:S(2)}, u32[]{:S(2)}) collective-permute-start(f32[16,32,256]{2,1,0:T(8,128)S(1)} %slice.3), channel_id=1, source_target_pairs={{0,12},{4,0},{8,4},{12,8},{1,13},{5,1},{9,5},{13,9},{2,14},{6,2},{... | collective-permute-start | bytes 1572872 | tf_op jit(solution)/shard_map/ppermute | solution.py:391
  3.7 1.2 copy-start
  4.9 0.7 copy-start.5
  5.6 0.7 copy-start.6
  6.3 0.7 copy-start.7
  14.4 4.9 %copy-start.2 = (bf16[16,256,256]{2,1,0:T(8,128)(2,1)}, bf16[16,256,256]{2,1,0:T(8,128)(2,1)S(1)}, u32[]{:S(2)}) copy-start(bf16[16,256,256]{2,1,0:T(8,128)(2,1)S(1)} %get-tuple-element.37.al_ref.refs_10_) | copy-start | bytes 6291460
  14.5 9.7 %copy-start.4 = (f32[31]{0:T(128)S(1)}, f32[31]{0:T(128)}, u32[]{:S(2)}) copy-start(f32[31]{0:T(128)} %tz_ref.21) | copy-start | bytes 376
  19.4 13.7 %collective-permute-start.1 = (f32[15,32,256]{2,1,0:T(8,128)S(1)}, f32[15,32,256]{2,1,0:T(8,128)S(1)}, u32[]{:S(2)}, u32[]{:S(2)}) collective-permute-start(f32[15,32,256]{2,1,0:T(8,128)S(1)} %get-tuple-element.40.refs_1_), channel_id=1, source_target_pairs={{0,1},{1,2},{2,3},{4,5},{5,6},{6,7},{8,9},{9,10},{10,11},{12,13},{... | collective-permute-start | bytes 1474568 | tf_op jit(solution)/shard_map/ppermute | solution.py:384
  22.9 14.3 %collective-permute-start.2 = (f32[15,32,256]{2,1,0:T(8,128)S(1)}, f32[15,32,256]{2,1,0:T(8,128)S(1)}, u32[]{:S(2)}, u32[]{:S(2)}) collective-permute-start(f32[15,32,256]{2,1,0:T(8,128)S(1)} %get-tuple-element.38.after_ref.refs_0_.refs_4_), channel_id=1, source_target_pairs={{1,0},{2,1},{3,2},{5,4},{6,5},{7,6},{9,8},{10,9},{11,10},{13,12},{... | collective-permute-start | bytes 1474568 | tf_op jit(solution)/shard_map/ppermute | solution.py:385
  39.1 15.1 %collective-permute-start.3 = (f32[15,32,256]{2,1,0:T(8,128)S(1)}, f32[15,32,256]{2,1,0:T(8,128)S(1)}, u32[]{:S(2)}, u32[]{:S(2)}) collective-permute-start(f32[15,32,256]{2,1,0:T(8,128)S(1)} %get-tuple-element.42.refs_1_), channel_id=1, source_target_pairs={{0,1},{1,2},{2,3},{4,5},{5,6},{6,7},{8,9},{9,10},{10,11},{12,13},{... | collective-permute-start | bytes 1474568 | tf_op jit(solution)/shard_map/ppermute | solution.py:384
  42.6 16.1 %collective-permute-start.4 = (f32[15,32,256]{2,1,0:T(8,128)S(1)}, f32[15,32,256]{2,1,0:T(8,128)S(1)}, u32[]{:S(2)}, u32[]{:S(2)}) collective-permute-start(f32[15,32,256]{2,1,0:T(8,128)S(1)} %get-tuple-element.41.refs_0_.refs_4_), channel_id=1, source_target_pairs={{1,0},{2,1},{3,2},{5,4},{6,5},{7,6},{9,8},{10,9},{11,10},{13,12},{... | collective-permute-start | bytes 1474568 | tf_op jit(solution)/shard_map/ppermute | solution.py:385
  43.9 22.4 %collective-permute-start.7 = (f32[15,32,256]{2,1,0:T(8,128)S(1)}, f32[15,32,256]{2,1,0:T(8,128)S(1)}, u32[]{:S(2)}, u32[]{:S(2)}) collective-permute-start(f32[15,32,256]{2,1,0:T(8,128)S(1)} %get-tuple-element.43.refs_0_), channel_id=1, source_target_pairs={{1,0},{2,1},{3,2},{5,4},{6,5},{7,6},{9,8},{10,9},{11,10},{13,12},{... | collective-permute-start | bytes 1474568 | tf_op jit(solution)/shard_map/ppermute | solution.py:385
  45.2 21.1 %collective-permute-start.6 = (f32[15,32,256]{2,1,0:T(8,128)S(1)}, f32[15,32,256]{2,1,0:T(8,128)S(1)}, u32[]{:S(2)}, u32[]{:S(2)}) collective-permute-start(f32[15,32,256]{2,1,0:T(8,128)S(1)} %get-tuple-element.44.refs_1_), channel_id=1, source_target_pairs={{0,1},{1,2},{2,3},{4,5},{5,6},{6,7},{8,9},{9,10},{10,11},{12,13},{... | collective-permute-start | bytes 1474568 | tf_op jit(solution)/shard_map/ppermute | solution.py:384
  60.4 25.4 %collective-permute-start.5 = (f32[16,32,256]{2,1,0:T(8,128)S(1)}, f32[16,32,256]{2,1,0:T(8,128)S(1)}, u32[]{:S(2)}, u32[]{:S(2)}) collective-permute-start(f32[16,32,256]{2,1,0:T(8,128)S(1)} %shard_map.59.refs_8_.refs_2_), channel_id=1, source_target_pairs={{0,4},{4,8},{8,12},{12,0},{1,5},{5,9},{9,13},{13,1},{2,6},{6,10},{... | collective-permute-start | bytes 1572872 | tf_op jit(solution)/shard_map/ppermute | solution.py:391
  67.4 12.9 %collective-permute-start.9 = (f32[15,16,256]{2,1,0:T(8,128)S(1)}, f32[15,16,256]{2,1,0:T(8,128)S(1)}, u32[]{:S(2)}, u32[]{:S(2)}) collective-permute-start(f32[15,16,256]{2,1,0:T(8,128)S(1)} %get-tuple-element.45.refs_0_), channel_id=1, source_target_pairs={{1,0},{2,1},{3,2},{5,4},{6,5},{7,6},{9,8},{10,9},{11,10},{13,12},{... | collective-permute-start | bytes 737288 | tf_op jit(solution)/shard_map/ppermute | solution.py:385
  68.7 11.6 %collective-permute-start.8 = (f32[15,16,256]{2,1,0:T(8,128)S(1)}, f32[15,16,256]{2,1,0:T(8,128)S(1)}, u32[]{:S(2)}, u32[]{:S(2)}) collective-permute-start(f32[15,16,256]{2,1,0:T(8,128)S(1)} %get-tuple-element.46.refs_1_), channel_id=1, source_target_pairs={{0,1},{1,2},{2,3},{4,5},{5,6},{6,7},{8,9},{9,10},{10,11},{12,13},{... | collective-permute-start | bytes 737288 | tf_op jit(solution)/shard_map/ppermute | solution.py:384
  74.5 8.1 %collective-permute-start.11 = (f32[15,16,256]{2,1,0:T(8,128)S(1)}, f32[15,16,256]{2,1,0:T(8,128)S(1)}, u32[]{:S(2)}, u32[]{:S(2)}) collective-permute-start(f32[15,16,256]{2,1,0:T(8,128)S(1)} %get-tuple-element.47.refs_4_), channel_id=1, source_target_pairs={{1,0},{2,1},{3,2},{5,4},{6,5},{7,6},{9,8},{10,9},{11,10},{13,12},{... | collective-permute-start | bytes 737288 | tf_op jit(solution)/shard_map/ppermute | solution.py:385
  75.8 8.3 %collective-permute-start.10 = (f32[15,16,256]{2,1,0:T(8,128)S(1)}, f32[15,16,256]{2,1,0:T(8,128)S(1)}, u32[]{:S(2)}, u32[]{:S(2)}) collective-permute-start(f32[15,16,256]{2,1,0:T(8,128)S(1)} %get-tuple-element.48.refs_5_), channel_id=1, source_target_pairs={{0,1},{1,2},{2,3},{4,5},{5,6},{6,7},{8,9},{9,10},{10,11},{12,13},{... | collective-permute-start | bytes 737288 | tf_op jit(solution)/shard_map/ppermute | solution.py:384
  85.8 18.0 %copy-start.3 = (bf16[16,256,256]{2,1,0:T(8,128)(2,1)S(1)}, bf16[16,256,256]{2,1,0:T(8,128)(2,1)}, u32[]{:S(2)}) copy-start(bf16[16,256,256]{2,1,0:T(8,128)(2,1)} %copy-done.2) | copy-start | bytes 6291460
  97.1 6.7 %collective-permute-start.12 = (f32[16,32,256]{2,1,0:T(8,128)S(1)}, f32[16,32,256]{2,1,0:T(8,128)S(1)}, u32[]{:S(2)}, u32[]{:S(2)}) collective-permute-start(f32[16,32,256]{2,1,0:T(8,128)S(1)} %get-tuple-element.54), channel_id=1, source_target_pairs={{0,12},{4,0},{8,4},{12,8},{1,13},{5,1},{9,5},{13,9},{2,14},{6,2},{... | collective-permute-start | bytes 1572872 | tf_op jit(solution)/shard_map/ppermute | solution.py:391
  108.7 14.1 %collective-permute-start.13 = (f32[15,32,256]{2,1,0:T(8,128)S(1)}, f32[15,32,256]{2,1,0:T(8,128)S(1)}, u32[]{:S(2)}, u32[]{:S(2)}) collective-permute-start(f32[15,32,256]{2,1,0:T(8,128)S(1)} %get-tuple-element.56.refs_1_), channel_id=1, source_target_pairs={{0,1},{1,2},{2,3},{4,5},{5,6},{6,7},{8,9},{9,10},{10,11},{12,13},{... | collective-permute-start | bytes 1474568 | tf_op jit(solution)/shard_map/ppermute | solution.py:384
  113.1 14.4 %collective-permute-start.14 = (f32[15,32,256]{2,1,0:T(8,128)S(1)}, f32[15,32,256]{2,1,0:T(8,128)S(1)}, u32[]{:S(2)}, u32[]{:S(2)}) collective-permute-start(f32[15,32,256]{2,1,0:T(8,128)S(1)} %get-tuple-element.55.refs_0_.refs_4_), channel_id=1, source_target_pairs={{1,0},{2,1},{3,2},{5,4},{6,5},{7,6},{9,8},{10,9},{11,10},{13,12},{... | collective-permute-start | bytes 1474568 | tf_op jit(solution)/shard_map/ppermute | solution.py:385
  129.3 14.6 %collective-permute-start.15 = (f32[15,32,256]{2,1,0:T(8,128)S(1)}, f32[15,32,256]{2,1,0:T(8,128)S(1)}, u32[]{:S(2)}, u32[]{:S(2)}) collective-permute-start(f32[15,32,256]{2,1,0:T(8,128)S(1)} %get-tuple-element.58.refs_1_), channel_id=1, source_target_pairs={{0,1},{1,2},{2,3},{4,5},{5,6},{6,7},{8,9},{9,10},{10,11},{12,13},{... | collective-permute-start | bytes 1474568 | tf_op jit(solution)/shard_map/ppermute | solution.py:384
  132.7 15.8 %collective-permute-start.16 = (f32[15,32,256]{2,1,0:T(8,128)S(1)}, f32[15,32,256]{2,1,0:T(8,128)S(1)}, u32[]{:S(2)}, u32[]{:S(2)}) collective-permute-start(f32[15,32,256]{2,1,0:T(8,128)S(1)} %get-tuple-element.57.refs_0_.refs_4_), channel_id=1, source_target_pairs={{1,0},{2,1},{3,2},{5,4},{6,5},{7,6},{9,8},{10,9},{11,10},{13,12},{... | collective-permute-start | bytes 1474568 | tf_op jit(solution)/shard_map/ppermute | solution.py:385
  134.0 25.0 %collective-permute-start.19 = (f32[15,32,256]{2,1,0:T(8,128)S(1)}, f32[15,32,256]{2,1,0:T(8,128)S(1)}, u32[]{:S(2)}, u32[]{:S(2)}) collective-permute-start(f32[15,32,256]{2,1,0:T(8,128)S(1)} %get-tuple-element.59.refs_0_), channel_id=1, source_target_pairs={{1,0},{2,1},{3,2},{5,4},{6,5},{7,6},{9,8},{10,9},{11,10},{13,12},{... | collective-permute-start | bytes 1474568 | tf_op jit(solution)/shard_map/ppermute | solution.py:385
  135.3 23.8 %collective-permute-start.18 = (f32[15,32,256]{2,1,0:T(8,128)S(1)}, f32[15,32,256]{2,1,0:T(8,128)S(1)}, u32[]{:S(2)}, u32[]{:S(2)}) collective-permute-start(f32[15,32,256]{2,1,0:T(8,128)S(1)} %get-tuple-element.60.refs_1_), channel_id=1, source_target_pairs={{0,1},{1,2},{2,3},{4,5},{5,6},{6,7},{8,9},{9,10},{10,11},{12,13},{... | collective-permute-start | bytes 1474568 | tf_op jit(solution)/shard_map/ppermute | solution.py:384
  150.3 29.3 %collective-permute-start.17 = (f32[16,32,256]{2,1,0:T(8,128)S(1)}, f32[16,32,256]{2,1,0:T(8,128)S(1)}, u32[]{:S(2)}, u32[]{:S(2)}) collective-permute-start(f32[16,32,256]{2,1,0:T(8,128)S(1)} %shard_map.66.refs_8_.refs_2_), channel_id=1, source_target_pairs={{0,4},{4,8},{8,12},{12,0},{1,5},{5,9},{9,13},{13,1},{2,6},{6,10},{... | collective-permute-start | bytes 1572872 | tf_op jit(solution)/shard_map/ppermute | solution.py:391
  160.3 12.9 %collective-permute-start.21 = (f32[15,16,256]{2,1,0:T(8,128)S(1)}, f32[15,16,256]{2,1,0:T(8,128)S(1)}, u32[]{:S(2)}, u32[]{:S(2)}) collective-permute-start(f32[15,16,256]{2,1,0:T(8,128)S(1)} %get-tuple-element.61.refs_0_), channel_id=1, source_target_pairs={{1,0},{2,1},{3,2},{5,4},{6,5},{7,6},{9,8},{10,9},{11,10},{13,12},{... | collective-permute-start | bytes 737288 | tf_op jit(solution)/shard_map/ppermute | solution.py:385
  161.6 11.6 %collective-permute-start.20 = (f32[15,16,256]{2,1,0:T(8,128)S(1)}, f32[15,16,256]{2,1,0:T(8,128)S(1)}, u32[]{:S(2)}, u32[]{:S(2)}) collective-permute-start(f32[15,16,256]{2,1,0:T(8,128)S(1)} %get-tuple-element.62.refs_1_), channel_id=1, source_target_pairs={{0,1},{1,2},{2,3},{4,5},{5,6},{6,7},{8,9},{9,10},{10,11},{12,13},{... | collective-permute-start | bytes 737288 | tf_op jit(solution)/shard_map/ppermute | solution.py:384
  167.3 9.3 %collective-permute-start.23 = (f32[15,16,256]{2,1,0:T(8,128)S(1)}, f32[15,16,256]{2,1,0:T(8,128)S(1)}, u32[]{:S(2)}, u32[]{:S(2)}) collective-permute-start(f32[15,16,256]{2,1,0:T(8,128)S(1)} %get-tuple-element.63.refs_4_), channel_id=1, source_target_pairs={{1,0},{2,1},{3,2},{5,4},{6,5},{7,6},{9,8},{10,9},{11,10},{13,12},{... | collective-permute-start | bytes 737288 | tf_op jit(solution)/shard_map/ppermute | solution.py:385
  168.6 9.2 %collective-permute-start.22 = (f32[15,16,256]{2,1,0:T(8,128)S(1)}, f32[15,16,256]{2,1,0:T(8,128)S(1)}, u32[]{:S(2)}, u32[]{:S(2)}) collective-permute-start(f32[15,16,256]{2,1,0:T(8,128)S(1)} %get-tuple-element.64.refs_5_), channel_id=1, source_target_pairs={{0,1},{1,2},{2,3},{4,5},{5,6},{6,7},{8,9},{9,10},{10,11},{12,13},{... | collective-permute-start | bytes 737288 | tf_op jit(solution)/shard_map/ppermute | solution.py:384

commit v3 on v2

--- a/solution.py
+++ b/solution.py
@@ -40,6 +40,12 @@
     u_hi, u_lo = split(u)
     both = mm(jnp.concatenate([u_hi, u_lo], axis=0), a_hi)
     return both[:count] + both[count:] + mm(u_hi, a_lo)
+
+
+def cost(microseconds):
+    return pl.CostEstimate(
+        flops=int(microseconds * 1e9), bytes_accessed=int(microseconds * 3.5e6), transcendentals=0
+    )
 
 
 def full(shape):
@@ -152,6 +158,7 @@
         out_specs=[planes(x.shape, per) for x in (a, a, w)] + [full(send.shape)] * 2,
         out_shape=[a, a, w, send, send],
         compiler_params=PARAMS,
+        cost_estimate=cost(1.0),
     )(place, band_index, taps_x, taps_y, est)
 
 
@@ -207,6 +214,7 @@
         out_specs=[planes(x.shape, per) for x in (a, a, w, field, field)],
         out_shape=[a, a, w, field, field],
         compiler_params=PARAMS,
+        cost_estimate=cost(1.0),
     )(place, band_index, taps_x, taps_y, taps_z, after, obs, beyond)
 
 
@@ -235,6 +243,7 @@
         out_specs=[full(send.shape)] * 2,
         out_shape=[send] * 2,
         compiler_params=PARAMS,
+        cost_estimate=cost(1.0),
     )(*args)
 
 
@@ -288,7 +297,7 @@
     tiles(count, columns, body)
 
 
-def depth_ratio(taps_z, obs, chunk, skip, obs_skip, count, after=None):
+def depth_ratio(taps_z, obs, chunk, skip, obs_skip, count, after=None, micro=1.0):
     n, _, columns = obs.shape
     radius = taps_z.shape[0] // 2
     send = shape_of(radius, count, columns)
@@ -299,42 +308,39 @@
         out_specs=[VMEM] * 2,
         out_shape=[send] * 2,
         compiler_params=PARAMS,
+        cost_estimate=cost(micro),
     )(taps_z, obs, *chunk, *extra)
 
 
-def back_kernel(n, radius, groups, tz_ref, *refs):
+def back_kernel(n, radius, tz_ref, *refs):
     out_ref = refs[-1]
-    columns = out_ref.shape[2]
-    first = 0
-    for g in range(groups):
-        own = refs[4 * g : 4 * g + 4]
-        count = own[0].shape[1]
-
-        def body(start, lanes):
-            total = depth_sum(n, radius, True, tz_ref, own, at(start, 0), lanes)
-            for i in range(n):
-                out_ref[i, at(start, first), lanes] = total[i]
-
-        tiles(count, columns, body)
-        first += count
-
-
-def depth_back(taps_z, chunks, n, after=None):
-    radius, _, columns = chunks[0][0].shape
-    count = sum(chunk[0].shape[1] for chunk in chunks)
-    extra = [] if after is None else [after]
-    return pl.pallas_call(
-        functools.partial(back_kernel, n, radius, len(chunks)),
-        in_specs=[SMEM] + [VMEM] * (4 * len(chunks)) + [ANY] * len(extra),
+    _, count, columns = out_ref.shape
+
+    def body(start, lanes):
+        rows = at(start, 0)
+        total = depth_sum(n, radius, True, tz_ref, refs[:4], rows, lanes)
+        for i in range(n):
+            out_ref[i, rows, lanes] = total[i]
+
+    tiles(count, columns, body)
+
+
+def depth_back(taps_z, chunk, n, after, micro=1.0):
+    radius, count, columns = chunk[0].shape
+    return pl.pallas_call(
+        functools.partial(back_kernel, n, radius),
+        in_specs=[SMEM] + [VMEM] * 4 + [ANY],
         out_specs=VMEM,
         out_shape=shape_of(n, count, columns),
         compiler_params=PARAMS,
-    )(taps_z, *(x for chunk in chunks for x in chunk), *extra)
+        cost_estimate=cost(micro),
+    )(taps_z, *chunk, after)
 
 
 def update_kernel(per, n, radius, last, *refs):
-    before_ref, inner_ref, edge_ref, est_ref, rn_ref, wa_ref, bh_ref, bl_ref = refs[:8]
-    refs = refs[8:]
+    pieces, edge_ref, refs = refs[:4], refs[3], refs[4:]
+    est_ref, rn_ref, wa_ref, bh_ref, bl_ref = refs[:5]
+    refs = refs[5:]
     rows = est_ref.shape[1]
     halo = edge_ref.shape[1]
     if last:
@@ -343,7 +349,7 @@
         wx_ref, ah_ref, al_ref, out_ref, top_ref, low_ref, high_ref = refs
     for p in range(per):
         plane = pl.program_id(0) * per + p
-        c = jnp.concatenate([before_ref[p], inner_ref[p], edge_ref[p]], axis=0)
+        c = jnp.concatenate([piece[p] for piece in pieces], axis=0)
         c_hi, c_lo = split(c)
         used = rows + halo
         u = blur_rows(wa_ref[p, 0, :, :used], wa_ref[p, 1, :, :used], c_hi, c_lo)
@@ -356,11 +362,11 @@
             store_sends(v, plane, n, radius, low_ref, high_ref)
 
 
-def update(before, inner, edge, est, rn, adjoint, forward, radius, per):
+def update(pieces, est, rn, adjoint, forward, radius, per):
     n, rows, columns = est.shape
-    halo = edge.shape[1]
+    halo = pieces[0].shape[1]
     last = forward is None
-    args = [before, inner, edge, est, rn, *adjoint] + ([] if last else [*forward])
+    args = [*pieces, est, rn, *adjoint] + ([] if last else [*forward])
     out_specs, out_shape = [planes(est.shape, per)], [shape_of(*est.shape)]
     if not last:
         top = shape_of(n, halo, columns)
@@ -374,6 +380,7 @@
         out_specs=out_specs,
         out_shape=out_shape,
         compiler_params=PARAMS,
+        cost_estimate=cost(1.0),
     )(*args)
 
 
@@ -422,19 +429,20 @@
         r_first = depth_exchange(
             *depth_ratio(taps_z, shifted, v_inner, 0, 0, half, after=low)
         )
-        r_edge = depth_exchange(*depth_ratio(taps_z, shifted, v_edge, 0, inner, halo))
+        r_edge = depth_exchange(*depth_ratio(taps_z, shifted, v_edge, 0, inner, halo, after=r_first[0]))
         r_second = depth_exchange(
             *depth_ratio(
                 taps_z, shifted, v_inner, half, half, inner - half, after=r_edge[0]
             )
         )
-        c_edge = depth_back(taps_z, [r_edge], n)
+        c_first = depth_back(taps_z, r_first, n, after=r_second[0], micro=5.0)
+        c_edge = depth_back(taps_z, r_edge, n, after=c_first, micro=1.0)
         before = ring(c_edge, 1)
-        c_inner = depth_back(taps_z, [r_first, r_second], n, after=c_edge)
+        c_second = depth_back(taps_z, r_second, n, after=c_edge, micro=100.0)
         last = step == ITERS - 1
         out = update(
-            before, c_inner, c_edge, est, rn, adjoint, None if last else (wx, ah, al),
-            radius, per,
+            (before, c_first, c_second, c_edge), est, rn, adjoint,
+            None if last else (wx, ah, al), radius, per,
         )
         est = out[0]
         if not last:

time: 184 us -> 150 us (0.82)
  the two profiles are of different devices: /device:TPU:0 before, /device:TPU:1 now
where the time goes in v3:
time: 150 us; the launch traced here: 149 us
  starting transfers between devices  62.3 us (42%)
  Pallas kernels  51.3 us (34%)
  waiting for transfers between devices  31.1 us (21%)
  local copies, waits for them, and re-layouts  4.39 us (3%)
    ppermute x10, starting transfers between devices, depth_exchange(): zlo = lax.ppermute(high, 'slab', forward)  38.2 us
    pallas_call x2, Pallas kernels, update(): pl.pallas_call(functools.partial(update_kernel, per, n, radius, last), gr...  14.6 us
    ppermute x4, waiting for transfers between devices, ring(): lax.ppermute(x, 'row', [(i, (i + step) % count) for i in range(count)])  13.8 us
    ppermute x10, starting transfers between devices, depth_exchange(): zhi = lax.ppermute(low, 'slab', backward)  12.9 us
    ppermute x10, waiting for transfers between devices, depth_exchange(): zhi = lax.ppermute(low, 'slab', backward)  11.7 us
    ppermute x4, starting transfers between devices, ring(): lax.ppermute(x, 'row', [(i, (i + step) % count) for i in range(count)])  11.2 us
    pallas_call x2, Pallas kernels, edge_blur(): pl.pallas_call(functools.partial(edge_kernel, per, n, radius, halo), grid...  9.72 us
    pallas_call x6, Pallas kernels, depth_ratio(): pl.pallas_call(functools.partial(ratio_kernel, n, radius, skip, obs_skip)...  8.44 us
  transfers between devices with their start and end apart: 24, of which 10 were waited for; matrix products, arithmetic and copies ran while one was open for 0% of the time, Pallas kernels for 25%

profile of v3, /device:TPU:1, one launch (start us, length us, event | category | flops | bytes accessed | tf_op | source)
XLA Modules:
  0.0 149.5 jit_solution(12947352433269956521)
XLA Ops:
  0.0 1.1 slice.3
  1.1 0.1 collective-permute-start
  1.2 0.1 pad_add_fusion.place_ref
  1.3 1.2 copy-done.2
  2.5 0.7 copy-done.4
  3.2 0.7 copy-done.5
  3.9 0.7 copy-done.6
  4.5 7.5 %shard_map.55 = (bf16[16,256,256]{2,1,0:T(8,128)(2,1)S(1)}, bf16[16,256,256]{2,1,0:T(8,128)(2,1)S(1)}, bf16[16,2,64,128]{3,2,1,0:T(8,128)(2,1)S(1)}, f32[15,32,256]{2,1,0:T(8,128)S(1)}, f32[15,32,256]{2,1,0:T(8,128)S(1)}) custom-call(s32[3]{0:T(128)S(1)} %pad_add_fusion.place_ref, s32[16]{0:T(128)S(1)} %copy-done.6, f32[16,31]{1,0:T(8,128)S(1)} %copy-done.4, ...), custom_call_target="tpu_custom_call" | custom-call | flops 1000000000 | bytes 3500000 | tf_op jit(solution)/shard_map/pallas_call | solution.py:154
  12.0 0.0 copy-start
  12.0 1.3 collective-permute-start.4
  13.3 5.3 %collective-permute-start.3 = (f32[15,32,256]{2,1,0:T(8,128)S(1)}, f32[15,32,256]{2,1,0:T(8,128)S(1)}, u32[]{:S(2)}, u32[]{:S(2)}) collective-permute-start(f32[15,32,256]{2,1,0:T(8,128)S(1)} %get-tuple-element.42.refs_1_), channel_id=1, source_target_pairs={{0,1},{1,2},{2,3},{4,5},{5,6},{6,7},{8,9},{9,10},{10,11},{12,13},{... | collective-permute-start | bytes 1474568 | tf_op jit(solution)/shard_map/ppermute | solution.py:391
  18.7 0.0 collective-permute-done.next_ref
  18.7 0.0 copy-start.7
  18.7 4.9 %shard_map.56 = (f32[15,32,256]{2,1,0:T(8,128)S(1)}, f32[15,32,256]{2,1,0:T(8,128)S(1)}) custom-call(f32[16,64,256]{2,1,0:T(8,128)S(1)} %copy-done.2, f32[16,32,256]{2,1,0:T(8,128)S(1)} %collective-permute-done.next_ref, bf16[16,2,64,128]{3,2,1,0:T(8,128)(2,1)S(1)} %get-tuple-element.35.wx_ref.refs_9_, ...), custom_call_target="tpu_custom_call" | custom-call | flops 1000000000 | bytes 3500000 | tf_op jit(solution)/shard_map/pallas_call | solution.py:239
  23.6 3.4 %collective-permute-start.1 = (f32[15,32,256]{2,1,0:T(8,128)S(1)}, f32[15,32,256]{2,1,0:T(8,128)S(1)}, u32[]{:S(2)}, u32[]{:S(2)}) collective-permute-start(f32[15,32,256]{2,1,0:T(8,128)S(1)} %get-tuple-element.40.refs_1_), channel_id=1, source_target_pairs={{0,1},{1,2},{2,3},{4,5},{5,6},{6,7},{8,9},{9,10},{10,11},{12,13},{... | collective-permute-start | bytes 1474568 | tf_op jit(solution)/shard_map/ppermute | solution.py:391
  26.9 1.3 collective-permute-start.2
  28.3 2.9 %shard_map.57 = (bf16[16,256,256]{2,1,0:T(8,128)(2,1)S(1)}, bf16[16,256,256]{2,1,0:T(8,128)(2,1)S(1)}, bf16[16,2,64,128]{3,2,1,0:T(8,128)(2,1)S(1)}, f32[16,64,256]{2,1,0:T(8,128)S(1)}, f32[16,64,256]{2,1,0:T(8,128)S(1)}) custom-call(s32[3]{0:T(128)S(1)} %pad_add_fusion.place_ref, s32[16]{0:T(128)S(1)} %copy-done.6, f32[16,31]{1,0:T(8,128)S(1)} %copy-done.4, ...), custom_call_target="tpu_custom_call" | custom-call | flops 1000000000 | bytes 3500000 | tf_op jit(solution)/shard_map/pallas_call | solution.py:210
  31.2 0.0 collective-permute-done.3.refs_2_
  31.2 1.2 shard_map.58
  32.4 4.0 %collective-permute-start.7 = (f32[15,16,256]{2,1,0:T(8,128)S(1)}, f32[15,16,256]{2,1,0:T(8,128)S(1)}, u32[]{:S(2)}, u32[]{:S(2)}) collective-permute-start(f32[15,16,256]{2,1,0:T(8,128)S(1)} %get-tuple-element.46.refs_1_), channel_id=1, source_target_pairs={{0,1},{1,2},{2,3},{4,5},{5,6},{6,7},{8,9},{9,10},{10,11},{12,13},{... | collective-permute-start | bytes 737288 | tf_op jit(solution)/shard_map/ppermute | solution.py:391
  36.4 1.3 collective-permute-start.8
  37.7 0.6 collective-permute-done.1.refs_2_
  38.3 1.5 collective-permute-done.2.refs_3_
  39.8 1.8 %shard_map.59 = (f32[15,32,256]{2,1,0:T(8,128)S(1)}, f32[15,32,256]{2,1,0:T(8,128)S(1)}) custom-call(f32[31]{0:T(128)S(1)} %copy-done.7, f32[16,64,256]{2,1,0:T(8,128)S(1)} %get-tuple-element.39.obs_ref, f32[15,32,256]{2,1,0:T(8,128)S(1)} %get-tuple-element.38.after_ref.refs_4_.refs_0_, f32[15,32,256]{2,1,0:T(8,128)S(1)} %get-tuple-element.40.refs_1_, ...), custom_call_target="tpu_custom_call" | custom-call | flops 1000000000 | bytes 3500000 | tf_op jit(solution)/shard_map/pallas_call | solution.py:305
  41.6 3.2 %collective-permute-start.5 = (f32[15,32,256]{2,1,0:T(8,128)S(1)}, f32[15,32,256]{2,1,0:T(8,128)S(1)}, u32[]{:S(2)}, u32[]{:S(2)}) collective-permute-start(f32[15,32,256]{2,1,0:T(8,128)S(1)} %get-tuple-element.45.refs_1_), channel_id=1, source_target_pairs={{0,1},{1,2},{2,3},{4,5},{5,6},{6,7},{8,9},{9,10},{10,11},{12,13},{... | collective-permute-start | bytes 1474568 | tf_op jit(solution)/shard_map/ppermute | solution.py:391
  44.9 1.3 collective-permute-start.6
  46.2 1.2 shard_map.60
  47.4 4.0 %collective-permute-start.10 = (f32[15,16,256]{2,1,0:T(8,128)S(1)}, f32[15,16,256]{2,1,0:T(8,128)S(1)}, u32[]{:S(2)}, u32[]{:S(2)}) collective-permute-start(f32[15,16,256]{2,1,0:T(8,128)S(1)} %get-tuple-element.48.refs_1_), channel_id=1, source_target_pairs={{0,1},{1,2},{2,3},{4,5},{5,6},{6,7},{8,9},{9,10},{10,11},{12,13},{... | collective-permute-start | bytes 737288 | tf_op jit(solution)/shard_map/ppermute | solution.py:391
  51.4 0.0 collective-permute-done.7.refs_2_
  51.4 1.3 collective-permute-start.11
  52.7 1.1 shard_map.61.refs_4_.refs_1_
  53.8 1.7 %collective-permute-done.6.refs_3_ = f32[15,32,256]{2,1,0:T(8,128)S(1)} collective-permute-done((f32[15,32,256]{2,1,0:T(8,128)S(1)}, f32[15,32,256]{2,1,0:T(8,128)S(1)}, u32[]{:S(2)}, u32[]{:S(2)}) %collective-permute-start.6) | collective-permute-done | bytes 491552 | tf_op jit(solution)/shard_map/ppermute | solution.py:392
  55.5 1.7 %shard_map.62.refs_4_.refs_3_ = f32[16,32,256]{2,1,0:T(8,128)S(1)} custom-call(f32[31]{0:T(128)S(1)} %copy-done.7, f32[15,32,256]{2,1,0:T(8,128)S(1)} %get-tuple-element.44.refs_4_.refs_0_, f32[15,32,256]{2,1,0:T(8,128)S(1)} %get-tuple-element.45.refs_1_, f32[15,32,256]{2,1,0:T(8,128)S(1)} %collective-permute-done.5.refs_2_, ...), custom_call_target="tpu_custom_call" | custom-call | flops 1000000000 | bytes 3500000 | tf_op jit(solution)/shard_map/pallas_call | solution.py:330
  57.3 0.0 copy-start.3
  57.3 9.6 %collective-permute-start.9 = (f32[16,32,256]{2,1,0:T(8,128)S(1)}, f32[16,32,256]{2,1,0:T(8,128)S(1)}, u32[]{:S(2)}, u32[]{:S(2)}) collective-permute-start(f32[16,32,256]{2,1,0:T(8,128)S(1)} %shard_map.62.refs_4_.refs_3_), channel_id=1, source_target_pairs={{0,4},{4,8},{8,12},{12,0},{1,5},{5,9},{9,13},{13,1},{2,6},{6,10},{... | collective-permute-start | bytes 1572872 | tf_op jit(solution)/shard_map/ppermute | solution.py:398
  66.9 1.1 shard_map.63.refs_2_
  68.0 5.0 %collective-permute-done.9.refs_0_ = f32[16,32,256]{2,1,0:T(8,128)S(1)} collective-permute-done((f32[16,32,256]{2,1,0:T(8,128)S(1)}, f32[16,32,256]{2,1,0:T(8,128)S(1)}, u32[]{:S(2)}, u32[]{:S(2)}) %collective-permute-start.9) | collective-permute-done | bytes 524320 | tf_op jit(solution)/shard_map/ppermute | solution.py:398
  73.0 11.3 %shard_map.64 = (f32[16,64,256]{2,1,0:T(8,128)S(1)}, f32[16,32,256]{2,1,0:T(8,128)S(1)}, f32[15,32,256]{2,1,0:T(8,128)S(1)}, f32[15,32,256]{2,1,0:T(8,128)S(1)}) custom-call(f32[16,32,256]{2,1,0:T(8,128)S(1)} %collective-permute-done.9.refs_0_, f32[16,16,256]{2,1,0:T(8,128)S(1)} %shard_map.61.refs_4_.refs_1_, f32[16,16,256]{2,1,0:T(8,128)S(1)} %shard_map.63.refs_2_, ...), custom_call_target="tpu_custom_call" | custom-call | flops 1000000000 | bytes 3500000 | tf_op jit(solution)/shard_map/pallas_call | solution.py:376
  84.3 0.5 collective-permute-start.12
  84.8 1.3 collective-permute-start.16
  86.1 4.0 %collective-permute-start.15 = (f32[15,32,256]{2,1,0:T(8,128)S(1)}, f32[15,32,256]{2,1,0:T(8,128)S(1)}, u32[]{:S(2)}, u32[]{:S(2)}) collective-permute-start(f32[15,32,256]{2,1,0:T(8,128)S(1)} %get-tuple-element.58.refs_1_), channel_id=1, source_target_pairs={{0,1},{1,2},{2,3},{4,5},{5,6},{6,7},{8,9},{9,10},{10,11},{12,13},{... | collective-permute-start | bytes 1474568 | tf_op jit(solution)/shard_map/ppermute | solution.py:391
  90.1 3.9 %collective-permute-done.12.next_ref = f32[16,32,256]{2,1,0:T(8,128)S(1)} collective-permute-done((f32[16,32,256]{2,1,0:T(8,128)S(1)}, f32[16,32,256]{2,1,0:T(8,128)S(1)}, u32[]{:S(2)}, u32[]{:S(2)}) %collective-permute-start.12) | collective-permute-done | bytes 524320 | tf_op jit(solution)/shard_map/ppermute | solution.py:398
  94.0 4.9 %shard_map.65 = (f32[15,32,256]{2,1,0:T(8,128)S(1)}, f32[15,32,256]{2,1,0:T(8,128)S(1)}) custom-call(f32[16,64,256]{2,1,0:T(8,128)S(1)} %get-tuple-element.53.est_ref.refs_4_, f32[16,32,256]{2,1,0:T(8,128)S(1)} %collective-permute-done.12.next_ref, bf16[16,2,64,128]{3,2,1,0:T(8,128)(2,1)S(1)} %get-tuple-element.35.wx_ref.refs_9_, ...), custom_call_target="tpu_custom_call" | custom-call | flops 1000000000 | bytes 3500000 | tf_op jit(solution)/shard_map/pallas_call | solution.py:239
  98.8 3.0 %collective-permute-start.13 = (f32[15,32,256]{2,1,0:T(8,128)S(1)}, f32[15,32,256]{2,1,0:T(8,128)S(1)}, u32[]{:S(2)}, u32[]{:S(2)}) collective-permute-start(f32[15,32,256]{2,1,0:T(8,128)S(1)} %get-tuple-element.56.refs_1_), channel_id=1, source_target_pairs={{0,1},{1,2},{2,3},{4,5},{5,6},{6,7},{8,9},{9,10},{10,11},{12,13},{... | collective-permute-start | bytes 1474568 | tf_op jit(solution)/shard_map/ppermute | solution.py:391
  101.9 1.3 collective-permute-start.14
  103.2 1.2 shard_map.66
  104.4 4.0 %collective-permute-start.19 = (f32[15,16,256]{2,1,0:T(8,128)S(1)}, f32[15,16,256]{2,1,0:T(8,128)S(1)}, u32[]{:S(2)}, u32[]{:S(2)}) collective-permute-start(f32[15,16,256]{2,1,0:T(8,128)S(1)} %get-tuple-element.62.refs_1_), channel_id=1, source_target_pairs={{0,1},{1,2},{2,3},{4,5},{5,6},{6,7},{8,9},{9,10},{10,11},{12,13},{... | collective-permute-start | bytes 737288 | tf_op jit(solution)/shard_map/ppermute | solution.py:391
  108.4 1.3 collective-permute-start.20
  109.7 3.2 %collective-permute-done.13.refs_2_ = f32[15,32,256]{2,1,0:T(8,128)S(1)} collective-permute-done((f32[15,32,256]{2,1,0:T(8,128)S(1)}, f32[15,32,256]{2,1,0:T(8,128)S(1)}, u32[]{:S(2)}, u32[]{:S(2)}) %collective-permute-start.13) | collective-permute-done | bytes 491552 | tf_op jit(solution)/shard_map/ppermute | solution.py:391
  112.9 4.1 %collective-permute-done.14.refs_3_ = f32[15,32,256]{2,1,0:T(8,128)S(1)} collective-permute-done((f32[15,32,256]{2,1,0:T(8,128)S(1)}, f32[15,32,256]{2,1,0:T(8,128)S(1)}, u32[]{:S(2)}, u32[]{:S(2)}) %collective-permute-start.14) | collective-permute-done | bytes 491552 | tf_op jit(solution)/shard_map/ppermute | solution.py:392
  117.1 1.8 %shard_map.67 = (f32[15,32,256]{2,1,0:T(8,128)S(1)}, f32[15,32,256]{2,1,0:T(8,128)S(1)}) custom-call(f32[31]{0:T(128)S(1)} %copy-done.7, f32[16,64,256]{2,1,0:T(8,128)S(1)} %get-tuple-element.39.obs_ref, f32[15,32,256]{2,1,0:T(8,128)S(1)} %get-tuple-element.55.refs_4_.refs_0_, f32[15,32,256]{2,1,0:T(8,128)S(1)} %get-tuple-element.56.refs_1_, ...), custom_call_target="tpu_custom_call" | custom-call | flops 1000000000 | bytes 3500000 | tf_op jit(solution)/shard_map/pallas_call | solution.py:305
  118.9 3.2 %collective-permute-start.17 = (f32[15,32,256]{2,1,0:T(8,128)S(1)}, f32[15,32,256]{2,1,0:T(8,128)S(1)}, u32[]{:S(2)}, u32[]{:S(2)}) collective-permute-start(f32[15,32,256]{2,1,0:T(8,128)S(1)} %get-tuple-element.61.refs_1_), channel_id=1, source_target_pairs={{0,1},{1,2},{2,3},{4,5},{5,6},{6,7},{8,9},{9,10},{10,11},{12,13},{... | collective-permute-start | bytes 1474568 | tf_op jit(solution)/shard_map/ppermute | solution.py:391
  122.2 1.3 collective-permute-start.18
  123.5 1.2 shard_map.68
  124.6 4.0 %collective-permute-start.22 = (f32[15,16,256]{2,1,0:T(8,128)S(1)}, f32[15,16,256]{2,1,0:T(8,128)S(1)}, u32[]{:S(2)}, u32[]{:S(2)}) collective-permute-start(f32[15,16,256]{2,1,0:T(8,128)S(1)} %get-tuple-element.64.refs_1_), channel_id=1, source_target_pairs={{0,1},{1,2},{2,3},{4,5},{5,6},{6,7},{8,9},{9,10},{10,11},{12,13},{... | collective-permute-start | bytes 737288 | tf_op jit(solution)/shard_map/ppermute | solution.py:391
  128.7 1.3 collective-permute-start.23
  130.0 1.1 shard_map.69.refs_4_.refs_1_
  131.1 1.7 %collective-permute-done.17.refs_2_ = f32[15,32,256]{2,1,0:T(8,128)S(1)} collective-permute-done((f32[15,32,256]{2,1,0:T(8,128)S(1)}, f32[15,32,256]{2,1,0:T(8,128)S(1)}, u32[]{:S(2)}, u32[]{:S(2)}) %collective-permute-start.17) | collective-permute-done | bytes 491552 | tf_op jit(solution)/shard_map/ppermute | solution.py:391
  132.8 4.4 %collective-permute-done.18.refs_3_ = f32[15,32,256]{2,1,0:T(8,128)S(1)} collective-permute-done((f32[15,32,256]{2,1,0:T(8,128)S(1)}, f32[15,32,256]{2,1,0:T(8,128)S(1)}, u32[]{:S(2)}, u32[]{:S(2)}) %collective-permute-start.18) | collective-permute-done | bytes 491552 | tf_op jit(solution)/shard_map/ppermute | solution.py:392
  137.3 1.7 %shard_map.70.refs_4_.refs_3_ = f32[16,32,256]{2,1,0:T(8,128)S(1)} custom-call(f32[31]{0:T(128)S(1)} %copy-done.7, f32[15,32,256]{2,1,0:T(8,128)S(1)} %get-tuple-element.60.refs_4_.refs_0_, f32[15,32,256]{2,1,0:T(8,128)S(1)} %get-tuple-element.61.refs_1_, f32[15,32,256]{2,1,0:T(8,128)S(1)} %collective-permute-done.17.refs_2_, ...), custom_call_target="tpu_custom_call" | custom-call | flops 1000000000 | bytes 3500000 | tf_op jit(solution)/shard_map/pallas_call | solution.py:330
  139.0 1.0 collective-permute-start.21
  140.0 1.1 shard_map.71.refs_2_
  141.1 5.0 %collective-permute-done.21.refs_0_ = f32[16,32,256]{2,1,0:T(8,128)S(1)} collective-permute-done((f32[16,32,256]{2,1,0:T(8,128)S(1)}, f32[16,32,256]{2,1,0:T(8,128)S(1)}, u32[]{:S(2)}, u32[]{:S(2)}) %collective-permute-start.21) | collective-permute-done | bytes 524320 | tf_op jit(solution)/shard_map/ppermute | solution.py:398
  146.1 3.3 %shard_map.72 = f32[16,64,256]{2,1,0:T(8,128)} custom-call(f32[16,32,256]{2,1,0:T(8,128)S(1)} %collective-permute-done.21.refs_0_, f32[16,16,256]{2,1,0:T(8,128)S(1)} %shard_map.69.refs_4_.refs_1_, f32[16,16,256]{2,1,0:T(8,128)S(1)} %shard_map.71.refs_2_, f32[16,32,256]{2,1,0:T(8,128)S(1)} %shard_map.70.refs_4_.refs_3_, ...), custom_call_target="tpu_custom_call" | custom-call | flops 1000000000 | bytes 3500000 | tf_op jit(solution)/shard_map/pallas_call | solution.py:376
  (20 shorter events, 0.0 us)
Async XLA Ops:
  1.1 17.6 %collective-permute-start = (f32[16,32,256]{2,1,0:T(8,128)S(1)}, f32[16,32,256]{2,1,0:T(8,128)S(1)}, u32[]{:S(2)}, u32[]{:S(2)}) collective-permute-start(f32[16,32,256]{2,1,0:T(8,128)S(1)} %slice.3), channel_id=1, source_target_pairs={{0,12},{4,0},{8,4},{12,8},{1,13},{5,1},{9,5},{13,9},{2,14},{6,2},{... | collective-permute-start | bytes 1572872 | tf_op jit(solution)/shard_map/ppermute | solution.py:398
  1.3 1.2 copy-start.2
  2.5 0.7 copy-start.4
  3.2 0.7 copy-start.5
  3.9 0.7 copy-start.6
  12.0 11.5 %copy-start = (bf16[16,256,256]{2,1,0:T(8,128)(2,1)}, bf16[16,256,256]{2,1,0:T(8,128)(2,1)S(1)}, u32[]{:S(2)}) copy-start(bf16[16,256,256]{2,1,0:T(8,128)(2,1)S(1)} %get-tuple-element.37.al_ref.refs_11_) | copy-start | bytes 6291460
  12.0 19.2 %collective-permute-start.4 = (f32[15,32,256]{2,1,0:T(8,128)S(1)}, f32[15,32,256]{2,1,0:T(8,128)S(1)}, u32[]{:S(2)}, u32[]{:S(2)}) collective-permute-start(f32[15,32,256]{2,1,0:T(8,128)S(1)} %get-tuple-element.41.refs_0_), channel_id=1, source_target_pairs={{1,0},{2,1},{3,2},{5,4},{6,5},{7,6},{9,8},{10,9},{11,10},{13,12},{... | collective-permute-start | bytes 1474568 | tf_op jit(solution)/shard_map/ppermute | solution.py:392
  13.3 17.9 %collective-permute-start.3 = (f32[15,32,256]{2,1,0:T(8,128)S(1)}, f32[15,32,256]{2,1,0:T(8,128)S(1)}, u32[]{:S(2)}, u32[]{:S(2)}) collective-permute-start(f32[15,32,256]{2,1,0:T(8,128)S(1)} %get-tuple-element.42.refs_1_), channel_id=1, source_target_pairs={{0,1},{1,2},{2,3},{4,5},{5,6},{6,7},{8,9},{9,10},{10,11},{12,13},{... | collective-permute-start | bytes 1474568 | tf_op jit(solution)/shard_map/ppermute | solution.py:391
  18.7 9.6 %copy-start.7 = (f32[31]{0:T(128)S(1)}, f32[31]{0:T(128)}, u32[]{:S(2)}) copy-start(f32[31]{0:T(128)} %tz_ref.25) | copy-start | bytes 376
  23.6 14.7 %collective-permute-start.1 = (f32[15,32,256]{2,1,0:T(8,128)S(1)}, f32[15,32,256]{2,1,0:T(8,128)S(1)}, u32[]{:S(2)}, u32[]{:S(2)}) collective-permute-start(f32[15,32,256]{2,1,0:T(8,128)S(1)} %get-tuple-element.40.refs_1_), channel_id=1, source_target_pairs={{0,1},{1,2},{2,3},{4,5},{5,6},{6,7},{8,9},{9,10},{10,11},{12,13},{... | collective-permute-start | bytes 1474568 | tf_op jit(solution)/shard_map/ppermute | solution.py:391
  26.9 12.8 %collective-permute-start.2 = (f32[15,32,256]{2,1,0:T(8,128)S(1)}, f32[15,32,256]{2,1,0:T(8,128)S(1)}, u32[]{:S(2)}, u32[]{:S(2)}) collective-permute-start(f32[15,32,256]{2,1,0:T(8,128)S(1)} %get-tuple-element.38.after_ref.refs_4_.refs_0_), channel_id=1, source_target_pairs={{1,0},{2,1},{3,2},{5,4},{6,5},{7,6},{9,8},{10,9},{11,10},{13,12},{... | collective-permute-start | bytes 1474568 | tf_op jit(solution)/shard_map/ppermute | solution.py:392
  32.4 19.0 %collective-permute-start.7 = (f32[15,16,256]{2,1,0:T(8,128)S(1)}, f32[15,16,256]{2,1,0:T(8,128)S(1)}, u32[]{:S(2)}, u32[]{:S(2)}) collective-permute-start(f32[15,16,256]{2,1,0:T(8,128)S(1)} %get-tuple-element.46.refs_1_), channel_id=1, source_target_pairs={{0,1},{1,2},{2,3},{4,5},{5,6},{6,7},{8,9},{9,10},{10,11},{12,13},{... | collective-permute-start | bytes 737288 | tf_op jit(solution)/shard_map/ppermute | solution.py:391
  36.4 16.3 %collective-permute-start.8 = (f32[15,16,256]{2,1,0:T(8,128)S(1)}, f32[15,16,256]{2,1,0:T(8,128)S(1)}, u32[]{:S(2)}, u32[]{:S(2)}) collective-permute-start(f32[15,16,256]{2,1,0:T(8,128)S(1)} %get-tuple-element.43.refs_4_.refs_0_), channel_id=1, source_target_pairs={{1,0},{2,1},{3,2},{5,4},{6,5},{7,6},{9,8},{10,9},{11,10},{13,12},{... | collective-permute-start | bytes 737288 | tf_op jit(solution)/shard_map/ppermute | solution.py:392
  41.6 12.2 %collective-permute-start.5 = (f32[15,32,256]{2,1,0:T(8,128)S(1)}, f32[15,32,256]{2,1,0:T(8,128)S(1)}, u32[]{:S(2)}, u32[]{:S(2)}) collective-permute-start(f32[15,32,256]{2,1,0:T(8,128)S(1)} %get-tuple-element.45.refs_1_), channel_id=1, source_target_pairs={{0,1},{1,2},{2,3},{4,5},{5,6},{6,7},{8,9},{9,10},{10,11},{12,13},{... | collective-permute-start | bytes 1474568 | tf_op jit(solution)/shard_map/ppermute | solution.py:391
  44.9 10.6 %collective-permute-start.6 = (f32[15,32,256]{2,1,0:T(8,128)S(1)}, f32[15,32,256]{2,1,0:T(8,128)S(1)}, u32[]{:S(2)}, u32[]{:S(2)}) collective-permute-start(f32[15,32,256]{2,1,0:T(8,128)S(1)} %get-tuple-element.44.refs_4_.refs_0_), channel_id=1, source_target_pairs={{1,0},{2,1},{3,2},{5,4},{6,5},{7,6},{9,8},{10,9},{11,10},{13,12},{... | collective-permute-start | bytes 1474568 | tf_op jit(solution)/shard_map/ppermute | solution.py:392
  47.4 19.5 %collective-permute-start.10 = (f32[15,16,256]{2,1,0:T(8,128)S(1)}, f32[15,16,256]{2,1,0:T(8,128)S(1)}, u32[]{:S(2)}, u32[]{:S(2)}) collective-permute-start(f32[15,16,256]{2,1,0:T(8,128)S(1)} %get-tuple-element.48.refs_1_), channel_id=1, source_target_pairs={{0,1},{1,2},{2,3},{4,5},{5,6},{6,7},{8,9},{9,10},{10,11},{12,13},{... | collective-permute-start | bytes 737288 | tf_op jit(solution)/shard_map/ppermute | solution.py:391
  51.4 15.5 %collective-permute-start.11 = (f32[15,16,256]{2,1,0:T(8,128)S(1)}, f32[15,16,256]{2,1,0:T(8,128)S(1)}, u32[]{:S(2)}, u32[]{:S(2)}) collective-permute-start(f32[15,16,256]{2,1,0:T(8,128)S(1)} %get-tuple-element.47.refs_4_.refs_0_), channel_id=1, source_target_pairs={{1,0},{2,1},{3,2},{5,4},{6,5},{7,6},{9,8},{10,9},{11,10},{13,12},{... | collective-permute-start | bytes 737288 | tf_op jit(solution)/shard_map/ppermute | solution.py:392
  57.3 15.7 %copy-start.3 = (f32[16,64,256]{2,1,0:T(8,128)S(1)}, f32[16,64,256]{2,1,0:T(8,128)}, u32[]{:S(2)}) copy-start(f32[16,64,256]{2,1,0:T(8,128)} %refs_4_.1) | copy-start | bytes 3145732
  57.3 15.7 %collective-permute-start.9 = (f32[16,32,256]{2,1,0:T(8,128)S(1)}, f32[16,32,256]{2,1,0:T(8,128)S(1)}, u32[]{:S(2)}, u32[]{:S(2)}) collective-permute-start(f32[16,32,256]{2,1,0:T(8,128)S(1)} %shard_map.62.refs_4_.refs_3_), channel_id=1, source_target_pairs={{0,4},{4,8},{8,12},{12,0},{1,5},{5,9},{9,13},{13,1},{2,6},{6,10},{... | collective-permute-start | bytes 1572872 | tf_op jit(solution)/shard_map/ppermute | solution.py:398
  73.0 21.0 %copy-start.1 = (bf16[16,256,256]{2,1,0:T(8,128)(2,1)S(1)}, bf16[16,256,256]{2,1,0:T(8,128)(2,1)}, u32[]{:S(2)}) copy-start(bf16[16,256,256]{2,1,0:T(8,128)(2,1)} %copy-done) | copy-start | bytes 6291460
  84.3 9.7 %collective-permute-start.12 = (f32[16,32,256]{2,1,0:T(8,128)S(1)}, f32[16,32,256]{2,1,0:T(8,128)S(1)}, u32[]{:S(2)}, u32[]{:S(2)}) collective-permute-start(f32[16,32,256]{2,1,0:T(8,128)S(1)} %get-tuple-element.54), channel_id=1, source_target_pairs={{0,12},{4,0},{8,4},{12,8},{1,13},{5,1},{9,5},{13,9},{2,14},{6,2},{... | collective-permute-start | bytes 1572872 | tf_op jit(solution)/shard_map/ppermute | solution.py:398
  84.8 18.4 %collective-permute-start.16 = (f32[15,32,256]{2,1,0:T(8,128)S(1)}, f32[15,32,256]{2,1,0:T(8,128)S(1)}, u32[]{:S(2)}, u32[]{:S(2)}) collective-permute-start(f32[15,32,256]{2,1,0:T(8,128)S(1)} %get-tuple-element.57.refs_0_), channel_id=1, source_target_pairs={{1,0},{2,1},{3,2},{5,4},{6,5},{7,6},{9,8},{10,9},{11,10},{13,12},{... | collective-permute-start | bytes 1474568 | tf_op jit(solution)/shard_map/ppermute | solution.py:392
  86.1 17.1 %collective-permute-start.15 = (f32[15,32,256]{2,1,0:T(8,128)S(1)}, f32[15,32,256]{2,1,0:T(8,128)S(1)}, u32[]{:S(2)}, u32[]{:S(2)}) collective-permute-start(f32[15,32,256]{2,1,0:T(8,128)S(1)} %get-tuple-element.58.refs_1_), channel_id=1, source_target_pairs={{0,1},{1,2},{2,3},{4,5},{5,6},{6,7},{8,9},{9,10},{10,11},{12,13},{... | collective-permute-start | bytes 1474568 | tf_op jit(solution)/shard_map/ppermute | solution.py:391
  98.8 14.1 %collective-permute-start.13 = (f32[15,32,256]{2,1,0:T(8,128)S(1)}, f32[15,32,256]{2,1,0:T(8,128)S(1)}, u32[]{:S(2)}, u32[]{:S(2)}) collective-permute-start(f32[15,32,256]{2,1,0:T(8,128)S(1)} %get-tuple-element.56.refs_1_), channel_id=1, source_target_pairs={{0,1},{1,2},{2,3},{4,5},{5,6},{6,7},{8,9},{9,10},{10,11},{12,13},{... | collective-permute-start | bytes 1474568 | tf_op jit(solution)/shard_map/ppermute | solution.py:391
  101.9 15.2 %collective-permute-start.14 = (f32[15,32,256]{2,1,0:T(8,128)S(1)}, f32[15,32,256]{2,1,0:T(8,128)S(1)}, u32[]{:S(2)}, u32[]{:S(2)}) collective-permute-start(f32[15,32,256]{2,1,0:T(8,128)S(1)} %get-tuple-element.55.refs_4_.refs_0_), channel_id=1, source_target_pairs={{1,0},{2,1},{3,2},{5,4},{6,5},{7,6},{9,8},{10,9},{11,10},{13,12},{... | collective-permute-start | bytes 1474568 | tf_op jit(solution)/shard_map/ppermute | solution.py:392
  104.4 24.3 %collective-permute-start.19 = (f32[15,16,256]{2,1,0:T(8,128)S(1)}, f32[15,16,256]{2,1,0:T(8,128)S(1)}, u32[]{:S(2)}, u32[]{:S(2)}) collective-permute-start(f32[15,16,256]{2,1,0:T(8,128)S(1)} %get-tuple-element.62.refs_1_), channel_id=1, source_target_pairs={{0,1},{1,2},{2,3},{4,5},{5,6},{6,7},{8,9},{9,10},{10,11},{12,13},{... | collective-permute-start | bytes 737288 | tf_op jit(solution)/shard_map/ppermute | solution.py:391
  108.4 21.6 %collective-permute-start.20 = (f32[15,16,256]{2,1,0:T(8,128)S(1)}, f32[15,16,256]{2,1,0:T(8,128)S(1)}, u32[]{:S(2)}, u32[]{:S(2)}) collective-permute-start(f32[15,16,256]{2,1,0:T(8,128)S(1)} %get-tuple-element.59.refs_4_.refs_0_), channel_id=1, source_target_pairs={{1,0},{2,1},{3,2},{5,4},{6,5},{7,6},{9,8},{10,9},{11,10},{13,12},{... | collective-permute-start | bytes 737288 | tf_op jit(solution)/shard_map/ppermute | solution.py:392
  118.9 13.9 %collective-permute-start.17 = (f32[15,32,256]{2,1,0:T(8,128)S(1)}, f32[15,32,256]{2,1,0:T(8,128)S(1)}, u32[]{:S(2)}, u32[]{:S(2)}) collective-permute-start(f32[15,32,256]{2,1,0:T(8,128)S(1)} %get-tuple-element.61.refs_1_), channel_id=1, source_target_pairs={{0,1},{1,2},{2,3},{4,5},{5,6},{6,7},{8,9},{9,10},{10,11},{12,13},{... | collective-permute-start | bytes 1474568 | tf_op jit(solution)/shard_map/ppermute | solution.py:391
  122.2 15.1 %collective-permute-start.18 = (f32[15,32,256]{2,1,0:T(8,128)S(1)}, f32[15,32,256]{2,1,0:T(8,128)S(1)}, u32[]{:S(2)}, u32[]{:S(2)}) collective-permute-start(f32[15,32,256]{2,1,0:T(8,128)S(1)} %get-tuple-element.60.refs_4_.refs_0_), channel_id=1, source_target_pairs={{1,0},{2,1},{3,2},{5,4},{6,5},{7,6},{9,8},{10,9},{11,10},{13,12},{... | collective-permute-start | bytes 1474568 | tf_op jit(solution)/shard_map/ppermute | solution.py:392
  124.6 15.4 %collective-permute-start.22 = (f32[15,16,256]{2,1,0:T(8,128)S(1)}, f32[15,16,256]{2,1,0:T(8,128)S(1)}, u32[]{:S(2)}, u32[]{:S(2)}) collective-permute-start(f32[15,16,256]{2,1,0:T(8,128)S(1)} %get-tuple-element.64.refs_1_), channel_id=1, source_target_pairs={{0,1},{1,2},{2,3},{4,5},{5,6},{6,7},{8,9},{9,10},{10,11},{12,13},{... | collective-permute-start | bytes 737288 | tf_op jit(solution)/shard_map/ppermute | solution.py:391
  128.7 11.3 %collective-permute-start.23 = (f32[15,16,256]{2,1,0:T(8,128)S(1)}, f32[15,16,256]{2,1,0:T(8,128)S(1)}, u32[]{:S(2)}, u32[]{:S(2)}) collective-permute-start(f32[15,16,256]{2,1,0:T(8,128)S(1)} %get-tuple-element.63.refs_4_.refs_0_), channel_id=1, source_target_pairs={{1,0},{2,1},{3,2},{5,4},{6,5},{7,6},{9,8},{10,9},{11,10},{13,12},{... | collective-permute-start | bytes 737288 | tf_op jit(solution)/shard_map/ppermute | solution.py:392
  139.0 7.1 %collective-permute-start.21 = (f32[16,32,256]{2,1,0:T(8,128)S(1)}, f32[16,32,256]{2,1,0:T(8,128)S(1)}, u32[]{:S(2)}, u32[]{:S(2)}) collective-permute-start(f32[16,32,256]{2,1,0:T(8,128)S(1)} %shard_map.70.refs_4_.refs_3_), channel_id=1, source_target_pairs={{0,4},{4,8},{8,12},{12,0},{1,5},{5,9},{9,13},{13,1},{2,6},{6,10},{... | collective-permute-start | bytes 1572872 | tf_op jit(solution)/shard_map/ppermute | solution.py:398

commit v4 on v3

--- a/solution.py
+++ b/solution.py
@@ -10,7 +10,7 @@
 ITERS = 2
 F32 = jnp.float32
 BF16 = jnp.bfloat16
-PARAMS = pltpu.CompilerParams(vmem_limit_bytes=40 * 1024 * 1024)
+PARAMS = pltpu.CompilerParams(vmem_limit_bytes=16 * 1024 * 1024)
 SMEM = pl.BlockSpec(memory_space=pltpu.SMEM)
 VMEM = pl.BlockSpec(memory_space=pltpu.VMEM)
 ANY = pl.BlockSpec(memory_space=pl.ANY)
@@ -46,14 +46,6 @@
     return pl.CostEstimate(
         flops=int(microseconds * 1e9), bytes_accessed=int(microseconds * 3.5e6), transcendentals=0
     )
-
-
-def full(shape):
-    return pl.BlockSpec(shape, lambda i: (0,) * len(shape))
-
-
-def planes(shape, per):
-    return pl.BlockSpec((per,) + shape[1:], lambda i: (i,) + (0,) * (len(shape) - 1))
 
 
 def shape_of(*dims, dtype=F32):
@@ -110,72 +102,75 @@
 
 
 def store_sends(v, plane, n, radius, low_ref, high_ref):
-    @pl.when(plane < radius)
-    def _():
-        low_ref[jnp.minimum(plane, radius - 1)] = v
-
-    @pl.when(plane >= n - radius)
-    def _():
-        high_ref[jnp.maximum(plane - (n - radius), 0)] = v
+    if plane < radius:
+        low_ref[plane] = v
+    if plane >= n - radius:
+        high_ref[plane - (n - radius)] = v
 
 
 def own_rows(est, wx_ref, ah_ref, al_ref, p, inner):
     rows = est.shape[0]
-    est_hi, est_lo = split(est)
-    u = blur_rows(wx_ref[p, 0, :inner, :rows], wx_ref[p, 1, :inner, :rows], est_hi, est_lo)
-    return blur_columns(u, ah_ref[p], al_ref[p])
+    w = blur_columns(est, ah_ref[p], al_ref[p])
+    w_hi, w_lo = split(w)
+    v = blur_rows(wx_ref[p, 0, :inner, :rows], wx_ref[p, 1, :inner, :rows], w_hi, w_lo)
+    return w, v
+
+
+def row_place():
+    row = lax.axis_index("row")
+    return row == 0, row == lax.axis_size("row") - 1
 
 
 def first_kernel(
-    per, n, radius, halo, place_ref, band_ref, tx_ref, ty_ref, est_ref,
-    ah_ref, al_ref, wx_ref, low_ref, high_ref,
+    n, radius, halo, band_ref, tx_ref, ty_ref, est_ref,
+    ah_ref, al_ref, wx_ref, w_ref, low_ref, high_ref,
 ):
     rows, width = wx_ref.shape[2], wx_ref.shape[3]
     _, lane = iotas(16, 128)
     _, wide = iotas(16, width)
     row, lanes = iotas(rows, width)
-    keep = (place_ref[2] == 0) | ((row < rows - radius) == (lanes < rows))
-    for p in range(per):
-        plane = pl.program_id(0) * per + p
-        band = band_ref[plane]
+    keep = jnp.logical_not(row_place()[1]) | ((row < rows - radius) == (lanes < rows))
+    for p in range(n):
+        band = band_ref[p]
         column_matrix(spread(ty_ref, band, lane, radius, True), radius, ah_ref, al_ref, p)
         matrix = row_matrix(spread(tx_ref, band, wide, radius, False), rows, 0, width)
         wx_ref[p, 0], wx_ref[p, 1] = split(jnp.where(keep, matrix, 0.0))
-        v = own_rows(est_ref[p], wx_ref, ah_ref, al_ref, p, rows - halo)
-        store_sends(v, plane, n, radius, low_ref, high_ref)
-
-
-def first_blur(place, band_index, taps_x, taps_y, est, halo, width, per):
+        w_ref[p], v = own_rows(est_ref[p], wx_ref, ah_ref, al_ref, p, rows - halo)
+        store_sends(v, p, n, radius, low_ref, high_ref)
+
+
+def first_blur(band_index, taps_x, taps_y, est, halo, width):
     n, rows, columns = est.shape
     radius = taps_x.shape[1] // 2
     a = shape_of(n, columns, columns, dtype=BF16)
     w = shape_of(n, 2, rows, width, dtype=BF16)
     send = shape_of(radius, rows - halo, columns)
     return pl.pallas_call(
-        functools.partial(first_kernel, per, n, radius, halo),
-        grid=(n // per,),
-        in_specs=[SMEM] * 4 + [planes(est.shape, per)],
-        out_specs=[planes(x.shape, per) for x in (a, a, w)] + [full(send.shape)] * 2,
-        out_shape=[a, a, w, send, send],
+        functools.partial(first_kernel, n, radius, halo),
+        in_specs=[SMEM] * 3 + [VMEM],
+        out_specs=[VMEM] * 6,
+        out_shape=[a, a, w, shape_of(*est.shape), send, send],
         compiler_params=PARAMS,
         cost_estimate=cost(1.0),
-    )(place, band_index, taps_x, taps_y, est)
+    )(band_index, taps_x, taps_y, est)
 
 
 def second_kernel(
-    per, n, radius, halo, depth, place_ref, band_ref, tx_ref, ty_ref, tz_ref, after_ref,
+    n, radius, halo, band_ref, tx_ref, ty_ref, tz_ref, after_ref,
     obs_ref, next_ref, ah_ref, al_ref, wx_ref, rn_ref, shifted_ref,
 ):
     rows, width = wx_ref.shape[2], wx_ref.shape[3]
+    first_row, last_row = row_place()
+    below = lax.axis_index("slab") * n
+    depth = lax.axis_size("slab") * n
     _, lane = iotas(16, 128)
     _, wide = iotas(16, width)
     _, lanes = iotas(rows, width)
-    lower = (place_ref[1] == 0) | (lanes >= rows - radius - (rows - halo))
-    upper = (place_ref[2] == 0) | (lanes < rows - radius + halo)
+    lower = jnp.logical_not(first_row) | (lanes >= halo - radius)
+    upper = jnp.logical_not(last_row) | (lanes < rows - radius + halo)
     keep = ((lanes < halo) & lower) | ((lanes >= halo) & upper)
-    for p in range(per):
-        plane = pl.program_id(0) * per + p
-        band = band_ref[plane]
+    for p in range(n):
+        band = band_ref[p]
         sums = column_matrix(
             spread(ty_ref, band, lane, radius, False), radius, ah_ref, al_ref, p
         )
@@ -186,7 +181,7 @@
         wx_ref[p, 0], wx_ref[p, 1] = split(matrix)
         along_x = jnp.sum(matrix, axis=1, keepdims=True)
         along_z = jnp.float32(0.0)
-        z = place_ref[0] + plane
+        z = below + p
         for k in range(2 * radius + 1):
             source = z - k + radius
             inside = (source >= 0) & (source < depth)
@@ -199,48 +194,46 @@
         shifted_ref[p, rows - radius :] = next_ref[p, :radius]
 
 
-def second_weights(
-    place, band_index, taps_x, taps_y, taps_z, after, obs, beyond, halo, width, depth, per
-):
+def second_weights(band_index, taps_x, taps_y, taps_z, after, obs, beyond, width):
     n, rows, columns = obs.shape
+    halo = beyond.shape[1]
     radius = taps_x.shape[1] // 2
     a = shape_of(n, columns, columns, dtype=BF16)
     w = shape_of(n, 2, rows, width, dtype=BF16)
     field = shape_of(*obs.shape)
     return pl.pallas_call(
-        functools.partial(second_kernel, per, n, radius, halo, depth),
-        grid=(n // per,),
-        in_specs=[SMEM] * 5 + [ANY] + [planes(x.shape, per) for x in (obs, beyond)],
-        out_specs=[planes(x.shape, per) for x in (a, a, w, field, field)],
+        functools.partial(second_kernel, n, radius, halo),
+        in_specs=[SMEM] * 4 + [ANY] + [VMEM] * 2,
+        out_specs=[VMEM] * 5,
         out_shape=[a, a, w, field, field],
         compiler_params=PARAMS,
         cost_estimate=cost(1.0),
-    )(place, band_index, taps_x, taps_y, taps_z, after, obs, beyond)
-
-
-def edge_kernel(
-    per, n, radius, halo, est_ref, next_ref, wx_ref, ah_ref, al_ref, low_ref, high_ref
-):
-    rows = est_ref.shape[1]
+    )(band_index, taps_x, taps_y, taps_z, after, obs, beyond)
+
+
+def edge_kernel(n, radius, blurred, w_ref, next_ref, wx_ref, *refs):
+    rows, halo = w_ref.shape[1], next_ref.shape[1]
     inner, used = rows - halo, rows + halo
-    for p in range(per):
-        plane = pl.program_id(0) * per + p
-        v_hi, v_lo = split(jnp.concatenate([est_ref[p], next_ref[p]], axis=0))
-        u = blur_rows(wx_ref[p, 0, inner:, :used], wx_ref[p, 1, inner:, :used], v_hi, v_lo)
-        v = blur_columns(u, ah_ref[p], al_ref[p])
-        store_sends(v, plane, n, radius, low_ref, high_ref)
-
-
-def edge_blur(est, beyond, wx, ah, al, radius, per):
-    n, _, columns = est.shape
+    if not blurred:
+        ah_ref, al_ref = refs[:2]
+    for p in range(n):
+        beyond = next_ref[p]
+        if not blurred:
+            beyond = blur_columns(beyond, ah_ref[p], al_ref[p])
+        w_hi, w_lo = split(jnp.concatenate([w_ref[p], beyond], axis=0))
+        v = blur_rows(wx_ref[p, 0, inner:, :used], wx_ref[p, 1, inner:, :used], w_hi, w_lo)
+        store_sends(v, p, n, radius, *refs[-2:])
+
+
+def edge_blur(w, beyond, wx, columns_matrix, radius):
+    n, _, columns = w.shape
     halo = beyond.shape[1]
     send = shape_of(radius, halo, columns)
-    args = (est, beyond, wx, ah, al)
-    return pl.pallas_call(
-        functools.partial(edge_kernel, per, n, radius, halo),
-        grid=(n // per,),
-        in_specs=[planes(x.shape, per) for x in args],
-        out_specs=[full(send.shape)] * 2,
+    args = (w, beyond, wx, *columns_matrix)
+    return pl.pallas_call(
+        functools.partial(edge_kernel, n, radius, not columns_matrix),
+        in_specs=[VMEM] * len(args),
+        out_specs=[VMEM] * 2,
         out_shape=[send] * 2,
         compiler_params=PARAMS,
         cost_estimate=cost(1.0),
@@ -337,47 +330,44 @@
     )(taps_z, *chunk, after)
 
 
-def update_kernel(per, n, radius, last, *refs):
+def update_kernel(n, radius, last, *refs):
     pieces, edge_ref, refs = refs[:4], refs[3], refs[4:]
     est_ref, rn_ref, wa_ref, bh_ref, bl_ref = refs[:5]
     refs = refs[5:]
     rows = est_ref.shape[1]
     halo = edge_ref.shape[1]
+    used = rows + halo
     if last:
         (out_ref,) = refs
     else:
-        wx_ref, ah_ref, al_ref, out_ref, top_ref, low_ref, high_ref = refs
-    for p in range(per):
-        plane = pl.program_id(0) * per + p
+        wx_ref, ah_ref, al_ref, out_ref, w_ref, top_ref, low_ref, high_ref = refs
+    for p in range(n):
         c = jnp.concatenate([piece[p] for piece in pieces], axis=0)
         c_hi, c_lo = split(c)
-        used = rows + halo
         u = blur_rows(wa_ref[p, 0, :, :used], wa_ref[p, 1, :, :used], c_hi, c_lo)
         u = blur_columns(u, bh_ref[p], bl_ref[p])
         est = est_ref[p] * u * rn_ref[p]
         out_ref[p] = est
         if not last:
-            top_ref[p] = est[:halo]
-            v = own_rows(est, wx_ref, ah_ref, al_ref, p, rows - halo)
-            store_sends(v, plane, n, radius, low_ref, high_ref)
-
-
-def update(pieces, est, rn, adjoint, forward, radius, per):
+            w, v = own_rows(est, wx_ref, ah_ref, al_ref, p, rows - halo)
+            w_ref[p] = w
+            top_ref[p] = w[:halo]
+            store_sends(v, p, n, radius, low_ref, high_ref)
+
+
+def update(pieces, est, rn, adjoint, forward, radius):
     n, rows, columns = est.shape
     halo = pieces[0].shape[1]
     last = forward is None
     args = [*pieces, est, rn, *adjoint] + ([] if last else [*forward])
-    out_specs, out_shape = [planes(est.shape, per)], [shape_of(*est.shape)]
+    out_shape = [shape_of(*est.shape)]
     if not last:
-        top = shape_of(n, halo, columns)
         send = shape_of(radius, rows - halo, columns)
-        out_specs += [planes(top.shape, per)] + [full(send.shape)] * 2
-        out_shape += [top, send, send]
-    return pl.pallas_call(
-        functools.partial(update_kernel, per, n, radius, last),
-        grid=(n // per,),
-        in_specs=[planes(x.shape, per) for x in args],
-        out_specs=out_specs,
+        out_shape += [shape_of(*est.shape), shape_of(n, halo, columns), send, send]
+    return pl.pallas_call(
+        functools.partial(update_kernel, n, radius, last),
+        in_specs=[VMEM] * len(args),
+        out_specs=[VMEM] * len(out_shape),
         out_shape=out_shape,
         compiler_params=PARAMS,
         cost_estimate=cost(1.0),
@@ -405,25 +395,18 @@
     inner = rows - halo
     half = up(inner // 2, 16)
     width = up(rows + halo, 128)
-    per = 4 if n % 4 == 0 else 1
-    depth = n * lax.axis_size("slab")
-    row = lax.axis_index("row")
-    last_row = row == lax.axis_size("row") - 1
-    place = jnp.stack([lax.axis_index("slab") * n, row == 0, last_row]).astype(jnp.int32)
-
     beyond = ring(observed[:, :halo], -1)
-    ah, al, wx, low, high = first_blur(
-        place, band_index, taps_x, taps_y, observed, halo, width, per
+    ah, al, wx, w, low, high = first_blur(
+        band_index, taps_x, taps_y, observed, halo, width
     )
     est, adjoint = observed, None
     for step in range(ITERS):
         v_inner = depth_exchange(low, high)
-        low, high = edge_blur(est, beyond, wx, ah, al, radius, per)
+        low, high = edge_blur(w, beyond, wx, () if step else (ah, al), radius)
         v_edge = depth_exchange(low, high)
         if adjoint is None:
             bh, bl, wa, rn, shifted = second_weights(
-                place, band_index, taps_x, taps_y, taps_z, low, observed, beyond, halo,
-                width, depth, per,
+                band_index, taps_x, taps_y, taps_z, low, observed, beyond, width
             )
             adjoint = (wa, bh, bl)
         r_first = depth_exchange(
@@ -442,11 +425,11 @@
         last = step == ITERS - 1
         out = update(
             (before, c_first, c_second, c_edge), est, rn, adjoint,
-            None if last else (wx, ah, al), radius, per,
+            None if last else (wx, ah, al), radius,
         )
         est = out[0]
         if not last:
-            top, low, high = out[1:]
+            w, top, low, high = out[1:]
             beyond = ring(top, -1)
     return est
 

time: 150 us -> 142 us (0.947)
  the two profiles are of different devices: /device:TPU:1 before, /device:TPU:0 now
where the time goes in v4:
time: 142 us; the launch traced here: 141 us
  starting transfers between devices  58.7 us (41%)
  waiting for transfers between devices  39.4 us (28%)
  Pallas kernels  38 us (27%)
  local copies, waits for them, and re-layouts  4.37 us (3%)
    ppermute x10, starting transfers between devices, depth_exchange(): zlo = lax.ppermute(high, 'slab', forward)  43.3 us
    ppermute x4, waiting for transfers between devices, ring(): lax.ppermute(x, 'row', [(i, (i + step) % count) for i in range(count)])  13.9 us
    ppermute x10, waiting for transfers between devices, depth_exchange(): zhi = lax.ppermute(low, 'slab', backward)  13 us
    ppermute x10, starting transfers between devices, depth_exchange(): zhi = lax.ppermute(low, 'slab', backward)  12.9 us
    ppermute x10, waiting for transfers between devices, depth_exchange(): zlo = lax.ppermute(high, 'slab', forward)  12.5 us
    pallas_call x2, Pallas kernels, update(): pl.pallas_call(functools.partial(update_kernel, n, radius, last), in_spec...  11.1 us
    pallas_call x6, Pallas kernels, depth_ratio(): pl.pallas_call(functools.partial(ratio_kernel, n, radius, skip, obs_skip)...  8.35 us
    pallas_call x6, Pallas kernels, depth_back(): pl.pallas_call(functools.partial(back_kernel, n, radius), in_specs=[SMEM]...  8.05 us
  transfers between devices with their start and end apart: 24, of which 14 were waited for; matrix products, arithmetic and copies ran while one was open for 0% of the time, Pallas kernels for 19%

profile of v4, /device:TPU:0, one launch (start us, length us, event | category | flops | bytes accessed | tf_op | source)
XLA Modules:
  0.0 140.8 jit_solution(5211405509799429888)
XLA Ops:
  0.0 1.1 slice.3
  1.1 2.4 %collective-permute-start = (f32[16,32,256]{2,1,0:T(8,128)S(1)}, f32[16,32,256]{2,1,0:T(8,128)S(1)}, u32[]{:S(2)}, u32[]{:S(2)}) collective-permute-start(f32[16,32,256]{2,1,0:T(8,128)S(1)} %slice.3), channel_id=1, source_target_pairs={{0,12},{4,0},{8,4},{12,8},{1,13},{5,1},{9,5},{13,9},{2,14},{6,2},{... | collective-permute-start | bytes 1572872 | tf_op jit(solution)/shard_map/ppermute | solution.py:388
  3.5 1.2 copy-done
  4.7 0.7 copy-done.2
  5.4 0.7 copy-done.3
  6.1 0.7 copy-done.4
  6.8 3.7 %shard_map.55 = (bf16[16,256,256]{2,1,0:T(8,128)(2,1)S(1)}, bf16[16,256,256]{2,1,0:T(8,128)(2,1)S(1)}, bf16[16,2,64,128]{3,2,1,0:T(8,128)(2,1)S(1)}, f32[16,64,2...) custom-call(s32[16]{0:T(128)S(1)} %copy-done.4, f32[16,31]{1,0:T(8,128)S(1)} %copy-done.2, ...), custom_call_target="tpu_custom_call" | custom-call | flops 1000000000 | bytes 3500000 | tf_op jit(solution)/shard_map/pallas_call | solution.py:148
  10.5 1.3 collective-permute-start.4
  11.8 4.6 %collective-permute-start.3 = (f32[15,32,256]{2,1,0:T(8,128)S(1)}, f32[15,32,256]{2,1,0:T(8,128)S(1)}, u32[]{:S(2)}, u32[]{:S(2)}) collective-permute-start(f32[15,32,256]{2,1,0:T(8,128)S(1)} %get-tuple-element.45.refs_1_), channel_id=1, source_target_pairs={{0,1},{1,2},{2,3},{4,5},{5,6},{6,7},{8,9},{9,10},{10,11},{12,13},{... | collective-permute-start | bytes 1474568 | tf_op jit(solution)/shard_map/ppermute | solution.py:381
  16.4 0.0 collective-permute-done.next_ref
  16.4 0.0 copy-start.5
  16.4 3.6 %shard_map.56 = (f32[15,32,256]{2,1,0:T(8,128)S(1)}, f32[15,32,256]{2,1,0:T(8,128)S(1)}) custom-call(f32[16,64,256]{2,1,0:T(8,128)S(1)} %get-tuple-element.37.w_ref, f32[16,32,256]{2,1,0:T(8,128)S(1)} %collective-permute-done.next_ref, bf16[16,2,64,128]{3,2,1,0:T(8,128)(2,1)S(1)} %get-tuple-element.38.wx_ref.refs_9_, ...), custom_call_target="tpu_custom_call" | custom-call | flops 1000000000 | bytes 3500000 | tf_op jit(solution)/shard_map/pallas_call | solution.py:233
  20.0 3.5 %collective-permute-start.1 = (f32[15,32,256]{2,1,0:T(8,128)S(1)}, f32[15,32,256]{2,1,0:T(8,128)S(1)}, u32[]{:S(2)}, u32[]{:S(2)}) collective-permute-start(f32[15,32,256]{2,1,0:T(8,128)S(1)} %get-tuple-element.43.refs_1_), channel_id=1, source_target_pairs={{0,1},{1,2},{2,3},{4,5},{5,6},{6,7},{8,9},{9,10},{10,11},{12,13},{... | collective-permute-start | bytes 1474568 | tf_op jit(solution)/shard_map/ppermute | solution.py:381
  23.5 1.3 collective-permute-start.2
  24.8 2.8 %shard_map.57 = (bf16[16,256,256]{2,1,0:T(8,128)(2,1)S(1)}, bf16[16,256,256]{2,1,0:T(8,128)(2,1)S(1)}, bf16[16,2,64,128]{3,2,1,0:T(8,128)(2,1)S(1)}, f32[16,64,256]{2,1,0:T(8,128)S(1)}, f32[16,64,256]{2,1,0:T(8,128)S(1)}) custom-call(s32[16]{0:T(128)S(1)} %copy-done.4, f32[16,31]{1,0:T(8,128)S(1)} %copy-done.2, f32[16,31]{1,0:T(8,128)S(1)} %copy-done.3, ...), custom_call_target="tpu_custom_call" | custom-call | flops 1000000000 | bytes 3500000 | tf_op jit(solution)/shard_map/pallas_call | solution.py:204
  27.6 0.0 collective-permute-done.4.refs_3_
  27.6 0.4 collective-permute-done.3.refs_2_
  28.0 1.2 shard_map.58
  29.2 4.4 %collective-permute-start.7 = (f32[15,16,256]{2,1,0:T(8,128)S(1)}, f32[15,16,256]{2,1,0:T(8,128)S(1)}, u32[]{:S(2)}, u32[]{:S(2)}) collective-permute-start(f32[15,16,256]{2,1,0:T(8,128)S(1)} %get-tuple-element.49.refs_1_), channel_id=1, source_target_pairs={{0,1},{1,2},{2,3},{4,5},{5,6},{6,7},{8,9},{9,10},{10,11},{12,13},{... | collective-permute-start | bytes 737288 | tf_op jit(solution)/shard_map/ppermute | solution.py:381
  33.6 1.3 collective-permute-start.8
  34.9 3.6 %collective-permute-done.1.refs_2_ = f32[15,32,256]{2,1,0:T(8,128)S(1)} collective-permute-done((f32[15,32,256]{2,1,0:T(8,128)S(1)}, f32[15,32,256]{2,1,0:T(8,128)S(1)}, u32[]{:S(2)}, u32[]{:S(2)}) %collective-permute-start.1) | collective-permute-done | bytes 491552 | tf_op jit(solution)/shard_map/ppermute | solution.py:381
  38.5 1.8 %shard_map.59 = (f32[15,32,256]{2,1,0:T(8,128)S(1)}, f32[15,32,256]{2,1,0:T(8,128)S(1)}) custom-call(f32[31]{0:T(128)S(1)} %copy-done.5, f32[16,64,256]{2,1,0:T(8,128)S(1)} %get-tuple-element.42.obs_ref, f32[15,32,256]{2,1,0:T(8,128)S(1)} %get-tuple-element.41.after_ref.refs_4_.refs_0_, f32[15,32,256]{2,1,0:T(8,128)S(1)} %get-tuple-element.43.refs_1_, ...), custom_call_target="tpu_custom_call" | custom-call | flops 1000000000 | bytes 3500000 | tf_op jit(solution)/shard_map/pallas_call | solution.py:298
  40.4 4.4 %collective-permute-start.5 = (f32[15,32,256]{2,1,0:T(8,128)S(1)}, f32[15,32,256]{2,1,0:T(8,128)S(1)}, u32[]{:S(2)}, u32[]{:S(2)}) collective-permute-start(f32[15,32,256]{2,1,0:T(8,128)S(1)} %get-tuple-element.48.refs_1_), channel_id=1, source_target_pairs={{0,1},{1,2},{2,3},{4,5},{5,6},{6,7},{8,9},{9,10},{10,11},{12,13},{... | collective-permute-start | bytes 1474568 | tf_op jit(solution)/shard_map/ppermute | solution.py:381
  44.8 1.3 collective-permute-start.6
  46.1 1.2 shard_map.60
  47.3 4.6 %collective-permute-start.10 = (f32[15,16,256]{2,1,0:T(8,128)S(1)}, f32[15,16,256]{2,1,0:T(8,128)S(1)}, u32[]{:S(2)}, u32[]{:S(2)}) collective-permute-start(f32[15,16,256]{2,1,0:T(8,128)S(1)} %get-tuple-element.51.refs_1_), channel_id=1, source_target_pairs={{0,1},{1,2},{2,3},{4,5},{5,6},{6,7},{8,9},{9,10},{10,11},{12,13},{... | collective-permute-start | bytes 737288 | tf_op jit(solution)/shard_map/ppermute | solution.py:381
  51.8 1.3 collective-permute-start.11
  53.2 1.1 shard_map.61.refs_4_.refs_1_
  54.3 0.8 collective-permute-done.5.refs_2_
  55.1 3.5 %collective-permute-done.6.refs_3_ = f32[15,32,256]{2,1,0:T(8,128)S(1)} collective-permute-done((f32[15,32,256]{2,1,0:T(8,128)S(1)}, f32[15,32,256]{2,1,0:T(8,128)S(1)}, u32[]{:S(2)}, u32[]{:S(2)}) %collective-permute-start.6) | collective-permute-done | bytes 491552 | tf_op jit(solution)/shard_map/ppermute | solution.py:382
  58.6 1.7 %shard_map.62.refs_4_.refs_3_ = f32[16,32,256]{2,1,0:T(8,128)S(1)} custom-call(f32[31]{0:T(128)S(1)} %copy-done.5, f32[15,32,256]{2,1,0:T(8,128)S(1)} %get-tuple-element.47.refs_4_.refs_0_, f32[15,32,256]{2,1,0:T(8,128)S(1)} %get-tuple-element.48.refs_1_, f32[15,32,256]{2,1,0:T(8,128)S(1)} %collective-permute-done.5.refs_2_, ...), custom_call_target="tpu_custom_call" | custom-call | flops 1000000000 | bytes 3500000 | tf_op jit(solution)/shard_map/pallas_call | solution.py:323
  60.4 0.0 copy-start.1
  60.4 0.1 collective-permute-start.9
  60.4 0.8 collective-permute-done.11.refs_3_
  61.2 1.1 shard_map.63.refs_2_
  62.4 6.6 %collective-permute-done.9.refs_0_ = f32[16,32,256]{2,1,0:T(8,128)S(1)} collective-permute-done((f32[16,32,256]{2,1,0:T(8,128)S(1)}, f32[16,32,256]{2,1,0:T(8,128)S(1)}, u32[]{:S(2)}, u32[]{:S(2)}) %collective-permute-start.9) | collective-permute-done | bytes 524320 | tf_op jit(solution)/shard_map/ppermute | solution.py:388
  69.0 8.2 %shard_map.64 = (f32[16,64,256]{2,1,0:T(8,128)S(1)}, f32[16,64,256]{2,1,0:T(8,128)S(1)}, f32[16,32,256]{2,1,0:T(8,128)S(1)}, f32[15,32,256]{2,1,0:T(8,128)S(1)}, f32[15,32,256]{2,1,0:T(8,128)S(1)}) custom-call(f32[16,32,256]{2,1,0:T(8,128)S(1)} %collective-permute-done.9.refs_0_, f32[16,16,256]{2,1,0:T(8,128)S(1)} %shard_map.61.refs_4_.refs_1_, ...), custom_call_target="tpu_custom_call" | custom-call | flops 1000000000 | bytes 3500000 | tf_op jit(solution)/shard_map/pallas_call | solution.py:367
  77.3 1.3 collective-permute-start.16
  78.6 4.8 %collective-permute-start.15 = (f32[15,32,256]{2,1,0:T(8,128)S(1)}, f32[15,32,256]{2,1,0:T(8,128)S(1)}, u32[]{:S(2)}, u32[]{:S(2)}) collective-permute-start(f32[15,32,256]{2,1,0:T(8,128)S(1)} %get-tuple-element.61.refs_1_), channel_id=1, source_target_pairs={{0,1},{1,2},{2,3},{4,5},{5,6},{6,7},{8,9},{9,10},{10,11},{12,13},{... | collective-permute-start | bytes 1474568 | tf_op jit(solution)/shard_map/ppermute | solution.py:381
  83.3 0.6 collective-permute-done.12.next_ref
  84.0 0.4 shard_map.65
  84.4 3.7 %collective-permute-start.13 = (f32[15,32,256]{2,1,0:T(8,128)S(1)}, f32[15,32,256]{2,1,0:T(8,128)S(1)}, u32[]{:S(2)}, u32[]{:S(2)}) collective-permute-start(f32[15,32,256]{2,1,0:T(8,128)S(1)} %get-tuple-element.59.refs_1_), channel_id=1, source_target_pairs={{0,1},{1,2},{2,3},{4,5},{5,6},{6,7},{8,9},{9,10},{10,11},{12,13},{... | collective-permute-start | bytes 1474568 | tf_op jit(solution)/shard_map/ppermute | solution.py:381
  88.1 1.3 collective-permute-start.14
  89.4 3.4 %collective-permute-done.16.refs_3_ = f32[15,32,256]{2,1,0:T(8,128)S(1)} collective-permute-done((f32[15,32,256]{2,1,0:T(8,128)S(1)}, f32[15,32,256]{2,1,0:T(8,128)S(1)}, u32[]{:S(2)}, u32[]{:S(2)}) %collective-permute-start.16) | collective-permute-done | bytes 491552 | tf_op jit(solution)/shard_map/ppermute | solution.py:382
  92.8 1.9 %collective-permute-done.15.refs_2_ = f32[15,32,256]{2,1,0:T(8,128)S(1)} collective-permute-done((f32[15,32,256]{2,1,0:T(8,128)S(1)}, f32[15,32,256]{2,1,0:T(8,128)S(1)}, u32[]{:S(2)}, u32[]{:S(2)}) %collective-permute-start.15) | collective-permute-done | bytes 491552 | tf_op jit(solution)/shard_map/ppermute | solution.py:381
  94.7 1.2 shard_map.66
  95.9 4.4 %collective-permute-start.19 = (f32[15,16,256]{2,1,0:T(8,128)S(1)}, f32[15,16,256]{2,1,0:T(8,128)S(1)}, u32[]{:S(2)}, u32[]{:S(2)}) collective-permute-start(f32[15,16,256]{2,1,0:T(8,128)S(1)} %get-tuple-element.65.refs_1_), channel_id=1, source_target_pairs={{0,1},{1,2},{2,3},{4,5},{5,6},{6,7},{8,9},{9,10},{10,11},{12,13},{... | collective-permute-start | bytes 737288 | tf_op jit(solution)/shard_map/ppermute | solution.py:381
  100.3 1.3 collective-permute-start.20
  101.6 3.6 %collective-permute-done.13.refs_2_ = f32[15,32,256]{2,1,0:T(8,128)S(1)} collective-permute-done((f32[15,32,256]{2,1,0:T(8,128)S(1)}, f32[15,32,256]{2,1,0:T(8,128)S(1)}, u32[]{:S(2)}, u32[]{:S(2)}) %collective-permute-start.13) | collective-permute-done | bytes 491552 | tf_op jit(solution)/shard_map/ppermute | solution.py:381
  105.2 1.8 %shard_map.67 = (f32[15,32,256]{2,1,0:T(8,128)S(1)}, f32[15,32,256]{2,1,0:T(8,128)S(1)}) custom-call(f32[31]{0:T(128)S(1)} %copy-done.5, f32[16,64,256]{2,1,0:T(8,128)S(1)} %get-tuple-element.42.obs_ref, f32[15,32,256]{2,1,0:T(8,128)S(1)} %get-tuple-element.58.refs_4_.refs_0_, f32[15,32,256]{2,1,0:T(8,128)S(1)} %get-tuple-element.59.refs_1_, ...), custom_call_target="tpu_custom_call" | custom-call | flops 1000000000 | bytes 3500000 | tf_op jit(solution)/shard_map/pallas_call | solution.py:298
  107.1 4.4 %collective-permute-start.17 = (f32[15,32,256]{2,1,0:T(8,128)S(1)}, f32[15,32,256]{2,1,0:T(8,128)S(1)}, u32[]{:S(2)}, u32[]{:S(2)}) collective-permute-start(f32[15,32,256]{2,1,0:T(8,128)S(1)} %get-tuple-element.64.refs_1_), channel_id=1, source_target_pairs={{0,1},{1,2},{2,3},{4,5},{5,6},{6,7},{8,9},{9,10},{10,11},{12,13},{... | collective-permute-start | bytes 1474568 | tf_op jit(solution)/shard_map/ppermute | solution.py:381
  111.5 1.3 collective-permute-start.18
  112.8 1.2 shard_map.68
  114.0 4.6 %collective-permute-start.22 = (f32[15,16,256]{2,1,0:T(8,128)S(1)}, f32[15,16,256]{2,1,0:T(8,128)S(1)}, u32[]{:S(2)}, u32[]{:S(2)}) collective-permute-start(f32[15,16,256]{2,1,0:T(8,128)S(1)} %get-tuple-element.67.refs_1_), channel_id=1, source_target_pairs={{0,1},{1,2},{2,3},{4,5},{5,6},{6,7},{8,9},{9,10},{10,11},{12,13},{... | collective-permute-start | bytes 737288 | tf_op jit(solution)/shard_map/ppermute | solution.py:381
  118.6 1.3 collective-permute-start.23
  119.9 1.1 shard_map.69.refs_4_.refs_1_
  121.0 2.1 %collective-permute-done.17.refs_2_ = f32[15,32,256]{2,1,0:T(8,128)S(1)} collective-permute-done((f32[15,32,256]{2,1,0:T(8,128)S(1)}, f32[15,32,256]{2,1,0:T(8,128)S(1)}, u32[]{:S(2)}, u32[]{:S(2)}) %collective-permute-start.17) | collective-permute-done | bytes 491552 | tf_op jit(solution)/shard_map/ppermute | solution.py:381
  123.1 4.4 %collective-permute-done.18.refs_3_ = f32[15,32,256]{2,1,0:T(8,128)S(1)} collective-permute-done((f32[15,32,256]{2,1,0:T(8,128)S(1)}, f32[15,32,256]{2,1,0:T(8,128)S(1)}, u32[]{:S(2)}, u32[]{:S(2)}) %collective-permute-start.18) | collective-permute-done | bytes 491552 | tf_op jit(solution)/shard_map/ppermute | solution.py:382
  127.5 1.7 %shard_map.70.refs_4_.refs_3_ = f32[16,32,256]{2,1,0:T(8,128)S(1)} custom-call(f32[31]{0:T(128)S(1)} %copy-done.5, f32[15,32,256]{2,1,0:T(8,128)S(1)} %get-tuple-element.63.refs_4_.refs_0_, f32[15,32,256]{2,1,0:T(8,128)S(1)} %get-tuple-element.64.refs_1_, f32[15,32,256]{2,1,0:T(8,128)S(1)} %collective-permute-done.17.refs_2_, ...), custom_call_target="tpu_custom_call" | custom-call | flops 1000000000 | bytes 3500000 | tf_op jit(solution)/shard_map/pallas_call | solution.py:323
  129.3 0.1 collective-permute-start.21
  129.4 0.8 collective-permute-done.23.refs_3_
  130.2 1.1 shard_map.71.refs_2_
  131.4 6.6 %collective-permute-done.21.refs_0_ = f32[16,32,256]{2,1,0:T(8,128)S(1)} collective-permute-done((f32[16,32,256]{2,1,0:T(8,128)S(1)}, f32[16,32,256]{2,1,0:T(8,128)S(1)}, u32[]{:S(2)}, u32[]{:S(2)}) %collective-permute-start.21) | collective-permute-done | bytes 524320 | tf_op jit(solution)/shard_map/ppermute | solution.py:388
  137.9 2.9 %shard_map.72 = f32[16,64,256]{2,1,0:T(8,128)} custom-call(f32[16,32,256]{2,1,0:T(8,128)S(1)} %collective-permute-done.21.refs_0_, f32[16,16,256]{2,1,0:T(8,128)S(1)} %shard_map.69.refs_4_.refs_1_, f32[16,16,256]{2,1,0:T(8,128)S(1)} %shard_map.71.refs_2_, f32[16,32,256]{2,1,0:T(8,128)S(1)} %shard_map.70.refs_4_.refs_3_, ...), custom_call_target="tpu_custom_call" | custom-call | flops 1000000000 | bytes 3500000 | tf_op jit(solution)/shard_map/pallas_call | solution.py:367
  (15 shorter events, 0.0 us)
Async XLA Ops:
  1.1 15.3 %collective-permute-start = (f32[16,32,256]{2,1,0:T(8,128)S(1)}, f32[16,32,256]{2,1,0:T(8,128)S(1)}, u32[]{:S(2)}, u32[]{:S(2)}) collective-permute-start(f32[16,32,256]{2,1,0:T(8,128)S(1)} %slice.3), channel_id=1, source_target_pairs={{0,12},{4,0},{8,4},{12,8},{1,13},{5,1},{9,5},{13,9},{2,14},{6,2},{... | collective-permute-start | bytes 1572872 | tf_op jit(solution)/shard_map/ppermute | solution.py:388
  3.5 1.2 copy-start
  4.7 0.7 copy-start.2
  5.4 0.7 copy-start.3
  6.1 0.7 copy-start.4
  10.5 17.1 %collective-permute-start.4 = (f32[15,32,256]{2,1,0:T(8,128)S(1)}, f32[15,32,256]{2,1,0:T(8,128)S(1)}, u32[]{:S(2)}, u32[]{:S(2)}) collective-permute-start(f32[15,32,256]{2,1,0:T(8,128)S(1)} %get-tuple-element.44.refs_0_), channel_id=1, source_target_pairs={{1,0},{2,1},{3,2},{5,4},{6,5},{7,6},{9,8},{10,9},{11,10},{13,12},{... | collective-permute-start | bytes 1474568 | tf_op jit(solution)/shard_map/ppermute | solution.py:382
  11.8 16.2 %collective-permute-start.3 = (f32[15,32,256]{2,1,0:T(8,128)S(1)}, f32[15,32,256]{2,1,0:T(8,128)S(1)}, u32[]{:S(2)}, u32[]{:S(2)}) collective-permute-start(f32[15,32,256]{2,1,0:T(8,128)S(1)} %get-tuple-element.45.refs_1_), channel_id=1, source_target_pairs={{0,1},{1,2},{2,3},{4,5},{5,6},{6,7},{8,9},{9,10},{10,11},{12,13},{... | collective-permute-start | bytes 1474568 | tf_op jit(solution)/shard_map/ppermute | solution.py:381
  16.4 8.4 %copy-start.5 = (f32[31]{0:T(128)S(1)}, f32[31]{0:T(128)}, u32[]{:S(2)}) copy-start(f32[31]{0:T(128)} %tz_ref.25) | copy-start | bytes 376
  20.0 18.6 %collective-permute-start.1 = (f32[15,32,256]{2,1,0:T(8,128)S(1)}, f32[15,32,256]{2,1,0:T(8,128)S(1)}, u32[]{:S(2)}, u32[]{:S(2)}) collective-permute-start(f32[15,32,256]{2,1,0:T(8,128)S(1)} %get-tuple-element.43.refs_1_), channel_id=1, source_target_pairs={{0,1},{1,2},{2,3},{4,5},{5,6},{6,7},{8,9},{9,10},{10,11},{12,13},{... | collective-permute-start | bytes 1474568 | tf_op jit(solution)/shard_map/ppermute | solution.py:381
  23.5 15.1 %collective-permute-start.2 = (f32[15,32,256]{2,1,0:T(8,128)S(1)}, f32[15,32,256]{2,1,0:T(8,128)S(1)}, u32[]{:S(2)}, u32[]{:S(2)}) collective-permute-start(f32[15,32,256]{2,1,0:T(8,128)S(1)} %get-tuple-element.41.after_ref.refs_4_.refs_0_), channel_id=1, source_target_pairs={{1,0},{2,1},{3,2},{5,4},{6,5},{7,6},{9,8},{10,9},{11,10},{13,12},{... | collective-permute-start | bytes 1474568 | tf_op jit(solution)/shard_map/ppermute | solution.py:382
  29.2 22.6 %collective-permute-start.7 = (f32[15,16,256]{2,1,0:T(8,128)S(1)}, f32[15,16,256]{2,1,0:T(8,128)S(1)}, u32[]{:S(2)}, u32[]{:S(2)}) collective-permute-start(f32[15,16,256]{2,1,0:T(8,128)S(1)} %get-tuple-element.49.refs_1_), channel_id=1, source_target_pairs={{0,1},{1,2},{2,3},{4,5},{5,6},{6,7},{8,9},{9,10},{10,11},{12,13},{... | collective-permute-start | bytes 737288 | tf_op jit(solution)/shard_map/ppermute | solution.py:381
  33.6 19.6 %collective-permute-start.8 = (f32[15,16,256]{2,1,0:T(8,128)S(1)}, f32[15,16,256]{2,1,0:T(8,128)S(1)}, u32[]{:S(2)}, u32[]{:S(2)}) collective-permute-start(f32[15,16,256]{2,1,0:T(8,128)S(1)} %get-tuple-element.46.refs_4_.refs_0_), channel_id=1, source_target_pairs={{1,0},{2,1},{3,2},{5,4},{6,5},{7,6},{9,8},{10,9},{11,10},{13,12},{... | collective-permute-start | bytes 737288 | tf_op jit(solution)/shard_map/ppermute | solution.py:382
  40.4 14.7 %collective-permute-start.5 = (f32[15,32,256]{2,1,0:T(8,128)S(1)}, f32[15,32,256]{2,1,0:T(8,128)S(1)}, u32[]{:S(2)}, u32[]{:S(2)}) collective-permute-start(f32[15,32,256]{2,1,0:T(8,128)S(1)} %get-tuple-element.48.refs_1_), channel_id=1, source_target_pairs={{0,1},{1,2},{2,3},{4,5},{5,6},{6,7},{8,9},{9,10},{10,11},{12,13},{... | collective-permute-start | bytes 1474568 | tf_op jit(solution)/shard_map/ppermute | solution.py:381
  44.8 13.8 %collective-permute-start.6 = (f32[15,32,256]{2,1,0:T(8,128)S(1)}, f32[15,32,256]{2,1,0:T(8,128)S(1)}, u32[]{:S(2)}, u32[]{:S(2)}) collective-permute-start(f32[15,32,256]{2,1,0:T(8,128)S(1)} %get-tuple-element.47.refs_4_.refs_0_), channel_id=1, source_target_pairs={{1,0},{2,1},{3,2},{5,4},{6,5},{7,6},{9,8},{10,9},{11,10},{13,12},{... | collective-permute-start | bytes 1474568 | tf_op jit(solution)/shard_map/ppermute | solution.py:382
  47.3 13.2 %collective-permute-start.10 = (f32[15,16,256]{2,1,0:T(8,128)S(1)}, f32[15,16,256]{2,1,0:T(8,128)S(1)}, u32[]{:S(2)}, u32[]{:S(2)}) collective-permute-start(f32[15,16,256]{2,1,0:T(8,128)S(1)} %get-tuple-element.51.refs_1_), channel_id=1, source_target_pairs={{0,1},{1,2},{2,3},{4,5},{5,6},{6,7},{8,9},{9,10},{10,11},{12,13},{... | collective-permute-start | bytes 737288 | tf_op jit(solution)/shard_map/ppermute | solution.py:381
  51.8 9.4 %collective-permute-start.11 = (f32[15,16,256]{2,1,0:T(8,128)S(1)}, f32[15,16,256]{2,1,0:T(8,128)S(1)}, u32[]{:S(2)}, u32[]{:S(2)}) collective-permute-start(f32[15,16,256]{2,1,0:T(8,128)S(1)} %get-tuple-element.50.refs_4_.refs_0_), channel_id=1, source_target_pairs={{1,0},{2,1},{3,2},{5,4},{6,5},{7,6},{9,8},{10,9},{11,10},{13,12},{... | collective-permute-start | bytes 737288 | tf_op jit(solution)/shard_map/ppermute | solution.py:382
  60.4 8.7 %copy-start.1 = (f32[16,64,256]{2,1,0:T(8,128)S(1)}, f32[16,64,256]{2,1,0:T(8,128)}, u32[]{:S(2)}) copy-start(f32[16,64,256]{2,1,0:T(8,128)} %refs_4_.1) | copy-start | bytes 3145732
  60.4 8.7 %collective-permute-start.9 = (f32[16,32,256]{2,1,0:T(8,128)S(1)}, f32[16,32,256]{2,1,0:T(8,128)S(1)}, u32[]{:S(2)}, u32[]{:S(2)}) collective-permute-start(f32[16,32,256]{2,1,0:T(8,128)S(1)} %shard_map.62.refs_4_.refs_3_), channel_id=1, source_target_pairs={{0,4},{4,8},{8,12},{12,0},{1,5},{5,9},{9,13},{13,1},{2,6},{6,10},{... | collective-permute-start | bytes 1572872 | tf_op jit(solution)/shard_map/ppermute | solution.py:388
  77.3 6.7 %collective-permute-start.12 = (f32[16,32,256]{2,1,0:T(8,128)S(1)}, f32[16,32,256]{2,1,0:T(8,128)S(1)}, u32[]{:S(2)}, u32[]{:S(2)}) collective-permute-start(f32[16,32,256]{2,1,0:T(8,128)S(1)} %get-tuple-element.57), channel_id=1, source_target_pairs={{0,12},{4,0},{8,4},{12,8},{1,13},{5,1},{9,5},{13,9},{2,14},{6,2},{... | collective-permute-start | bytes 1572872 | tf_op jit(solution)/shard_map/ppermute | solution.py:388
  77.3 15.5 %collective-permute-start.16 = (f32[15,32,256]{2,1,0:T(8,128)S(1)}, f32[15,32,256]{2,1,0:T(8,128)S(1)}, u32[]{:S(2)}, u32[]{:S(2)}) collective-permute-start(f32[15,32,256]{2,1,0:T(8,128)S(1)} %get-tuple-element.60.refs_0_), channel_id=1, source_target_pairs={{1,0},{2,1},{3,2},{5,4},{6,5},{7,6},{9,8},{10,9},{11,10},{13,12},{... | collective-permute-start | bytes 1474568 | tf_op jit(solution)/shard_map/ppermute | solution.py:382
  78.6 16.1 %collective-permute-start.15 = (f32[15,32,256]{2,1,0:T(8,128)S(1)}, f32[15,32,256]{2,1,0:T(8,128)S(1)}, u32[]{:S(2)}, u32[]{:S(2)}) collective-permute-start(f32[15,32,256]{2,1,0:T(8,128)S(1)} %get-tuple-element.61.refs_1_), channel_id=1, source_target_pairs={{0,1},{1,2},{2,3},{4,5},{5,6},{6,7},{8,9},{9,10},{10,11},{12,13},{... | collective-permute-start | bytes 1474568 | tf_op jit(solution)/shard_map/ppermute | solution.py:381
  84.4 20.8 %collective-permute-start.13 = (f32[15,32,256]{2,1,0:T(8,128)S(1)}, f32[15,32,256]{2,1,0:T(8,128)S(1)}, u32[]{:S(2)}, u32[]{:S(2)}) collective-permute-start(f32[15,32,256]{2,1,0:T(8,128)S(1)} %get-tuple-element.59.refs_1_), channel_id=1, source_target_pairs={{0,1},{1,2},{2,3},{4,5},{5,6},{6,7},{8,9},{9,10},{10,11},{12,13},{... | collective-permute-start | bytes 1474568 | tf_op jit(solution)/shard_map/ppermute | solution.py:381
  88.1 17.1 %collective-permute-start.14 = (f32[15,32,256]{2,1,0:T(8,128)S(1)}, f32[15,32,256]{2,1,0:T(8,128)S(1)}, u32[]{:S(2)}, u32[]{:S(2)}) collective-permute-start(f32[15,32,256]{2,1,0:T(8,128)S(1)} %get-tuple-element.58.refs_4_.refs_0_), channel_id=1, source_target_pairs={{1,0},{2,1},{3,2},{5,4},{6,5},{7,6},{9,8},{10,9},{11,10},{13,12},{... | collective-permute-start | bytes 1474568 | tf_op jit(solution)/shard_map/ppermute | solution.py:382
  95.9 22.7 %collective-permute-start.19 = (f32[15,16,256]{2,1,0:T(8,128)S(1)}, f32[15,16,256]{2,1,0:T(8,128)S(1)}, u32[]{:S(2)}, u32[]{:S(2)}) collective-permute-start(f32[15,16,256]{2,1,0:T(8,128)S(1)} %get-tuple-element.65.refs_1_), channel_id=1, source_target_pairs={{0,1},{1,2},{2,3},{4,5},{5,6},{6,7},{8,9},{9,10},{10,11},{12,13},{... | collective-permute-start | bytes 737288 | tf_op jit(solution)/shard_map/ppermute | solution.py:381
  100.3 19.6 %collective-permute-start.20 = (f32[15,16,256]{2,1,0:T(8,128)S(1)}, f32[15,16,256]{2,1,0:T(8,128)S(1)}, u32[]{:S(2)}, u32[]{:S(2)}) collective-permute-start(f32[15,16,256]{2,1,0:T(8,128)S(1)} %get-tuple-element.62.refs_4_.refs_0_), channel_id=1, source_target_pairs={{1,0},{2,1},{3,2},{5,4},{6,5},{7,6},{9,8},{10,9},{11,10},{13,12},{... | collective-permute-start | bytes 737288 | tf_op jit(solution)/shard_map/ppermute | solution.py:382
  107.1 16.1 %collective-permute-start.17 = (f32[15,32,256]{2,1,0:T(8,128)S(1)}, f32[15,32,256]{2,1,0:T(8,128)S(1)}, u32[]{:S(2)}, u32[]{:S(2)}) collective-permute-start(f32[15,32,256]{2,1,0:T(8,128)S(1)} %get-tuple-element.64.refs_1_), channel_id=1, source_target_pairs={{0,1},{1,2},{2,3},{4,5},{5,6},{6,7},{8,9},{9,10},{10,11},{12,13},{... | collective-permute-start | bytes 1474568 | tf_op jit(solution)/shard_map/ppermute | solution.py:381
  111.5 16.1 %collective-permute-start.18 = (f32[15,32,256]{2,1,0:T(8,128)S(1)}, f32[15,32,256]{2,1,0:T(8,128)S(1)}, u32[]{:S(2)}, u32[]{:S(2)}) collective-permute-start(f32[15,32,256]{2,1,0:T(8,128)S(1)} %get-tuple-element.63.refs_4_.refs_0_), channel_id=1, source_target_pairs={{1,0},{2,1},{3,2},{5,4},{6,5},{7,6},{9,8},{10,9},{11,10},{13,12},{... | collective-permute-start | bytes 1474568 | tf_op jit(solution)/shard_map/ppermute | solution.py:382
  114.0 15.4 %collective-permute-start.22 = (f32[15,16,256]{2,1,0:T(8,128)S(1)}, f32[15,16,256]{2,1,0:T(8,128)S(1)}, u32[]{:S(2)}, u32[]{:S(2)}) collective-permute-start(f32[15,16,256]{2,1,0:T(8,128)S(1)} %get-tuple-element.67.refs_1_), channel_id=1, source_target_pairs={{0,1},{1,2},{2,3},{4,5},{5,6},{6,7},{8,9},{9,10},{10,11},{12,13},{... | collective-permute-start | bytes 737288 | tf_op jit(solution)/shard_map/ppermute | solution.py:381
  118.6 11.7 %collective-permute-start.23 = (f32[15,16,256]{2,1,0:T(8,128)S(1)}, f32[15,16,256]{2,1,0:T(8,128)S(1)}, u32[]{:S(2)}, u32[]{:S(2)}) collective-permute-start(f32[15,16,256]{2,1,0:T(8,128)S(1)} %get-tuple-element.66.refs_4_.refs_0_), channel_id=1, source_target_pairs={{1,0},{2,1},{3,2},{5,4},{6,5},{7,6},{9,8},{10,9},{11,10},{13,12},{... | collective-permute-start | bytes 737288 | tf_op jit(solution)/shard_map/ppermute | solution.py:382
  129.3 8.7 %collective-permute-start.21 = (f32[16,32,256]{2,1,0:T(8,128)S(1)}, f32[16,32,256]{2,1,0:T(8,128)S(1)}, u32[]{:S(2)}, u32[]{:S(2)}) collective-permute-start(f32[16,32,256]{2,1,0:T(8,128)S(1)} %shard_map.70.refs_4_.refs_3_), channel_id=1, source_target_pairs={{0,4},{4,8},{8,12},{12,0},{1,5},{5,9},{9,13},{13,1},{2,6},{6,10},{... | collective-permute-start | bytes 1572872 | tf_op jit(solution)/shard_map/ppermute | solution.py:388

commit v5 on v4

--- a/solution.py
+++ b/solution.py
@@ -108,12 +108,18 @@
         high_ref[plane - (n - radius)] = v
 
 
-def own_rows(est, wx_ref, ah_ref, al_ref, p, inner):
-    rows = est.shape[0]
-    w = blur_columns(est, ah_ref[p], al_ref[p])
-    w_hi, w_lo = split(w)
-    v = blur_rows(wx_ref[p, 0, :inner, :rows], wx_ref[p, 1, :inner, :rows], w_hi, w_lo)
-    return w, v
+def all_columns(source, a_refs, out_ref):
+    for p in range(out_ref.shape[0]):
+        out_ref[p] = blur_columns(source(p), a_refs[0][p], a_refs[1][p])
+
+
+def own_rows(w_ref, wx_ref, low_ref, high_ref):
+    n, rows, _ = w_ref.shape
+    radius, inner, _ = low_ref.shape
+    for p in range(n):
+        w_hi, w_lo = split(w_ref[p])
+        v = blur_rows(wx_ref[p, 0, :inner, :rows], wx_ref[p, 1, :inner, :rows], w_hi, w_lo)
+        store_sends(v, p, n, radius, low_ref, high_ref)
 
 
 def row_place():
@@ -122,21 +128,28 @@
 
 
 def first_kernel(
-    n, radius, halo, band_ref, tx_ref, ty_ref, est_ref,
+    n, radius, band_hbm, tx_hbm, ty_hbm, est_hbm,
     ah_ref, al_ref, wx_ref, w_ref, low_ref, high_ref,
+    band_ref, tx_ref, ty_ref, est_ref, sems,
 ):
+    pairs = ((band_hbm, band_ref), (tx_hbm, tx_ref), (ty_hbm, ty_ref), (est_hbm, est_ref))
+    copies = [pltpu.make_async_copy(a, b, sems.at[k]) for k, (a, b) in enumerate(pairs)]
+    for copy in copies:
+        copy.start()
     rows, width = wx_ref.shape[2], wx_ref.shape[3]
     _, lane = iotas(16, 128)
     _, wide = iotas(16, width)
     row, lanes = iotas(rows, width)
     keep = jnp.logical_not(row_place()[1]) | ((row < rows - radius) == (lanes < rows))
+    for copy in copies:
+        copy.wait()
     for p in range(n):
         band = band_ref[p]
         column_matrix(spread(ty_ref, band, lane, radius, True), radius, ah_ref, al_ref, p)
         matrix = row_matrix(spread(tx_ref, band, wide, radius, False), rows, 0, width)
         wx_ref[p, 0], wx_ref[p, 1] = split(jnp.where(keep, matrix, 0.0))
-        w_ref[p], v = own_rows(est_ref[p], wx_ref, ah_ref, al_ref, p, rows - halo)
-        store_sends(v, p, n, radius, low_ref, high_ref)
+    all_columns(lambda p: est_ref[p], (ah_ref, al_ref), w_ref)
+    own_rows(w_ref, wx_ref, low_ref, high_ref)
 
 
 def first_blur(band_index, taps_x, taps_y, est, halo, width):
@@ -146,8 +159,15 @@
     w = shape_of(n, 2, rows, width, dtype=BF16)
     send = shape_of(radius, rows - halo, columns)
     return pl.pallas_call(
-        functools.partial(first_kernel, n, radius, halo),
-        in_specs=[SMEM] * 3 + [VMEM],
+        functools.partial(first_kernel, n, radius),
+        in_specs=[pl.BlockSpec(memory_space=pltpu.HBM)] * 4,
+        scratch_shapes=[
+            pltpu.SMEM(band_index.shape, jnp.int32),
+            pltpu.SMEM(taps_x.shape, F32),
+            pltpu.SMEM(taps_y.shape, F32),
+            pltpu.VMEM(est.shape, F32),
+            pltpu.SemaphoreType.DMA((4,)),
+        ],
         out_specs=[VMEM] * 6,
         out_shape=[a, a, w, shape_of(*est.shape), send, send],
         compiler_params=PARAMS,
@@ -214,13 +234,12 @@
 def edge_kernel(n, radius, blurred, w_ref, next_ref, wx_ref, *refs):
     rows, halo = w_ref.shape[1], next_ref.shape[1]
     inner, used = rows - halo, rows + halo
+    beyond_ref = next_ref
     if not blurred:
-        ah_ref, al_ref = refs[:2]
-    for p in range(n):
-        beyond = next_ref[p]
-        if not blurred:
-            beyond = blur_columns(beyond, ah_ref[p], al_ref[p])
-        w_hi, w_lo = split(jnp.concatenate([w_ref[p], beyond], axis=0))
+        beyond_ref, refs = refs[-1], refs[:-1]
+        all_columns(lambda p: next_ref[p], refs[:2], beyond_ref)
+    for p in range(n):
+        w_hi, w_lo = split(jnp.concatenate([w_ref[p], beyond_ref[p]], axis=0))
         v = blur_rows(wx_ref[p, 0, inner:, :used], wx_ref[p, 1, inner:, :used], w_hi, w_lo)
         store_sends(v, p, n, radius, *refs[-2:])
 
@@ -235,6 +254,7 @@
         in_specs=[VMEM] * len(args),
         out_specs=[VMEM] * 2,
         out_shape=[send] * 2,
+        scratch_shapes=[pltpu.VMEM(beyond.shape, F32)] if columns_matrix else [],
         compiler_params=PARAMS,
         cost_estimate=cost(1.0),
     )(*args)
@@ -330,29 +350,29 @@
     )(taps_z, *chunk, after)
 
 
-def update_kernel(n, radius, last, *refs):
+def update_kernel(n, last, *refs):
     pieces, edge_ref, refs = refs[:4], refs[3], refs[4:]
     est_ref, rn_ref, wa_ref, bh_ref, bl_ref = refs[:5]
     refs = refs[5:]
     rows = est_ref.shape[1]
     halo = edge_ref.shape[1]
     used = rows + halo
+    u_ref, refs = refs[-1], refs[:-1]
     if last:
         (out_ref,) = refs
     else:
         wx_ref, ah_ref, al_ref, out_ref, w_ref, top_ref, low_ref, high_ref = refs
     for p in range(n):
-        c = jnp.concatenate([piece[p] for piece in pieces], axis=0)
-        c_hi, c_lo = split(c)
-        u = blur_rows(wa_ref[p, 0, :, :used], wa_ref[p, 1, :, :used], c_hi, c_lo)
-        u = blur_columns(u, bh_ref[p], bl_ref[p])
-        est = est_ref[p] * u * rn_ref[p]
-        out_ref[p] = est
-        if not last:
-            w, v = own_rows(est, wx_ref, ah_ref, al_ref, p, rows - halo)
-            w_ref[p] = w
-            top_ref[p] = w[:halo]
-            store_sends(v, p, n, radius, low_ref, high_ref)
+        c_hi, c_lo = split(jnp.concatenate([piece[p] for piece in pieces], axis=0))
+        u_ref[p] = blur_rows(wa_ref[p, 0, :, :used], wa_ref[p, 1, :, :used], c_hi, c_lo)
+    for p in range(n):
+        u = blur_columns(u_ref[p], bh_ref[p], bl_ref[p])
+        out_ref[p] = est_ref[p] * u * rn_ref[p]
+    if not last:
+        all_columns(lambda p: out_ref[p], (ah_ref, al_ref), w_ref)
+        for p in range(n):
+            top_ref[p] = w_ref[p, :halo]
+        own_rows(w_ref, wx_ref, low_ref, high_ref)
 
 
 def update(pieces, est, rn, adjoint, forward, radius):
@@ -365,10 +385,11 @@
         send = shape_of(radius, rows - halo, columns)
         out_shape += [shape_of(*est.shape), shape_of(n, halo, columns), send, send]
     return pl.pallas_call(
-        functools.partial(update_kernel, n, radius, last),
+        functools.partial(update_kernel, n, last),
         in_specs=[VMEM] * len(args),
         out_specs=[VMEM] * len(out_shape),
         out_shape=out_shape,
+        scratch_shapes=[pltpu.VMEM(est.shape, F32)],
         compiler_params=PARAMS,
         cost_estimate=cost(1.0),
     )(*args)

time: 142 us -> 134 us (0.944)
  Pallas kernels: 38 us -> 27.7 us
  waiting for transfers between devices: 39.4 us -> 42.1 us
    pallas_call x3, Pallas kernels: 14.8 us -> 6.96 us  [the longest x2 4.56 us: update(): pl.pallas_call(functools.partial(update_kernel, n, last), in_specs=[VMEM]...]
    pallas_call x2, Pallas kernels: 3.99 us -> 1.51 us  [edge_blur(): pl.pallas_call(functools.partial(edge_kernel, n, radius, not columns_matr...]
    ppermute x10, waiting for transfers between devices: 12.5 us -> 14.5 us  [depth_exchange(): zlo = lax.ppermute(high, 'slab', forward)]
  transfers between devices with their start and end apart: 24 -> 24, of which waited for: 14 -> 15; matrix products, arithmetic and copies ran while one was open for 0% -> 0% of each run, Pallas kernels for 19% -> 17%
where the time goes in v5:
time: 134 us; the launch traced here: 133 us
  starting transfers between devices  58.6 us (44%)
  waiting for transfers between devices  42.1 us (31%)
  Pallas kernels  27.7 us (21%)
  local copies, waits for them, and re-layouts  4.37 us (3%)
    ppermute x10, starting transfers between devices, depth_exchange(): zlo = lax.ppermute(high, 'slab', forward)  43.1 us
    ppermute x10, waiting for transfers between devices, depth_exchange(): zlo = lax.ppermute(high, 'slab', forward)  14.5 us
    ppermute x4, waiting for transfers between devices, ring(): lax.ppermute(x, 'row', [(i, (i + step) % count) for i in range(count)])  14.1 us
    ppermute x10, waiting for transfers between devices, depth_exchange(): zhi = lax.ppermute(low, 'slab', backward)  13.5 us
    ppermute x10, starting transfers between devices, depth_exchange(): zhi = lax.ppermute(low, 'slab', backward)  12.9 us
    pallas_call x6, Pallas kernels, depth_ratio(): pl.pallas_call(functools.partial(ratio_kernel, n, radius, skip, obs_skip)...  8.35 us
    pallas_call x6, Pallas kernels, depth_back(): pl.pallas_call(functools.partial(back_kernel, n, radius), in_specs=[SMEM]...  8.05 us
    pallas_call x2, Pallas kernels, update(): pl.pallas_call(functools.partial(update_kernel, n, last), in_specs=[VMEM]...  4.56 us
  transfers between devices with their start and end apart: 24, of which 15 were waited for; matrix products, arithmetic and copies ran while one was open for 0% of the time, Pallas kernels for 17%

profile of v5, /device:TPU:0, one launch (start us, length us, event | category | flops | bytes accessed | tf_op | source)
XLA Modules:
  0.0 133.0 jit_solution(11879841915206965900)
XLA Ops:
  0.0 1.1 slice.3
  1.1 2.4 %collective-permute-start = (f32[16,32,256]{2,1,0:T(8,128)S(1)}, f32[16,32,256]{2,1,0:T(8,128)S(1)}, u32[]{:S(2)}, u32[]{:S(2)}) collective-permute-start(f32[16,32,256]{2,1,0:T(8,128)S(1)} %slice.3), channel_id=1, source_target_pairs={{0,12},{4,0},{8,4},{12,8},{1,13},{5,1},{9,5},{13,9},{2,14},{6,2},{... | collective-permute-start | bytes 1572872 | tf_op jit(solution)/shard_map/ppermute | solution.py:409
  3.5 1.2 copy-done
  4.7 0.7 copy-done.2
  5.4 0.7 copy-done.3
  6.1 0.7 copy-done.4
  6.8 2.4 %shard_map.55 = (bf16[16,256,256]{2,1,0:T(8,128)(2,1)S(1)}, bf16[16,256,256]{2,1,0:T(8,128)(2,1)S(1)}, bf16[16,2,64,128]{3,2,1,0:T(8,128)(2,1)S(1)}, f32[16,64,2...) custom-call(s32[16]{0:T(128)S(1)} %copy-done.4, f32[16,31]{1,0:T(8,128)S(1)} %copy-done.2, ...), custom_call_target="tpu_custom_call" | custom-call | flops 1000000000 | bytes 3500000 | tf_op jit(solution)/shard_map/pallas_call | solution.py:161
  9.2 1.3 collective-permute-start.4
  10.5 4.6 %collective-permute-start.3 = (f32[15,32,256]{2,1,0:T(8,128)S(1)}, f32[15,32,256]{2,1,0:T(8,128)S(1)}, u32[]{:S(2)}, u32[]{:S(2)}) collective-permute-start(f32[15,32,256]{2,1,0:T(8,128)S(1)} %get-tuple-element.45.refs_1_), channel_id=1, source_target_pairs={{0,1},{1,2},{2,3},{4,5},{5,6},{6,7},{8,9},{9,10},{10,11},{12,13},{... | collective-permute-start | bytes 1474568 | tf_op jit(solution)/shard_map/ppermute | solution.py:402
  15.1 0.0 copy-start.5
  15.1 1.1 shard_map.56
  16.2 3.5 %collective-permute-start.1 = (f32[15,32,256]{2,1,0:T(8,128)S(1)}, f32[15,32,256]{2,1,0:T(8,128)S(1)}, u32[]{:S(2)}, u32[]{:S(2)}) collective-permute-start(f32[15,32,256]{2,1,0:T(8,128)S(1)} %get-tuple-element.43.refs_1_), channel_id=1, source_target_pairs={{0,1},{1,2},{2,3},{4,5},{5,6},{6,7},{8,9},{9,10},{10,11},{12,13},{... | collective-permute-start | bytes 1474568 | tf_op jit(solution)/shard_map/ppermute | solution.py:402
  19.7 1.3 collective-permute-start.2
  21.0 2.8 %shard_map.57 = (bf16[16,256,256]{2,1,0:T(8,128)(2,1)S(1)}, bf16[16,256,256]{2,1,0:T(8,128)(2,1)S(1)}, bf16[16,2,64,128]{3,2,1,0:T(8,128)(2,1)S(1)}, f32[16,64,256]{2,1,0:T(8,128)S(1)}, f32[16,64,256]{2,1,0:T(8,128)S(1)}) custom-call(s32[16]{0:T(128)S(1)} %copy-done.4, f32[16,31]{1,0:T(8,128)S(1)} %copy-done.2, f32[16,31]{1,0:T(8,128)S(1)} %copy-done.3, ...), custom_call_target="tpu_custom_call" | custom-call | flops 1000000000 | bytes 3500000 | tf_op jit(solution)/shard_map/pallas_call | solution.py:224
  23.8 0.5 collective-permute-done.4.refs_3_
  24.3 2.4 %collective-permute-done.3.refs_2_ = f32[15,32,256]{2,1,0:T(8,128)S(1)} collective-permute-done((f32[15,32,256]{2,1,0:T(8,128)S(1)}, f32[15,32,256]{2,1,0:T(8,128)S(1)}, u32[]{:S(2)}, u32[]{:S(2)}) %collective-permute-start.3) | collective-permute-done | bytes 491552 | tf_op jit(solution)/shard_map/ppermute | solution.py:402
  26.7 1.2 shard_map.58
  27.9 4.4 %collective-permute-start.7 = (f32[15,16,256]{2,1,0:T(8,128)S(1)}, f32[15,16,256]{2,1,0:T(8,128)S(1)}, u32[]{:S(2)}, u32[]{:S(2)}) collective-permute-start(f32[15,16,256]{2,1,0:T(8,128)S(1)} %get-tuple-element.49.refs_1_), channel_id=1, source_target_pairs={{0,1},{1,2},{2,3},{4,5},{5,6},{6,7},{8,9},{9,10},{10,11},{12,13},{... | collective-permute-start | bytes 737288 | tf_op jit(solution)/shard_map/ppermute | solution.py:402
  32.3 1.3 collective-permute-start.8
  33.6 3.6 %collective-permute-done.1.refs_2_ = f32[15,32,256]{2,1,0:T(8,128)S(1)} collective-permute-done((f32[15,32,256]{2,1,0:T(8,128)S(1)}, f32[15,32,256]{2,1,0:T(8,128)S(1)}, u32[]{:S(2)}, u32[]{:S(2)}) %collective-permute-start.1) | collective-permute-done | bytes 491552 | tf_op jit(solution)/shard_map/ppermute | solution.py:402
  37.3 1.8 %shard_map.59 = (f32[15,32,256]{2,1,0:T(8,128)S(1)}, f32[15,32,256]{2,1,0:T(8,128)S(1)}) custom-call(f32[31]{0:T(128)S(1)} %copy-done.5, f32[16,64,256]{2,1,0:T(8,128)S(1)} %get-tuple-element.42.obs_ref, f32[15,32,256]{2,1,0:T(8,128)S(1)} %get-tuple-element.41.after_ref.refs_4_.refs_0_, f32[15,32,256]{2,1,0:T(8,128)S(1)} %get-tuple-element.43.refs_1_, ...), custom_call_target="tpu_custom_call" | custom-call | flops 1000000000 | bytes 3500000 | tf_op jit(solution)/shard_map/pallas_call | solution.py:318
  39.1 4.4 %collective-permute-start.5 = (f32[15,32,256]{2,1,0:T(8,128)S(1)}, f32[15,32,256]{2,1,0:T(8,128)S(1)}, u32[]{:S(2)}, u32[]{:S(2)}) collective-permute-start(f32[15,32,256]{2,1,0:T(8,128)S(1)} %get-tuple-element.48.refs_1_), channel_id=1, source_target_pairs={{0,1},{1,2},{2,3},{4,5},{5,6},{6,7},{8,9},{9,10},{10,11},{12,13},{... | collective-permute-start | bytes 1474568 | tf_op jit(solution)/shard_map/ppermute | solution.py:402
  43.5 1.3 collective-permute-start.6
  44.8 1.2 shard_map.60
  46.0 4.6 %collective-permute-start.10 = (f32[15,16,256]{2,1,0:T(8,128)S(1)}, f32[15,16,256]{2,1,0:T(8,128)S(1)}, u32[]{:S(2)}, u32[]{:S(2)}) collective-permute-start(f32[15,16,256]{2,1,0:T(8,128)S(1)} %get-tuple-element.51.refs_1_), channel_id=1, source_target_pairs={{0,1},{1,2},{2,3},{4,5},{5,6},{6,7},{8,9},{9,10},{10,11},{12,13},{... | collective-permute-start | bytes 737288 | tf_op jit(solution)/shard_map/ppermute | solution.py:402
  50.6 1.3 collective-permute-start.11
  51.9 1.1 shard_map.61.refs_4_.refs_1_
  53.0 0.8 collective-permute-done.5.refs_2_
  53.8 3.5 %collective-permute-done.6.refs_3_ = f32[15,32,256]{2,1,0:T(8,128)S(1)} collective-permute-done((f32[15,32,256]{2,1,0:T(8,128)S(1)}, f32[15,32,256]{2,1,0:T(8,128)S(1)}, u32[]{:S(2)}, u32[]{:S(2)}) %collective-permute-start.6) | collective-permute-done | bytes 491552 | tf_op jit(solution)/shard_map/ppermute | solution.py:403
  57.3 1.7 %shard_map.62.refs_4_.refs_3_ = f32[16,32,256]{2,1,0:T(8,128)S(1)} custom-call(f32[31]{0:T(128)S(1)} %copy-done.5, f32[15,32,256]{2,1,0:T(8,128)S(1)} %get-tuple-element.47.refs_4_.refs_0_, f32[15,32,256]{2,1,0:T(8,128)S(1)} %get-tuple-element.48.refs_1_, f32[15,32,256]{2,1,0:T(8,128)S(1)} %collective-permute-done.5.refs_2_, ...), custom_call_target="tpu_custom_call" | custom-call | flops 1000000000 | bytes 3500000 | tf_op jit(solution)/shard_map/pallas_call | solution.py:343
  59.1 0.0 copy-start.1
  59.1 0.1 collective-permute-start.9
  59.2 0.8 collective-permute-done.11.refs_3_
  60.0 1.1 shard_map.63.refs_2_
  61.1 6.6 %collective-permute-done.9.refs_0_ = f32[16,32,256]{2,1,0:T(8,128)S(1)} collective-permute-done((f32[16,32,256]{2,1,0:T(8,128)S(1)}, f32[16,32,256]{2,1,0:T(8,128)S(1)}, u32[]{:S(2)}, u32[]{:S(2)}) %collective-permute-start.9) | collective-permute-done | bytes 524320 | tf_op jit(solution)/shard_map/ppermute | solution.py:409
  67.8 2.3 %shard_map.64 = (f32[16,64,256]{2,1,0:T(8,128)S(1)}, f32[16,64,256]{2,1,0:T(8,128)S(1)}, f32[16,32,256]{2,1,0:T(8,128)S(1)}, f32[15,32,256]{2,1,0:T(8,128)S(1)}, f32[15,32,256]{2,1,0:T(8,128)S(1)}) custom-call(f32[16,32,256]{2,1,0:T(8,128)S(1)} %collective-permute-done.9.refs_0_, f32[16,16,256]{2,1,0:T(8,128)S(1)} %shard_map.61.refs_4_.refs_1_, ...), custom_call_target="tpu_custom_call" | custom-call | flops 1000000000 | bytes 3500000 | tf_op jit(solution)/shard_map/pallas_call | solution.py:387
  70.1 0.0 collective-permute-start.12
  70.1 1.3 collective-permute-start.16
  71.4 4.6 %collective-permute-start.15 = (f32[15,32,256]{2,1,0:T(8,128)S(1)}, f32[15,32,256]{2,1,0:T(8,128)S(1)}, u32[]{:S(2)}, u32[]{:S(2)}) collective-permute-start(f32[15,32,256]{2,1,0:T(8,128)S(1)} %get-tuple-element.61.refs_1_), channel_id=1, source_target_pairs={{0,1},{1,2},{2,3},{4,5},{5,6},{6,7},{8,9},{9,10},{10,11},{12,13},{... | collective-permute-start | bytes 1474568 | tf_op jit(solution)/shard_map/ppermute | solution.py:402
  76.0 0.8 collective-permute-done.12.next_ref
  76.8 0.4 shard_map.65
  77.2 3.7 %collective-permute-start.13 = (f32[15,32,256]{2,1,0:T(8,128)S(1)}, f32[15,32,256]{2,1,0:T(8,128)S(1)}, u32[]{:S(2)}, u32[]{:S(2)}) collective-permute-start(f32[15,32,256]{2,1,0:T(8,128)S(1)} %get-tuple-element.59.refs_1_), channel_id=1, source_target_pairs={{0,1},{1,2},{2,3},{4,5},{5,6},{6,7},{8,9},{9,10},{10,11},{12,13},{... | collective-permute-start | bytes 1474568 | tf_op jit(solution)/shard_map/ppermute | solution.py:402
  80.9 1.3 collective-permute-start.14
  82.2 3.4 %collective-permute-done.16.refs_3_ = f32[15,32,256]{2,1,0:T(8,128)S(1)} collective-permute-done((f32[15,32,256]{2,1,0:T(8,128)S(1)}, f32[15,32,256]{2,1,0:T(8,128)S(1)}, u32[]{:S(2)}, u32[]{:S(2)}) %collective-permute-start.16) | collective-permute-done | bytes 491552 | tf_op jit(solution)/shard_map/ppermute | solution.py:403
  85.6 1.9 %collective-permute-done.15.refs_2_ = f32[15,32,256]{2,1,0:T(8,128)S(1)} collective-permute-done((f32[15,32,256]{2,1,0:T(8,128)S(1)}, f32[15,32,256]{2,1,0:T(8,128)S(1)}, u32[]{:S(2)}, u32[]{:S(2)}) %collective-permute-start.15) | collective-permute-done | bytes 491552 | tf_op jit(solution)/shard_map/ppermute | solution.py:402
  87.5 1.2 shard_map.66
  88.7 4.4 %collective-permute-start.19 = (f32[15,16,256]{2,1,0:T(8,128)S(1)}, f32[15,16,256]{2,1,0:T(8,128)S(1)}, u32[]{:S(2)}, u32[]{:S(2)}) collective-permute-start(f32[15,16,256]{2,1,0:T(8,128)S(1)} %get-tuple-element.65.refs_1_), channel_id=1, source_target_pairs={{0,1},{1,2},{2,3},{4,5},{5,6},{6,7},{8,9},{9,10},{10,11},{12,13},{... | collective-permute-start | bytes 737288 | tf_op jit(solution)/shard_map/ppermute | solution.py:402
  93.1 1.3 collective-permute-start.20
  94.4 3.6 %collective-permute-done.13.refs_2_ = f32[15,32,256]{2,1,0:T(8,128)S(1)} collective-permute-done((f32[15,32,256]{2,1,0:T(8,128)S(1)}, f32[15,32,256]{2,1,0:T(8,128)S(1)}, u32[]{:S(2)}, u32[]{:S(2)}) %collective-permute-start.13) | collective-permute-done | bytes 491552 | tf_op jit(solution)/shard_map/ppermute | solution.py:402
  98.1 1.8 %shard_map.67 = (f32[15,32,256]{2,1,0:T(8,128)S(1)}, f32[15,32,256]{2,1,0:T(8,128)S(1)}) custom-call(f32[31]{0:T(128)S(1)} %copy-done.5, f32[16,64,256]{2,1,0:T(8,128)S(1)} %get-tuple-element.42.obs_ref, f32[15,32,256]{2,1,0:T(8,128)S(1)} %get-tuple-element.58.refs_4_.refs_0_, f32[15,32,256]{2,1,0:T(8,128)S(1)} %get-tuple-element.59.refs_1_, ...), custom_call_target="tpu_custom_call" | custom-call | flops 1000000000 | bytes 3500000 | tf_op jit(solution)/shard_map/pallas_call | solution.py:318
  99.9 4.4 %collective-permute-start.17 = (f32[15,32,256]{2,1,0:T(8,128)S(1)}, f32[15,32,256]{2,1,0:T(8,128)S(1)}, u32[]{:S(2)}, u32[]{:S(2)}) collective-permute-start(f32[15,32,256]{2,1,0:T(8,128)S(1)} %get-tuple-element.64.refs_1_), channel_id=1, source_target_pairs={{0,1},{1,2},{2,3},{4,5},{5,6},{6,7},{8,9},{9,10},{10,11},{12,13},{... | collective-permute-start | bytes 1474568 | tf_op jit(solution)/shard_map/ppermute | solution.py:402
  104.3 1.3 collective-permute-start.18
  105.6 1.2 shard_map.68
  106.8 4.6 %collective-permute-start.22 = (f32[15,16,256]{2,1,0:T(8,128)S(1)}, f32[15,16,256]{2,1,0:T(8,128)S(1)}, u32[]{:S(2)}, u32[]{:S(2)}) collective-permute-start(f32[15,16,256]{2,1,0:T(8,128)S(1)} %get-tuple-element.67.refs_1_), channel_id=1, source_target_pairs={{0,1},{1,2},{2,3},{4,5},{5,6},{6,7},{8,9},{9,10},{10,11},{12,13},{... | collective-permute-start | bytes 737288 | tf_op jit(solution)/shard_map/ppermute | solution.py:402
  111.4 1.3 collective-permute-start.23
  112.7 1.1 shard_map.69.refs_4_.refs_1_
  113.8 2.1 %collective-permute-done.17.refs_2_ = f32[15,32,256]{2,1,0:T(8,128)S(1)} collective-permute-done((f32[15,32,256]{2,1,0:T(8,128)S(1)}, f32[15,32,256]{2,1,0:T(8,128)S(1)}, u32[]{:S(2)}, u32[]{:S(2)}) %collective-permute-start.17) | collective-permute-done | bytes 491552 | tf_op jit(solution)/shard_map/ppermute | solution.py:402
  115.9 4.4 %collective-permute-done.18.refs_3_ = f32[15,32,256]{2,1,0:T(8,128)S(1)} collective-permute-done((f32[15,32,256]{2,1,0:T(8,128)S(1)}, f32[15,32,256]{2,1,0:T(8,128)S(1)}, u32[]{:S(2)}, u32[]{:S(2)}) %collective-permute-start.18) | collective-permute-done | bytes 491552 | tf_op jit(solution)/shard_map/ppermute | solution.py:403
  120.3 1.7 %shard_map.70.refs_4_.refs_3_ = f32[16,32,256]{2,1,0:T(8,128)S(1)} custom-call(f32[31]{0:T(128)S(1)} %copy-done.5, f32[15,32,256]{2,1,0:T(8,128)S(1)} %get-tuple-element.63.refs_4_.refs_0_, f32[15,32,256]{2,1,0:T(8,128)S(1)} %get-tuple-element.64.refs_1_, f32[15,32,256]{2,1,0:T(8,128)S(1)} %collective-permute-done.17.refs_2_, ...), custom_call_target="tpu_custom_call" | custom-call | flops 1000000000 | bytes 3500000 | tf_op jit(solution)/shard_map/pallas_call | solution.py:343
  122.1 0.1 collective-permute-start.21
  122.2 0.8 collective-permute-done.23.refs_3_
  123.0 1.1 shard_map.71.refs_2_
  124.1 6.6 %collective-permute-done.21.refs_0_ = f32[16,32,256]{2,1,0:T(8,128)S(1)} collective-permute-done((f32[16,32,256]{2,1,0:T(8,128)S(1)}, f32[16,32,256]{2,1,0:T(8,128)S(1)}, u32[]{:S(2)}, u32[]{:S(2)}) %collective-permute-start.21) | collective-permute-done | bytes 524320 | tf_op jit(solution)/shard_map/ppermute | solution.py:409
  130.7 2.3 %shard_map.72 = f32[16,64,256]{2,1,0:T(8,128)} custom-call(f32[16,32,256]{2,1,0:T(8,128)S(1)} %collective-permute-done.21.refs_0_, f32[16,16,256]{2,1,0:T(8,128)S(1)} %shard_map.69.refs_4_.refs_1_, f32[16,16,256]{2,1,0:T(8,128)S(1)} %shard_map.71.refs_2_, f32[16,32,256]{2,1,0:T(8,128)S(1)} %shard_map.70.refs_4_.refs_3_, ...), custom_call_target="tpu_custom_call" | custom-call | flops 1000000000 | bytes 3500000 | tf_op jit(solution)/shard_map/pallas_call | solution.py:387
  (15 shorter events, 0.0 us)
Async XLA Ops:
  1.1 14.0 %collective-permute-start = (f32[16,32,256]{2,1,0:T(8,128)S(1)}, f32[16,32,256]{2,1,0:T(8,128)S(1)}, u32[]{:S(2)}, u32[]{:S(2)}) collective-permute-start(f32[16,32,256]{2,1,0:T(8,128)S(1)} %slice.3), channel_id=1, source_target_pairs={{0,12},{4,0},{8,4},{12,8},{1,13},{5,1},{9,5},{13,9},{2,14},{6,2},{... | collective-permute-start | bytes 1572872 | tf_op jit(solution)/shard_map/ppermute | solution.py:409
  3.5 1.2 copy-start
  4.7 0.7 copy-start.2
  5.4 0.7 copy-start.3
  6.1 0.7 copy-start.4
  9.2 15.1 %collective-permute-start.4 = (f32[15,32,256]{2,1,0:T(8,128)S(1)}, f32[15,32,256]{2,1,0:T(8,128)S(1)}, u32[]{:S(2)}, u32[]{:S(2)}) collective-permute-start(f32[15,32,256]{2,1,0:T(8,128)S(1)} %get-tuple-element.44.refs_0_), channel_id=1, source_target_pairs={{1,0},{2,1},{3,2},{5,4},{6,5},{7,6},{9,8},{10,9},{11,10},{13,12},{... | collective-permute-start | bytes 1474568 | tf_op jit(solution)/shard_map/ppermute | solution.py:403
  10.5 16.2 %collective-permute-start.3 = (f32[15,32,256]{2,1,0:T(8,128)S(1)}, f32[15,32,256]{2,1,0:T(8,128)S(1)}, u32[]{:S(2)}, u32[]{:S(2)}) collective-permute-start(f32[15,32,256]{2,1,0:T(8,128)S(1)} %get-tuple-element.45.refs_1_), channel_id=1, source_target_pairs={{0,1},{1,2},{2,3},{4,5},{5,6},{6,7},{8,9},{9,10},{10,11},{12,13},{... | collective-permute-start | bytes 1474568 | tf_op jit(solution)/shard_map/ppermute | solution.py:402
  15.1 5.9 %copy-start.5 = (f32[31]{0:T(128)S(1)}, f32[31]{0:T(128)}, u32[]{:S(2)}) copy-start(f32[31]{0:T(128)} %tz_ref.25) | copy-start | bytes 376
  16.2 21.0 %collective-permute-start.1 = (f32[15,32,256]{2,1,0:T(8,128)S(1)}, f32[15,32,256]{2,1,0:T(8,128)S(1)}, u32[]{:S(2)}, u32[]{:S(2)}) collective-permute-start(f32[15,32,256]{2,1,0:T(8,128)S(1)} %get-tuple-element.43.refs_1_), channel_id=1, source_target_pairs={{0,1},{1,2},{2,3},{4,5},{5,6},{6,7},{8,9},{9,10},{10,11},{12,13},{... | collective-permute-start | bytes 1474568 | tf_op jit(solution)/shard_map/ppermute | solution.py:402
  19.7 17.6 %collective-permute-start.2 = (f32[15,32,256]{2,1,0:T(8,128)S(1)}, f32[15,32,256]{2,1,0:T(8,128)S(1)}, u32[]{:S(2)}, u32[]{:S(2)}) collective-permute-start(f32[15,32,256]{2,1,0:T(8,128)S(1)} %get-tuple-element.41.after_ref.refs_4_.refs_0_), channel_id=1, source_target_pairs={{1,0},{2,1},{3,2},{5,4},{6,5},{7,6},{9,8},{10,9},{11,10},{13,12},{... | collective-permute-start | bytes 1474568 | tf_op jit(solution)/shard_map/ppermute | solution.py:403
  27.9 22.6 %collective-permute-start.7 = (f32[15,16,256]{2,1,0:T(8,128)S(1)}, f32[15,16,256]{2,1,0:T(8,128)S(1)}, u32[]{:S(2)}, u32[]{:S(2)}) collective-permute-start(f32[15,16,256]{2,1,0:T(8,128)S(1)} %get-tuple-element.49.refs_1_), channel_id=1, source_target_pairs={{0,1},{1,2},{2,3},{4,5},{5,6},{6,7},{8,9},{9,10},{10,11},{12,13},{... | collective-permute-start | bytes 737288 | tf_op jit(solution)/shard_map/ppermute | solution.py:402
  32.3 19.6 %collective-permute-start.8 = (f32[15,16,256]{2,1,0:T(8,128)S(1)}, f32[15,16,256]{2,1,0:T(8,128)S(1)}, u32[]{:S(2)}, u32[]{:S(2)}) collective-permute-start(f32[15,16,256]{2,1,0:T(8,128)S(1)} %get-tuple-element.46.refs_4_.refs_0_), channel_id=1, source_target_pairs={{1,0},{2,1},{3,2},{5,4},{6,5},{7,6},{9,8},{10,9},{11,10},{13,12},{... | collective-permute-start | bytes 737288 | tf_op jit(solution)/shard_map/ppermute | solution.py:403
  39.1 14.7 %collective-permute-start.5 = (f32[15,32,256]{2,1,0:T(8,128)S(1)}, f32[15,32,256]{2,1,0:T(8,128)S(1)}, u32[]{:S(2)}, u32[]{:S(2)}) collective-permute-start(f32[15,32,256]{2,1,0:T(8,128)S(1)} %get-tuple-element.48.refs_1_), channel_id=1, source_target_pairs={{0,1},{1,2},{2,3},{4,5},{5,6},{6,7},{8,9},{9,10},{10,11},{12,13},{... | collective-permute-start | bytes 1474568 | tf_op jit(solution)/shard_map/ppermute | solution.py:402
  43.5 13.8 %collective-permute-start.6 = (f32[15,32,256]{2,1,0:T(8,128)S(1)}, f32[15,32,256]{2,1,0:T(8,128)S(1)}, u32[]{:S(2)}, u32[]{:S(2)}) collective-permute-start(f32[15,32,256]{2,1,0:T(8,128)S(1)} %get-tuple-element.47.refs_4_.refs_0_), channel_id=1, source_target_pairs={{1,0},{2,1},{3,2},{5,4},{6,5},{7,6},{9,8},{10,9},{11,10},{13,12},{... | collective-permute-start | bytes 1474568 | tf_op jit(solution)/shard_map/ppermute | solution.py:403
  46.0 13.2 %collective-permute-start.10 = (f32[15,16,256]{2,1,0:T(8,128)S(1)}, f32[15,16,256]{2,1,0:T(8,128)S(1)}, u32[]{:S(2)}, u32[]{:S(2)}) collective-permute-start(f32[15,16,256]{2,1,0:T(8,128)S(1)} %get-tuple-element.51.refs_1_), channel_id=1, source_target_pairs={{0,1},{1,2},{2,3},{4,5},{5,6},{6,7},{8,9},{9,10},{10,11},{12,13},{... | collective-permute-start | bytes 737288 | tf_op jit(solution)/shard_map/ppermute | solution.py:402
  50.6 9.4 %collective-permute-start.11 = (f32[15,16,256]{2,1,0:T(8,128)S(1)}, f32[15,16,256]{2,1,0:T(8,128)S(1)}, u32[]{:S(2)}, u32[]{:S(2)}) collective-permute-start(f32[15,16,256]{2,1,0:T(8,128)S(1)} %get-tuple-element.50.refs_4_.refs_0_), channel_id=1, source_target_pairs={{1,0},{2,1},{3,2},{5,4},{6,5},{7,6},{9,8},{10,9},{11,10},{13,12},{... | collective-permute-start | bytes 737288 | tf_op jit(solution)/shard_map/ppermute | solution.py:403
  59.1 8.7 %copy-start.1 = (f32[16,64,256]{2,1,0:T(8,128)S(1)}, f32[16,64,256]{2,1,0:T(8,128)}, u32[]{:S(2)}) copy-start(f32[16,64,256]{2,1,0:T(8,128)} %refs_4_.1) | copy-start | bytes 3145732
  59.1 8.7 %collective-permute-start.9 = (f32[16,32,256]{2,1,0:T(8,128)S(1)}, f32[16,32,256]{2,1,0:T(8,128)S(1)}, u32[]{:S(2)}, u32[]{:S(2)}) collective-permute-start(f32[16,32,256]{2,1,0:T(8,128)S(1)} %shard_map.62.refs_4_.refs_3_), channel_id=1, source_target_pairs={{0,4},{4,8},{8,12},{12,0},{1,5},{5,9},{9,13},{13,1},{2,6},{6,10},{... | collective-permute-start | bytes 1572872 | tf_op jit(solution)/shard_map/ppermute | solution.py:409
  70.1 6.7 %collective-permute-start.12 = (f32[16,32,256]{2,1,0:T(8,128)S(1)}, f32[16,32,256]{2,1,0:T(8,128)S(1)}, u32[]{:S(2)}, u32[]{:S(2)}) collective-permute-start(f32[16,32,256]{2,1,0:T(8,128)S(1)} %get-tuple-element.57), channel_id=1, source_target_pairs={{0,12},{4,0},{8,4},{12,8},{1,13},{5,1},{9,5},{13,9},{2,14},{6,2},{... | collective-permute-start | bytes 1572872 | tf_op jit(solution)/shard_map/ppermute | solution.py:409
  70.1 15.5 %collective-permute-start.16 = (f32[15,32,256]{2,1,0:T(8,128)S(1)}, f32[15,32,256]{2,1,0:T(8,128)S(1)}, u32[]{:S(2)}, u32[]{:S(2)}) collective-permute-start(f32[15,32,256]{2,1,0:T(8,128)S(1)} %get-tuple-element.60.refs_0_), channel_id=1, source_target_pairs={{1,0},{2,1},{3,2},{5,4},{6,5},{7,6},{9,8},{10,9},{11,10},{13,12},{... | collective-permute-start | bytes 1474568 | tf_op jit(solution)/shard_map/ppermute | solution.py:403
  71.4 16.1 %collective-permute-start.15 = (f32[15,32,256]{2,1,0:T(8,128)S(1)}, f32[15,32,256]{2,1,0:T(8,128)S(1)}, u32[]{:S(2)}, u32[]{:S(2)}) collective-permute-start(f32[15,32,256]{2,1,0:T(8,128)S(1)} %get-tuple-element.61.refs_1_), channel_id=1, source_target_pairs={{0,1},{1,2},{2,3},{4,5},{5,6},{6,7},{8,9},{9,10},{10,11},{12,13},{... | collective-permute-start | bytes 1474568 | tf_op jit(solution)/shard_map/ppermute | solution.py:402
  77.2 20.8 %collective-permute-start.13 = (f32[15,32,256]{2,1,0:T(8,128)S(1)}, f32[15,32,256]{2,1,0:T(8,128)S(1)}, u32[]{:S(2)}, u32[]{:S(2)}) collective-permute-start(f32[15,32,256]{2,1,0:T(8,128)S(1)} %get-tuple-element.59.refs_1_), channel_id=1, source_target_pairs={{0,1},{1,2},{2,3},{4,5},{5,6},{6,7},{8,9},{9,10},{10,11},{12,13},{... | collective-permute-start | bytes 1474568 | tf_op jit(solution)/shard_map/ppermute | solution.py:402
  80.9 17.2 %collective-permute-start.14 = (f32[15,32,256]{2,1,0:T(8,128)S(1)}, f32[15,32,256]{2,1,0:T(8,128)S(1)}, u32[]{:S(2)}, u32[]{:S(2)}) collective-permute-start(f32[15,32,256]{2,1,0:T(8,128)S(1)} %get-tuple-element.58.refs_4_.refs_0_), channel_id=1, source_target_pairs={{1,0},{2,1},{3,2},{5,4},{6,5},{7,6},{9,8},{10,9},{11,10},{13,12},{... | collective-permute-start | bytes 1474568 | tf_op jit(solution)/shard_map/ppermute | solution.py:403
  88.7 22.7 %collective-permute-start.19 = (f32[15,16,256]{2,1,0:T(8,128)S(1)}, f32[15,16,256]{2,1,0:T(8,128)S(1)}, u32[]{:S(2)}, u32[]{:S(2)}) collective-permute-start(f32[15,16,256]{2,1,0:T(8,128)S(1)} %get-tuple-element.65.refs_1_), channel_id=1, source_target_pairs={{0,1},{1,2},{2,3},{4,5},{5,6},{6,7},{8,9},{9,10},{10,11},{12,13},{... | collective-permute-start | bytes 737288 | tf_op jit(solution)/shard_map/ppermute | solution.py:402
  93.1 19.6 %collective-permute-start.20 = (f32[15,16,256]{2,1,0:T(8,128)S(1)}, f32[15,16,256]{2,1,0:T(8,128)S(1)}, u32[]{:S(2)}, u32[]{:S(2)}) collective-permute-start(f32[15,16,256]{2,1,0:T(8,128)S(1)} %get-tuple-element.62.refs_4_.refs_0_), channel_id=1, source_target_pairs={{1,0},{2,1},{3,2},{5,4},{6,5},{7,6},{9,8},{10,9},{11,10},{13,12},{... | collective-permute-start | bytes 737288 | tf_op jit(solution)/shard_map/ppermute | solution.py:403
  99.9 16.1 %collective-permute-start.17 = (f32[15,32,256]{2,1,0:T(8,128)S(1)}, f32[15,32,256]{2,1,0:T(8,128)S(1)}, u32[]{:S(2)}, u32[]{:S(2)}) collective-permute-start(f32[15,32,256]{2,1,0:T(8,128)S(1)} %get-tuple-element.64.refs_1_), channel_id=1, source_target_pairs={{0,1},{1,2},{2,3},{4,5},{5,6},{6,7},{8,9},{9,10},{10,11},{12,13},{... | collective-permute-start | bytes 1474568 | tf_op jit(solution)/shard_map/ppermute | solution.py:402
  104.3 16.0 %collective-permute-start.18 = (f32[15,32,256]{2,1,0:T(8,128)S(1)}, f32[15,32,256]{2,1,0:T(8,128)S(1)}, u32[]{:S(2)}, u32[]{:S(2)}) collective-permute-start(f32[15,32,256]{2,1,0:T(8,128)S(1)} %get-tuple-element.63.refs_4_.refs_0_), channel_id=1, source_target_pairs={{1,0},{2,1},{3,2},{5,4},{6,5},{7,6},{9,8},{10,9},{11,10},{13,12},{... | collective-permute-start | bytes 1474568 | tf_op jit(solution)/shard_map/ppermute | solution.py:403
  106.8 15.3 %collective-permute-start.22 = (f32[15,16,256]{2,1,0:T(8,128)S(1)}, f32[15,16,256]{2,1,0:T(8,128)S(1)}, u32[]{:S(2)}, u32[]{:S(2)}) collective-permute-start(f32[15,16,256]{2,1,0:T(8,128)S(1)} %get-tuple-element.67.refs_1_), channel_id=1, source_target_pairs={{0,1},{1,2},{2,3},{4,5},{5,6},{6,7},{8,9},{9,10},{10,11},{12,13},{... | collective-permute-start | bytes 737288 | tf_op jit(solution)/shard_map/ppermute | solution.py:402
  111.4 11.6 %collective-permute-start.23 = (f32[15,16,256]{2,1,0:T(8,128)S(1)}, f32[15,16,256]{2,1,0:T(8,128)S(1)}, u32[]{:S(2)}, u32[]{:S(2)}) collective-permute-start(f32[15,16,256]{2,1,0:T(8,128)S(1)} %get-tuple-element.66.refs_4_.refs_0_), channel_id=1, source_target_pairs={{1,0},{2,1},{3,2},{5,4},{6,5},{7,6},{9,8},{10,9},{11,10},{13,12},{... | collective-permute-start | bytes 737288 | tf_op jit(solution)/shard_map/ppermute | solution.py:403
  122.1 8.7 %collective-permute-start.21 = (f32[16,32,256]{2,1,0:T(8,128)S(1)}, f32[16,32,256]{2,1,0:T(8,128)S(1)}, u32[]{:S(2)}, u32[]{:S(2)}) collective-permute-start(f32[16,32,256]{2,1,0:T(8,128)S(1)} %shard_map.70.refs_4_.refs_3_), channel_id=1, source_target_pairs={{0,4},{4,8},{8,12},{12,0},{1,5},{5,9},{9,13},{13,1},{2,6},{6,10},{... | collective-permute-start | bytes 1572872 | tf_op jit(solution)/shard_map/ppermute | solution.py:409

commit v6 on v5

--- a/solution.py
+++ b/solution.py
@@ -129,7 +129,7 @@
 
 def first_kernel(
     n, radius, band_hbm, tx_hbm, ty_hbm, est_hbm,
-    ah_ref, al_ref, wx_ref, w_ref, low_ref, high_ref,
+    ah_ref, al_ref, wx_ref, w_ref,
     band_ref, tx_ref, ty_ref, est_ref, sems,
 ):
     pairs = ((band_hbm, band_ref), (tx_hbm, tx_ref), (ty_hbm, ty_ref), (est_hbm, est_ref))
@@ -149,15 +149,13 @@
         matrix = row_matrix(spread(tx_ref, band, wide, radius, False), rows, 0, width)
         wx_ref[p, 0], wx_ref[p, 1] = split(jnp.where(keep, matrix, 0.0))
     all_columns(lambda p: est_ref[p], (ah_ref, al_ref), w_ref)
-    own_rows(w_ref, wx_ref, low_ref, high_ref)
-
-
-def first_blur(band_index, taps_x, taps_y, est, halo, width):
+
+
+def first_blur(band_index, taps_x, taps_y, est, width):
     n, rows, columns = est.shape
     radius = taps_x.shape[1] // 2
     a = shape_of(n, columns, columns, dtype=BF16)
     w = shape_of(n, 2, rows, width, dtype=BF16)
-    send = shape_of(radius, rows - halo, columns)
     return pl.pallas_call(
         functools.partial(first_kernel, n, radius),
         in_specs=[pl.BlockSpec(memory_space=pltpu.HBM)] * 4,
@@ -168,8 +166,8 @@
             pltpu.VMEM(est.shape, F32),
             pltpu.SemaphoreType.DMA((4,)),
         ],
-        out_specs=[VMEM] * 6,
-        out_shape=[a, a, w, shape_of(*est.shape), send, send],
+        out_specs=[VMEM] * 4,
+        out_shape=[a, a, w, shape_of(*est.shape)],
         compiler_params=PARAMS,
         cost_estimate=cost(1.0),
     )(band_index, taps_x, taps_y, est)
@@ -231,6 +229,23 @@
     )(band_index, taps_x, taps_y, taps_z, after, obs, beyond)
 
 
+def inner_kernel(w_ref, wx_ref, after_ref, low_ref, high_ref):
+    own_rows(w_ref, wx_ref, low_ref, high_ref)
+
+
+def inner_blur(w, wx, halo, radius, after):
+    _, rows, columns = w.shape
+    send = shape_of(radius, rows - halo, columns)
+    return pl.pallas_call(
+        inner_kernel,
+        in_specs=[VMEM] * 2 + [ANY],
+        out_specs=[VMEM] * 2,
+        out_shape=[send] * 2,
+        compiler_params=PARAMS,
+        cost_estimate=cost(1.0),
+    )(w, wx, after)
+
+
 def edge_kernel(n, radius, blurred, w_ref, next_ref, wx_ref, *refs):
     rows, halo = w_ref.shape[1], next_ref.shape[1]
     inner, used = rows - halo, rows + halo
@@ -293,15 +308,15 @@
     return pl.ds(pl.multiple_of(start + offset, 8), 8)
 
 
-def ratio_kernel(n, radius, skip, obs_skip, tz_ref, obs_ref, *refs):
+def ratio_kernel(n, radius, skip, tz_ref, obs_ref, *refs):
     rlow_ref, rhigh_ref = refs[-2:]
     _, count, columns = rlow_ref.shape
 
     def body(start, lanes):
-        total = depth_sum(n, radius, False, tz_ref, refs[:4], at(start, skip), lanes)
         rows = at(start, 0)
+        total = depth_sum(n, radius, False, tz_ref, refs[:4], rows, lanes)
         for i in range(n):
-            ratio = obs_ref[i, at(start, obs_skip), lanes] / total[i]
+            ratio = obs_ref[i, at(start, skip), lanes] / total[i]
             if i < radius:
                 rlow_ref[i, rows, lanes] = ratio
             if i >= n - radius:
@@ -310,19 +325,18 @@
     tiles(count, columns, body)
 
 
-def depth_ratio(taps_z, obs, chunk, skip, obs_skip, count, after=None, micro=1.0):
+def depth_ratio(taps_z, obs, chunk, skip, count, after, micro=1.0):
     n, _, columns = obs.shape
     radius = taps_z.shape[0] // 2
     send = shape_of(radius, count, columns)
-    extra = [] if after is None else [after]
-    return pl.pallas_call(
-        functools.partial(ratio_kernel, n, radius, skip, obs_skip),
-        in_specs=[SMEM] + [VMEM] * 5 + [ANY] * len(extra),
+    return pl.pallas_call(
+        functools.partial(ratio_kernel, n, radius, skip),
+        in_specs=[SMEM] + [VMEM] * 5 + [ANY],
         out_specs=[VMEM] * 2,
         out_shape=[send] * 2,
         compiler_params=PARAMS,
         cost_estimate=cost(micro),
-    )(taps_z, obs, *chunk, *extra)
+    )(taps_z, obs, *chunk, after)
 
 
 def back_kernel(n, radius, tz_ref, *refs):
@@ -351,7 +365,7 @@
 
 
 def update_kernel(n, last, *refs):
-    pieces, edge_ref, refs = refs[:4], refs[3], refs[4:]
+    pieces, edge_ref, refs = refs[:3], refs[2], refs[3:]
     est_ref, rn_ref, wa_ref, bh_ref, bl_ref = refs[:5]
     refs = refs[5:]
     rows = est_ref.shape[1]
@@ -414,43 +428,43 @@
     radius = taps_z.shape[0] // 2
     halo = up(2 * radius, 16)
     inner = rows - halo
-    half = up(inner // 2, 16)
     width = up(rows + halo, 128)
     beyond = ring(observed[:, :halo], -1)
-    ah, al, wx, w, low, high = first_blur(
-        band_index, taps_x, taps_y, observed, halo, width
-    )
+    ah, al, wx, w = first_blur(band_index, taps_x, taps_y, observed, width)
     est, adjoint = observed, None
     for step in range(ITERS):
-        v_inner = depth_exchange(low, high)
-        low, high = edge_blur(w, beyond, wx, () if step else (ah, al), radius)
-        v_edge = depth_exchange(low, high)
-        if adjoint is None:
+        if step:
+            v_inner = depth_exchange(*inner_sends)
+            edge_sends = edge_blur(w, beyond, wx, (), radius)
+            v_edge = depth_exchange(*edge_sends)
+            after = edge_sends[0]
+        else:
+            edge_sends = edge_blur(w, beyond, wx, (ah, al), radius)
+            v_edge = depth_exchange(*edge_sends)
+            inner_sends = inner_blur(w, wx, halo, radius, edge_sends[0])
+            v_inner = depth_exchange(*inner_sends)
             bh, bl, wa, rn, shifted = second_weights(
-                band_index, taps_x, taps_y, taps_z, low, observed, beyond, width
+                band_index, taps_x, taps_y, taps_z, inner_sends[0], observed, beyond, width
             )
             adjoint = (wa, bh, bl)
-        r_first = depth_exchange(
-            *depth_ratio(taps_z, shifted, v_inner, 0, 0, half, after=low)
+            after = inner_sends[0]
+        r_edge = depth_exchange(
+            *depth_ratio(taps_z, shifted, v_edge, inner, halo, after)
         )
-        r_edge = depth_exchange(*depth_ratio(taps_z, shifted, v_edge, 0, inner, halo, after=r_first[0]))
-        r_second = depth_exchange(
-            *depth_ratio(
-                taps_z, shifted, v_inner, half, half, inner - half, after=r_edge[0]
-            )
+        r_inner = depth_exchange(
+            *depth_ratio(taps_z, shifted, v_inner, 0, inner, r_edge[0])
         )
-        c_first = depth_back(taps_z, r_first, n, after=r_second[0], micro=5.0)
-        c_edge = depth_back(taps_z, r_edge, n, after=c_first, micro=1.0)
+        c_edge = depth_back(taps_z, r_edge, n, r_inner[0])
         before = ring(c_edge, 1)
-        c_second = depth_back(taps_z, r_second, n, after=c_edge, micro=100.0)
+        c_inner = depth_back(taps_z, r_inner, n, c_edge, 100.0)
         last = step == ITERS - 1
         out = update(
-            (before, c_first, c_second, c_edge), est, rn, adjoint,
+            (before, c_inner, c_edge), est, rn, adjoint,
             None if last else (wx, ah, al), radius,
         )
         est = out[0]
         if not last:
-            w, top, low, high = out[1:]
+            w, top, *inner_sends = out[1:]
             beyond = ring(top, -1)
     return est
 

time: 134 us -> 127 us (0.948)
  starting transfers between devices: 58.6 us -> 46.7 us
  waiting for transfers between devices: 42.1 us -> 49.6 us
  Pallas kernels: 27.7 us -> 25.7 us
    ppermute x10 -> x8, starting transfers between devices: 43.1 us -> 33.2 us  [depth_exchange(): zlo = lax.ppermute(high, 'slab', forward)]
    ppermute x10 -> x8, waiting for transfers between devices: 13.5 us -> 22.2 us  [depth_exchange(): zhi = lax.ppermute(low, 'slab', backward)]
    ppermute x4, waiting for transfers between devices: 14.1 us -> 7.89 us  [ring(): lax.ppermute(x, 'row', [(i, (i + step) % count) for i in range(count)])]
    ppermute x10 -> x8, waiting for transfers between devices: 14.5 us -> 19.5 us  [depth_exchange(): zlo = lax.ppermute(high, 'slab', forward)]
    ppermute x10 -> x8, starting transfers between devices: 12.9 us -> 10.3 us  [depth_exchange(): zhi = lax.ppermute(low, 'slab', backward)]
    pallas_call x6 -> x4, Pallas kernels: 8.05 us -> 6.98 us  [depth_back(): pl.pallas_call(functools.partial(back_kernel, n, radius), in_specs=[SMEM]...]
    pallas_call x6 -> x5, Pallas kernels: 8.35 us -> 7.65 us  [the longest x4 7.3 us: depth_ratio(): pl.pallas_call(functools.partial(ratio_kernel, n, radius, skip), in_specs...]
  transfers between devices with their start and end apart: 24 -> 20, of which waited for: 15 -> 14; matrix products, arithmetic and copies ran while one was open for 0% -> 0% of each run, Pallas kernels for 17% -> 15%
where the time goes in v6:
time: 127 us
  waiting for transfers between devices  49.6 us (39%)
  starting transfers between devices  46.7 us (37%)
  Pallas kernels  25.7 us (20%)
  local copies, waits for them, and re-layouts  4.36 us (3%)
    ppermute x8, starting transfers between devices, depth_exchange(): zlo = lax.ppermute(high, 'slab', forward)  33.2 us
    ppermute x8, waiting for transfers between devices, depth_exchange(): zhi = lax.ppermute(low, 'slab', backward)  22.2 us
    ppermute x8, waiting for transfers between devices, depth_exchange(): zlo = lax.ppermute(high, 'slab', forward)  19.5 us
    ppermute x8, starting transfers between devices, depth_exchange(): zhi = lax.ppermute(low, 'slab', backward)  10.3 us
    ppermute x4, waiting for transfers between devices, ring(): lax.ppermute(x, 'row', [(i, (i + step) % count) for i in range(count)])  7.89 us
    pallas_call x4, Pallas kernels, depth_ratio(): pl.pallas_call(functools.partial(ratio_kernel, n, radius, skip), in_specs...  7.3 us
    pallas_call x4, Pallas kernels, depth_back(): pl.pallas_call(functools.partial(back_kernel, n, radius), in_specs=[SMEM]...  6.98 us
    pallas_call x2, Pallas kernels, update(): pl.pallas_call(functools.partial(update_kernel, n, last), in_specs=[VMEM]...  4.56 us
  transfers between devices with their start and end apart: 20, of which 14 were waited for; matrix products, arithmetic and copies ran while one was open for 0% of the time, Pallas kernels for 15%

profile of v6, /device:TPU:0, one launch (start us, length us, event | category | flops | bytes accessed | tf_op | source)
XLA Modules:
  0.0 126.6 jit_solution(4586955888525602950)
XLA Ops:
  0.0 1.1 slice.3
  1.1 2.4 %collective-permute-start = (f32[16,32,256]{2,1,0:T(8,128)S(1)}, f32[16,32,256]{2,1,0:T(8,128)S(1)}, u32[]{:S(2)}, u32[]{:S(2)}) collective-permute-start(f32[16,32,256]{2,1,0:T(8,128)S(1)} %slice.3), channel_id=1, source_target_pairs={{0,12},{4,0},{8,4},{12,8},{1,13},{5,1},{9,5},{13,9},{2,14},{6,2},{... | collective-permute-start | bytes 1572872 | tf_op jit(solution)/shard_map/ppermute | solution.py:423
  3.5 0.0 copy-start
  3.5 1.2 copy-done
  4.7 0.7 copy-done.2
  5.4 0.7 copy-done.3
  6.1 0.7 copy-done.4
  6.8 2.2 %shard_map.55 = (bf16[16,256,256]{2,1,0:T(8,128)(2,1)S(1)}, bf16[16,256,256]{2,1,0:T(8,128)(2,1)S(1)}, bf16[16,2,64,128]{3,2,1,0:T(8,128)(2,1)S(1)}, f32[16,64,256]{2,1,0:T(8,128)S(1)}) custom-call(s32[16]{0:T(128)S(1)} %copy-done.4, f32[16,31]{1,0:T(8,128)S(1)} %copy-done.2, f32[16,31]{1,0:T(8,128)S(1)} %copy-done.3, f32[16,64,256]{2,1,0:T(8,128)S(1)} %copy-done), custom_call_target="tpu_custom_call" | custom-call | flops 1000000000 | bytes 3500000 | tf_op jit(solution)/shard_map/pallas_call | solution.py:159
  9.0 1.2 collective-permute-done.next_ref
  10.2 1.1 shard_map.56
  11.3 0.0 copy-start.5
  11.3 3.6 %collective-permute-start.1 = (f32[15,32,256]{2,1,0:T(8,128)S(1)}, f32[15,32,256]{2,1,0:T(8,128)S(1)}, u32[]{:S(2)}, u32[]{:S(2)}) collective-permute-start(f32[15,32,256]{2,1,0:T(8,128)S(1)} %get-tuple-element.40.refs_1_), channel_id=1, source_target_pairs={{0,1},{1,2},{2,3},{4,5},{5,6},{6,7},{8,9},{9,10},{10,11},{12,13},{... | collective-permute-start | bytes 1474568 | tf_op jit(solution)/shard_map/ppermute | solution.py:416
  15.0 1.3 %collective-permute-start.2 = (f32[15,32,256]{2,1,0:T(8,128)S(1)}, f32[15,32,256]{2,1,0:T(8,128)S(1)}, u32[]{:S(2)}, u32[]{:S(2)}) collective-permute-start(f32[15,32,256]{2,1,0:T(8,128)S(1)} %get-tuple-element.37.after_ref.refs_0_), channel_id=1, source_target_pairs={{1,0},{2,1},{3,2},{5,4},{6,5},{7,6},{9,8},{10,9},{11,10},{13,12},{... | collective-permute-start | bytes 1474568 | tf_op jit(solution)/shard_map/ppermute | solution.py:417
  16.3 0.3 shard_map.57
  16.6 4.6 %collective-permute-start.5 = (f32[15,32,256]{2,1,0:T(8,128)S(1)}, f32[15,32,256]{2,1,0:T(8,128)S(1)}, u32[]{:S(2)}, u32[]{:S(2)}) collective-permute-start(f32[15,32,256]{2,1,0:T(8,128)S(1)} %get-tuple-element.43.refs_1_), channel_id=1, source_target_pairs={{0,1},{1,2},{2,3},{4,5},{5,6},{6,7},{8,9},{9,10},{10,11},{12,13},{... | collective-permute-start | bytes 1474568 | tf_op jit(solution)/shard_map/ppermute | solution.py:416
  21.2 1.3 %collective-permute-start.6 = (f32[15,32,256]{2,1,0:T(8,128)S(1)}, f32[15,32,256]{2,1,0:T(8,128)S(1)}, u32[]{:S(2)}, u32[]{:S(2)}) collective-permute-start(f32[15,32,256]{2,1,0:T(8,128)S(1)} %get-tuple-element.38.after_ref.refs_4_.refs_0_), channel_id=1, source_target_pairs={{1,0},{2,1},{3,2},{5,4},{6,5},{7,6},{9,8},{10,9},{11,10},{13,12},{... | collective-permute-start | bytes 1474568 | tf_op jit(solution)/shard_map/ppermute | solution.py:417
  22.5 0.0 copy-done.1
  22.5 0.0 copy-done.5
  22.5 2.8 %shard_map.58 = (bf16[16,256,256]{2,1,0:T(8,128)(2,1)S(1)}, bf16[16,256,256]{2,1,0:T(8,128)(2,1)S(1)}, bf16[16,2,64,128]{3,2,1,0:T(8,128)(2,1)S(1)}, f32[16,64,256]{2,1,0:T(8,128)S(1)}, f32[16,64,256]{2,1,0:T(8,128)S(1)}) custom-call(s32[16]{0:T(128)S(1)} %copy-done.4, f32[16,31]{1,0:T(8,128)S(1)} %copy-done.2, f32[16,31]{1,0:T(8,128)S(1)} %copy-done.3, ...), custom_call_target="tpu_custom_call" | custom-call | flops 1000000000 | bytes 3500000 | tf_op jit(solution)/shard_map/pallas_call | solution.py:222
  25.3 1.2 collective-permute-done.1.refs_2_
  26.5 4.3 %collective-permute-done.2.refs_3_ = f32[15,32,256]{2,1,0:T(8,128)S(1)} collective-permute-done((f32[15,32,256]{2,1,0:T(8,128)S(1)}, f32[15,32,256]{2,1,0:T(8,128)S(1)}, u32[]{:S(2)}, u32[]{:S(2)}) %collective-permute-start.2) | collective-permute-done | bytes 491552 | tf_op jit(solution)/shard_map/ppermute | solution.py:417
  30.9 1.8 %shard_map.59 = (f32[15,32,256]{2,1,0:T(8,128)S(1)}, f32[15,32,256]{2,1,0:T(8,128)S(1)}) custom-call(f32[31]{0:T(128)S(1)} %copy-done.5, f32[16,64,256]{2,1,0:T(8,128)S(1)} %get-tuple-element.39.obs_ref, f32[15,32,256]{2,1,0:T(8,128)S(1)} %get-tuple-element.37.after_ref.refs_0_, f32[15,32,256]{2,1,0:T(8,128)S(1)} %get-tuple-element.40.refs_1_, ...), custom_call_target="tpu_custom_call" | custom-call | flops 1000000000 | bytes 3500000 | tf_op jit(solution)/shard_map/pallas_call | solution.py:332
  32.7 3.5 %collective-permute-start.3 = (f32[15,32,256]{2,1,0:T(8,128)S(1)}, f32[15,32,256]{2,1,0:T(8,128)S(1)}, u32[]{:S(2)}, u32[]{:S(2)}) collective-permute-start(f32[15,32,256]{2,1,0:T(8,128)S(1)} %get-tuple-element.42.refs_1_), channel_id=1, source_target_pairs={{0,1},{1,2},{2,3},{4,5},{5,6},{6,7},{8,9},{9,10},{10,11},{12,13},{... | collective-permute-start | bytes 1474568 | tf_op jit(solution)/shard_map/ppermute | solution.py:416
  36.2 1.3 %collective-permute-start.4 = (f32[15,32,256]{2,1,0:T(8,128)S(1)}, f32[15,32,256]{2,1,0:T(8,128)S(1)}, u32[]{:S(2)}, u32[]{:S(2)}) collective-permute-start(f32[15,32,256]{2,1,0:T(8,128)S(1)} %get-tuple-element.41.refs_4_.refs_0_), channel_id=1, source_target_pairs={{1,0},{2,1},{3,2},{5,4},{6,5},{7,6},{9,8},{10,9},{11,10},{13,12},{... | collective-permute-start | bytes 1474568 | tf_op jit(solution)/shard_map/ppermute | solution.py:417
  37.5 0.0 collective-permute-done.5.refs_2_
  37.5 3.9 %collective-permute-done.6.refs_3_ = f32[15,32,256]{2,1,0:T(8,128)S(1)} collective-permute-done((f32[15,32,256]{2,1,0:T(8,128)S(1)}, f32[15,32,256]{2,1,0:T(8,128)S(1)}, u32[]{:S(2)}, u32[]{:S(2)}) %collective-permute-start.6) | collective-permute-done | bytes 491552 | tf_op jit(solution)/shard_map/ppermute | solution.py:417
  41.4 1.8 %shard_map.60 = (f32[15,32,256]{2,1,0:T(8,128)S(1)}, f32[15,32,256]{2,1,0:T(8,128)S(1)}) custom-call(f32[31]{0:T(128)S(1)} %copy-done.5, f32[16,64,256]{2,1,0:T(8,128)S(1)} %get-tuple-element.39.obs_ref, f32[15,32,256]{2,1,0:T(8,128)S(1)} %get-tuple-element.38.after_ref.refs_4_.refs_0_, f32[15,32,256]{2,1,0:T(8,128)S(1)} %get-tuple-element.43.refs_1_, ...), custom_call_target="tpu_custom_call" | custom-call | flops 1000000000 | bytes 3500000 | tf_op jit(solution)/shard_map/pallas_call | solution.py:332
  43.2 3.5 %collective-permute-start.8 = (f32[15,32,256]{2,1,0:T(8,128)S(1)}, f32[15,32,256]{2,1,0:T(8,128)S(1)}, u32[]{:S(2)}, u32[]{:S(2)}) collective-permute-start(f32[15,32,256]{2,1,0:T(8,128)S(1)} %get-tuple-element.45.refs_1_), channel_id=1, source_target_pairs={{0,1},{1,2},{2,3},{4,5},{5,6},{6,7},{8,9},{9,10},{10,11},{12,13},{... | collective-permute-start | bytes 1474568 | tf_op jit(solution)/shard_map/ppermute | solution.py:416
  46.7 1.3 %collective-permute-start.9 = (f32[15,32,256]{2,1,0:T(8,128)S(1)}, f32[15,32,256]{2,1,0:T(8,128)S(1)}, u32[]{:S(2)}, u32[]{:S(2)}) collective-permute-start(f32[15,32,256]{2,1,0:T(8,128)S(1)} %get-tuple-element.44.refs_4_.refs_0_), channel_id=1, source_target_pairs={{1,0},{2,1},{3,2},{5,4},{6,5},{7,6},{9,8},{10,9},{11,10},{13,12},{... | collective-permute-start | bytes 1474568 | tf_op jit(solution)/shard_map/ppermute | solution.py:417
  48.0 0.0 collective-permute-done.3.refs_2_
  48.0 4.2 %collective-permute-done.4.refs_3_ = f32[15,32,256]{2,1,0:T(8,128)S(1)} collective-permute-done((f32[15,32,256]{2,1,0:T(8,128)S(1)}, f32[15,32,256]{2,1,0:T(8,128)S(1)}, u32[]{:S(2)}, u32[]{:S(2)}) %collective-permute-start.4) | collective-permute-done | bytes 491552 | tf_op jit(solution)/shard_map/ppermute | solution.py:417
  52.3 1.7 %shard_map.61.refs_4_.refs_2_ = f32[16,32,256]{2,1,0:T(8,128)S(1)} custom-call(f32[31]{0:T(128)S(1)} %copy-done.5, f32[15,32,256]{2,1,0:T(8,128)S(1)} %get-tuple-element.41.refs_4_.refs_0_, f32[15,32,256]{2,1,0:T(8,128)S(1)} %get-tuple-element.42.refs_1_, f32[15,32,256]{2,1,0:T(8,128)S(1)} %collective-permute-done.3.refs_2_, ...), custom_call_target="tpu_custom_call" | custom-call | flops 1000000000 | bytes 3500000 | tf_op jit(solution)/shard_map/pallas_call | solution.py:357
  54.0 0.1 collective-permute-start.7
  54.1 3.9 %collective-permute-done.8.refs_2_ = f32[15,32,256]{2,1,0:T(8,128)S(1)} collective-permute-done((f32[15,32,256]{2,1,0:T(8,128)S(1)}, f32[15,32,256]{2,1,0:T(8,128)S(1)}, u32[]{:S(2)}, u32[]{:S(2)}) %collective-permute-start.8) | collective-permute-done | bytes 491552 | tf_op jit(solution)/shard_map/ppermute | solution.py:416
  58.0 4.1 %collective-permute-done.9.refs_3_ = f32[15,32,256]{2,1,0:T(8,128)S(1)} collective-permute-done((f32[15,32,256]{2,1,0:T(8,128)S(1)}, f32[15,32,256]{2,1,0:T(8,128)S(1)}, u32[]{:S(2)}, u32[]{:S(2)}) %collective-permute-start.9) | collective-permute-done | bytes 491552 | tf_op jit(solution)/shard_map/ppermute | solution.py:417
  62.2 1.8 %shard_map.62.refs_1_ = f32[16,32,256]{2,1,0:T(8,128)S(1)} custom-call(f32[31]{0:T(128)S(1)} %copy-done.5, f32[15,32,256]{2,1,0:T(8,128)S(1)} %get-tuple-element.44.refs_4_.refs_0_, f32[15,32,256]{2,1,0:T(8,128)S(1)} %get-tuple-element.45.refs_1_, f32[15,32,256]{2,1,0:T(8,128)S(1)} %collective-permute-done.8.refs_2_, ...), custom_call_target="tpu_custom_call" | custom-call | flops 99999997952 | bytes 350000000 | tf_op jit(solution)/shard_map/pallas_call | solution.py:357
  63.9 0.0 collective-permute-done.7.refs_0_
  63.9 2.3 %shard_map.63 = (f32[16,64,256]{2,1,0:T(8,128)S(1)}, f32[16,64,256]{2,1,0:T(8,128)S(1)}, f32[16,32,256]{2,1,0:T(8,128)S(1)}, f32[15,32,256]{2,1,0:T(8,128)S(1)}, f32[15,32,256]{2,1,0:T(8,128)S(1)}) custom-call(f32[16,32,256]{2,1,0:T(8,128)S(1)} %collective-permute-done.7.refs_0_, f32[16,32,256]{2,1,0:T(8,128)S(1)} %shard_map.62.refs_1_, ...), custom_call_target="tpu_custom_call" | custom-call | flops 1000000000 | bytes 3500000 | tf_op jit(solution)/shard_map/pallas_call | solution.py:401
  66.2 0.6 collective-permute-start.10
  66.9 6.7 %collective-permute-done.10.next_ref = f32[16,32,256]{2,1,0:T(8,128)S(1)} collective-permute-done((f32[16,32,256]{2,1,0:T(8,128)S(1)}, f32[16,32,256]{2,1,0:T(8,128)S(1)}, u32[]{:S(2)}, u32[]{:S(2)}) %collective-permute-start.10) | collective-permute-done | bytes 524320 | tf_op jit(solution)/shard_map/ppermute | solution.py:423
  73.6 0.4 shard_map.64
  74.0 1.3 %collective-permute-start.12 = (f32[15,32,256]{2,1,0:T(8,128)S(1)}, f32[15,32,256]{2,1,0:T(8,128)S(1)}, u32[]{:S(2)}, u32[]{:S(2)}) collective-permute-start(f32[15,32,256]{2,1,0:T(8,128)S(1)} %get-tuple-element.52.refs_0_.refs_4_), channel_id=1, source_target_pairs={{1,0},{2,1},{3,2},{5,4},{6,5},{7,6},{9,8},{10,9},{11,10},{13,12},{... | collective-permute-start | bytes 1474568 | tf_op jit(solution)/shard_map/ppermute | solution.py:417
  75.3 4.6 %collective-permute-start.11 = (f32[15,32,256]{2,1,0:T(8,128)S(1)}, f32[15,32,256]{2,1,0:T(8,128)S(1)}, u32[]{:S(2)}, u32[]{:S(2)}) collective-permute-start(f32[15,32,256]{2,1,0:T(8,128)S(1)} %get-tuple-element.53.refs_1_), channel_id=1, source_target_pairs={{0,1},{1,2},{2,3},{4,5},{5,6},{6,7},{8,9},{9,10},{10,11},{12,13},{... | collective-permute-start | bytes 1474568 | tf_op jit(solution)/shard_map/ppermute | solution.py:416
  79.9 1.3 %collective-permute-start.16 = (f32[15,32,256]{2,1,0:T(8,128)S(1)}, f32[15,32,256]{2,1,0:T(8,128)S(1)}, u32[]{:S(2)}, u32[]{:S(2)}) collective-permute-start(f32[15,32,256]{2,1,0:T(8,128)S(1)} %get-tuple-element.56.refs_0_), channel_id=1, source_target_pairs={{1,0},{2,1},{3,2},{5,4},{6,5},{7,6},{9,8},{10,9},{11,10},{13,12},{... | collective-permute-start | bytes 1474568 | tf_op jit(solution)/shard_map/ppermute | solution.py:417
  81.2 4.6 %collective-permute-start.15 = (f32[15,32,256]{2,1,0:T(8,128)S(1)}, f32[15,32,256]{2,1,0:T(8,128)S(1)}, u32[]{:S(2)}, u32[]{:S(2)}) collective-permute-start(f32[15,32,256]{2,1,0:T(8,128)S(1)} %get-tuple-element.57.refs_1_), channel_id=1, source_target_pairs={{0,1},{1,2},{2,3},{4,5},{5,6},{6,7},{8,9},{9,10},{10,11},{12,13},{... | collective-permute-start | bytes 1474568 | tf_op jit(solution)/shard_map/ppermute | solution.py:416
  85.7 4.2 %collective-permute-done.12.refs_3_ = f32[15,32,256]{2,1,0:T(8,128)S(1)} collective-permute-done((f32[15,32,256]{2,1,0:T(8,128)S(1)}, f32[15,32,256]{2,1,0:T(8,128)S(1)}, u32[]{:S(2)}, u32[]{:S(2)}) %collective-permute-start.12) | collective-permute-done | bytes 491552 | tf_op jit(solution)/shard_map/ppermute | solution.py:417
  90.0 1.4 %collective-permute-done.11.refs_2_ = f32[15,32,256]{2,1,0:T(8,128)S(1)} collective-permute-done((f32[15,32,256]{2,1,0:T(8,128)S(1)}, f32[15,32,256]{2,1,0:T(8,128)S(1)}, u32[]{:S(2)}, u32[]{:S(2)}) %collective-permute-start.11) | collective-permute-done | bytes 491552 | tf_op jit(solution)/shard_map/ppermute | solution.py:416
  91.3 1.8 %shard_map.65 = (f32[15,32,256]{2,1,0:T(8,128)S(1)}, f32[15,32,256]{2,1,0:T(8,128)S(1)}) custom-call(f32[31]{0:T(128)S(1)} %copy-done.5, f32[16,64,256]{2,1,0:T(8,128)S(1)} %get-tuple-element.39.obs_ref, f32[15,32,256]{2,1,0:T(8,128)S(1)} %get-tuple-element.52.refs_0_.refs_4_, f32[15,32,256]{2,1,0:T(8,128)S(1)} %get-tuple-element.53.refs_1_, ...), custom_call_target="tpu_custom_call" | custom-call | flops 1000000000 | bytes 3500000 | tf_op jit(solution)/shard_map/pallas_call | solution.py:332
  93.2 4.4 %collective-permute-start.13 = (f32[15,32,256]{2,1,0:T(8,128)S(1)}, f32[15,32,256]{2,1,0:T(8,128)S(1)}, u32[]{:S(2)}, u32[]{:S(2)}) collective-permute-start(f32[15,32,256]{2,1,0:T(8,128)S(1)} %get-tuple-element.55.refs_1_), channel_id=1, source_target_pairs={{0,1},{1,2},{2,3},{4,5},{5,6},{6,7},{8,9},{9,10},{10,11},{12,13},{... | collective-permute-start | bytes 1474568 | tf_op jit(solution)/shard_map/ppermute | solution.py:416
  97.6 1.3 %collective-permute-start.14 = (f32[15,32,256]{2,1,0:T(8,128)S(1)}, f32[15,32,256]{2,1,0:T(8,128)S(1)}, u32[]{:S(2)}, u32[]{:S(2)}) collective-permute-start(f32[15,32,256]{2,1,0:T(8,128)S(1)} %get-tuple-element.54.refs_4_.refs_0_), channel_id=1, source_target_pairs={{1,0},{2,1},{3,2},{5,4},{6,5},{7,6},{9,8},{10,9},{11,10},{13,12},{... | collective-permute-start | bytes 1474568 | tf_op jit(solution)/shard_map/ppermute | solution.py:417
  98.9 1.4 %collective-permute-done.16.refs_3_ = f32[15,32,256]{2,1,0:T(8,128)S(1)} collective-permute-done((f32[15,32,256]{2,1,0:T(8,128)S(1)}, f32[15,32,256]{2,1,0:T(8,128)S(1)}, u32[]{:S(2)}, u32[]{:S(2)}) %collective-permute-start.16) | collective-permute-done | bytes 491552 | tf_op jit(solution)/shard_map/ppermute | solution.py:417
  100.3 1.6 %collective-permute-done.15.refs_2_ = f32[15,32,256]{2,1,0:T(8,128)S(1)} collective-permute-done((f32[15,32,256]{2,1,0:T(8,128)S(1)}, f32[15,32,256]{2,1,0:T(8,128)S(1)}, u32[]{:S(2)}, u32[]{:S(2)}) %collective-permute-start.15) | collective-permute-done | bytes 491552 | tf_op jit(solution)/shard_map/ppermute | solution.py:416
  101.9 1.8 %shard_map.66 = (f32[15,32,256]{2,1,0:T(8,128)S(1)}, f32[15,32,256]{2,1,0:T(8,128)S(1)}) custom-call(f32[31]{0:T(128)S(1)} %copy-done.5, f32[16,64,256]{2,1,0:T(8,128)S(1)} %get-tuple-element.39.obs_ref, f32[15,32,256]{2,1,0:T(8,128)S(1)} %get-tuple-element.56.refs_0_, f32[15,32,256]{2,1,0:T(8,128)S(1)} %get-tuple-element.57.refs_1_, ...), custom_call_target="tpu_custom_call" | custom-call | flops 1000000000 | bytes 3500000 | tf_op jit(solution)/shard_map/pallas_call | solution.py:332
  103.7 4.4 %collective-permute-start.18 = (f32[15,32,256]{2,1,0:T(8,128)S(1)}, f32[15,32,256]{2,1,0:T(8,128)S(1)}, u32[]{:S(2)}, u32[]{:S(2)}) collective-permute-start(f32[15,32,256]{2,1,0:T(8,128)S(1)} %get-tuple-element.59.refs_1_), channel_id=1, source_target_pairs={{0,1},{1,2},{2,3},{4,5},{5,6},{6,7},{8,9},{9,10},{10,11},{12,13},{... | collective-permute-start | bytes 1474568 | tf_op jit(solution)/shard_map/ppermute | solution.py:416
  108.1 1.3 %collective-permute-start.19 = (f32[15,32,256]{2,1,0:T(8,128)S(1)}, f32[15,32,256]{2,1,0:T(8,128)S(1)}, u32[]{:S(2)}, u32[]{:S(2)}) collective-permute-start(f32[15,32,256]{2,1,0:T(8,128)S(1)} %get-tuple-element.58.refs_4_.refs_0_), channel_id=1, source_target_pairs={{1,0},{2,1},{3,2},{5,4},{6,5},{7,6},{9,8},{10,9},{11,10},{13,12},{... | collective-permute-start | bytes 1474568 | tf_op jit(solution)/shard_map/ppermute | solution.py:417
  109.4 3.0 %collective-permute-done.13.refs_2_ = f32[15,32,256]{2,1,0:T(8,128)S(1)} collective-permute-done((f32[15,32,256]{2,1,0:T(8,128)S(1)}, f32[15,32,256]{2,1,0:T(8,128)S(1)}, u32[]{:S(2)}, u32[]{:S(2)}) %collective-permute-start.13) | collective-permute-done | bytes 491552 | tf_op jit(solution)/shard_map/ppermute | solution.py:416
  112.4 0.0 collective-permute-done.14.refs_3_
  112.4 1.7 %shard_map.67.refs_4_.refs_2_ = f32[16,32,256]{2,1,0:T(8,128)S(1)} custom-call(f32[31]{0:T(128)S(1)} %copy-done.5, f32[15,32,256]{2,1,0:T(8,128)S(1)} %get-tuple-element.54.refs_4_.refs_0_, f32[15,32,256]{2,1,0:T(8,128)S(1)} %get-tuple-element.55.refs_1_, f32[15,32,256]{2,1,0:T(8,128)S(1)} %collective-permute-done.13.refs_2_, ...), custom_call_target="tpu_custom_call" | custom-call | flops 1000000000 | bytes 3500000 | tf_op jit(solution)/shard_map/pallas_call | solution.py:357
  114.2 0.1 collective-permute-start.17
  114.2 8.3 %collective-permute-done.18.refs_2_ = f32[15,32,256]{2,1,0:T(8,128)S(1)} collective-permute-done((f32[15,32,256]{2,1,0:T(8,128)S(1)}, f32[15,32,256]{2,1,0:T(8,128)S(1)}, u32[]{:S(2)}, u32[]{:S(2)}) %collective-permute-start.18) | collective-permute-done | bytes 491552 | tf_op jit(solution)/shard_map/ppermute | solution.py:416
  122.6 0.0 collective-permute-done.19.refs_3_
  122.6 1.7 %shard_map.68.refs_1_ = f32[16,32,256]{2,1,0:T(8,128)S(1)} custom-call(f32[31]{0:T(128)S(1)} %copy-done.5, f32[15,32,256]{2,1,0:T(8,128)S(1)} %get-tuple-element.58.refs_4_.refs_0_, f32[15,32,256]{2,1,0:T(8,128)S(1)} %get-tuple-element.59.refs_1_, f32[15,32,256]{2,1,0:T(8,128)S(1)} %collective-permute-done.18.refs_2_, ...), custom_call_target="tpu_custom_call" | custom-call | flops 99999997952 | bytes 350000000 | tf_op jit(solution)/shard_map/pallas_call | solution.py:357
  124.3 0.0 collective-permute-done.17.refs_0_
  124.3 2.3 %shard_map.69 = f32[16,64,256]{2,1,0:T(8,128)} custom-call(f32[16,32,256]{2,1,0:T(8,128)S(1)} %collective-permute-done.17.refs_0_, f32[16,32,256]{2,1,0:T(8,128)S(1)} %shard_map.68.refs_1_, f32[16,32,256]{2,1,0:T(8,128)S(1)} %shard_map.67.refs_4_.refs_2_, f32[16,64,256]{2,1,0:T(8,128)S(1)} %get-tuple-element.60.refs_3_, ...), custom_call_target="tpu_custom_call" | custom-call | flops 1000000000 | bytes 3500000 | tf_op jit(solution)/shard_map/pallas_call | solution.py:401
  (4 shorter events, 0.0 us)
Async XLA Ops:
  1.1 9.1 %collective-permute-start = (f32[16,32,256]{2,1,0:T(8,128)S(1)}, f32[16,32,256]{2,1,0:T(8,128)S(1)}, u32[]{:S(2)}, u32[]{:S(2)}) collective-permute-start(f32[16,32,256]{2,1,0:T(8,128)S(1)} %slice.3), channel_id=1, source_target_pairs={{0,12},{4,0},{8,4},{12,8},{1,13},{5,1},{9,5},{13,9},{2,14},{6,2},{... | collective-permute-start | bytes 1572872 | tf_op jit(solution)/shard_map/ppermute | solution.py:423
  3.5 1.2 copy-start
  4.7 0.7 copy-start.2
  5.4 0.7 copy-start.3
  6.1 0.7 copy-start.4
  11.3 11.2 %copy-start.1 = (f32[16,64,256]{2,1,0:T(8,128)S(1)}, f32[16,64,256]{2,1,0:T(8,128)}, u32[]{:S(2)}) copy-start(f32[16,64,256]{2,1,0:T(8,128)} %refs_3_.1) | copy-start | bytes 3145732
  11.3 11.2 %copy-start.5 = (f32[31]{0:T(128)S(1)}, f32[31]{0:T(128)}, u32[]{:S(2)}) copy-start(f32[31]{0:T(128)} %tz_ref.17) | copy-start | bytes 376
  11.3 15.2 %collective-permute-start.1 = (f32[15,32,256]{2,1,0:T(8,128)S(1)}, f32[15,32,256]{2,1,0:T(8,128)S(1)}, u32[]{:S(2)}, u32[]{:S(2)}) collective-permute-start(f32[15,32,256]{2,1,0:T(8,128)S(1)} %get-tuple-element.40.refs_1_), channel_id=1, source_target_pairs={{0,1},{1,2},{2,3},{4,5},{5,6},{6,7},{8,9},{9,10},{10,11},{12,13},{... | collective-permute-start | bytes 1474568 | tf_op jit(solution)/shard_map/ppermute | solution.py:416
  15.0 15.9 %collective-permute-start.2 = (f32[15,32,256]{2,1,0:T(8,128)S(1)}, f32[15,32,256]{2,1,0:T(8,128)S(1)}, u32[]{:S(2)}, u32[]{:S(2)}) collective-permute-start(f32[15,32,256]{2,1,0:T(8,128)S(1)} %get-tuple-element.37.after_ref.refs_0_), channel_id=1, source_target_pairs={{1,0},{2,1},{3,2},{5,4},{6,5},{7,6},{9,8},{10,9},{11,10},{13,12},{... | collective-permute-start | bytes 1474568 | tf_op jit(solution)/shard_map/ppermute | solution.py:417
  16.6 20.9 %collective-permute-start.5 = (f32[15,32,256]{2,1,0:T(8,128)S(1)}, f32[15,32,256]{2,1,0:T(8,128)S(1)}, u32[]{:S(2)}, u32[]{:S(2)}) collective-permute-start(f32[15,32,256]{2,1,0:T(8,128)S(1)} %get-tuple-element.43.refs_1_), channel_id=1, source_target_pairs={{0,1},{1,2},{2,3},{4,5},{5,6},{6,7},{8,9},{9,10},{10,11},{12,13},{... | collective-permute-start | bytes 1474568 | tf_op jit(solution)/shard_map/ppermute | solution.py:416
  21.2 20.2 %collective-permute-start.6 = (f32[15,32,256]{2,1,0:T(8,128)S(1)}, f32[15,32,256]{2,1,0:T(8,128)S(1)}, u32[]{:S(2)}, u32[]{:S(2)}) collective-permute-start(f32[15,32,256]{2,1,0:T(8,128)S(1)} %get-tuple-element.38.after_ref.refs_4_.refs_0_), channel_id=1, source_target_pairs={{1,0},{2,1},{3,2},{5,4},{6,5},{7,6},{9,8},{10,9},{11,10},{13,12},{... | collective-permute-start | bytes 1474568 | tf_op jit(solution)/shard_map/ppermute | solution.py:417
  32.7 15.3 %collective-permute-start.3 = (f32[15,32,256]{2,1,0:T(8,128)S(1)}, f32[15,32,256]{2,1,0:T(8,128)S(1)}, u32[]{:S(2)}, u32[]{:S(2)}) collective-permute-start(f32[15,32,256]{2,1,0:T(8,128)S(1)} %get-tuple-element.42.refs_1_), channel_id=1, source_target_pairs={{0,1},{1,2},{2,3},{4,5},{5,6},{6,7},{8,9},{9,10},{10,11},{12,13},{... | collective-permute-start | bytes 1474568 | tf_op jit(solution)/shard_map/ppermute | solution.py:416
  36.2 16.1 %collective-permute-start.4 = (f32[15,32,256]{2,1,0:T(8,128)S(1)}, f32[15,32,256]{2,1,0:T(8,128)S(1)}, u32[]{:S(2)}, u32[]{:S(2)}) collective-permute-start(f32[15,32,256]{2,1,0:T(8,128)S(1)} %get-tuple-element.41.refs_4_.refs_0_), channel_id=1, source_target_pairs={{1,0},{2,1},{3,2},{5,4},{6,5},{7,6},{9,8},{10,9},{11,10},{13,12},{... | collective-permute-start | bytes 1474568 | tf_op jit(solution)/shard_map/ppermute | solution.py:417
  43.2 14.8 %collective-permute-start.8 = (f32[15,32,256]{2,1,0:T(8,128)S(1)}, f32[15,32,256]{2,1,0:T(8,128)S(1)}, u32[]{:S(2)}, u32[]{:S(2)}) collective-permute-start(f32[15,32,256]{2,1,0:T(8,128)S(1)} %get-tuple-element.45.refs_1_), channel_id=1, source_target_pairs={{0,1},{1,2},{2,3},{4,5},{5,6},{6,7},{8,9},{9,10},{10,11},{12,13},{... | collective-permute-start | bytes 1474568 | tf_op jit(solution)/shard_map/ppermute | solution.py:416
  46.7 15.4 %collective-permute-start.9 = (f32[15,32,256]{2,1,0:T(8,128)S(1)}, f32[15,32,256]{2,1,0:T(8,128)S(1)}, u32[]{:S(2)}, u32[]{:S(2)}) collective-permute-start(f32[15,32,256]{2,1,0:T(8,128)S(1)} %get-tuple-element.44.refs_4_.refs_0_), channel_id=1, source_target_pairs={{1,0},{2,1},{3,2},{5,4},{6,5},{7,6},{9,8},{10,9},{11,10},{13,12},{... | collective-permute-start | bytes 1474568 | tf_op jit(solution)/shard_map/ppermute | solution.py:417
  54.0 9.9 %collective-permute-start.7 = (f32[16,32,256]{2,1,0:T(8,128)S(1)}, f32[16,32,256]{2,1,0:T(8,128)S(1)}, u32[]{:S(2)}, u32[]{:S(2)}) collective-permute-start(f32[16,32,256]{2,1,0:T(8,128)S(1)} %shard_map.61.refs_4_.refs_2_), channel_id=1, source_target_pairs={{0,4},{4,8},{8,12},{12,0},{1,5},{5,9},{9,13},{13,1},{2,6},{6,10},{... | collective-permute-start | bytes 1572872 | tf_op jit(solution)/shard_map/ppermute | solution.py:423
  66.2 7.3 %collective-permute-start.10 = (f32[16,32,256]{2,1,0:T(8,128)S(1)}, f32[16,32,256]{2,1,0:T(8,128)S(1)}, u32[]{:S(2)}, u32[]{:S(2)}) collective-permute-start(f32[16,32,256]{2,1,0:T(8,128)S(1)} %get-tuple-element.51), channel_id=1, source_target_pairs={{0,12},{4,0},{8,4},{12,8},{1,13},{5,1},{9,5},{13,9},{2,14},{6,2},{... | collective-permute-start | bytes 1572872 | tf_op jit(solution)/shard_map/ppermute | solution.py:423
  74.0 16.0 %collective-permute-start.12 = (f32[15,32,256]{2,1,0:T(8,128)S(1)}, f32[15,32,256]{2,1,0:T(8,128)S(1)}, u32[]{:S(2)}, u32[]{:S(2)}) collective-permute-start(f32[15,32,256]{2,1,0:T(8,128)S(1)} %get-tuple-element.52.refs_0_.refs_4_), channel_id=1, source_target_pairs={{1,0},{2,1},{3,2},{5,4},{6,5},{7,6},{9,8},{10,9},{11,10},{13,12},{... | collective-permute-start | bytes 1474568 | tf_op jit(solution)/shard_map/ppermute | solution.py:417
  75.3 16.1 %collective-permute-start.11 = (f32[15,32,256]{2,1,0:T(8,128)S(1)}, f32[15,32,256]{2,1,0:T(8,128)S(1)}, u32[]{:S(2)}, u32[]{:S(2)}) collective-permute-start(f32[15,32,256]{2,1,0:T(8,128)S(1)} %get-tuple-element.53.refs_1_), channel_id=1, source_target_pairs={{0,1},{1,2},{2,3},{4,5},{5,6},{6,7},{8,9},{9,10},{10,11},{12,13},{... | collective-permute-start | bytes 1474568 | tf_op jit(solution)/shard_map/ppermute | solution.py:416
  79.9 20.5 %collective-permute-start.16 = (f32[15,32,256]{2,1,0:T(8,128)S(1)}, f32[15,32,256]{2,1,0:T(8,128)S(1)}, u32[]{:S(2)}, u32[]{:S(2)}) collective-permute-start(f32[15,32,256]{2,1,0:T(8,128)S(1)} %get-tuple-element.56.refs_0_), channel_id=1, source_target_pairs={{1,0},{2,1},{3,2},{5,4},{6,5},{7,6},{9,8},{10,9},{11,10},{13,12},{... | collective-permute-start | bytes 1474568 | tf_op jit(solution)/shard_map/ppermute | solution.py:417
  81.2 20.7 %collective-permute-start.15 = (f32[15,32,256]{2,1,0:T(8,128)S(1)}, f32[15,32,256]{2,1,0:T(8,128)S(1)}, u32[]{:S(2)}, u32[]{:S(2)}) collective-permute-start(f32[15,32,256]{2,1,0:T(8,128)S(1)} %get-tuple-element.57.refs_1_), channel_id=1, source_target_pairs={{0,1},{1,2},{2,3},{4,5},{5,6},{6,7},{8,9},{9,10},{10,11},{12,13},{... | collective-permute-start | bytes 1474568 | tf_op jit(solution)/shard_map/ppermute | solution.py:416
  93.2 19.2 %collective-permute-start.13 = (f32[15,32,256]{2,1,0:T(8,128)S(1)}, f32[15,32,256]{2,1,0:T(8,128)S(1)}, u32[]{:S(2)}, u32[]{:S(2)}) collective-permute-start(f32[15,32,256]{2,1,0:T(8,128)S(1)} %get-tuple-element.55.refs_1_), channel_id=1, source_target_pairs={{0,1},{1,2},{2,3},{4,5},{5,6},{6,7},{8,9},{9,10},{10,11},{12,13},{... | collective-permute-start | bytes 1474568 | tf_op jit(solution)/shard_map/ppermute | solution.py:416
  97.6 14.8 %collective-permute-start.14 = (f32[15,32,256]{2,1,0:T(8,128)S(1)}, f32[15,32,256]{2,1,0:T(8,128)S(1)}, u32[]{:S(2)}, u32[]{:S(2)}) collective-permute-start(f32[15,32,256]{2,1,0:T(8,128)S(1)} %get-tuple-element.54.refs_4_.refs_0_), channel_id=1, source_target_pairs={{1,0},{2,1},{3,2},{5,4},{6,5},{7,6},{9,8},{10,9},{11,10},{13,12},{... | collective-permute-start | bytes 1474568 | tf_op jit(solution)/shard_map/ppermute | solution.py:417
  103.7 18.9 %collective-permute-start.18 = (f32[15,32,256]{2,1,0:T(8,128)S(1)}, f32[15,32,256]{2,1,0:T(8,128)S(1)}, u32[]{:S(2)}, u32[]{:S(2)}) collective-permute-start(f32[15,32,256]{2,1,0:T(8,128)S(1)} %get-tuple-element.59.refs_1_), channel_id=1, source_target_pairs={{0,1},{1,2},{2,3},{4,5},{5,6},{6,7},{8,9},{9,10},{10,11},{12,13},{... | collective-permute-start | bytes 1474568 | tf_op jit(solution)/shard_map/ppermute | solution.py:416
  108.1 14.4 %collective-permute-start.19 = (f32[15,32,256]{2,1,0:T(8,128)S(1)}, f32[15,32,256]{2,1,0:T(8,128)S(1)}, u32[]{:S(2)}, u32[]{:S(2)}) collective-permute-start(f32[15,32,256]{2,1,0:T(8,128)S(1)} %get-tuple-element.58.refs_4_.refs_0_), channel_id=1, source_target_pairs={{1,0},{2,1},{3,2},{5,4},{6,5},{7,6},{9,8},{10,9},{11,10},{13,12},{... | collective-permute-start | bytes 1474568 | tf_op jit(solution)/shard_map/ppermute | solution.py:417
  114.2 10.2 %collective-permute-start.17 = (f32[16,32,256]{2,1,0:T(8,128)S(1)}, f32[16,32,256]{2,1,0:T(8,128)S(1)}, u32[]{:S(2)}, u32[]{:S(2)}) collective-permute-start(f32[16,32,256]{2,1,0:T(8,128)S(1)} %shard_map.67.refs_4_.refs_2_), channel_id=1, source_target_pairs={{0,4},{4,8},{8,12},{12,0},{1,5},{5,9},{9,13},{13,1},{2,6},{6,10},{... | collective-permute-start | bytes 1572872 | tf_op jit(solution)/shard_map/ppermute | solution.py:423

commit v7 on v6

--- a/solution.py
+++ b/solution.py
@@ -113,12 +113,13 @@
         out_ref[p] = blur_columns(source(p), a_refs[0][p], a_refs[1][p])
 
 
-def own_rows(w_ref, wx_ref, low_ref, high_ref):
+def own_rows(w_ref, wx_ref, low_ref, high_ref, first=0):
     n, rows, _ = w_ref.shape
-    radius, inner, _ = low_ref.shape
+    radius, count, _ = low_ref.shape
+    part = slice(first, first + count)
     for p in range(n):
         w_hi, w_lo = split(w_ref[p])
-        v = blur_rows(wx_ref[p, 0, :inner, :rows], wx_ref[p, 1, :inner, :rows], w_hi, w_lo)
+        v = blur_rows(wx_ref[p, 0, part, :rows], wx_ref[p, 1, part, :rows], w_hi, w_lo)
         store_sends(v, p, n, radius, low_ref, high_ref)
 
 
@@ -229,21 +230,20 @@
     )(band_index, taps_x, taps_y, taps_z, after, obs, beyond)
 
 
-def inner_kernel(w_ref, wx_ref, after_ref, low_ref, high_ref):
-    own_rows(w_ref, wx_ref, low_ref, high_ref)
-
-
-def inner_blur(w, wx, halo, radius, after):
-    _, rows, columns = w.shape
-    send = shape_of(radius, rows - halo, columns)
-    return pl.pallas_call(
-        inner_kernel,
-        in_specs=[VMEM] * 2 + [ANY],
+def inner_kernel(first, w_ref, wx_ref, *refs):
+    own_rows(w_ref, wx_ref, *refs[-2:], first)
+
+
+def inner_blur(w, wx, first, count, radius, after, micro):
+    send = shape_of(radius, count, w.shape[2])
+    return pl.pallas_call(
+        functools.partial(inner_kernel, first),
+        in_specs=[VMEM] * 2 + [ANY] * len(after),
         out_specs=[VMEM] * 2,
         out_shape=[send] * 2,
         compiler_params=PARAMS,
-        cost_estimate=cost(1.0),
-    )(w, wx, after)
+        cost_estimate=cost(micro),
+    )(w, wx, *after)
 
 
 def edge_kernel(n, radius, blurred, w_ref, next_ref, wx_ref, *refs):
@@ -310,33 +310,40 @@
 
 def ratio_kernel(n, radius, skip, tz_ref, obs_ref, *refs):
     rlow_ref, rhigh_ref = refs[-2:]
-    _, count, columns = rlow_ref.shape
-
-    def body(start, lanes):
-        rows = at(start, 0)
-        total = depth_sum(n, radius, False, tz_ref, refs[:4], rows, lanes)
-        for i in range(n):
-            ratio = obs_ref[i, at(start, skip), lanes] / total[i]
-            if i < radius:
-                rlow_ref[i, rows, lanes] = ratio
-            if i >= n - radius:
-                rhigh_ref[i - (n - radius), rows, lanes] = ratio
-
-    tiles(count, columns, body)
-
-
-def depth_ratio(taps_z, obs, chunk, skip, count, after, micro=1.0):
+    columns = obs_ref.shape[2]
+
+    def run(own, first):
+        def body(start, lanes):
+            total = depth_sum(n, radius, False, tz_ref, own, at(start, 0), lanes)
+            rows = at(start, first)
+            for i in range(n):
+                ratio = obs_ref[i, at(start, skip + first), lanes] / total[i]
+                if i < radius:
+                    rlow_ref[i, rows, lanes] = ratio
+                if i >= n - radius:
+                    rhigh_ref[i - (n - radius), rows, lanes] = ratio
+
+        tiles(own[0].shape[1], columns, body)
+
+    first = 0
+    while first < rlow_ref.shape[1]:
+        run(refs[:4], first)
+        first += refs[0].shape[1]
+        refs = refs[4:]
+
+
+def depth_ratio(taps_z, obs, chunks, skip, after):
     n, _, columns = obs.shape
     radius = taps_z.shape[0] // 2
-    send = shape_of(radius, count, columns)
+    send = shape_of(radius, sum(chunk[0].shape[1] for chunk in chunks), columns)
     return pl.pallas_call(
         functools.partial(ratio_kernel, n, radius, skip),
-        in_specs=[SMEM] + [VMEM] * 5 + [ANY],
+        in_specs=[SMEM] + [VMEM] * (1 + 4 * len(chunks)) + [ANY] * len(after),
         out_specs=[VMEM] * 2,
         out_shape=[send] * 2,
         compiler_params=PARAMS,
-        cost_estimate=cost(micro),
-    )(taps_z, obs, *chunk, after)
+        cost_estimate=cost(1.0),
+    )(taps_z, obs, *(x for chunk in chunks for x in chunk), *after)
 
 
 def back_kernel(n, radius, tz_ref, *refs):
@@ -389,14 +396,14 @@
         own_rows(w_ref, wx_ref, low_ref, high_ref)
 
 
-def update(pieces, est, rn, adjoint, forward, radius):
+def update(pieces, est, rn, adjoint, forward, count, radius):
     n, rows, columns = est.shape
     halo = pieces[0].shape[1]
     last = forward is None
     args = [*pieces, est, rn, *adjoint] + ([] if last else [*forward])
     out_shape = [shape_of(*est.shape)]
     if not last:
-        send = shape_of(radius, rows - halo, columns)
+        send = shape_of(radius, count, columns)
         out_shape += [shape_of(*est.shape), shape_of(n, halo, columns), send, send]
     return pl.pallas_call(
         functools.partial(update_kernel, n, last),
@@ -428,31 +435,33 @@
     radius = taps_z.shape[0] // 2
     halo = up(2 * radius, 16)
     inner = rows - halo
+    half = up(inner // 2, 16)
     width = up(rows + halo, 128)
     beyond = ring(observed[:, :halo], -1)
     ah, al, wx, w = first_blur(band_index, taps_x, taps_y, observed, width)
     est, adjoint = observed, None
     for step in range(ITERS):
         if step:
-            v_inner = depth_exchange(*inner_sends)
+            v_first = depth_exchange(*first_sends)
             edge_sends = edge_blur(w, beyond, wx, (), radius)
             v_edge = depth_exchange(*edge_sends)
-            after = edge_sends[0]
+            after = (edge_sends[0],) + v_first[2:]
+            inner_sends = inner_blur(w, wx, half, inner - half, radius, after, 20.0)
+            v_inner = [v_first, depth_exchange(*inner_sends)]
         else:
             edge_sends = edge_blur(w, beyond, wx, (ah, al), radius)
             v_edge = depth_exchange(*edge_sends)
-            inner_sends = inner_blur(w, wx, halo, radius, edge_sends[0])
-            v_inner = depth_exchange(*inner_sends)
+            inner_sends = inner_blur(w, wx, 0, inner, radius, (edge_sends[0],), 1.0)
+            v_inner = [depth_exchange(*inner_sends)]
             bh, bl, wa, rn, shifted = second_weights(
                 band_index, taps_x, taps_y, taps_z, inner_sends[0], observed, beyond, width
             )
             adjoint = (wa, bh, bl)
-            after = inner_sends[0]
         r_edge = depth_exchange(
-            *depth_ratio(taps_z, shifted, v_edge, inner, halo, after)
+            *depth_ratio(taps_z, shifted, [v_edge], inner, (inner_sends[0],))
         )
         r_inner = depth_exchange(
-            *depth_ratio(taps_z, shifted, v_inner, 0, inner, r_edge[0])
+            *depth_ratio(taps_z, shifted, v_inner, 0, (r_edge[0],))
         )
         c_edge = depth_back(taps_z, r_edge, n, r_inner[0])
         before = ring(c_edge, 1)
@@ -460,11 +469,11 @@
         last = step == ITERS - 1
         out = update(
             (before, c_inner, c_edge), est, rn, adjoint,
-            None if last else (wx, ah, al), radius,
+            None if last else (wx, ah, al), half, radius,
         )
         est = out[0]
         if not last:
-            w, top, *inner_sends = out[1:]
+            w, top, *first_sends = out[1:]
             beyond = ring(top, -1)
     return est
 

time: 127 us -> 128 us (level)
  starting transfers between devices: 46.7 us -> 52.6 us
  waiting for transfers between devices: 49.6 us -> 43.8 us
    ppermute x8 -> x9, waiting for transfers between devices: 22.2 us -> 16.9 us  [depth_exchange(): zhi = lax.ppermute(low, 'slab', backward)]
    ppermute x4, waiting for transfers between devices: 7.89 us -> 2.63 us  [ring(): lax.ppermute(x, 'row', [(i, (i + step) % count) for i in range(count)])]
    ppermute x8 -> x9, waiting for transfers between devices: 19.5 us -> 24.2 us  [depth_exchange(): zlo = lax.ppermute(high, 'slab', forward)]
    ppermute x8 -> x9, starting transfers between devices: 33.2 us -> 37.5 us  [depth_exchange(): zlo = lax.ppermute(high, 'slab', forward)]
    ppermute x8 -> x9, starting transfers between devices: 10.3 us -> 11.8 us  [depth_exchange(): zhi = lax.ppermute(low, 'slab', backward)]
  transfers between devices with their start and end apart: 20 -> 22, of which waited for: 14 -> 15; matrix products, arithmetic and copies ran while one was open for 0% -> 0% of each run, Pallas kernels for 15% -> 16%
where the time goes in v7:
time: 128 us; the launch traced here: 127 us
  starting transfers between devices  52.6 us (41%)
  waiting for transfers between devices  43.8 us (34%)
  Pallas kernels  26 us (20%)
  local copies, waits for them, and re-layouts  4.36 us (3%)
    ppermute x9, starting transfers between devices, depth_exchange(): zlo = lax.ppermute(high, 'slab', forward)  37.5 us
    ppermute x9, waiting for transfers between devices, depth_exchange(): zlo = lax.ppermute(high, 'slab', forward)  24.2 us
    ppermute x9, waiting for transfers between devices, depth_exchange(): zhi = lax.ppermute(low, 'slab', backward)  16.9 us
    ppermute x9, starting transfers between devices, depth_exchange(): zhi = lax.ppermute(low, 'slab', backward)  11.8 us
    pallas_call x4, Pallas kernels, depth_ratio(): pl.pallas_call(functools.partial(ratio_kernel, n, radius, skip), in_specs...  7.28 us
    pallas_call x4, Pallas kernels, depth_back(): pl.pallas_call(functools.partial(back_kernel, n, radius), in_specs=[SMEM]...  6.99 us
    pallas_call x2, Pallas kernels, update(): pl.pallas_call(functools.partial(update_kernel, n, last), in_specs=[VMEM]...  4.53 us
    ppermute x4, starting transfers between devices, ring(): lax.ppermute(x, 'row', [(i, (i + step) % count) for i in range(count)])  3.39 us
  transfers between devices with their start and end apart: 22, of which 15 were waited for; matrix products, arithmetic and copies ran while one was open for 0% of the time, Pallas kernels for 16%

profile of v7, /device:TPU:0, one launch (start us, length us, event | category | flops | bytes accessed | tf_op | source)
XLA Modules:
  0.0 127.1 jit_solution(5591386840083466436)
XLA Ops:
  0.0 1.1 slice.3
  1.1 2.4 %collective-permute-start = (f32[16,32,256]{2,1,0:T(8,128)S(1)}, f32[16,32,256]{2,1,0:T(8,128)S(1)}, u32[]{:S(2)}, u32[]{:S(2)}) collective-permute-start(f32[16,32,256]{2,1,0:T(8,128)S(1)} %slice.3), channel_id=1, source_target_pairs={{0,12},{4,0},{8,4},{12,8},{1,13},{5,1},{9,5},{13,9},{2,14},{6,2},{... | collective-permute-start | bytes 1572872 | tf_op jit(solution)/shard_map/ppermute | solution.py:430
  3.5 1.2 copy-done
  4.7 0.7 copy-done.2
  5.4 0.7 copy-done.3
  6.1 0.7 copy-done.4
  6.8 2.2 %shard_map.55 = (bf16[16,256,256]{2,1,0:T(8,128)(2,1)S(1)}, bf16[16,256,256]{2,1,0:T(8,128)(2,1)S(1)}, bf16[16,2,64,128]{3,2,1,0:T(8,128)(2,1)S(1)}, f32[16,64,256]{2,1,0:T(8,128)S(1)}) custom-call(s32[16]{0:T(128)S(1)} %copy-done.4, f32[16,31]{1,0:T(8,128)S(1)} %copy-done.2, f32[16,31]{1,0:T(8,128)S(1)} %copy-done.3, f32[16,64,256]{2,1,0:T(8,128)S(1)} %copy-done), custom_call_target="tpu_custom_call" | custom-call | flops 1000000000 | bytes 3500000 | tf_op jit(solution)/shard_map/pallas_call | solution.py:160
  9.0 1.2 collective-permute-done.next_ref
  10.2 1.1 shard_map.56
  11.3 0.0 copy-start.5
  11.3 1.4 %collective-permute-start.2 = (f32[15,32,256]{2,1,0:T(8,128)S(1)}, f32[15,32,256]{2,1,0:T(8,128)S(1)}, u32[]{:S(2)}, u32[]{:S(2)}) collective-permute-start(f32[15,32,256]{2,1,0:T(8,128)S(1)} %get-tuple-element.39.refs_0_), channel_id=1, source_target_pairs={{1,0},{2,1},{3,2},{5,4},{6,5},{7,6},{9,8},{10,9},{11,10},{13,12},{... | collective-permute-start | bytes 1474568 | tf_op jit(solution)/shard_map/ppermute | solution.py:424
  12.8 4.6 %collective-permute-start.1 = (f32[15,32,256]{2,1,0:T(8,128)S(1)}, f32[15,32,256]{2,1,0:T(8,128)S(1)}, u32[]{:S(2)}, u32[]{:S(2)}) collective-permute-start(f32[15,32,256]{2,1,0:T(8,128)S(1)} %get-tuple-element.42.refs_1_), channel_id=1, source_target_pairs={{0,1},{1,2},{2,3},{4,5},{5,6},{6,7},{8,9},{9,10},{10,11},{12,13},{... | collective-permute-start | bytes 1474568 | tf_op jit(solution)/shard_map/ppermute | solution.py:423
  17.3 0.4 shard_map.57
  17.7 1.3 %collective-permute-start.6 = (f32[15,32,256]{2,1,0:T(8,128)S(1)}, f32[15,32,256]{2,1,0:T(8,128)S(1)}, u32[]{:S(2)}, u32[]{:S(2)}) collective-permute-start(f32[15,32,256]{2,1,0:T(8,128)S(1)} %get-tuple-element.40.after_ref.refs_4_.refs_0_), channel_id=1, source_target_pairs={{1,0},{2,1},{3,2},{5,4},{6,5},{7,6},{9,8},{10,9},{11,10},{13,12},{... | collective-permute-start | bytes 1474568 | tf_op jit(solution)/shard_map/ppermute | solution.py:424
  19.0 4.6 %collective-permute-start.5 = (f32[15,32,256]{2,1,0:T(8,128)S(1)}, f32[15,32,256]{2,1,0:T(8,128)S(1)}, u32[]{:S(2)}, u32[]{:S(2)}) collective-permute-start(f32[15,32,256]{2,1,0:T(8,128)S(1)} %get-tuple-element.45.refs_1_), channel_id=1, source_target_pairs={{0,1},{1,2},{2,3},{4,5},{5,6},{6,7},{8,9},{9,10},{10,11},{12,13},{... | collective-permute-start | bytes 1474568 | tf_op jit(solution)/shard_map/ppermute | solution.py:423
  23.6 2.8 %shard_map.58 = (bf16[16,256,256]{2,1,0:T(8,128)(2,1)S(1)}, bf16[16,256,256]{2,1,0:T(8,128)(2,1)S(1)}, bf16[16,2,64,128]{3,2,1,0:T(8,128)(2,1)S(1)}, f32[16,64,256]{2,1,0:T(8,128)S(1)}, f32[16,64,256]{2,1,0:T(8,128)S(1)}) custom-call(s32[16]{0:T(128)S(1)} %copy-done.4, f32[16,31]{1,0:T(8,128)S(1)} %copy-done.2, f32[16,31]{1,0:T(8,128)S(1)} %copy-done.3, ...), custom_call_target="tpu_custom_call" | custom-call | flops 1000000000 | bytes 3500000 | tf_op jit(solution)/shard_map/pallas_call | solution.py:223
  26.4 1.1 collective-permute-done.2.refs_3_
  27.4 1.4 %collective-permute-done.1.refs_2_ = f32[15,32,256]{2,1,0:T(8,128)S(1)} collective-permute-done((f32[15,32,256]{2,1,0:T(8,128)S(1)}, f32[15,32,256]{2,1,0:T(8,128)S(1)}, u32[]{:S(2)}, u32[]{:S(2)}) %collective-permute-start.1) | collective-permute-done | bytes 491552 | tf_op jit(solution)/shard_map/ppermute | solution.py:423
  28.8 1.8 %shard_map.59 = (f32[15,32,256]{2,1,0:T(8,128)S(1)}, f32[15,32,256]{2,1,0:T(8,128)S(1)}) custom-call(f32[31]{0:T(128)S(1)} %copy-done.5, f32[16,64,256]{2,1,0:T(8,128)S(1)} %get-tuple-element.41.obs_ref, f32[15,32,256]{2,1,0:T(8,128)S(1)} %get-tuple-element.39.refs_0_, f32[15,32,256]{2,1,0:T(8,128)S(1)} %get-tuple-element.42.refs_1_, ...), custom_call_target="tpu_custom_call" | custom-call | flops 1000000000 | bytes 3500000 | tf_op jit(solution)/shard_map/pallas_call | solution.py:339
  30.7 4.4 %collective-permute-start.3 = (f32[15,32,256]{2,1,0:T(8,128)S(1)}, f32[15,32,256]{2,1,0:T(8,128)S(1)}, u32[]{:S(2)}, u32[]{:S(2)}) collective-permute-start(f32[15,32,256]{2,1,0:T(8,128)S(1)} %get-tuple-element.44.refs_1_), channel_id=1, source_target_pairs={{0,1},{1,2},{2,3},{4,5},{5,6},{6,7},{8,9},{9,10},{10,11},{12,13},{... | collective-permute-start | bytes 1474568 | tf_op jit(solution)/shard_map/ppermute | solution.py:423
  35.1 1.3 %collective-permute-start.4 = (f32[15,32,256]{2,1,0:T(8,128)S(1)}, f32[15,32,256]{2,1,0:T(8,128)S(1)}, u32[]{:S(2)}, u32[]{:S(2)}) collective-permute-start(f32[15,32,256]{2,1,0:T(8,128)S(1)} %get-tuple-element.43.refs_4_.refs_0_), channel_id=1, source_target_pairs={{1,0},{2,1},{3,2},{5,4},{6,5},{7,6},{9,8},{10,9},{11,10},{13,12},{... | collective-permute-start | bytes 1474568 | tf_op jit(solution)/shard_map/ppermute | solution.py:424
  36.4 1.5 %collective-permute-done.6.refs_3_ = f32[15,32,256]{2,1,0:T(8,128)S(1)} collective-permute-done((f32[15,32,256]{2,1,0:T(8,128)S(1)}, f32[15,32,256]{2,1,0:T(8,128)S(1)}, u32[]{:S(2)}, u32[]{:S(2)}) %collective-permute-start.6) | collective-permute-done | bytes 491552 | tf_op jit(solution)/shard_map/ppermute | solution.py:424
  37.9 1.5 %collective-permute-done.5.refs_2_ = f32[15,32,256]{2,1,0:T(8,128)S(1)} collective-permute-done((f32[15,32,256]{2,1,0:T(8,128)S(1)}, f32[15,32,256]{2,1,0:T(8,128)S(1)}, u32[]{:S(2)}, u32[]{:S(2)}) %collective-permute-start.5) | collective-permute-done | bytes 491552 | tf_op jit(solution)/shard_map/ppermute | solution.py:423
  39.4 1.8 %shard_map.60 = (f32[15,32,256]{2,1,0:T(8,128)S(1)}, f32[15,32,256]{2,1,0:T(8,128)S(1)}) custom-call(f32[31]{0:T(128)S(1)} %copy-done.5, f32[16,64,256]{2,1,0:T(8,128)S(1)} %get-tuple-element.41.obs_ref, f32[15,32,256]{2,1,0:T(8,128)S(1)} %get-tuple-element.40.after_ref.refs_4_.refs_0_, f32[15,32,256]{2,1,0:T(8,128)S(1)} %get-tuple-element.45.refs_1_, ...), custom_call_target="tpu_custom_call" | custom-call | flops 1000000000 | bytes 3500000 | tf_op jit(solution)/shard_map/pallas_call | solution.py:339
  41.2 4.4 %collective-permute-start.8 = (f32[15,32,256]{2,1,0:T(8,128)S(1)}, f32[15,32,256]{2,1,0:T(8,128)S(1)}, u32[]{:S(2)}, u32[]{:S(2)}) collective-permute-start(f32[15,32,256]{2,1,0:T(8,128)S(1)} %get-tuple-element.47.refs_1_), channel_id=1, source_target_pairs={{0,1},{1,2},{2,3},{4,5},{5,6},{6,7},{8,9},{9,10},{10,11},{12,13},{... | collective-permute-start | bytes 1474568 | tf_op jit(solution)/shard_map/ppermute | solution.py:423
  45.6 1.3 %collective-permute-start.9 = (f32[15,32,256]{2,1,0:T(8,128)S(1)}, f32[15,32,256]{2,1,0:T(8,128)S(1)}, u32[]{:S(2)}, u32[]{:S(2)}) collective-permute-start(f32[15,32,256]{2,1,0:T(8,128)S(1)} %get-tuple-element.46.refs_4_.refs_0_), channel_id=1, source_target_pairs={{1,0},{2,1},{3,2},{5,4},{6,5},{7,6},{9,8},{10,9},{11,10},{13,12},{... | collective-permute-start | bytes 1474568 | tf_op jit(solution)/shard_map/ppermute | solution.py:424
  46.9 3.0 %collective-permute-done.3.refs_2_ = f32[15,32,256]{2,1,0:T(8,128)S(1)} collective-permute-done((f32[15,32,256]{2,1,0:T(8,128)S(1)}, f32[15,32,256]{2,1,0:T(8,128)S(1)}, u32[]{:S(2)}, u32[]{:S(2)}) %collective-permute-start.3) | collective-permute-done | bytes 491552 | tf_op jit(solution)/shard_map/ppermute | solution.py:423
  49.9 0.0 collective-permute-done.4.refs_3_
  49.9 1.7 %shard_map.61.refs_4_.refs_2_ = f32[16,32,256]{2,1,0:T(8,128)S(1)} custom-call(f32[31]{0:T(128)S(1)} %copy-done.5, f32[15,32,256]{2,1,0:T(8,128)S(1)} %get-tuple-element.43.refs_4_.refs_0_, f32[15,32,256]{2,1,0:T(8,128)S(1)} %get-tuple-element.44.refs_1_, f32[15,32,256]{2,1,0:T(8,128)S(1)} %collective-permute-done.3.refs_2_, ...), custom_call_target="tpu_custom_call" | custom-call | flops 1000000000 | bytes 3500000 | tf_op jit(solution)/shard_map/pallas_call | solution.py:364
  51.6 0.1 collective-permute-start.7
  51.7 8.4 %collective-permute-done.8.refs_2_ = f32[15,32,256]{2,1,0:T(8,128)S(1)} collective-permute-done((f32[15,32,256]{2,1,0:T(8,128)S(1)}, f32[15,32,256]{2,1,0:T(8,128)S(1)}, u32[]{:S(2)}, u32[]{:S(2)}) %collective-permute-start.8) | collective-permute-done | bytes 491552 | tf_op jit(solution)/shard_map/ppermute | solution.py:423
  60.1 0.0 collective-permute-done.9.refs_3_
  60.1 1.8 %shard_map.62.refs_1_ = f32[16,32,256]{2,1,0:T(8,128)S(1)} custom-call(f32[31]{0:T(128)S(1)} %copy-done.5, f32[15,32,256]{2,1,0:T(8,128)S(1)} %get-tuple-element.46.refs_4_.refs_0_, f32[15,32,256]{2,1,0:T(8,128)S(1)} %get-tuple-element.47.refs_1_, f32[15,32,256]{2,1,0:T(8,128)S(1)} %collective-permute-done.8.refs_2_, ...), custom_call_target="tpu_custom_call" | custom-call | flops 99999997952 | bytes 350000000 | tf_op jit(solution)/shard_map/pallas_call | solution.py:364
  61.9 0.0 collective-permute-done.7.refs_0_
  61.9 2.3 %shard_map.63 = (f32[16,64,256]{2,1,0:T(8,128)S(1)}, f32[16,64,256]{2,1,0:T(8,128)S(1)}, f32[16,32,256]{2,1,0:T(8,128)S(1)}, f32[15,16,256]{2,1,0:T(8,128)S(1)}, f32[15,16,256]{2,1,0:T(8,128)S(1)}) custom-call(f32[16,32,256]{2,1,0:T(8,128)S(1)} %collective-permute-done.7.refs_0_, f32[16,32,256]{2,1,0:T(8,128)S(1)} %shard_map.62.refs_1_, ...), custom_call_target="tpu_custom_call" | custom-call | flops 1000000000 | bytes 3500000 | tf_op jit(solution)/shard_map/pallas_call | solution.py:408
  64.1 0.8 collective-permute-start.10
  65.0 4.0 %collective-permute-start.13 = (f32[15,16,256]{2,1,0:T(8,128)S(1)}, f32[15,16,256]{2,1,0:T(8,128)S(1)}, u32[]{:S(2)}, u32[]{:S(2)}) collective-permute-start(f32[15,16,256]{2,1,0:T(8,128)S(1)} %get-tuple-element.56.refs_1_), channel_id=1, source_target_pairs={{0,1},{1,2},{2,3},{4,5},{5,6},{6,7},{8,9},{9,10},{10,11},{12,13},{... | collective-permute-start | bytes 737288 | tf_op jit(solution)/shard_map/ppermute | solution.py:423
  68.9 1.3 %collective-permute-start.14 = (f32[15,16,256]{2,1,0:T(8,128)S(1)}, f32[15,16,256]{2,1,0:T(8,128)S(1)}, u32[]{:S(2)}, u32[]{:S(2)}) collective-permute-start(f32[15,16,256]{2,1,0:T(8,128)S(1)} %get-tuple-element.57.refs_0_), channel_id=1, source_target_pairs={{1,0},{2,1},{3,2},{5,4},{6,5},{7,6},{9,8},{10,9},{11,10},{13,12},{... | collective-permute-start | bytes 737288 | tf_op jit(solution)/shard_map/ppermute | solution.py:424
  70.2 1.4 %collective-permute-done.10.next_ref = f32[16,32,256]{2,1,0:T(8,128)S(1)} collective-permute-done((f32[16,32,256]{2,1,0:T(8,128)S(1)}, f32[16,32,256]{2,1,0:T(8,128)S(1)}, u32[]{:S(2)}, u32[]{:S(2)}) %collective-permute-start.10) | collective-permute-done | bytes 524320 | tf_op jit(solution)/shard_map/ppermute | solution.py:430
  71.7 0.4 shard_map.64
  72.1 4.0 %collective-permute-start.11 = (f32[15,32,256]{2,1,0:T(8,128)S(1)}, f32[15,32,256]{2,1,0:T(8,128)S(1)}, u32[]{:S(2)}, u32[]{:S(2)}) collective-permute-start(f32[15,32,256]{2,1,0:T(8,128)S(1)} %get-tuple-element.55.refs_1_), channel_id=1, source_target_pairs={{0,1},{1,2},{2,3},{4,5},{5,6},{6,7},{8,9},{9,10},{10,11},{12,13},{... | collective-permute-start | bytes 1474568 | tf_op jit(solution)/shard_map/ppermute | solution.py:423
  76.1 1.3 %collective-permute-start.12 = (f32[15,32,256]{2,1,0:T(8,128)S(1)}, f32[15,32,256]{2,1,0:T(8,128)S(1)}, u32[]{:S(2)}, u32[]{:S(2)}) collective-permute-start(f32[15,32,256]{2,1,0:T(8,128)S(1)} %get-tuple-element.54.refs_0_), channel_id=1, source_target_pairs={{1,0},{2,1},{3,2},{5,4},{6,5},{7,6},{9,8},{10,9},{11,10},{13,12},{... | collective-permute-start | bytes 1474568 | tf_op jit(solution)/shard_map/ppermute | solution.py:424
  77.4 0.0 collective-permute-done.13.refs_1_.refs_2_
  77.4 1.1 collective-permute-done.14.refs_2_.refs_3_
  78.5 0.3 shard_map.65
  78.8 3.5 %collective-permute-start.17 = (f32[15,16,256]{2,1,0:T(8,128)S(1)}, f32[15,16,256]{2,1,0:T(8,128)S(1)}, u32[]{:S(2)}, u32[]{:S(2)}) collective-permute-start(f32[15,16,256]{2,1,0:T(8,128)S(1)} %get-tuple-element.61.refs_5_), channel_id=1, source_target_pairs={{0,1},{1,2},{2,3},{4,5},{5,6},{6,7},{8,9},{9,10},{10,11},{12,13},{... | collective-permute-start | bytes 737288 | tf_op jit(solution)/shard_map/ppermute | solution.py:423
  82.3 1.3 %collective-permute-start.18 = (f32[15,16,256]{2,1,0:T(8,128)S(1)}, f32[15,16,256]{2,1,0:T(8,128)S(1)}, u32[]{:S(2)}, u32[]{:S(2)}) collective-permute-start(f32[15,16,256]{2,1,0:T(8,128)S(1)} %get-tuple-element.58.refs_4_), channel_id=1, source_target_pairs={{1,0},{2,1},{3,2},{5,4},{6,5},{7,6},{9,8},{10,9},{11,10},{13,12},{... | collective-permute-start | bytes 737288 | tf_op jit(solution)/shard_map/ppermute | solution.py:424
  83.6 3.4 %collective-permute-done.11.refs_2_ = f32[15,32,256]{2,1,0:T(8,128)S(1)} collective-permute-done((f32[15,32,256]{2,1,0:T(8,128)S(1)}, f32[15,32,256]{2,1,0:T(8,128)S(1)}, u32[]{:S(2)}, u32[]{:S(2)}) %collective-permute-start.11) | collective-permute-done | bytes 491552 | tf_op jit(solution)/shard_map/ppermute | solution.py:423
  87.1 4.7 %collective-permute-done.12.refs_3_ = f32[15,32,256]{2,1,0:T(8,128)S(1)} collective-permute-done((f32[15,32,256]{2,1,0:T(8,128)S(1)}, f32[15,32,256]{2,1,0:T(8,128)S(1)}, u32[]{:S(2)}, u32[]{:S(2)}) %collective-permute-start.12) | collective-permute-done | bytes 491552 | tf_op jit(solution)/shard_map/ppermute | solution.py:424
  91.8 1.8 %shard_map.66 = (f32[15,32,256]{2,1,0:T(8,128)S(1)}, f32[15,32,256]{2,1,0:T(8,128)S(1)}) custom-call(f32[31]{0:T(128)S(1)} %copy-done.5, f32[16,64,256]{2,1,0:T(8,128)S(1)} %get-tuple-element.41.obs_ref, f32[15,32,256]{2,1,0:T(8,128)S(1)} %get-tuple-element.54.refs_0_, f32[15,32,256]{2,1,0:T(8,128)S(1)} %get-tuple-element.55.refs_1_, ...), custom_call_target="tpu_custom_call" | custom-call | flops 1000000000 | bytes 3500000 | tf_op jit(solution)/shard_map/pallas_call | solution.py:339
  93.6 3.5 %collective-permute-start.15 = (f32[15,32,256]{2,1,0:T(8,128)S(1)}, f32[15,32,256]{2,1,0:T(8,128)S(1)}, u32[]{:S(2)}, u32[]{:S(2)}) collective-permute-start(f32[15,32,256]{2,1,0:T(8,128)S(1)} %get-tuple-element.60.refs_1_), channel_id=1, source_target_pairs={{0,1},{1,2},{2,3},{4,5},{5,6},{6,7},{8,9},{9,10},{10,11},{12,13},{... | collective-permute-start | bytes 1474568 | tf_op jit(solution)/shard_map/ppermute | solution.py:423
  97.1 1.3 %collective-permute-start.16 = (f32[15,32,256]{2,1,0:T(8,128)S(1)}, f32[15,32,256]{2,1,0:T(8,128)S(1)}, u32[]{:S(2)}, u32[]{:S(2)}) collective-permute-start(f32[15,32,256]{2,1,0:T(8,128)S(1)} %get-tuple-element.59.refs_8_.refs_0_), channel_id=1, source_target_pairs={{1,0},{2,1},{3,2},{5,4},{6,5},{7,6},{9,8},{10,9},{11,10},{13,12},{... | collective-permute-start | bytes 1474568 | tf_op jit(solution)/shard_map/ppermute | solution.py:424
  98.4 0.0 collective-permute-done.17.refs_6_
  98.5 1.8 %shard_map.67 = (f32[15,32,256]{2,1,0:T(8,128)S(1)}, f32[15,32,256]{2,1,0:T(8,128)S(1)}) custom-call(f32[31]{0:T(128)S(1)} %copy-done.5, f32[16,64,256]{2,1,0:T(8,128)S(1)} %get-tuple-element.41.obs_ref, f32[15,16,256]{2,1,0:T(8,128)S(1)} %get-tuple-element.57.refs_0_, f32[15,16,256]{2,1,0:T(8,128)S(1)} %get-tuple-element.56.refs_1_, ...), custom_call_target="tpu_custom_call" | custom-call | flops 1000000000 | bytes 3500000 | tf_op jit(solution)/shard_map/pallas_call | solution.py:339
  100.3 4.6 %collective-permute-start.20 = (f32[15,32,256]{2,1,0:T(8,128)S(1)}, f32[15,32,256]{2,1,0:T(8,128)S(1)}, u32[]{:S(2)}, u32[]{:S(2)}) collective-permute-start(f32[15,32,256]{2,1,0:T(8,128)S(1)} %get-tuple-element.63.refs_1_), channel_id=1, source_target_pairs={{0,1},{1,2},{2,3},{4,5},{5,6},{6,7},{8,9},{9,10},{10,11},{12,13},{... | collective-permute-start | bytes 1474568 | tf_op jit(solution)/shard_map/ppermute | solution.py:423
  104.9 1.3 %collective-permute-start.21 = (f32[15,32,256]{2,1,0:T(8,128)S(1)}, f32[15,32,256]{2,1,0:T(8,128)S(1)}, u32[]{:S(2)}, u32[]{:S(2)}) collective-permute-start(f32[15,32,256]{2,1,0:T(8,128)S(1)} %get-tuple-element.62.refs_4_.refs_0_), channel_id=1, source_target_pairs={{1,0},{2,1},{3,2},{5,4},{6,5},{7,6},{9,8},{10,9},{11,10},{13,12},{... | collective-permute-start | bytes 1474568 | tf_op jit(solution)/shard_map/ppermute | solution.py:424
  106.2 2.5 %collective-permute-done.15.refs_2_ = f32[15,32,256]{2,1,0:T(8,128)S(1)} collective-permute-done((f32[15,32,256]{2,1,0:T(8,128)S(1)}, f32[15,32,256]{2,1,0:T(8,128)S(1)}, u32[]{:S(2)}, u32[]{:S(2)}) %collective-permute-start.15) | collective-permute-done | bytes 491552 | tf_op jit(solution)/shard_map/ppermute | solution.py:423
  108.7 4.4 %collective-permute-done.16.refs_3_ = f32[15,32,256]{2,1,0:T(8,128)S(1)} collective-permute-done((f32[15,32,256]{2,1,0:T(8,128)S(1)}, f32[15,32,256]{2,1,0:T(8,128)S(1)}, u32[]{:S(2)}, u32[]{:S(2)}) %collective-permute-start.16) | collective-permute-done | bytes 491552 | tf_op jit(solution)/shard_map/ppermute | solution.py:424
  113.1 1.7 %shard_map.68.refs_4_.refs_2_ = f32[16,32,256]{2,1,0:T(8,128)S(1)} custom-call(f32[31]{0:T(128)S(1)} %copy-done.5, f32[15,32,256]{2,1,0:T(8,128)S(1)} %get-tuple-element.59.refs_8_.refs_0_, f32[15,32,256]{2,1,0:T(8,128)S(1)} %get-tuple-element.60.refs_1_, f32[15,32,256]{2,1,0:T(8,128)S(1)} %collective-permute-done.15.refs_2_, ...), custom_call_target="tpu_custom_call" | custom-call | flops 1000000000 | bytes 3500000 | tf_op jit(solution)/shard_map/pallas_call | solution.py:364
  114.8 0.1 collective-permute-start.19
  114.9 4.0 %collective-permute-done.20.refs_2_ = f32[15,32,256]{2,1,0:T(8,128)S(1)} collective-permute-done((f32[15,32,256]{2,1,0:T(8,128)S(1)}, f32[15,32,256]{2,1,0:T(8,128)S(1)}, u32[]{:S(2)}, u32[]{:S(2)}) %collective-permute-start.20) | collective-permute-done | bytes 491552 | tf_op jit(solution)/shard_map/ppermute | solution.py:423
  118.9 4.1 %collective-permute-done.21.refs_3_ = f32[15,32,256]{2,1,0:T(8,128)S(1)} collective-permute-done((f32[15,32,256]{2,1,0:T(8,128)S(1)}, f32[15,32,256]{2,1,0:T(8,128)S(1)}, u32[]{:S(2)}, u32[]{:S(2)}) %collective-permute-start.21) | collective-permute-done | bytes 491552 | tf_op jit(solution)/shard_map/ppermute | solution.py:424
  123.0 1.8 %shard_map.69.refs_1_ = f32[16,32,256]{2,1,0:T(8,128)S(1)} custom-call(f32[31]{0:T(128)S(1)} %copy-done.5, f32[15,32,256]{2,1,0:T(8,128)S(1)} %get-tuple-element.62.refs_4_.refs_0_, f32[15,32,256]{2,1,0:T(8,128)S(1)} %get-tuple-element.63.refs_1_, f32[15,32,256]{2,1,0:T(8,128)S(1)} %collective-permute-done.20.refs_2_, ...), custom_call_target="tpu_custom_call" | custom-call | flops 99999997952 | bytes 350000000 | tf_op jit(solution)/shard_map/pallas_call | solution.py:364
  124.8 2.3 %shard_map.70 = f32[16,64,256]{2,1,0:T(8,128)} custom-call(f32[16,32,256]{2,1,0:T(8,128)S(1)} %collective-permute-done.19.refs_0_, f32[16,32,256]{2,1,0:T(8,128)S(1)} %shard_map.69.refs_1_, f32[16,32,256]{2,1,0:T(8,128)S(1)} %shard_map.68.refs_4_.refs_2_, f32[16,64,256]{2,1,0:T(8,128)S(1)} %get-tuple-element.64.refs_3_, ...), custom_call_target="tpu_custom_call" | custom-call | flops 1000000000 | bytes 3500000 | tf_op jit(solution)/shard_map/pallas_call | solution.py:408
  (9 shorter events, 0.0 us)
Async XLA Ops:
  1.1 9.1 %collective-permute-start = (f32[16,32,256]{2,1,0:T(8,128)S(1)}, f32[16,32,256]{2,1,0:T(8,128)S(1)}, u32[]{:S(2)}, u32[]{:S(2)}) collective-permute-start(f32[16,32,256]{2,1,0:T(8,128)S(1)} %slice.3), channel_id=1, source_target_pairs={{0,12},{4,0},{8,4},{12,8},{1,13},{5,1},{9,5},{13,9},{2,14},{6,2},{... | collective-permute-start | bytes 1572872 | tf_op jit(solution)/shard_map/ppermute | solution.py:430
  3.5 1.2 copy-start
  4.7 0.7 copy-start.2
  5.4 0.7 copy-start.3
  6.1 0.7 copy-start.4
  11.3 12.3 %copy-start.1 = (f32[16,64,256]{2,1,0:T(8,128)S(1)}, f32[16,64,256]{2,1,0:T(8,128)}, u32[]{:S(2)}) copy-start(f32[16,64,256]{2,1,0:T(8,128)} %refs_3_.1) | copy-start | bytes 3145732
  11.3 12.3 %copy-start.5 = (f32[31]{0:T(128)S(1)}, f32[31]{0:T(128)}, u32[]{:S(2)}) copy-start(f32[31]{0:T(128)} %tz_ref.17) | copy-start | bytes 376
  11.3 16.1 %collective-permute-start.2 = (f32[15,32,256]{2,1,0:T(8,128)S(1)}, f32[15,32,256]{2,1,0:T(8,128)S(1)}, u32[]{:S(2)}, u32[]{:S(2)}) collective-permute-start(f32[15,32,256]{2,1,0:T(8,128)S(1)} %get-tuple-element.39.refs_0_), channel_id=1, source_target_pairs={{1,0},{2,1},{3,2},{5,4},{6,5},{7,6},{9,8},{10,9},{11,10},{13,12},{... | collective-permute-start | bytes 1474568 | tf_op jit(solution)/shard_map/ppermute | solution.py:424
  12.8 16.1 %collective-permute-start.1 = (f32[15,32,256]{2,1,0:T(8,128)S(1)}, f32[15,32,256]{2,1,0:T(8,128)S(1)}, u32[]{:S(2)}, u32[]{:S(2)}) collective-permute-start(f32[15,32,256]{2,1,0:T(8,128)S(1)} %get-tuple-element.42.refs_1_), channel_id=1, source_target_pairs={{0,1},{1,2},{2,3},{4,5},{5,6},{6,7},{8,9},{9,10},{10,11},{12,13},{... | collective-permute-start | bytes 1474568 | tf_op jit(solution)/shard_map/ppermute | solution.py:423
  17.7 20.2 %collective-permute-start.6 = (f32[15,32,256]{2,1,0:T(8,128)S(1)}, f32[15,32,256]{2,1,0:T(8,128)S(1)}, u32[]{:S(2)}, u32[]{:S(2)}) collective-permute-start(f32[15,32,256]{2,1,0:T(8,128)S(1)} %get-tuple-element.40.after_ref.refs_4_.refs_0_), channel_id=1, source_target_pairs={{1,0},{2,1},{3,2},{5,4},{6,5},{7,6},{9,8},{10,9},{11,10},{13,12},{... | collective-permute-start | bytes 1474568 | tf_op jit(solution)/shard_map/ppermute | solution.py:424
  19.0 20.4 %collective-permute-start.5 = (f32[15,32,256]{2,1,0:T(8,128)S(1)}, f32[15,32,256]{2,1,0:T(8,128)S(1)}, u32[]{:S(2)}, u32[]{:S(2)}) collective-permute-start(f32[15,32,256]{2,1,0:T(8,128)S(1)} %get-tuple-element.45.refs_1_), channel_id=1, source_target_pairs={{0,1},{1,2},{2,3},{4,5},{5,6},{6,7},{8,9},{9,10},{10,11},{12,13},{... | collective-permute-start | bytes 1474568 | tf_op jit(solution)/shard_map/ppermute | solution.py:423
  30.7 19.2 %collective-permute-start.3 = (f32[15,32,256]{2,1,0:T(8,128)S(1)}, f32[15,32,256]{2,1,0:T(8,128)S(1)}, u32[]{:S(2)}, u32[]{:S(2)}) collective-permute-start(f32[15,32,256]{2,1,0:T(8,128)S(1)} %get-tuple-element.44.refs_1_), channel_id=1, source_target_pairs={{0,1},{1,2},{2,3},{4,5},{5,6},{6,7},{8,9},{9,10},{10,11},{12,13},{... | collective-permute-start | bytes 1474568 | tf_op jit(solution)/shard_map/ppermute | solution.py:423
  35.1 14.8 %collective-permute-start.4 = (f32[15,32,256]{2,1,0:T(8,128)S(1)}, f32[15,32,256]{2,1,0:T(8,128)S(1)}, u32[]{:S(2)}, u32[]{:S(2)}) collective-permute-start(f32[15,32,256]{2,1,0:T(8,128)S(1)} %get-tuple-element.43.refs_4_.refs_0_), channel_id=1, source_target_pairs={{1,0},{2,1},{3,2},{5,4},{6,5},{7,6},{9,8},{10,9},{11,10},{13,12},{... | collective-permute-start | bytes 1474568 | tf_op jit(solution)/shard_map/ppermute | solution.py:424
  41.2 18.9 %collective-permute-start.8 = (f32[15,32,256]{2,1,0:T(8,128)S(1)}, f32[15,32,256]{2,1,0:T(8,128)S(1)}, u32[]{:S(2)}, u32[]{:S(2)}) collective-permute-start(f32[15,32,256]{2,1,0:T(8,128)S(1)} %get-tuple-element.47.refs_1_), channel_id=1, source_target_pairs={{0,1},{1,2},{2,3},{4,5},{5,6},{6,7},{8,9},{9,10},{10,11},{12,13},{... | collective-permute-start | bytes 1474568 | tf_op jit(solution)/shard_map/ppermute | solution.py:423
  45.6 14.5 %collective-permute-start.9 = (f32[15,32,256]{2,1,0:T(8,128)S(1)}, f32[15,32,256]{2,1,0:T(8,128)S(1)}, u32[]{:S(2)}, u32[]{:S(2)}) collective-permute-start(f32[15,32,256]{2,1,0:T(8,128)S(1)} %get-tuple-element.46.refs_4_.refs_0_), channel_id=1, source_target_pairs={{1,0},{2,1},{3,2},{5,4},{6,5},{7,6},{9,8},{10,9},{11,10},{13,12},{... | collective-permute-start | bytes 1474568 | tf_op jit(solution)/shard_map/ppermute | solution.py:424
  51.6 10.2 %collective-permute-start.7 = (f32[16,32,256]{2,1,0:T(8,128)S(1)}, f32[16,32,256]{2,1,0:T(8,128)S(1)}, u32[]{:S(2)}, u32[]{:S(2)}) collective-permute-start(f32[16,32,256]{2,1,0:T(8,128)S(1)} %shard_map.61.refs_4_.refs_2_), channel_id=1, source_target_pairs={{0,4},{4,8},{8,12},{12,0},{1,5},{5,9},{9,13},{13,1},{2,6},{6,10},{... | collective-permute-start | bytes 1572872 | tf_op jit(solution)/shard_map/ppermute | solution.py:430
  64.1 7.5 %collective-permute-start.10 = (f32[16,32,256]{2,1,0:T(8,128)S(1)}, f32[16,32,256]{2,1,0:T(8,128)S(1)}, u32[]{:S(2)}, u32[]{:S(2)}) collective-permute-start(f32[16,32,256]{2,1,0:T(8,128)S(1)} %get-tuple-element.53), channel_id=1, source_target_pairs={{0,12},{4,0},{8,4},{12,8},{1,13},{5,1},{9,5},{13,9},{2,14},{6,2},{... | collective-permute-start | bytes 1572872 | tf_op jit(solution)/shard_map/ppermute | solution.py:430
  65.0 12.4 %collective-permute-start.13 = (f32[15,16,256]{2,1,0:T(8,128)S(1)}, f32[15,16,256]{2,1,0:T(8,128)S(1)}, u32[]{:S(2)}, u32[]{:S(2)}) collective-permute-start(f32[15,16,256]{2,1,0:T(8,128)S(1)} %get-tuple-element.56.refs_1_), channel_id=1, source_target_pairs={{0,1},{1,2},{2,3},{4,5},{5,6},{6,7},{8,9},{9,10},{10,11},{12,13},{... | collective-permute-start | bytes 737288 | tf_op jit(solution)/shard_map/ppermute | solution.py:423
  68.9 9.6 %collective-permute-start.14 = (f32[15,16,256]{2,1,0:T(8,128)S(1)}, f32[15,16,256]{2,1,0:T(8,128)S(1)}, u32[]{:S(2)}, u32[]{:S(2)}) collective-permute-start(f32[15,16,256]{2,1,0:T(8,128)S(1)} %get-tuple-element.57.refs_0_), channel_id=1, source_target_pairs={{1,0},{2,1},{3,2},{5,4},{6,5},{7,6},{9,8},{10,9},{11,10},{13,12},{... | collective-permute-start | bytes 737288 | tf_op jit(solution)/shard_map/ppermute | solution.py:424
  72.1 15.0 %collective-permute-start.11 = (f32[15,32,256]{2,1,0:T(8,128)S(1)}, f32[15,32,256]{2,1,0:T(8,128)S(1)}, u32[]{:S(2)}, u32[]{:S(2)}) collective-permute-start(f32[15,32,256]{2,1,0:T(8,128)S(1)} %get-tuple-element.55.refs_1_), channel_id=1, source_target_pairs={{0,1},{1,2},{2,3},{4,5},{5,6},{6,7},{8,9},{9,10},{10,11},{12,13},{... | collective-permute-start | bytes 1474568 | tf_op jit(solution)/shard_map/ppermute | solution.py:423
  76.1 15.7 %collective-permute-start.12 = (f32[15,32,256]{2,1,0:T(8,128)S(1)}, f32[15,32,256]{2,1,0:T(8,128)S(1)}, u32[]{:S(2)}, u32[]{:S(2)}) collective-permute-start(f32[15,32,256]{2,1,0:T(8,128)S(1)} %get-tuple-element.54.refs_0_), channel_id=1, source_target_pairs={{1,0},{2,1},{3,2},{5,4},{6,5},{7,6},{9,8},{10,9},{11,10},{13,12},{... | collective-permute-start | bytes 1474568 | tf_op jit(solution)/shard_map/ppermute | solution.py:424
  78.8 19.6 %collective-permute-start.17 = (f32[15,16,256]{2,1,0:T(8,128)S(1)}, f32[15,16,256]{2,1,0:T(8,128)S(1)}, u32[]{:S(2)}, u32[]{:S(2)}) collective-permute-start(f32[15,16,256]{2,1,0:T(8,128)S(1)} %get-tuple-element.61.refs_5_), channel_id=1, source_target_pairs={{0,1},{1,2},{2,3},{4,5},{5,6},{6,7},{8,9},{9,10},{10,11},{12,13},{... | collective-permute-start | bytes 737288 | tf_op jit(solution)/shard_map/ppermute | solution.py:423
  82.3 16.1 %collective-permute-start.18 = (f32[15,16,256]{2,1,0:T(8,128)S(1)}, f32[15,16,256]{2,1,0:T(8,128)S(1)}, u32[]{:S(2)}, u32[]{:S(2)}) collective-permute-start(f32[15,16,256]{2,1,0:T(8,128)S(1)} %get-tuple-element.58.refs_4_), channel_id=1, source_target_pairs={{1,0},{2,1},{3,2},{5,4},{6,5},{7,6},{9,8},{10,9},{11,10},{13,12},{... | collective-permute-start | bytes 737288 | tf_op jit(solution)/shard_map/ppermute | solution.py:424
  93.6 15.1 %collective-permute-start.15 = (f32[15,32,256]{2,1,0:T(8,128)S(1)}, f32[15,32,256]{2,1,0:T(8,128)S(1)}, u32[]{:S(2)}, u32[]{:S(2)}) collective-permute-start(f32[15,32,256]{2,1,0:T(8,128)S(1)} %get-tuple-element.60.refs_1_), channel_id=1, source_target_pairs={{0,1},{1,2},{2,3},{4,5},{5,6},{6,7},{8,9},{9,10},{10,11},{12,13},{... | collective-permute-start | bytes 1474568 | tf_op jit(solution)/shard_map/ppermute | solution.py:423
  97.1 15.9 %collective-permute-start.16 = (f32[15,32,256]{2,1,0:T(8,128)S(1)}, f32[15,32,256]{2,1,0:T(8,128)S(1)}, u32[]{:S(2)}, u32[]{:S(2)}) collective-permute-start(f32[15,32,256]{2,1,0:T(8,128)S(1)} %get-tuple-element.59.refs_8_.refs_0_), channel_id=1, source_target_pairs={{1,0},{2,1},{3,2},{5,4},{6,5},{7,6},{9,8},{10,9},{11,10},{13,12},{... | collective-permute-start | bytes 1474568 | tf_op jit(solution)/shard_map/ppermute | solution.py:424
  100.3 18.6 %collective-permute-start.20 = (f32[15,32,256]{2,1,0:T(8,128)S(1)}, f32[15,32,256]{2,1,0:T(8,128)S(1)}, u32[]{:S(2)}, u32[]{:S(2)}) collective-permute-start(f32[15,32,256]{2,1,0:T(8,128)S(1)} %get-tuple-element.63.refs_1_), channel_id=1, source_target_pairs={{0,1},{1,2},{2,3},{4,5},{5,6},{6,7},{8,9},{9,10},{10,11},{12,13},{... | collective-permute-start | bytes 1474568 | tf_op jit(solution)/shard_map/ppermute | solution.py:423
  104.9 18.2 %collective-permute-start.21 = (f32[15,32,256]{2,1,0:T(8,128)S(1)}, f32[15,32,256]{2,1,0:T(8,128)S(1)}, u32[]{:S(2)}, u32[]{:S(2)}) collective-permute-start(f32[15,32,256]{2,1,0:T(8,128)S(1)} %get-tuple-element.62.refs_4_.refs_0_), channel_id=1, source_target_pairs={{1,0},{2,1},{3,2},{5,4},{6,5},{7,6},{9,8},{10,9},{11,10},{13,12},{... | collective-permute-start | bytes 1474568 | tf_op jit(solution)/shard_map/ppermute | solution.py:424
  114.8 10.0 %collective-permute-start.19 = (f32[16,32,256]{2,1,0:T(8,128)S(1)}, f32[16,32,256]{2,1,0:T(8,128)S(1)}, u32[]{:S(2)}, u32[]{:S(2)}) collective-permute-start(f32[16,32,256]{2,1,0:T(8,128)S(1)} %shard_map.68.refs_4_.refs_2_), channel_id=1, source_target_pairs={{0,4},{4,8},{8,12},{12,0},{1,5},{5,9},{9,13},{13,1},{2,6},{6,10},{... | collective-permute-start | bytes 1572872 | tf_op jit(solution)/shard_map/ppermute | solution.py:430

commit v8 on v7

--- a/solution.py
+++ b/solution.py
@@ -176,7 +176,7 @@
 
 def second_kernel(
     n, radius, halo, band_ref, tx_ref, ty_ref, tz_ref, after_ref,
-    obs_ref, next_ref, ah_ref, al_ref, wx_ref, rn_ref, shifted_ref,
+    obs_ref, next_ref, ah_ref, al_ref, wx_ref, rn_ref, shifted_ref, taps_ref,
 ):
     rows, width = wx_ref.shape[2], wx_ref.shape[3]
     first_row, last_row = row_place()
@@ -188,6 +188,8 @@
     lower = jnp.logical_not(first_row) | (lanes >= halo - radius)
     upper = jnp.logical_not(last_row) | (lanes < rows - radius + halo)
     keep = ((lanes < halo) & lower) | ((lanes >= halo) & upper)
+    for k in range(2 * radius + 1):
+        taps_ref[k] = jnp.full(taps_ref.shape[1:], tz_ref[k], F32)
     for p in range(n):
         band = band_ref[p]
         sums = column_matrix(
@@ -223,8 +225,8 @@
     return pl.pallas_call(
         functools.partial(second_kernel, n, radius, halo),
         in_specs=[SMEM] * 4 + [ANY] + [VMEM] * 2,
-        out_specs=[VMEM] * 5,
-        out_shape=[a, a, w, field, field],
+        out_specs=[VMEM] * 6,
+        out_shape=[a, a, w, field, field, shape_of(2 * radius + 1, 8, 128)],
         compiler_params=PARAMS,
         cost_estimate=cost(1.0),
     )(band_index, taps_x, taps_y, taps_z, after, obs, beyond)
@@ -332,17 +334,17 @@
         refs = refs[4:]
 
 
-def depth_ratio(taps_z, obs, chunks, skip, after):
+def depth_ratio(taps_z, obs, chunks, skip, after, micro):
     n, _, columns = obs.shape
-    radius = taps_z.shape[0] // 2
+    radius = chunks[0][0].shape[0]
     send = shape_of(radius, sum(chunk[0].shape[1] for chunk in chunks), columns)
     return pl.pallas_call(
         functools.partial(ratio_kernel, n, radius, skip),
-        in_specs=[SMEM] + [VMEM] * (1 + 4 * len(chunks)) + [ANY] * len(after),
+        in_specs=[VMEM] * (2 + 4 * len(chunks)) + [ANY] * len(after),
         out_specs=[VMEM] * 2,
         out_shape=[send] * 2,
         compiler_params=PARAMS,
-        cost_estimate=cost(1.0),
+        cost_estimate=cost(micro),
     )(taps_z, obs, *(x for chunk in chunks for x in chunk), *after)
 
 
@@ -363,7 +365,7 @@
     radius, count, columns = chunk[0].shape
     return pl.pallas_call(
         functools.partial(back_kernel, n, radius),
-        in_specs=[SMEM] + [VMEM] * 4 + [ANY],
+        in_specs=[VMEM] * 5 + [ANY],
         out_specs=VMEM,
         out_shape=shape_of(n, count, columns),
         compiler_params=PARAMS,
@@ -371,8 +373,8 @@
     )(taps_z, *chunk, after)
 
 
-def update_kernel(n, last, *refs):
-    pieces, edge_ref, refs = refs[:3], refs[2], refs[3:]
+def update_kernel(n, last, count, *refs):
+    pieces, edge_ref, refs = refs[:count], refs[count - 1], refs[count:]
     est_ref, rn_ref, wa_ref, bh_ref, bl_ref = refs[:5]
     refs = refs[5:]
     rows = est_ref.shape[1]
@@ -406,7 +408,7 @@
         send = shape_of(radius, count, columns)
         out_shape += [shape_of(*est.shape), shape_of(n, halo, columns), send, send]
     return pl.pallas_call(
-        functools.partial(update_kernel, n, last),
+        functools.partial(update_kernel, n, last, len(pieces)),
         in_specs=[VMEM] * len(args),
         out_specs=[VMEM] * len(out_shape),
         out_shape=out_shape,
@@ -445,30 +447,41 @@
             v_first = depth_exchange(*first_sends)
             edge_sends = edge_blur(w, beyond, wx, (), radius)
             v_edge = depth_exchange(*edge_sends)
-            after = (edge_sends[0],) + v_first[2:]
-            inner_sends = inner_blur(w, wx, half, inner - half, radius, after, 20.0)
-            v_inner = [v_first, depth_exchange(*inner_sends)]
+            r_sends = depth_ratio(taps, shifted, [v_first], 0, (edge_sends[0],), 1.0)
+            r_inner = [depth_exchange(*r_sends)]
+            after = (r_sends[0],)
+            inner_sends = inner_blur(w, wx, half, inner - half, radius, after, 1.0)
+            v_inner = depth_exchange(*inner_sends)
         else:
             edge_sends = edge_blur(w, beyond, wx, (ah, al), radius)
             v_edge = depth_exchange(*edge_sends)
-            inner_sends = inner_blur(w, wx, 0, inner, radius, (edge_sends[0],), 1.0)
-            v_inner = [depth_exchange(*inner_sends)]
-            bh, bl, wa, rn, shifted = second_weights(
+            after = (edge_sends[0],)
+            inner_sends = inner_blur(w, wx, 0, inner, radius, after, 1.0)
+            v_inner = depth_exchange(*inner_sends)
+            r_inner = []
+            bh, bl, wa, rn, shifted, taps = second_weights(
                 band_index, taps_x, taps_y, taps_z, inner_sends[0], observed, beyond, width
             )
             adjoint = (wa, bh, bl)
+        after = (inner_sends[0],)
         r_edge = depth_exchange(
-            *depth_ratio(taps_z, shifted, [v_edge], inner, (inner_sends[0],))
+            *depth_ratio(taps, shifted, [v_edge], inner, after, 1.0 if step else 1.0)
         )
-        r_inner = depth_exchange(
-            *depth_ratio(taps_z, shifted, v_inner, 0, (r_edge[0],))
+        r_sends = depth_ratio(
+            taps, shifted, [v_inner], half if step else 0, (r_edge[0],), 1.0
         )
-        c_edge = depth_back(taps_z, r_edge, n, r_inner[0])
+        r_inner.append(depth_exchange(*r_sends))
+        after = r_sends[0]
+        c_inner = []
+        if step:
+            c_inner.append(depth_back(taps, r_inner[0], n, after, 5.0))
+            after = c_inner[0]
+        c_edge = depth_back(taps, r_edge, n, after, 1.0 if step else 1.0)
         before = ring(c_edge, 1)
-        c_inner = depth_back(taps_z, r_inner, n, c_edge, 100.0)
+        c_inner.append(depth_back(taps, r_inner[-1], n, c_edge, 100.0))
         last = step == ITERS - 1
         out = update(
-            (before, c_inner, c_edge), est, rn, adjoint,
+            (before, *c_inner, c_edge), est, rn, adjoint,
             None if last else (wx, ah, al), half, radius,
         )
         est = out[0]

time: 128 us -> 125 us (0.977)
  starting transfers between devices: 52.6 us -> 59.3 us
  waiting for transfers between devices: 43.8 us -> 38.8 us
  Pallas kernels: 26 us -> 21.6 us
    ppermute x9 -> x10, waiting for transfers between devices: 24.2 us -> 18.5 us  [depth_exchange(): zlo = lax.ppermute(high, 'slab', forward)]
    ppermute x9 -> x10, starting transfers between devices: 37.5 us -> 42.3 us  [depth_exchange(): zlo = lax.ppermute(high, 'slab', forward)]
    ppermute x4, waiting for transfers between devices: 2.63 us -> 6.48 us  [ring(): lax.ppermute(x, 'row', [(i, (i + step) % count) for i in range(count)])]
    ppermute x9 -> x10, waiting for transfers between devices: 16.9 us -> 13.8 us  [depth_exchange(): zhi = lax.ppermute(low, 'slab', backward)]
    pallas_call x6 -> x7, Pallas kernels: 11.5 us -> 9.25 us  [the longest x5 4.74 us: depth_back(): pl.pallas_call(functools.partial(back_kernel, n, radius), in_specs=[VMEM]...]
    pallas_call x4 -> x5, Pallas kernels: 7.28 us -> 5.19 us  [depth_ratio(): pl.pallas_call(functools.partial(ratio_kernel, n, radius, skip), in_specs...]
    ppermute x9 -> x10, starting transfers between devices: 11.8 us -> 13.1 us  [depth_exchange(): zhi = lax.ppermute(low, 'slab', backward)]
  transfers between devices with their start and end apart: 22 -> 24, of which waited for: 15 -> 14; matrix products, arithmetic and copies ran while one was open for 0% -> 0% of each run, Pallas kernels for 16% -> 13%
where the time goes in v8:
time: 125 us; the launch traced here: 124 us
  starting transfers between devices  59.3 us (47%)
  waiting for transfers between devices  38.8 us (31%)
  Pallas kernels  21.6 us (17%)
  local copies, waits for them, and re-layouts  4.36 us (3%)
    ppermute x10, starting transfers between devices, depth_exchange(): zlo = lax.ppermute(high, 'slab', forward)  42.3 us
    ppermute x10, waiting for transfers between devices, depth_exchange(): zlo = lax.ppermute(high, 'slab', forward)  18.5 us
    ppermute x10, waiting for transfers between devices, depth_exchange(): zhi = lax.ppermute(low, 'slab', backward)  13.8 us
    ppermute x10, starting transfers between devices, depth_exchange(): zhi = lax.ppermute(low, 'slab', backward)  13.1 us
    ppermute x4, waiting for transfers between devices, ring(): lax.ppermute(x, 'row', [(i, (i + step) % count) for i in range(count)])  6.48 us
    pallas_call x5, Pallas kernels, depth_ratio(): pl.pallas_call(functools.partial(ratio_kernel, n, radius, skip), in_specs...  5.19 us
    pallas_call x5, Pallas kernels, depth_back(): pl.pallas_call(functools.partial(back_kernel, n, radius), in_specs=[VMEM]...  4.74 us
    pallas_call x2, Pallas kernels, update(): pl.pallas_call(functools.partial(update_kernel, n, last, len(pieces)), in...  4.51 us
  transfers between devices with their start and end apart: 24, of which 14 were waited for; matrix products, arithmetic and copies ran while one was open for 0% of the time, Pallas kernels for 13%

profile of v8, /device:TPU:0, one launch (start us, length us, event | category | flops | bytes accessed | tf_op | source)
XLA Modules:
  0.0 124.4 jit_solution(2272018973333669190)
XLA Ops:
  0.0 1.1 slice.3
  1.1 2.4 %collective-permute-start = (f32[16,32,256]{2,1,0:T(8,128)S(1)}, f32[16,32,256]{2,1,0:T(8,128)S(1)}, u32[]{:S(2)}, u32[]{:S(2)}) collective-permute-start(f32[16,32,256]{2,1,0:T(8,128)S(1)} %slice.3), channel_id=1, source_target_pairs={{0,12},{4,0},{8,4},{12,8},{1,13},{5,1},{9,5},{13,9},{2,14},{6,2},{... | collective-permute-start | bytes 1572872 | tf_op jit(solution)/shard_map/ppermute | solution.py:432
  3.5 1.2 copy-done
  4.7 0.7 copy-done.2
  5.4 0.7 copy-done.3
  6.1 0.7 copy-done.4
  6.8 2.2 %shard_map.55 = (bf16[16,256,256]{2,1,0:T(8,128)(2,1)S(1)}, bf16[16,256,256]{2,1,0:T(8,128)(2,1)S(1)}, bf16[16,2,64,128]{3,2,1,0:T(8,128)(2,1)S(1)}, f32[16,64,256]{2,1,0:T(8,128)S(1)}) custom-call(s32[16]{0:T(128)S(1)} %copy-done.4, f32[16,31]{1,0:T(8,128)S(1)} %copy-done.2, f32[16,31]{1,0:T(8,128)S(1)} %copy-done.3, f32[16,64,256]{2,1,0:T(8,128)S(1)} %copy-done), custom_call_target="tpu_custom_call" | custom-call | flops 1000000000 | bytes 3500000 | tf_op jit(solution)/shard_map/pallas_call | solution.py:160
  9.0 1.2 collective-permute-done.next_ref
  10.2 1.1 shard_map.56
  11.3 0.0 copy-start.5
  11.3 1.4 %collective-permute-start.2 = (f32[15,32,256]{2,1,0:T(8,128)S(1)}, f32[15,32,256]{2,1,0:T(8,128)S(1)}, u32[]{:S(2)}, u32[]{:S(2)}) collective-permute-start(f32[15,32,256]{2,1,0:T(8,128)S(1)} %get-tuple-element.42.refs_0_), channel_id=1, source_target_pairs={{1,0},{2,1},{3,2},{5,4},{6,5},{7,6},{9,8},{10,9},{11,10},{13,12},{... | collective-permute-start | bytes 1474568 | tf_op jit(solution)/shard_map/ppermute | solution.py:426
  12.8 4.6 %collective-permute-start.1 = (f32[15,32,256]{2,1,0:T(8,128)S(1)}, f32[15,32,256]{2,1,0:T(8,128)S(1)}, u32[]{:S(2)}, u32[]{:S(2)}) collective-permute-start(f32[15,32,256]{2,1,0:T(8,128)S(1)} %get-tuple-element.46.refs_1_), channel_id=1, source_target_pairs={{0,1},{1,2},{2,3},{4,5},{5,6},{6,7},{8,9},{9,10},{10,11},{12,13},{... | collective-permute-start | bytes 1474568 | tf_op jit(solution)/shard_map/ppermute | solution.py:425
  17.3 0.4 shard_map.57
  17.7 1.3 %collective-permute-start.6 = (f32[15,32,256]{2,1,0:T(8,128)S(1)}, f32[15,32,256]{2,1,0:T(8,128)S(1)}, u32[]{:S(2)}, u32[]{:S(2)}) collective-permute-start(f32[15,32,256]{2,1,0:T(8,128)S(1)} %get-tuple-element.43.after_ref.refs_4_.refs_0_), channel_id=1, source_target_pairs={{1,0},{2,1},{3,2},{5,4},{6,5},{7,6},{9,8},{10,9},{11,10},{13,12},{... | collective-permute-start | bytes 1474568 | tf_op jit(solution)/shard_map/ppermute | solution.py:426
  19.0 4.6 %collective-permute-start.5 = (f32[15,32,256]{2,1,0:T(8,128)S(1)}, f32[15,32,256]{2,1,0:T(8,128)S(1)}, u32[]{:S(2)}, u32[]{:S(2)}) collective-permute-start(f32[15,32,256]{2,1,0:T(8,128)S(1)} %get-tuple-element.49.refs_1_), channel_id=1, source_target_pairs={{0,1},{1,2},{2,3},{4,5},{5,6},{6,7},{8,9},{9,10},{10,11},{12,13},{... | collective-permute-start | bytes 1474568 | tf_op jit(solution)/shard_map/ppermute | solution.py:425
  23.6 2.8 %shard_map.58 = (bf16[16,256,256]{2,1,0:T(8,128)(2,1)S(1)}, bf16[16,256,256]{2,1,0:T(8,128)(2,1)S(1)}, bf16[16,2,64,128]{3,2,1,0:T(8,128)(2,1)S(1)}, f32[16,64,2...) custom-call(s32[16]{0:T(128)S(1)} %copy-done.4, f32[16,31]{1,0:T(8,128)S(1)} %copy-done.2, ...), custom_call_target="tpu_custom_call" | custom-call | flops 1000000000 | bytes 3500000 | tf_op jit(solution)/shard_map/pallas_call | solution.py:225
  26.4 1.1 collective-permute-done.2.refs_3_
  27.4 1.4 %collective-permute-done.1.refs_2_ = f32[15,32,256]{2,1,0:T(8,128)S(1)} collective-permute-done((f32[15,32,256]{2,1,0:T(8,128)S(1)}, f32[15,32,256]{2,1,0:T(8,128)S(1)}, u32[]{:S(2)}, u32[]{:S(2)}) %collective-permute-start.1) | collective-permute-done | bytes 491552 | tf_op jit(solution)/shard_map/ppermute | solution.py:425
  28.8 1.3 %shard_map.59 = (f32[15,32,256]{2,1,0:T(8,128)S(1)}, f32[15,32,256]{2,1,0:T(8,128)S(1)}) custom-call(f32[31,8,128]{2,1,0:T(8,128)S(1)} %get-tuple-element.44.tz_ref, f32[16,64,256]{2,1,0:T(8,128)S(1)} %get-tuple-element.45.obs_ref, f32[15,32,256]{2,1,0:T(8,128)S(1)} %get-tuple-element.42.refs_0_, f32[15,32,256]{2,1,0:T(8,128)S(1)} %get-tuple-element.46.refs_1_, ...), custom_call_target="tpu_custom_call" | custom-call | flops 1000000000 | bytes 3500000 | tf_op jit(solution)/shard_map/pallas_call | solution.py:341
  30.1 4.4 %collective-permute-start.3 = (f32[15,32,256]{2,1,0:T(8,128)S(1)}, f32[15,32,256]{2,1,0:T(8,128)S(1)}, u32[]{:S(2)}, u32[]{:S(2)}) collective-permute-start(f32[15,32,256]{2,1,0:T(8,128)S(1)} %get-tuple-element.48.refs_1_), channel_id=1, source_target_pairs={{0,1},{1,2},{2,3},{4,5},{5,6},{6,7},{8,9},{9,10},{10,11},{12,13},{... | collective-permute-start | bytes 1474568 | tf_op jit(solution)/shard_map/ppermute | solution.py:425
  34.6 1.3 %collective-permute-start.4 = (f32[15,32,256]{2,1,0:T(8,128)S(1)}, f32[15,32,256]{2,1,0:T(8,128)S(1)}, u32[]{:S(2)}, u32[]{:S(2)}) collective-permute-start(f32[15,32,256]{2,1,0:T(8,128)S(1)} %get-tuple-element.47.refs_4_.refs_0_), channel_id=1, source_target_pairs={{1,0},{2,1},{3,2},{5,4},{6,5},{7,6},{9,8},{10,9},{11,10},{13,12},{... | collective-permute-start | bytes 1474568 | tf_op jit(solution)/shard_map/ppermute | solution.py:426
  35.9 2.0 %collective-permute-done.6.refs_3_ = f32[15,32,256]{2,1,0:T(8,128)S(1)} collective-permute-done((f32[15,32,256]{2,1,0:T(8,128)S(1)}, f32[15,32,256]{2,1,0:T(8,128)S(1)}, u32[]{:S(2)}, u32[]{:S(2)}) %collective-permute-start.6) | collective-permute-done | bytes 491552 | tf_op jit(solution)/shard_map/ppermute | solution.py:426
  37.9 1.5 %collective-permute-done.5.refs_2_ = f32[15,32,256]{2,1,0:T(8,128)S(1)} collective-permute-done((f32[15,32,256]{2,1,0:T(8,128)S(1)}, f32[15,32,256]{2,1,0:T(8,128)S(1)}, u32[]{:S(2)}, u32[]{:S(2)}) %collective-permute-start.5) | collective-permute-done | bytes 491552 | tf_op jit(solution)/shard_map/ppermute | solution.py:425
  39.4 1.3 %shard_map.60 = (f32[15,32,256]{2,1,0:T(8,128)S(1)}, f32[15,32,256]{2,1,0:T(8,128)S(1)}) custom-call(f32[31,8,128]{2,1,0:T(8,128)S(1)} %get-tuple-element.44.tz_ref, f32[16,64,256]{2,1,0:T(8,128)S(1)} %get-tuple-element.45.obs_ref, f32[15,32,256]{2,1,0:T(8,128)S(1)} %get-tuple-element.43.after_ref.refs_4_.refs_0_, ...), custom_call_target="tpu_custom_call" | custom-call | flops 1000000000 | bytes 3500000 | tf_op jit(solution)/shard_map/pallas_call | solution.py:341
  40.6 4.4 %collective-permute-start.8 = (f32[15,32,256]{2,1,0:T(8,128)S(1)}, f32[15,32,256]{2,1,0:T(8,128)S(1)}, u32[]{:S(2)}, u32[]{:S(2)}) collective-permute-start(f32[15,32,256]{2,1,0:T(8,128)S(1)} %get-tuple-element.51.refs_1_), channel_id=1, source_target_pairs={{0,1},{1,2},{2,3},{4,5},{5,6},{6,7},{8,9},{9,10},{10,11},{12,13},{... | collective-permute-start | bytes 1474568 | tf_op jit(solution)/shard_map/ppermute | solution.py:425
  45.1 1.3 %collective-permute-start.9 = (f32[15,32,256]{2,1,0:T(8,128)S(1)}, f32[15,32,256]{2,1,0:T(8,128)S(1)}, u32[]{:S(2)}, u32[]{:S(2)}) collective-permute-start(f32[15,32,256]{2,1,0:T(8,128)S(1)} %get-tuple-element.50.refs_4_.refs_0_), channel_id=1, source_target_pairs={{1,0},{2,1},{3,2},{5,4},{6,5},{7,6},{9,8},{10,9},{11,10},{13,12},{... | collective-permute-start | bytes 1474568 | tf_op jit(solution)/shard_map/ppermute | solution.py:426
  46.4 3.5 %collective-permute-done.3.refs_2_ = f32[15,32,256]{2,1,0:T(8,128)S(1)} collective-permute-done((f32[15,32,256]{2,1,0:T(8,128)S(1)}, f32[15,32,256]{2,1,0:T(8,128)S(1)}, u32[]{:S(2)}, u32[]{:S(2)}) %collective-permute-start.3) | collective-permute-done | bytes 491552 | tf_op jit(solution)/shard_map/ppermute | solution.py:425
  49.9 1.2 shard_map.61.refs_4_.refs_2_
  51.1 0.1 collective-permute-start.7
  51.1 9.0 %collective-permute-done.8.refs_2_ = f32[15,32,256]{2,1,0:T(8,128)S(1)} collective-permute-done((f32[15,32,256]{2,1,0:T(8,128)S(1)}, f32[15,32,256]{2,1,0:T(8,128)S(1)}, u32[]{:S(2)}, u32[]{:S(2)}) %collective-permute-start.8) | collective-permute-done | bytes 491552 | tf_op jit(solution)/shard_map/ppermute | solution.py:425
  60.1 0.0 collective-permute-done.9.refs_3_
  60.1 1.2 shard_map.62.refs_1_
  61.3 0.0 collective-permute-done.7.refs_0_
  61.3 2.2 %shard_map.63 = (f32[16,64,256]{2,1,0:T(8,128)S(1)}, f32[16,64,256]{2,1,0:T(8,128)S(1)}, f32[16,32,256]{2,1,0:T(8,128)S(1)}, f32[15,16,256]{2,1,0:T(8,128)S(1)}, f32[15,16,256]{2,1,0:T(8,128)S(1)}) custom-call(f32[16,32,256]{2,1,0:T(8,128)S(1)} %collective-permute-done.7.refs_0_, f32[16,32,256]{2,1,0:T(8,128)S(1)} %shard_map.62.refs_1_, ...), custom_call_target="tpu_custom_call" | custom-call | flops 1000000000 | bytes 3500000 | tf_op jit(solution)/shard_map/pallas_call | solution.py:410
  63.5 0.7 collective-permute-start.10
  64.3 4.1 %collective-permute-start.13 = (f32[15,16,256]{2,1,0:T(8,128)S(1)}, f32[15,16,256]{2,1,0:T(8,128)S(1)}, u32[]{:S(2)}, u32[]{:S(2)}) collective-permute-start(f32[15,16,256]{2,1,0:T(8,128)S(1)} %get-tuple-element.61.refs_1_), channel_id=1, source_target_pairs={{0,1},{1,2},{2,3},{4,5},{5,6},{6,7},{8,9},{9,10},{10,11},{12,13},{... | collective-permute-start | bytes 737288 | tf_op jit(solution)/shard_map/ppermute | solution.py:425
  68.4 1.3 %collective-permute-start.14 = (f32[15,16,256]{2,1,0:T(8,128)S(1)}, f32[15,16,256]{2,1,0:T(8,128)S(1)}, u32[]{:S(2)}, u32[]{:S(2)}) collective-permute-start(f32[15,16,256]{2,1,0:T(8,128)S(1)} %get-tuple-element.60.refs_0_), channel_id=1, source_target_pairs={{1,0},{2,1},{3,2},{5,4},{6,5},{7,6},{9,8},{10,9},{11,10},{13,12},{... | collective-permute-start | bytes 737288 | tf_op jit(solution)/shard_map/ppermute | solution.py:426
  69.7 1.3 %collective-permute-done.10.next_ref = f32[16,32,256]{2,1,0:T(8,128)S(1)} collective-permute-done((f32[16,32,256]{2,1,0:T(8,128)S(1)}, f32[16,32,256]{2,1,0:T(8,128)S(1)}, u32[]{:S(2)}, u32[]{:S(2)}) %collective-permute-start.10) | collective-permute-done | bytes 524320 | tf_op jit(solution)/shard_map/ppermute | solution.py:432
  71.0 0.4 shard_map.64
  71.4 4.1 %collective-permute-start.11 = (f32[15,32,256]{2,1,0:T(8,128)S(1)}, f32[15,32,256]{2,1,0:T(8,128)S(1)}, u32[]{:S(2)}, u32[]{:S(2)}) collective-permute-start(f32[15,32,256]{2,1,0:T(8,128)S(1)} %get-tuple-element.59.refs_1_), channel_id=1, source_target_pairs={{0,1},{1,2},{2,3},{4,5},{5,6},{6,7},{8,9},{9,10},{10,11},{12,13},{... | collective-permute-start | bytes 1474568 | tf_op jit(solution)/shard_map/ppermute | solution.py:425
  75.5 1.3 %collective-permute-start.12 = (f32[15,32,256]{2,1,0:T(8,128)S(1)}, f32[15,32,256]{2,1,0:T(8,128)S(1)}, u32[]{:S(2)}, u32[]{:S(2)}) collective-permute-start(f32[15,32,256]{2,1,0:T(8,128)S(1)} %get-tuple-element.58.refs_4_.refs_0_), channel_id=1, source_target_pairs={{1,0},{2,1},{3,2},{5,4},{6,5},{7,6},{9,8},{10,9},{11,10},{13,12},{... | collective-permute-start | bytes 1474568 | tf_op jit(solution)/shard_map/ppermute | solution.py:426
  76.8 1.1 collective-permute-done.14.refs_3_
  77.9 0.6 shard_map.65
  78.6 0.3 shard_map.66
  78.9 3.5 %collective-permute-start.19 = (f32[15,16,256]{2,1,0:T(8,128)S(1)}, f32[15,16,256]{2,1,0:T(8,128)S(1)}, u32[]{:S(2)}, u32[]{:S(2)}) collective-permute-start(f32[15,16,256]{2,1,0:T(8,128)S(1)} %get-tuple-element.67.refs_1_), channel_id=1, source_target_pairs={{0,1},{1,2},{2,3},{4,5},{5,6},{6,7},{8,9},{9,10},{10,11},{12,13},{... | collective-permute-start | bytes 737288 | tf_op jit(solution)/shard_map/ppermute | solution.py:425
  82.4 1.3 %collective-permute-start.20 = (f32[15,16,256]{2,1,0:T(8,128)S(1)}, f32[15,16,256]{2,1,0:T(8,128)S(1)}, u32[]{:S(2)}, u32[]{:S(2)}) collective-permute-start(f32[15,16,256]{2,1,0:T(8,128)S(1)} %get-tuple-element.63.refs_4_.refs_0_), channel_id=1, source_target_pairs={{1,0},{2,1},{3,2},{5,4},{6,5},{7,6},{9,8},{10,9},{11,10},{13,12},{... | collective-permute-start | bytes 737288 | tf_op jit(solution)/shard_map/ppermute | solution.py:426
  83.7 4.6 %collective-permute-start.17 = (f32[15,16,256]{2,1,0:T(8,128)S(1)}, f32[15,16,256]{2,1,0:T(8,128)S(1)}, u32[]{:S(2)}, u32[]{:S(2)}) collective-permute-start(f32[15,16,256]{2,1,0:T(8,128)S(1)} %get-tuple-element.66.refs_1_), channel_id=1, source_target_pairs={{0,1},{1,2},{2,3},{4,5},{5,6},{6,7},{8,9},{9,10},{10,11},{12,13},{... | collective-permute-start | bytes 737288 | tf_op jit(solution)/shard_map/ppermute | solution.py:425
  88.3 1.3 %collective-permute-start.18 = (f32[15,16,256]{2,1,0:T(8,128)S(1)}, f32[15,16,256]{2,1,0:T(8,128)S(1)}, u32[]{:S(2)}, u32[]{:S(2)}) collective-permute-start(f32[15,16,256]{2,1,0:T(8,128)S(1)} %get-tuple-element.62.refs_0_), channel_id=1, source_target_pairs={{1,0},{2,1},{3,2},{5,4},{6,5},{7,6},{9,8},{10,9},{11,10},{13,12},{... | collective-permute-start | bytes 737288 | tf_op jit(solution)/shard_map/ppermute | solution.py:426
  89.6 1.6 %collective-permute-done.12.refs_3_ = f32[15,32,256]{2,1,0:T(8,128)S(1)} collective-permute-done((f32[15,32,256]{2,1,0:T(8,128)S(1)}, f32[15,32,256]{2,1,0:T(8,128)S(1)}, u32[]{:S(2)}, u32[]{:S(2)}) %collective-permute-start.12) | collective-permute-done | bytes 491552 | tf_op jit(solution)/shard_map/ppermute | solution.py:426
  91.2 1.3 %shard_map.67 = (f32[15,32,256]{2,1,0:T(8,128)S(1)}, f32[15,32,256]{2,1,0:T(8,128)S(1)}) custom-call(f32[31,8,128]{2,1,0:T(8,128)S(1)} %get-tuple-element.44.tz_ref, f32[16,64,256]{2,1,0:T(8,128)S(1)} %get-tuple-element.45.obs_ref, f32[15,32,256]{2,1,0:T(8,128)S(1)} %get-tuple-element.58.refs_4_.refs_0_, f32[15,32,256]{2,1,0:T(8,128)S(1)} %get-tuple-element.59.refs_1_, ...), custom_call_target="tpu_custom_call" | custom-call | flops 1000000000 | bytes 3500000 | tf_op jit(solution)/shard_map/pallas_call | solution.py:341
  92.5 3.5 %collective-permute-start.15 = (f32[15,32,256]{2,1,0:T(8,128)S(1)}, f32[15,32,256]{2,1,0:T(8,128)S(1)}, u32[]{:S(2)}, u32[]{:S(2)}) collective-permute-start(f32[15,32,256]{2,1,0:T(8,128)S(1)} %get-tuple-element.65.refs_1_), channel_id=1, source_target_pairs={{0,1},{1,2},{2,3},{4,5},{5,6},{6,7},{8,9},{9,10},{10,11},{12,13},{... | collective-permute-start | bytes 1474568 | tf_op jit(solution)/shard_map/ppermute | solution.py:425
  96.1 1.3 %collective-permute-start.16 = (f32[15,32,256]{2,1,0:T(8,128)S(1)}, f32[15,32,256]{2,1,0:T(8,128)S(1)}, u32[]{:S(2)}, u32[]{:S(2)}) collective-permute-start(f32[15,32,256]{2,1,0:T(8,128)S(1)} %get-tuple-element.64.refs_4_.refs_0_), channel_id=1, source_target_pairs={{1,0},{2,1},{3,2},{5,4},{6,5},{7,6},{9,8},{10,9},{11,10},{13,12},{... | collective-permute-start | bytes 1474568 | tf_op jit(solution)/shard_map/ppermute | solution.py:426
  97.4 0.7 shard_map.68
  98.0 4.6 %collective-permute-start.22 = (f32[15,16,256]{2,1,0:T(8,128)S(1)}, f32[15,16,256]{2,1,0:T(8,128)S(1)}, u32[]{:S(2)}, u32[]{:S(2)}) collective-permute-start(f32[15,16,256]{2,1,0:T(8,128)S(1)} %get-tuple-element.69.refs_1_), channel_id=1, source_target_pairs={{0,1},{1,2},{2,3},{4,5},{5,6},{6,7},{8,9},{9,10},{10,11},{12,13},{... | collective-permute-start | bytes 737288 | tf_op jit(solution)/shard_map/ppermute | solution.py:425
  102.6 1.3 %collective-permute-start.23 = (f32[15,16,256]{2,1,0:T(8,128)S(1)}, f32[15,16,256]{2,1,0:T(8,128)S(1)}, u32[]{:S(2)}, u32[]{:S(2)}) collective-permute-start(f32[15,16,256]{2,1,0:T(8,128)S(1)} %get-tuple-element.68.refs_4_.refs_0_), channel_id=1, source_target_pairs={{1,0},{2,1},{3,2},{5,4},{6,5},{7,6},{9,8},{10,9},{11,10},{13,12},{... | collective-permute-start | bytes 737288 | tf_op jit(solution)/shard_map/ppermute | solution.py:426
  103.9 0.6 shard_map.69.refs_4_.refs_1_
  104.5 3.1 %collective-permute-done.15.refs_2_ = f32[15,32,256]{2,1,0:T(8,128)S(1)} collective-permute-done((f32[15,32,256]{2,1,0:T(8,128)S(1)}, f32[15,32,256]{2,1,0:T(8,128)S(1)}, u32[]{:S(2)}, u32[]{:S(2)}) %collective-permute-start.15) | collective-permute-done | bytes 491552 | tf_op jit(solution)/shard_map/ppermute | solution.py:425
  107.7 4.6 %collective-permute-done.16.refs_3_ = f32[15,32,256]{2,1,0:T(8,128)S(1)} collective-permute-done((f32[15,32,256]{2,1,0:T(8,128)S(1)}, f32[15,32,256]{2,1,0:T(8,128)S(1)}, u32[]{:S(2)}, u32[]{:S(2)}) %collective-permute-start.16) | collective-permute-done | bytes 491552 | tf_op jit(solution)/shard_map/ppermute | solution.py:426
  112.3 1.2 shard_map.70.refs_4_.refs_3_
  113.5 0.7 collective-permute-start.21
  114.2 3.4 %collective-permute-done.23.refs_3_ = f32[15,16,256]{2,1,0:T(8,128)S(1)} collective-permute-done((f32[15,16,256]{2,1,0:T(8,128)S(1)}, f32[15,16,256]{2,1,0:T(8,128)S(1)}, u32[]{:S(2)}, u32[]{:S(2)}) %collective-permute-start.23) | collective-permute-done | bytes 245792 | tf_op jit(solution)/shard_map/ppermute | solution.py:426
  117.6 0.6 shard_map.71.refs_2_
  118.2 4.0 %collective-permute-done.21.refs_0_ = f32[16,32,256]{2,1,0:T(8,128)S(1)} collective-permute-done((f32[16,32,256]{2,1,0:T(8,128)S(1)}, f32[16,32,256]{2,1,0:T(8,128)S(1)}, u32[]{:S(2)}, u32[]{:S(2)}) %collective-permute-start.21) | collective-permute-done | bytes 524320 | tf_op jit(solution)/shard_map/ppermute | solution.py:432
  122.1 2.3 %shard_map.72 = f32[16,64,256]{2,1,0:T(8,128)} custom-call(f32[16,32,256]{2,1,0:T(8,128)S(1)} %collective-permute-done.21.refs_0_, f32[16,16,256]{2,1,0:T(8,128)S(1)} %shard_map.69.refs_4_.refs_1_, f32[16,16,256]{2,1,0:T(8,128)S(1)} %shard_map.71.refs_2_, f32[16,32,256]{2,1,0:T(8,128)S(1)} %shard_map.70.refs_4_.refs_3_, ...), custom_call_target="tpu_custom_call" | custom-call | flops 1000000000 | bytes 3500000 | tf_op jit(solution)/shard_map/pallas_call | solution.py:410
  (15 shorter events, 0.0 us)
Async XLA Ops:
  1.1 9.1 %collective-permute-start = (f32[16,32,256]{2,1,0:T(8,128)S(1)}, f32[16,32,256]{2,1,0:T(8,128)S(1)}, u32[]{:S(2)}, u32[]{:S(2)}) collective-permute-start(f32[16,32,256]{2,1,0:T(8,128)S(1)} %slice.3), channel_id=1, source_target_pairs={{0,12},{4,0},{8,4},{12,8},{1,13},{5,1},{9,5},{13,9},{2,14},{6,2},{... | collective-permute-start | bytes 1572872 | tf_op jit(solution)/shard_map/ppermute | solution.py:432
  3.5 1.2 copy-start
  4.7 0.7 copy-start.2
  5.4 0.7 copy-start.3
  6.1 0.7 copy-start.4
  11.3 12.3 %copy-start.1 = (f32[16,64,256]{2,1,0:T(8,128)S(1)}, f32[16,64,256]{2,1,0:T(8,128)}, u32[]{:S(2)}) copy-start(f32[16,64,256]{2,1,0:T(8,128)} %refs_3_.1) | copy-start | bytes 3145732
  11.3 12.3 %copy-start.5 = (f32[31]{0:T(128)S(1)}, f32[31]{0:T(128)}, u32[]{:S(2)}) copy-start(f32[31]{0:T(128)} %tz_ref.1) | copy-start | bytes 376
  11.3 16.1 %collective-permute-start.2 = (f32[15,32,256]{2,1,0:T(8,128)S(1)}, f32[15,32,256]{2,1,0:T(8,128)S(1)}, u32[]{:S(2)}, u32[]{:S(2)}) collective-permute-start(f32[15,32,256]{2,1,0:T(8,128)S(1)} %get-tuple-element.42.refs_0_), channel_id=1, source_target_pairs={{1,0},{2,1},{3,2},{5,4},{6,5},{7,6},{9,8},{10,9},{11,10},{13,12},{... | collective-permute-start | bytes 1474568 | tf_op jit(solution)/shard_map/ppermute | solution.py:426
  12.8 16.1 %collective-permute-start.1 = (f32[15,32,256]{2,1,0:T(8,128)S(1)}, f32[15,32,256]{2,1,0:T(8,128)S(1)}, u32[]{:S(2)}, u32[]{:S(2)}) collective-permute-start(f32[15,32,256]{2,1,0:T(8,128)S(1)} %get-tuple-element.46.refs_1_), channel_id=1, source_target_pairs={{0,1},{1,2},{2,3},{4,5},{5,6},{6,7},{8,9},{9,10},{10,11},{12,13},{... | collective-permute-start | bytes 1474568 | tf_op jit(solution)/shard_map/ppermute | solution.py:425
  17.7 20.2 %collective-permute-start.6 = (f32[15,32,256]{2,1,0:T(8,128)S(1)}, f32[15,32,256]{2,1,0:T(8,128)S(1)}, u32[]{:S(2)}, u32[]{:S(2)}) collective-permute-start(f32[15,32,256]{2,1,0:T(8,128)S(1)} %get-tuple-element.43.after_ref.refs_4_.refs_0_), channel_id=1, source_target_pairs={{1,0},{2,1},{3,2},{5,4},{6,5},{7,6},{9,8},{10,9},{11,10},{13,12},{... | collective-permute-start | bytes 1474568 | tf_op jit(solution)/shard_map/ppermute | solution.py:426
  19.0 20.4 %collective-permute-start.5 = (f32[15,32,256]{2,1,0:T(8,128)S(1)}, f32[15,32,256]{2,1,0:T(8,128)S(1)}, u32[]{:S(2)}, u32[]{:S(2)}) collective-permute-start(f32[15,32,256]{2,1,0:T(8,128)S(1)} %get-tuple-element.49.refs_1_), channel_id=1, source_target_pairs={{0,1},{1,2},{2,3},{4,5},{5,6},{6,7},{8,9},{9,10},{10,11},{12,13},{... | collective-permute-start | bytes 1474568 | tf_op jit(solution)/shard_map/ppermute | solution.py:425
  30.1 19.8 %collective-permute-start.3 = (f32[15,32,256]{2,1,0:T(8,128)S(1)}, f32[15,32,256]{2,1,0:T(8,128)S(1)}, u32[]{:S(2)}, u32[]{:S(2)}) collective-permute-start(f32[15,32,256]{2,1,0:T(8,128)S(1)} %get-tuple-element.48.refs_1_), channel_id=1, source_target_pairs={{0,1},{1,2},{2,3},{4,5},{5,6},{6,7},{8,9},{9,10},{10,11},{12,13},{... | collective-permute-start | bytes 1474568 | tf_op jit(solution)/shard_map/ppermute | solution.py:425
  34.6 15.3 %collective-permute-start.4 = (f32[15,32,256]{2,1,0:T(8,128)S(1)}, f32[15,32,256]{2,1,0:T(8,128)S(1)}, u32[]{:S(2)}, u32[]{:S(2)}) collective-permute-start(f32[15,32,256]{2,1,0:T(8,128)S(1)} %get-tuple-element.47.refs_4_.refs_0_), channel_id=1, source_target_pairs={{1,0},{2,1},{3,2},{5,4},{6,5},{7,6},{9,8},{10,9},{11,10},{13,12},{... | collective-permute-start | bytes 1474568 | tf_op jit(solution)/shard_map/ppermute | solution.py:426
  40.6 19.5 %collective-permute-start.8 = (f32[15,32,256]{2,1,0:T(8,128)S(1)}, f32[15,32,256]{2,1,0:T(8,128)S(1)}, u32[]{:S(2)}, u32[]{:S(2)}) collective-permute-start(f32[15,32,256]{2,1,0:T(8,128)S(1)} %get-tuple-element.51.refs_1_), channel_id=1, source_target_pairs={{0,1},{1,2},{2,3},{4,5},{5,6},{6,7},{8,9},{9,10},{10,11},{12,13},{... | collective-permute-start | bytes 1474568 | tf_op jit(solution)/shard_map/ppermute | solution.py:425
  45.1 15.0 %collective-permute-start.9 = (f32[15,32,256]{2,1,0:T(8,128)S(1)}, f32[15,32,256]{2,1,0:T(8,128)S(1)}, u32[]{:S(2)}, u32[]{:S(2)}) collective-permute-start(f32[15,32,256]{2,1,0:T(8,128)S(1)} %get-tuple-element.50.refs_4_.refs_0_), channel_id=1, source_target_pairs={{1,0},{2,1},{3,2},{5,4},{6,5},{7,6},{9,8},{10,9},{11,10},{13,12},{... | collective-permute-start | bytes 1474568 | tf_op jit(solution)/shard_map/ppermute | solution.py:426
  51.1 10.2 %collective-permute-start.7 = (f32[16,32,256]{2,1,0:T(8,128)S(1)}, f32[16,32,256]{2,1,0:T(8,128)S(1)}, u32[]{:S(2)}, u32[]{:S(2)}) collective-permute-start(f32[16,32,256]{2,1,0:T(8,128)S(1)} %shard_map.61.refs_4_.refs_2_), channel_id=1, source_target_pairs={{0,4},{4,8},{8,12},{12,0},{1,5},{5,9},{9,13},{13,1},{2,6},{6,10},{... | collective-permute-start | bytes 1572872 | tf_op jit(solution)/shard_map/ppermute | solution.py:432
  63.5 7.4 %collective-permute-start.10 = (f32[16,32,256]{2,1,0:T(8,128)S(1)}, f32[16,32,256]{2,1,0:T(8,128)S(1)}, u32[]{:S(2)}, u32[]{:S(2)}) collective-permute-start(f32[16,32,256]{2,1,0:T(8,128)S(1)} %get-tuple-element.57), channel_id=1, source_target_pairs={{0,12},{4,0},{8,4},{12,8},{1,13},{5,1},{9,5},{13,9},{2,14},{6,2},{... | collective-permute-start | bytes 1572872 | tf_op jit(solution)/shard_map/ppermute | solution.py:432
  64.3 12.5 %collective-permute-start.13 = (f32[15,16,256]{2,1,0:T(8,128)S(1)}, f32[15,16,256]{2,1,0:T(8,128)S(1)}, u32[]{:S(2)}, u32[]{:S(2)}) collective-permute-start(f32[15,16,256]{2,1,0:T(8,128)S(1)} %get-tuple-element.61.refs_1_), channel_id=1, source_target_pairs={{0,1},{1,2},{2,3},{4,5},{5,6},{6,7},{8,9},{9,10},{10,11},{12,13},{... | collective-permute-start | bytes 737288 | tf_op jit(solution)/shard_map/ppermute | solution.py:425
  68.4 9.6 %collective-permute-start.14 = (f32[15,16,256]{2,1,0:T(8,128)S(1)}, f32[15,16,256]{2,1,0:T(8,128)S(1)}, u32[]{:S(2)}, u32[]{:S(2)}) collective-permute-start(f32[15,16,256]{2,1,0:T(8,128)S(1)} %get-tuple-element.60.refs_0_), channel_id=1, source_target_pairs={{1,0},{2,1},{3,2},{5,4},{6,5},{7,6},{9,8},{10,9},{11,10},{13,12},{... | collective-permute-start | bytes 737288 | tf_op jit(solution)/shard_map/ppermute | solution.py:426
  71.4 16.9 %collective-permute-start.11 = (f32[15,32,256]{2,1,0:T(8,128)S(1)}, f32[15,32,256]{2,1,0:T(8,128)S(1)}, u32[]{:S(2)}, u32[]{:S(2)}) collective-permute-start(f32[15,32,256]{2,1,0:T(8,128)S(1)} %get-tuple-element.59.refs_1_), channel_id=1, source_target_pairs={{0,1},{1,2},{2,3},{4,5},{5,6},{6,7},{8,9},{9,10},{10,11},{12,13},{... | collective-permute-start | bytes 1474568 | tf_op jit(solution)/shard_map/ppermute | solution.py:425
  75.5 15.7 %collective-permute-start.12 = (f32[15,32,256]{2,1,0:T(8,128)S(1)}, f32[15,32,256]{2,1,0:T(8,128)S(1)}, u32[]{:S(2)}, u32[]{:S(2)}) collective-permute-start(f32[15,32,256]{2,1,0:T(8,128)S(1)} %get-tuple-element.58.refs_4_.refs_0_), channel_id=1, source_target_pairs={{1,0},{2,1},{3,2},{5,4},{6,5},{7,6},{9,8},{10,9},{11,10},{13,12},{... | collective-permute-start | bytes 1474568 | tf_op jit(solution)/shard_map/ppermute | solution.py:426
  78.9 17.1 %collective-permute-start.19 = (f32[15,16,256]{2,1,0:T(8,128)S(1)}, f32[15,16,256]{2,1,0:T(8,128)S(1)}, u32[]{:S(2)}, u32[]{:S(2)}) collective-permute-start(f32[15,16,256]{2,1,0:T(8,128)S(1)} %get-tuple-element.67.refs_1_), channel_id=1, source_target_pairs={{0,1},{1,2},{2,3},{4,5},{5,6},{6,7},{8,9},{9,10},{10,11},{12,13},{... | collective-permute-start | bytes 737288 | tf_op jit(solution)/shard_map/ppermute | solution.py:425
  82.4 15.0 %collective-permute-start.20 = (f32[15,16,256]{2,1,0:T(8,128)S(1)}, f32[15,16,256]{2,1,0:T(8,128)S(1)}, u32[]{:S(2)}, u32[]{:S(2)}) collective-permute-start(f32[15,16,256]{2,1,0:T(8,128)S(1)} %get-tuple-element.63.refs_4_.refs_0_), channel_id=1, source_target_pairs={{1,0},{2,1},{3,2},{5,4},{6,5},{7,6},{9,8},{10,9},{11,10},{13,12},{... | collective-permute-start | bytes 737288 | tf_op jit(solution)/shard_map/ppermute | solution.py:426
  83.7 18.9 %collective-permute-start.17 = (f32[15,16,256]{2,1,0:T(8,128)S(1)}, f32[15,16,256]{2,1,0:T(8,128)S(1)}, u32[]{:S(2)}, u32[]{:S(2)}) collective-permute-start(f32[15,16,256]{2,1,0:T(8,128)S(1)} %get-tuple-element.66.refs_1_), channel_id=1, source_target_pairs={{0,1},{1,2},{2,3},{4,5},{5,6},{6,7},{8,9},{9,10},{10,11},{12,13},{... | collective-permute-start | bytes 737288 | tf_op jit(solution)/shard_map/ppermute | solution.py:425
  88.3 15.6 %collective-permute-start.18 = (f32[15,16,256]{2,1,0:T(8,128)S(1)}, f32[15,16,256]{2,1,0:T(8,128)S(1)}, u32[]{:S(2)}, u32[]{:S(2)}) collective-permute-start(f32[15,16,256]{2,1,0:T(8,128)S(1)} %get-tuple-element.62.refs_0_), channel_id=1, source_target_pairs={{1,0},{2,1},{3,2},{5,4},{6,5},{7,6},{9,8},{10,9},{11,10},{13,12},{... | collective-permute-start | bytes 737288 | tf_op jit(solution)/shard_map/ppermute | solution.py:426
  92.5 15.1 %collective-permute-start.15 = (f32[15,32,256]{2,1,0:T(8,128)S(1)}, f32[15,32,256]{2,1,0:T(8,128)S(1)}, u32[]{:S(2)}, u32[]{:S(2)}) collective-permute-start(f32[15,32,256]{2,1,0:T(8,128)S(1)} %get-tuple-element.65.refs_1_), channel_id=1, source_target_pairs={{0,1},{1,2},{2,3},{4,5},{5,6},{6,7},{8,9},{9,10},{10,11},{12,13},{... | collective-permute-start | bytes 1474568 | tf_op jit(solution)/shard_map/ppermute | solution.py:425
  96.1 16.2 %collective-permute-start.16 = (f32[15,32,256]{2,1,0:T(8,128)S(1)}, f32[15,32,256]{2,1,0:T(8,128)S(1)}, u32[]{:S(2)}, u32[]{:S(2)}) collective-permute-start(f32[15,32,256]{2,1,0:T(8,128)S(1)} %get-tuple-element.64.refs_4_.refs_0_), channel_id=1, source_target_pairs={{1,0},{2,1},{3,2},{5,4},{6,5},{7,6},{9,8},{10,9},{11,10},{13,12},{... | collective-permute-start | bytes 1474568 | tf_op jit(solution)/shard_map/ppermute | solution.py:426
  98.0 16.2 %collective-permute-start.22 = (f32[15,16,256]{2,1,0:T(8,128)S(1)}, f32[15,16,256]{2,1,0:T(8,128)S(1)}, u32[]{:S(2)}, u32[]{:S(2)}) collective-permute-start(f32[15,16,256]{2,1,0:T(8,128)S(1)} %get-tuple-element.69.refs_1_), channel_id=1, source_target_pairs={{0,1},{1,2},{2,3},{4,5},{5,6},{6,7},{8,9},{9,10},{10,11},{12,13},{... | collective-permute-start | bytes 737288 | tf_op jit(solution)/shard_map/ppermute | solution.py:425
  102.6 14.9 %collective-permute-start.23 = (f32[15,16,256]{2,1,0:T(8,128)S(1)}, f32[15,16,256]{2,1,0:T(8,128)S(1)}, u32[]{:S(2)}, u32[]{:S(2)}) collective-permute-start(f32[15,16,256]{2,1,0:T(8,128)S(1)} %get-tuple-element.68.refs_4_.refs_0_), channel_id=1, source_target_pairs={{1,0},{2,1},{3,2},{5,4},{6,5},{7,6},{9,8},{10,9},{11,10},{13,12},{... | collective-permute-start | bytes 737288 | tf_op jit(solution)/shard_map/ppermute | solution.py:426
  113.5 8.7 %collective-permute-start.21 = (f32[16,32,256]{2,1,0:T(8,128)S(1)}, f32[16,32,256]{2,1,0:T(8,128)S(1)}, u32[]{:S(2)}, u32[]{:S(2)}) collective-permute-start(f32[16,32,256]{2,1,0:T(8,128)S(1)} %shard_map.70.refs_4_.refs_3_), channel_id=1, source_target_pairs={{0,4},{4,8},{8,12},{12,0},{1,5},{5,9},{9,13},{13,1},{2,6},{6,10},{... | collective-permute-start | bytes 1572872 | tf_op jit(solution)/shard_map/ppermute | solution.py:432

commit v9 on v8

--- a/solution.py
+++ b/solution.py
@@ -373,46 +373,103 @@
     )(taps_z, *chunk, after)
 
 
-def update_kernel(n, last, count, *refs):
-    pieces, edge_ref, refs = refs[:count], refs[count - 1], refs[count:]
-    est_ref, rn_ref, wa_ref, bh_ref, bl_ref = refs[:5]
-    refs = refs[5:]
-    rows = est_ref.shape[1]
-    halo = edge_ref.shape[1]
-    used = rows + halo
-    u_ref, refs = refs[-1], refs[:-1]
-    if last:
-        (out_ref,) = refs
-    else:
-        wx_ref, ah_ref, al_ref, out_ref, w_ref, top_ref, low_ref, high_ref = refs
+def adjoint_rows(pieces, wa_ref, b_refs, est_ref, rn_ref, part, u_ref, store):
+    n = est_ref.shape[0]
+    used = sum(piece.shape[1] for piece in pieces)
     for p in range(n):
         c_hi, c_lo = split(jnp.concatenate([piece[p] for piece in pieces], axis=0))
-        u_ref[p] = blur_rows(wa_ref[p, 0, :, :used], wa_ref[p, 1, :, :used], c_hi, c_lo)
-    for p in range(n):
-        u = blur_columns(u_ref[p], bh_ref[p], bl_ref[p])
-        out_ref[p] = est_ref[p] * u * rn_ref[p]
-    if not last:
-        all_columns(lambda p: out_ref[p], (ah_ref, al_ref), w_ref)
-        for p in range(n):
-            top_ref[p] = w_ref[p, :halo]
-        own_rows(w_ref, wx_ref, low_ref, high_ref)
+        w_hi, w_lo = wa_ref[p, 0, part, :used], wa_ref[p, 1, part, :used]
+        u_ref[p] = blur_rows(w_hi, w_lo, c_hi, c_lo)
+    for p in range(n):
+        u = blur_columns(u_ref[p], b_refs[0][p], b_refs[1][p])
+        store(p, est_ref[p, part] * u * rn_ref[p, part])
+
+
+def update_kernel(count, *refs):
+    pieces, refs = refs[:count], refs[count:]
+    est_ref, rn_ref, wa_ref, bh_ref, bl_ref, wx_ref, ah_ref, al_ref = refs[:8]
+    out_ref, w_ref, top_ref, low_ref, high_ref, u_ref = refs[8:]
+    n, rows, _ = est_ref.shape
+
+    def store(p, value):
+        out_ref[p] = value
+
+    part = slice(0, rows)
+    adjoint_rows(pieces, wa_ref, (bh_ref, bl_ref), est_ref, rn_ref, part, u_ref, store)
+    all_columns(lambda p: out_ref[p], (ah_ref, al_ref), w_ref)
+    for p in range(n):
+        top_ref[p] = w_ref[p, : top_ref.shape[1]]
+    own_rows(w_ref, wx_ref, low_ref, high_ref)
 
 
 def update(pieces, est, rn, adjoint, forward, count, radius):
     n, rows, columns = est.shape
     halo = pieces[0].shape[1]
-    last = forward is None
-    args = [*pieces, est, rn, *adjoint] + ([] if last else [*forward])
-    out_shape = [shape_of(*est.shape)]
-    if not last:
-        send = shape_of(radius, count, columns)
-        out_shape += [shape_of(*est.shape), shape_of(n, halo, columns), send, send]
-    return pl.pallas_call(
-        functools.partial(update_kernel, n, last, len(pieces)),
+    args = [*pieces, est, rn, *adjoint, *forward]
+    send = shape_of(radius, count, columns)
+    field = shape_of(*est.shape)
+    return pl.pallas_call(
+        functools.partial(update_kernel, len(pieces)),
         in_specs=[VMEM] * len(args),
-        out_specs=[VMEM] * len(out_shape),
-        out_shape=out_shape,
+        out_specs=[VMEM] * 5,
+        out_shape=[field, field, shape_of(n, halo, columns), send, send],
         scratch_shapes=[pltpu.VMEM(est.shape, F32)],
+        compiler_params=PARAMS,
+        cost_estimate=cost(1.0),
+    )(*args)
+
+
+def far_kernel(count, *refs):
+    pieces, refs = refs[:count], refs[count:]
+    est_ref, rn_ref, wa_ref, bh_ref, bl_ref, far_ref, zero_ref, u_ref = refs
+    rows, halo = est_ref.shape[1], zero_ref.shape[1]
+    zero_ref[...] = jnp.zeros(zero_ref.shape, F32)
+
+    def store(p, value):
+        far_ref[p] = value
+
+    pieces = (zero_ref, *pieces)
+    part = slice(halo, rows)
+    adjoint_rows(pieces, wa_ref, (bh_ref, bl_ref), est_ref, rn_ref, part, u_ref, store)
+
+
+def far_rows(pieces, halo, est, rn, adjoint):
+    n, rows, columns = est.shape
+    args = [*pieces, est, rn, *adjoint]
+    far = (n, rows - halo, columns)
+    return pl.pallas_call(
+        functools.partial(far_kernel, len(pieces)),
+        in_specs=[VMEM] * len(args),
+        out_specs=VMEM,
+        out_shape=shape_of(*far),
+        scratch_shapes=[pltpu.VMEM((n, halo, columns), F32), pltpu.VMEM(far, F32)],
+        compiler_params=PARAMS,
+        cost_estimate=cost(100.0),
+    )(*args)
+
+
+def near_kernel(count, *refs):
+    pieces, refs = refs[:count], refs[count:]
+    est_ref, rn_ref, wa_ref, bh_ref, bl_ref, far_ref, out_ref, u_ref = refs
+    halo = u_ref.shape[1]
+    out_ref[:, halo:] = far_ref[...]
+
+    def store(p, value):
+        out_ref[p, :halo] = value
+
+    part = slice(0, halo)
+    adjoint_rows(pieces, wa_ref, (bh_ref, bl_ref), est_ref, rn_ref, part, u_ref, store)
+
+
+def near_rows(pieces, est, rn, adjoint, far):
+    n, _, columns = est.shape
+    args = [*pieces, est, rn, *adjoint, far]
+    return pl.pallas_call(
+        functools.partial(near_kernel, len(pieces)),
+        in_specs=[VMEM] * len(args),
+        out_specs=VMEM,
+        out_shape=shape_of(*est.shape),
+        scratch_shapes=[pltpu.VMEM((n, pieces[0].shape[1], columns), F32)],
         compiler_params=PARAMS,
         cost_estimate=cost(1.0),
     )(*args)
@@ -447,7 +504,7 @@
             v_first = depth_exchange(*first_sends)
             edge_sends = edge_blur(w, beyond, wx, (), radius)
             v_edge = depth_exchange(*edge_sends)
-            r_sends = depth_ratio(taps, shifted, [v_first], 0, (edge_sends[0],), 1.0)
+            r_sends = depth_ratio(taps, shifted, [v_first], 0, (edge_sends[0],), 20.0)
             r_inner = [depth_exchange(*r_sends)]
             after = (r_sends[0],)
             inner_sends = inner_blur(w, wx, half, inner - half, radius, after, 1.0)
@@ -467,28 +524,26 @@
         r_edge = depth_exchange(
             *depth_ratio(taps, shifted, [v_edge], inner, after, 1.0 if step else 1.0)
         )
+        after, c_inner = r_edge[0], []
+        if step:
+            after = depth_back(taps, r_inner[0], n, after, 5.0)
+            c_inner.append(after)
         r_sends = depth_ratio(
-            taps, shifted, [v_inner], half if step else 0, (r_edge[0],), 1.0
+            taps, shifted, [v_inner], half if step else 0, (after,), 1.0 if step else 1.0
         )
         r_inner.append(depth_exchange(*r_sends))
         after = r_sends[0]
-        c_inner = []
-        if step:
-            c_inner.append(depth_back(taps, r_inner[0], n, after, 5.0))
-            after = c_inner[0]
         c_edge = depth_back(taps, r_edge, n, after, 1.0 if step else 1.0)
         before = ring(c_edge, 1)
         c_inner.append(depth_back(taps, r_inner[-1], n, c_edge, 100.0))
-        last = step == ITERS - 1
-        out = update(
-            (before, *c_inner, c_edge), est, rn, adjoint,
-            None if last else (wx, ah, al), half, radius,
+        own = (*c_inner, c_edge)
+        if step == ITERS - 1:
+            far = far_rows(own, halo, est, rn, adjoint)
+            return near_rows((before, *own), est, rn, adjoint, far)
+        est, w, top, *first_sends = update(
+            (before, *own), est, rn, adjoint, (wx, ah, al), half, radius
         )
-        est = out[0]
-        if not last:
-            w, top, *first_sends = out[1:]
-            beyond = ring(top, -1)
-    return est
+        beyond = ring(top, -1)
 
 
 def solution(mesh):

time: 125 us -> 127 us (1.016)
  Pallas kernels: 21.6 us -> 25.5 us
    pallas_call x2 -> x3, Pallas kernels: 4.51 us -> 7.64 us  [the longest x1 3.26 us: near_rows(): pl.pallas_call(functools.partial(near_kernel, len(pieces)), in_specs=[VME...]
    ppermute x10, waiting for transfers between devices: 13.8 us -> 16.9 us  [depth_exchange(): zhi = lax.ppermute(low, 'slab', backward)]
    ppermute x10, waiting for transfers between devices: 18.5 us -> 15.8 us  [depth_exchange(): zlo = lax.ppermute(high, 'slab', forward)]
  transfers between devices with their start and end apart: 24 -> 24, of which waited for: 14 -> 15; matrix products, arithmetic and copies ran while one was open for 0% -> 0% of each run, Pallas kernels for 13% -> 15%
where the time goes in v9:
time: 127 us; the launch traced here: 126 us
  starting transfers between devices  58.1 us (46%)
  waiting for transfers between devices  38.1 us (30%)
  Pallas kernels  25.5 us (20%)
  local copies, waits for them, and re-layouts  4.36 us (3%)
    ppermute x10, starting transfers between devices, depth_exchange(): zlo = lax.ppermute(high, 'slab', forward)  41.2 us
    ppermute x10, waiting for transfers between devices, depth_exchange(): zhi = lax.ppermute(low, 'slab', backward)  16.9 us
    ppermute x10, waiting for transfers between devices, depth_exchange(): zlo = lax.ppermute(high, 'slab', forward)  15.8 us
    ppermute x10, starting transfers between devices, depth_exchange(): zhi = lax.ppermute(low, 'slab', backward)  13.1 us
    pallas_call x5, Pallas kernels, depth_back(): pl.pallas_call(functools.partial(back_kernel, n, radius), in_specs=[VMEM]...  5.53 us
    ppermute x4, waiting for transfers between devices, ring(): lax.ppermute(x, 'row', [(i, (i + step) % count) for i in range(count)])  5.38 us
    pallas_call x5, Pallas kernels, depth_ratio(): pl.pallas_call(functools.partial(ratio_kernel, n, radius, skip), in_specs...  5.17 us
    ppermute x4, starting transfers between devices, ring(): lax.ppermute(x, 'row', [(i, (i + step) % count) for i in range(count)])  3.85 us
  transfers between devices with their start and end apart: 24, of which 15 were waited for; matrix products, arithmetic and copies ran while one was open for 0% of the time, Pallas kernels for 15%

profile of v9, /device:TPU:0, one launch (start us, length us, event | category | flops | bytes accessed | tf_op | source)
XLA Modules:
  0.0 126.4 jit_solution(4016026814222877587)
XLA Ops:
  0.0 1.1 slice.3
  1.1 2.4 %collective-permute-start = (f32[16,32,256]{2,1,0:T(8,128)S(1)}, f32[16,32,256]{2,1,0:T(8,128)S(1)}, u32[]{:S(2)}, u32[]{:S(2)}) collective-permute-start(f32[16,32,256]{2,1,0:T(8,128)S(1)} %slice.3), channel_id=1, source_target_pairs={{0,12},{4,0},{8,4},{12,8},{1,13},{5,1},{9,5},{13,9},{2,14},{6,2},{... | collective-permute-start | bytes 1572872 | tf_op jit(solution)/shard_map/ppermute | solution.py:489
  3.5 1.2 copy-done
  4.7 0.7 copy-done.2
  5.4 0.7 copy-done.3
  6.1 0.7 copy-done.4
  6.8 2.2 %shard_map.55 = (bf16[16,256,256]{2,1,0:T(8,128)(2,1)S(1)}, bf16[16,256,256]{2,1,0:T(8,128)(2,1)S(1)}, bf16[16,2,64,128]{3,2,1,0:T(8,128)(2,1)S(1)}, f32[16,64,256]{2,1,0:T(8,128)S(1)}) custom-call(s32[16]{0:T(128)S(1)} %copy-done.4, f32[16,31]{1,0:T(8,128)S(1)} %copy-done.2, f32[16,31]{1,0:T(8,128)S(1)} %copy-done.3, f32[16,64,256]{2,1,0:T(8,128)S(1)} %copy-done), custom_call_target="tpu_custom_call" | custom-call | flops 1000000000 | bytes 3500000 | tf_op jit(solution)/shard_map/pallas_call | solution.py:160
  9.0 1.2 collective-permute-done.next_ref
  10.2 1.1 shard_map.56
  11.3 0.0 copy-start.5
  11.3 1.4 %collective-permute-start.2 = (f32[15,32,256]{2,1,0:T(8,128)S(1)}, f32[15,32,256]{2,1,0:T(8,128)S(1)}, u32[]{:S(2)}, u32[]{:S(2)}) collective-permute-start(f32[15,32,256]{2,1,0:T(8,128)S(1)} %get-tuple-element.42.refs_0_), channel_id=1, source_target_pairs={{1,0},{2,1},{3,2},{5,4},{6,5},{7,6},{9,8},{10,9},{11,10},{13,12},{... | collective-permute-start | bytes 1474568 | tf_op jit(solution)/shard_map/ppermute | solution.py:483
  12.8 4.6 %collective-permute-start.1 = (f32[15,32,256]{2,1,0:T(8,128)S(1)}, f32[15,32,256]{2,1,0:T(8,128)S(1)}, u32[]{:S(2)}, u32[]{:S(2)}) collective-permute-start(f32[15,32,256]{2,1,0:T(8,128)S(1)} %get-tuple-element.46.refs_1_), channel_id=1, source_target_pairs={{0,1},{1,2},{2,3},{4,5},{5,6},{6,7},{8,9},{9,10},{10,11},{12,13},{... | collective-permute-start | bytes 1474568 | tf_op jit(solution)/shard_map/ppermute | solution.py:482
  17.3 0.4 shard_map.57
  17.7 1.3 %collective-permute-start.6 = (f32[15,32,256]{2,1,0:T(8,128)S(1)}, f32[15,32,256]{2,1,0:T(8,128)S(1)}, u32[]{:S(2)}, u32[]{:S(2)}) collective-permute-start(f32[15,32,256]{2,1,0:T(8,128)S(1)} %get-tuple-element.43.after_ref.refs_4_.refs_0_), channel_id=1, source_target_pairs={{1,0},{2,1},{3,2},{5,4},{6,5},{7,6},{9,8},{10,9},{11,10},{13,12},{... | collective-permute-start | bytes 1474568 | tf_op jit(solution)/shard_map/ppermute | solution.py:483
  19.0 4.6 %collective-permute-start.5 = (f32[15,32,256]{2,1,0:T(8,128)S(1)}, f32[15,32,256]{2,1,0:T(8,128)S(1)}, u32[]{:S(2)}, u32[]{:S(2)}) collective-permute-start(f32[15,32,256]{2,1,0:T(8,128)S(1)} %get-tuple-element.49.refs_1_), channel_id=1, source_target_pairs={{0,1},{1,2},{2,3},{4,5},{5,6},{6,7},{8,9},{9,10},{10,11},{12,13},{... | collective-permute-start | bytes 1474568 | tf_op jit(solution)/shard_map/ppermute | solution.py:482
  23.6 2.8 %shard_map.58 = (bf16[16,256,256]{2,1,0:T(8,128)(2,1)S(1)}, bf16[16,256,256]{2,1,0:T(8,128)(2,1)S(1)}, bf16[16,2,64,128]{3,2,1,0:T(8,128)(2,1)S(1)}, f32[16,64,2...) custom-call(s32[16]{0:T(128)S(1)} %copy-done.4, f32[16,31]{1,0:T(8,128)S(1)} %copy-done.2, ...), custom_call_target="tpu_custom_call" | custom-call | flops 1000000000 | bytes 3500000 | tf_op jit(solution)/shard_map/pallas_call | solution.py:225
  26.4 1.1 collective-permute-done.2.refs_3_
  27.4 1.4 %collective-permute-done.1.refs_2_ = f32[15,32,256]{2,1,0:T(8,128)S(1)} collective-permute-done((f32[15,32,256]{2,1,0:T(8,128)S(1)}, f32[15,32,256]{2,1,0:T(8,128)S(1)}, u32[]{:S(2)}, u32[]{:S(2)}) %collective-permute-start.1) | collective-permute-done | bytes 491552 | tf_op jit(solution)/shard_map/ppermute | solution.py:482
  28.8 1.3 %shard_map.59 = (f32[15,32,256]{2,1,0:T(8,128)S(1)}, f32[15,32,256]{2,1,0:T(8,128)S(1)}) custom-call(f32[31,8,128]{2,1,0:T(8,128)S(1)} %get-tuple-element.44.tz_ref, f32[16,64,256]{2,1,0:T(8,128)S(1)} %get-tuple-element.45.obs_ref, f32[15,32,256]{2,1,0:T(8,128)S(1)} %get-tuple-element.42.refs_0_, f32[15,32,256]{2,1,0:T(8,128)S(1)} %get-tuple-element.46.refs_1_, ...), custom_call_target="tpu_custom_call" | custom-call | flops 1000000000 | bytes 3500000 | tf_op jit(solution)/shard_map/pallas_call | solution.py:341
  30.1 4.4 %collective-permute-start.3 = (f32[15,32,256]{2,1,0:T(8,128)S(1)}, f32[15,32,256]{2,1,0:T(8,128)S(1)}, u32[]{:S(2)}, u32[]{:S(2)}) collective-permute-start(f32[15,32,256]{2,1,0:T(8,128)S(1)} %get-tuple-element.48.refs_1_), channel_id=1, source_target_pairs={{0,1},{1,2},{2,3},{4,5},{5,6},{6,7},{8,9},{9,10},{10,11},{12,13},{... | collective-permute-start | bytes 1474568 | tf_op jit(solution)/shard_map/ppermute | solution.py:482
  34.6 1.3 %collective-permute-start.4 = (f32[15,32,256]{2,1,0:T(8,128)S(1)}, f32[15,32,256]{2,1,0:T(8,128)S(1)}, u32[]{:S(2)}, u32[]{:S(2)}) collective-permute-start(f32[15,32,256]{2,1,0:T(8,128)S(1)} %get-tuple-element.47.refs_4_.refs_0_), channel_id=1, source_target_pairs={{1,0},{2,1},{3,2},{5,4},{6,5},{7,6},{9,8},{10,9},{11,10},{13,12},{... | collective-permute-start | bytes 1474568 | tf_op jit(solution)/shard_map/ppermute | solution.py:483
  35.9 2.0 %collective-permute-done.6.refs_3_ = f32[15,32,256]{2,1,0:T(8,128)S(1)} collective-permute-done((f32[15,32,256]{2,1,0:T(8,128)S(1)}, f32[15,32,256]{2,1,0:T(8,128)S(1)}, u32[]{:S(2)}, u32[]{:S(2)}) %collective-permute-start.6) | collective-permute-done | bytes 491552 | tf_op jit(solution)/shard_map/ppermute | solution.py:483
  37.9 1.5 %collective-permute-done.5.refs_2_ = f32[15,32,256]{2,1,0:T(8,128)S(1)} collective-permute-done((f32[15,32,256]{2,1,0:T(8,128)S(1)}, f32[15,32,256]{2,1,0:T(8,128)S(1)}, u32[]{:S(2)}, u32[]{:S(2)}) %collective-permute-start.5) | collective-permute-done | bytes 491552 | tf_op jit(solution)/shard_map/ppermute | solution.py:482
  39.4 1.3 %shard_map.60 = (f32[15,32,256]{2,1,0:T(8,128)S(1)}, f32[15,32,256]{2,1,0:T(8,128)S(1)}) custom-call(f32[31,8,128]{2,1,0:T(8,128)S(1)} %get-tuple-element.44.tz_ref, f32[16,64,256]{2,1,0:T(8,128)S(1)} %get-tuple-element.45.obs_ref, f32[15,32,256]{2,1,0:T(8,128)S(1)} %get-tuple-element.43.after_ref.refs_4_.refs_0_, ...), custom_call_target="tpu_custom_call" | custom-call | flops 1000000000 | bytes 3500000 | tf_op jit(solution)/shard_map/pallas_call | solution.py:341
  40.6 4.4 %collective-permute-start.8 = (f32[15,32,256]{2,1,0:T(8,128)S(1)}, f32[15,32,256]{2,1,0:T(8,128)S(1)}, u32[]{:S(2)}, u32[]{:S(2)}) collective-permute-start(f32[15,32,256]{2,1,0:T(8,128)S(1)} %get-tuple-element.51.refs_1_), channel_id=1, source_target_pairs={{0,1},{1,2},{2,3},{4,5},{5,6},{6,7},{8,9},{9,10},{10,11},{12,13},{... | collective-permute-start | bytes 1474568 | tf_op jit(solution)/shard_map/ppermute | solution.py:482
  45.1 1.3 %collective-permute-start.9 = (f32[15,32,256]{2,1,0:T(8,128)S(1)}, f32[15,32,256]{2,1,0:T(8,128)S(1)}, u32[]{:S(2)}, u32[]{:S(2)}) collective-permute-start(f32[15,32,256]{2,1,0:T(8,128)S(1)} %get-tuple-element.50.refs_4_.refs_0_), channel_id=1, source_target_pairs={{1,0},{2,1},{3,2},{5,4},{6,5},{7,6},{9,8},{10,9},{11,10},{13,12},{... | collective-permute-start | bytes 1474568 | tf_op jit(solution)/shard_map/ppermute | solution.py:483
  46.4 3.5 %collective-permute-done.3.refs_2_ = f32[15,32,256]{2,1,0:T(8,128)S(1)} collective-permute-done((f32[15,32,256]{2,1,0:T(8,128)S(1)}, f32[15,32,256]{2,1,0:T(8,128)S(1)}, u32[]{:S(2)}, u32[]{:S(2)}) %collective-permute-start.3) | collective-permute-done | bytes 491552 | tf_op jit(solution)/shard_map/ppermute | solution.py:482
  49.9 1.2 shard_map.61.refs_4_.refs_2_
  51.1 0.1 collective-permute-start.7
  51.1 9.0 %collective-permute-done.8.refs_2_ = f32[15,32,256]{2,1,0:T(8,128)S(1)} collective-permute-done((f32[15,32,256]{2,1,0:T(8,128)S(1)}, f32[15,32,256]{2,1,0:T(8,128)S(1)}, u32[]{:S(2)}, u32[]{:S(2)}) %collective-permute-start.8) | collective-permute-done | bytes 491552 | tf_op jit(solution)/shard_map/ppermute | solution.py:482
  60.1 1.2 shard_map.62.refs_1_
  61.3 2.2 %shard_map.63 = (f32[16,64,256]{2,1,0:T(8,128)S(1)}, f32[16,64,256]{2,1,0:T(8,128)S(1)}, f32[16,32,256]{2,1,0:T(8,128)S(1)}, f32[15,16,256]{2,1,0:T(8,128)S(1)}, f32[15,16,256]{2,1,0:T(8,128)S(1)}) custom-call(f32[16,32,256]{2,1,0:T(8,128)S(1)} %collective-permute-done.7.refs_0_, f32[16,32,256]{2,1,0:T(8,128)S(1)} %shard_map.62.refs_1_, ...), custom_call_target="tpu_custom_call" | custom-call | flops 1000000000 | bytes 3500000 | tf_op jit(solution)/shard_map/pallas_call | solution.py:411
  63.5 0.7 collective-permute-start.10
  64.3 4.1 %collective-permute-start.13 = (f32[15,16,256]{2,1,0:T(8,128)S(1)}, f32[15,16,256]{2,1,0:T(8,128)S(1)}, u32[]{:S(2)}, u32[]{:S(2)}) collective-permute-start(f32[15,16,256]{2,1,0:T(8,128)S(1)} %get-tuple-element.61.refs_1_), channel_id=1, source_target_pairs={{0,1},{1,2},{2,3},{4,5},{5,6},{6,7},{8,9},{9,10},{10,11},{12,13},{... | collective-permute-start | bytes 737288 | tf_op jit(solution)/shard_map/ppermute | solution.py:482
  68.4 1.3 %collective-permute-start.14 = (f32[15,16,256]{2,1,0:T(8,128)S(1)}, f32[15,16,256]{2,1,0:T(8,128)S(1)}, u32[]{:S(2)}, u32[]{:S(2)}) collective-permute-start(f32[15,16,256]{2,1,0:T(8,128)S(1)} %get-tuple-element.60.refs_0_), channel_id=1, source_target_pairs={{1,0},{2,1},{3,2},{5,4},{6,5},{7,6},{9,8},{10,9},{11,10},{13,12},{... | collective-permute-start | bytes 737288 | tf_op jit(solution)/shard_map/ppermute | solution.py:483
  69.7 1.3 %collective-permute-done.10.next_ref = f32[16,32,256]{2,1,0:T(8,128)S(1)} collective-permute-done((f32[16,32,256]{2,1,0:T(8,128)S(1)}, f32[16,32,256]{2,1,0:T(8,128)S(1)}, u32[]{:S(2)}, u32[]{:S(2)}) %collective-permute-start.10) | collective-permute-done | bytes 524320 | tf_op jit(solution)/shard_map/ppermute | solution.py:489
  71.0 0.4 shard_map.64
  71.4 4.1 %collective-permute-start.11 = (f32[15,32,256]{2,1,0:T(8,128)S(1)}, f32[15,32,256]{2,1,0:T(8,128)S(1)}, u32[]{:S(2)}, u32[]{:S(2)}) collective-permute-start(f32[15,32,256]{2,1,0:T(8,128)S(1)} %get-tuple-element.59.refs_1_), channel_id=1, source_target_pairs={{0,1},{1,2},{2,3},{4,5},{5,6},{6,7},{8,9},{9,10},{10,11},{12,13},{... | collective-permute-start | bytes 1474568 | tf_op jit(solution)/shard_map/ppermute | solution.py:482
  75.5 1.3 %collective-permute-start.12 = (f32[15,32,256]{2,1,0:T(8,128)S(1)}, f32[15,32,256]{2,1,0:T(8,128)S(1)}, u32[]{:S(2)}, u32[]{:S(2)}) collective-permute-start(f32[15,32,256]{2,1,0:T(8,128)S(1)} %get-tuple-element.58.refs_4_.refs_0_), channel_id=1, source_target_pairs={{1,0},{2,1},{3,2},{5,4},{6,5},{7,6},{9,8},{10,9},{11,10},{13,12},{... | collective-permute-start | bytes 1474568 | tf_op jit(solution)/shard_map/ppermute | solution.py:483
  76.8 1.1 collective-permute-done.14.refs_3_
  77.9 0.6 shard_map.65
  78.6 3.5 %collective-permute-start.19 = (f32[15,16,256]{2,1,0:T(8,128)S(1)}, f32[15,16,256]{2,1,0:T(8,128)S(1)}, u32[]{:S(2)}, u32[]{:S(2)}) collective-permute-start(f32[15,16,256]{2,1,0:T(8,128)S(1)} %get-tuple-element.67.refs_1_), channel_id=1, source_target_pairs={{0,1},{1,2},{2,3},{4,5},{5,6},{6,7},{8,9},{9,10},{10,11},{12,13},{... | collective-permute-start | bytes 737288 | tf_op jit(solution)/shard_map/ppermute | solution.py:482
  82.1 1.3 %collective-permute-start.20 = (f32[15,16,256]{2,1,0:T(8,128)S(1)}, f32[15,16,256]{2,1,0:T(8,128)S(1)}, u32[]{:S(2)}, u32[]{:S(2)}) collective-permute-start(f32[15,16,256]{2,1,0:T(8,128)S(1)} %get-tuple-element.62.refs_0_), channel_id=1, source_target_pairs={{1,0},{2,1},{3,2},{5,4},{6,5},{7,6},{9,8},{10,9},{11,10},{13,12},{... | collective-permute-start | bytes 737288 | tf_op jit(solution)/shard_map/ppermute | solution.py:483
  83.4 0.3 shard_map.66
  83.7 4.6 %collective-permute-start.17 = (f32[15,16,256]{2,1,0:T(8,128)S(1)}, f32[15,16,256]{2,1,0:T(8,128)S(1)}, u32[]{:S(2)}, u32[]{:S(2)}) collective-permute-start(f32[15,16,256]{2,1,0:T(8,128)S(1)} %get-tuple-element.66.refs_1_), channel_id=1, source_target_pairs={{0,1},{1,2},{2,3},{4,5},{5,6},{6,7},{8,9},{9,10},{10,11},{12,13},{... | collective-permute-start | bytes 737288 | tf_op jit(solution)/shard_map/ppermute | solution.py:482
  88.3 1.3 %collective-permute-start.18 = (f32[15,16,256]{2,1,0:T(8,128)S(1)}, f32[15,16,256]{2,1,0:T(8,128)S(1)}, u32[]{:S(2)}, u32[]{:S(2)}) collective-permute-start(f32[15,16,256]{2,1,0:T(8,128)S(1)} %get-tuple-element.63.refs_4_.refs_0_), channel_id=1, source_target_pairs={{1,0},{2,1},{3,2},{5,4},{6,5},{7,6},{9,8},{10,9},{11,10},{13,12},{... | collective-permute-start | bytes 737288 | tf_op jit(solution)/shard_map/ppermute | solution.py:483
  89.6 1.7 %collective-permute-done.12.refs_3_ = f32[15,32,256]{2,1,0:T(8,128)S(1)} collective-permute-done((f32[15,32,256]{2,1,0:T(8,128)S(1)}, f32[15,32,256]{2,1,0:T(8,128)S(1)}, u32[]{:S(2)}, u32[]{:S(2)}) %collective-permute-start.12) | collective-permute-done | bytes 491552 | tf_op jit(solution)/shard_map/ppermute | solution.py:483
  91.2 1.3 %shard_map.67 = (f32[15,32,256]{2,1,0:T(8,128)S(1)}, f32[15,32,256]{2,1,0:T(8,128)S(1)}) custom-call(f32[31,8,128]{2,1,0:T(8,128)S(1)} %get-tuple-element.44.tz_ref, f32[16,64,256]{2,1,0:T(8,128)S(1)} %get-tuple-element.45.obs_ref, f32[15,32,256]{2,1,0:T(8,128)S(1)} %get-tuple-element.58.refs_4_.refs_0_, f32[15,32,256]{2,1,0:T(8,128)S(1)} %get-tuple-element.59.refs_1_, ...), custom_call_target="tpu_custom_call" | custom-call | flops 1000000000 | bytes 3500000 | tf_op jit(solution)/shard_map/pallas_call | solution.py:341
  92.5 3.5 %collective-permute-start.15 = (f32[15,32,256]{2,1,0:T(8,128)S(1)}, f32[15,32,256]{2,1,0:T(8,128)S(1)}, u32[]{:S(2)}, u32[]{:S(2)}) collective-permute-start(f32[15,32,256]{2,1,0:T(8,128)S(1)} %get-tuple-element.65.refs_1_), channel_id=1, source_target_pairs={{0,1},{1,2},{2,3},{4,5},{5,6},{6,7},{8,9},{9,10},{10,11},{12,13},{... | collective-permute-start | bytes 1474568 | tf_op jit(solution)/shard_map/ppermute | solution.py:482
  96.0 1.3 %collective-permute-start.16 = (f32[15,32,256]{2,1,0:T(8,128)S(1)}, f32[15,32,256]{2,1,0:T(8,128)S(1)}, u32[]{:S(2)}, u32[]{:S(2)}) collective-permute-start(f32[15,32,256]{2,1,0:T(8,128)S(1)} %get-tuple-element.64.refs_4_.refs_0_), channel_id=1, source_target_pairs={{1,0},{2,1},{3,2},{5,4},{6,5},{7,6},{9,8},{10,9},{11,10},{13,12},{... | collective-permute-start | bytes 1474568 | tf_op jit(solution)/shard_map/ppermute | solution.py:483
  97.3 0.6 shard_map.68.refs_4_.refs_0_.refs_1_
  97.9 3.8 %collective-permute-done.18.refs_3_ = f32[15,16,256]{2,1,0:T(8,128)S(1)} collective-permute-done((f32[15,16,256]{2,1,0:T(8,128)S(1)}, f32[15,16,256]{2,1,0:T(8,128)S(1)}, u32[]{:S(2)}, u32[]{:S(2)}) %collective-permute-start.18) | collective-permute-done | bytes 245792 | tf_op jit(solution)/shard_map/ppermute | solution.py:483
  101.8 0.6 shard_map.69
  102.4 3.5 %collective-permute-start.22 = (f32[15,16,256]{2,1,0:T(8,128)S(1)}, f32[15,16,256]{2,1,0:T(8,128)S(1)}, u32[]{:S(2)}, u32[]{:S(2)}) collective-permute-start(f32[15,16,256]{2,1,0:T(8,128)S(1)} %get-tuple-element.69.refs_1_), channel_id=1, source_target_pairs={{0,1},{1,2},{2,3},{4,5},{5,6},{6,7},{8,9},{9,10},{10,11},{12,13},{... | collective-permute-start | bytes 737288 | tf_op jit(solution)/shard_map/ppermute | solution.py:482
  105.9 1.3 %collective-permute-start.23 = (f32[15,16,256]{2,1,0:T(8,128)S(1)}, f32[15,16,256]{2,1,0:T(8,128)S(1)}, u32[]{:S(2)}, u32[]{:S(2)}) collective-permute-start(f32[15,16,256]{2,1,0:T(8,128)S(1)} %get-tuple-element.68.refs_4_.refs_0_), channel_id=1, source_target_pairs={{1,0},{2,1},{3,2},{5,4},{6,5},{7,6},{9,8},{10,9},{11,10},{13,12},{... | collective-permute-start | bytes 737288 | tf_op jit(solution)/shard_map/ppermute | solution.py:483
  107.2 0.5 collective-permute-done.15.refs_2_
  107.7 4.6 %collective-permute-done.16.refs_3_ = f32[15,32,256]{2,1,0:T(8,128)S(1)} collective-permute-done((f32[15,32,256]{2,1,0:T(8,128)S(1)}, f32[15,32,256]{2,1,0:T(8,128)S(1)}, u32[]{:S(2)}, u32[]{:S(2)}) %collective-permute-start.16) | collective-permute-done | bytes 491552 | tf_op jit(solution)/shard_map/ppermute | solution.py:483
  112.3 2.0 %shard_map.70.refs_4_.refs_2_.refs_3_ = f32[16,32,256]{2,1,0:T(8,128)} custom-call(f32[31,8,128]{2,1,0:T(8,128)S(1)} %get-tuple-element.44.tz_ref, f32[15,32,256]{2,1,0:T(8,128)S(1)} %get-tuple-element.64.refs_4_.refs_0_, f32[15,32,256]{2,1,0:T(8,128)S(1)} %get-tuple-element.65.refs_1_, f32[15,32,256]{2,1,0:T(8,128)S(1)} %collective-permute-done.15.refs_2_, ...), custom_call_target="tpu_custom_call" | custom-call | flops 1000000000 | bytes 3500000 | tf_op jit(solution)/shard_map/pallas_call | solution.py:366
  114.3 0.6 collective-permute-start.21
  114.9 2.7 %collective-permute-done.23.refs_3_ = f32[15,16,256]{2,1,0:T(8,128)S(1)} collective-permute-done((f32[15,16,256]{2,1,0:T(8,128)S(1)}, f32[15,16,256]{2,1,0:T(8,128)S(1)}, u32[]{:S(2)}, u32[]{:S(2)}) %collective-permute-start.23) | collective-permute-done | bytes 245792 | tf_op jit(solution)/shard_map/ppermute | solution.py:483
  117.6 0.6 shard_map.71.refs_1_.refs_2_
  118.2 2.1 %shard_map.72.refs_9_ = f32[16,32,256]{2,1,0:T(8,128)S(1)} custom-call(f32[16,16,256]{2,1,0:T(8,128)S(1)} %shard_map.68.refs_4_.refs_0_.refs_1_, f32[16,16,256]{2,1,0:T(8,128)S(1)} %shard_map.71.refs_1_.refs_2_, f32[16,32,256]{2,1,0:T(8,128)} %shard_map.70.refs_4_.refs_2_.refs_3_, f32[16,64,256]{2,1,0:T(8,128)S(1)} %get-tuple-element.70.refs_3_.refs_4_, ...), custom_call_target="tpu_custom_call" | custom-call | flops 99999997952 | bytes 350000000 | tf_op jit(solution)/shard_map/pallas_call | solution.py:440
  120.3 2.9 %collective-permute-done.21.refs_0_ = f32[16,32,256]{2,1,0:T(8,128)} collective-permute-done((f32[16,32,256]{2,1,0:T(8,128)}, f32[16,32,256]{2,1,0:T(8,128)}, u32[]{:S(2)}, u32[]{:S(2)}) %collective-permute-start.21) | collective-permute-done | bytes 524320 | tf_op jit(solution)/shard_map/ppermute | solution.py:489
  123.2 3.3 %shard_map.73 = f32[16,64,256]{2,1,0:T(8,128)} custom-call(f32[16,32,256]{2,1,0:T(8,128)} %collective-permute-done.21.refs_0_, f32[16,16,256]{2,1,0:T(8,128)S(1)} %shard_map.68.refs_4_.refs_0_.refs_1_, f32[16,16,256]{2,1,0:T(8,128)S(1)} %shard_map.71.refs_1_.refs_2_, f32[16,32,256]{2,1,0:T(8,128)} %shard_map.70.refs_4_.refs_2_.refs_3_, ...), custom_call_target="tpu_custom_call" | custom-call | flops 1000000000 | bytes 3500000 | tf_op jit(solution)/shard_map/pallas_call | solution.py:467
  (16 shorter events, 0.0 us)
Async XLA Ops:
  1.1 9.1 %collective-permute-start = (f32[16,32,256]{2,1,0:T(8,128)S(1)}, f32[16,32,256]{2,1,0:T(8,128)S(1)}, u32[]{:S(2)}, u32[]{:S(2)}) collective-permute-start(f32[16,32,256]{2,1,0:T(8,128)S(1)} %slice.3), channel_id=1, source_target_pairs={{0,12},{4,0},{8,4},{12,8},{1,13},{5,1},{9,5},{13,9},{2,14},{6,2},{... | collective-permute-start | bytes 1572872 | tf_op jit(solution)/shard_map/ppermute | solution.py:489
  3.5 1.2 copy-start
  4.7 0.7 copy-start.2
  5.4 0.7 copy-start.3
  6.1 0.7 copy-start.4
  11.3 12.3 %copy-start.1 = (f32[16,64,256]{2,1,0:T(8,128)S(1)}, f32[16,64,256]{2,1,0:T(8,128)}, u32[]{:S(2)}) copy-start(f32[16,64,256]{2,1,0:T(8,128)} %refs_3_.1) | copy-start | bytes 3145732
  11.3 12.3 %copy-start.5 = (f32[31]{0:T(128)S(1)}, f32[31]{0:T(128)}, u32[]{:S(2)}) copy-start(f32[31]{0:T(128)} %tz_ref.1) | copy-start | bytes 376
  11.3 16.1 %collective-permute-start.2 = (f32[15,32,256]{2,1,0:T(8,128)S(1)}, f32[15,32,256]{2,1,0:T(8,128)S(1)}, u32[]{:S(2)}, u32[]{:S(2)}) collective-permute-start(f32[15,32,256]{2,1,0:T(8,128)S(1)} %get-tuple-element.42.refs_0_), channel_id=1, source_target_pairs={{1,0},{2,1},{3,2},{5,4},{6,5},{7,6},{9,8},{10,9},{11,10},{13,12},{... | collective-permute-start | bytes 1474568 | tf_op jit(solution)/shard_map/ppermute | solution.py:483
  12.8 16.1 %collective-permute-start.1 = (f32[15,32,256]{2,1,0:T(8,128)S(1)}, f32[15,32,256]{2,1,0:T(8,128)S(1)}, u32[]{:S(2)}, u32[]{:S(2)}) collective-permute-start(f32[15,32,256]{2,1,0:T(8,128)S(1)} %get-tuple-element.46.refs_1_), channel_id=1, source_target_pairs={{0,1},{1,2},{2,3},{4,5},{5,6},{6,7},{8,9},{9,10},{10,11},{12,13},{... | collective-permute-start | bytes 1474568 | tf_op jit(solution)/shard_map/ppermute | solution.py:482
  17.7 20.2 %collective-permute-start.6 = (f32[15,32,256]{2,1,0:T(8,128)S(1)}, f32[15,32,256]{2,1,0:T(8,128)S(1)}, u32[]{:S(2)}, u32[]{:S(2)}) collective-permute-start(f32[15,32,256]{2,1,0:T(8,128)S(1)} %get-tuple-element.43.after_ref.refs_4_.refs_0_), channel_id=1, source_target_pairs={{1,0},{2,1},{3,2},{5,4},{6,5},{7,6},{9,8},{10,9},{11,10},{13,12},{... | collective-permute-start | bytes 1474568 | tf_op jit(solution)/shard_map/ppermute | solution.py:483
  19.0 20.4 %collective-permute-start.5 = (f32[15,32,256]{2,1,0:T(8,128)S(1)}, f32[15,32,256]{2,1,0:T(8,128)S(1)}, u32[]{:S(2)}, u32[]{:S(2)}) collective-permute-start(f32[15,32,256]{2,1,0:T(8,128)S(1)} %get-tuple-element.49.refs_1_), channel_id=1, source_target_pairs={{0,1},{1,2},{2,3},{4,5},{5,6},{6,7},{8,9},{9,10},{10,11},{12,13},{... | collective-permute-start | bytes 1474568 | tf_op jit(solution)/shard_map/ppermute | solution.py:482
  30.1 19.8 %collective-permute-start.3 = (f32[15,32,256]{2,1,0:T(8,128)S(1)}, f32[15,32,256]{2,1,0:T(8,128)S(1)}, u32[]{:S(2)}, u32[]{:S(2)}) collective-permute-start(f32[15,32,256]{2,1,0:T(8,128)S(1)} %get-tuple-element.48.refs_1_), channel_id=1, source_target_pairs={{0,1},{1,2},{2,3},{4,5},{5,6},{6,7},{8,9},{9,10},{10,11},{12,13},{... | collective-permute-start | bytes 1474568 | tf_op jit(solution)/shard_map/ppermute | solution.py:482
  34.6 15.3 %collective-permute-start.4 = (f32[15,32,256]{2,1,0:T(8,128)S(1)}, f32[15,32,256]{2,1,0:T(8,128)S(1)}, u32[]{:S(2)}, u32[]{:S(2)}) collective-permute-start(f32[15,32,256]{2,1,0:T(8,128)S(1)} %get-tuple-element.47.refs_4_.refs_0_), channel_id=1, source_target_pairs={{1,0},{2,1},{3,2},{5,4},{6,5},{7,6},{9,8},{10,9},{11,10},{13,12},{... | collective-permute-start | bytes 1474568 | tf_op jit(solution)/shard_map/ppermute | solution.py:483
  40.6 19.5 %collective-permute-start.8 = (f32[15,32,256]{2,1,0:T(8,128)S(1)}, f32[15,32,256]{2,1,0:T(8,128)S(1)}, u32[]{:S(2)}, u32[]{:S(2)}) collective-permute-start(f32[15,32,256]{2,1,0:T(8,128)S(1)} %get-tuple-element.51.refs_1_), channel_id=1, source_target_pairs={{0,1},{1,2},{2,3},{4,5},{5,6},{6,7},{8,9},{9,10},{10,11},{12,13},{... | collective-permute-start | bytes 1474568 | tf_op jit(solution)/shard_map/ppermute | solution.py:482
  45.1 15.0 %collective-permute-start.9 = (f32[15,32,256]{2,1,0:T(8,128)S(1)}, f32[15,32,256]{2,1,0:T(8,128)S(1)}, u32[]{:S(2)}, u32[]{:S(2)}) collective-permute-start(f32[15,32,256]{2,1,0:T(8,128)S(1)} %get-tuple-element.50.refs_4_.refs_0_), channel_id=1, source_target_pairs={{1,0},{2,1},{3,2},{5,4},{6,5},{7,6},{9,8},{10,9},{11,10},{13,12},{... | collective-permute-start | bytes 1474568 | tf_op jit(solution)/shard_map/ppermute | solution.py:483
  51.1 10.2 %collective-permute-start.7 = (f32[16,32,256]{2,1,0:T(8,128)S(1)}, f32[16,32,256]{2,1,0:T(8,128)S(1)}, u32[]{:S(2)}, u32[]{:S(2)}) collective-permute-start(f32[16,32,256]{2,1,0:T(8,128)S(1)} %shard_map.61.refs_4_.refs_2_), channel_id=1, source_target_pairs={{0,4},{4,8},{8,12},{12,0},{1,5},{5,9},{9,13},{13,1},{2,6},{6,10},{... | collective-permute-start | bytes 1572872 | tf_op jit(solution)/shard_map/ppermute | solution.py:489
  63.5 7.4 %collective-permute-start.10 = (f32[16,32,256]{2,1,0:T(8,128)S(1)}, f32[16,32,256]{2,1,0:T(8,128)S(1)}, u32[]{:S(2)}, u32[]{:S(2)}) collective-permute-start(f32[16,32,256]{2,1,0:T(8,128)S(1)} %get-tuple-element.57), channel_id=1, source_target_pairs={{0,12},{4,0},{8,4},{12,8},{1,13},{5,1},{9,5},{13,9},{2,14},{6,2},{... | collective-permute-start | bytes 1572872 | tf_op jit(solution)/shard_map/ppermute | solution.py:489
  64.3 12.5 %collective-permute-start.13 = (f32[15,16,256]{2,1,0:T(8,128)S(1)}, f32[15,16,256]{2,1,0:T(8,128)S(1)}, u32[]{:S(2)}, u32[]{:S(2)}) collective-permute-start(f32[15,16,256]{2,1,0:T(8,128)S(1)} %get-tuple-element.61.refs_1_), channel_id=1, source_target_pairs={{0,1},{1,2},{2,3},{4,5},{5,6},{6,7},{8,9},{9,10},{10,11},{12,13},{... | collective-permute-start | bytes 737288 | tf_op jit(solution)/shard_map/ppermute | solution.py:482
  68.4 9.6 %collective-permute-start.14 = (f32[15,16,256]{2,1,0:T(8,128)S(1)}, f32[15,16,256]{2,1,0:T(8,128)S(1)}, u32[]{:S(2)}, u32[]{:S(2)}) collective-permute-start(f32[15,16,256]{2,1,0:T(8,128)S(1)} %get-tuple-element.60.refs_0_), channel_id=1, source_target_pairs={{1,0},{2,1},{3,2},{5,4},{6,5},{7,6},{9,8},{10,9},{11,10},{13,12},{... | collective-permute-start | bytes 737288 | tf_op jit(solution)/shard_map/ppermute | solution.py:483
  71.4 16.9 %collective-permute-start.11 = (f32[15,32,256]{2,1,0:T(8,128)S(1)}, f32[15,32,256]{2,1,0:T(8,128)S(1)}, u32[]{:S(2)}, u32[]{:S(2)}) collective-permute-start(f32[15,32,256]{2,1,0:T(8,128)S(1)} %get-tuple-element.59.refs_1_), channel_id=1, source_target_pairs={{0,1},{1,2},{2,3},{4,5},{5,6},{6,7},{8,9},{9,10},{10,11},{12,13},{... | collective-permute-start | bytes 1474568 | tf_op jit(solution)/shard_map/ppermute | solution.py:482
  75.5 15.7 %collective-permute-start.12 = (f32[15,32,256]{2,1,0:T(8,128)S(1)}, f32[15,32,256]{2,1,0:T(8,128)S(1)}, u32[]{:S(2)}, u32[]{:S(2)}) collective-permute-start(f32[15,32,256]{2,1,0:T(8,128)S(1)} %get-tuple-element.58.refs_4_.refs_0_), channel_id=1, source_target_pairs={{1,0},{2,1},{3,2},{5,4},{6,5},{7,6},{9,8},{10,9},{11,10},{13,12},{... | collective-permute-start | bytes 1474568 | tf_op jit(solution)/shard_map/ppermute | solution.py:483
  78.6 17.4 %collective-permute-start.19 = (f32[15,16,256]{2,1,0:T(8,128)S(1)}, f32[15,16,256]{2,1,0:T(8,128)S(1)}, u32[]{:S(2)}, u32[]{:S(2)}) collective-permute-start(f32[15,16,256]{2,1,0:T(8,128)S(1)} %get-tuple-element.67.refs_1_), channel_id=1, source_target_pairs={{0,1},{1,2},{2,3},{4,5},{5,6},{6,7},{8,9},{9,10},{10,11},{12,13},{... | collective-permute-start | bytes 737288 | tf_op jit(solution)/shard_map/ppermute | solution.py:482
  82.1 15.2 %collective-permute-start.20 = (f32[15,16,256]{2,1,0:T(8,128)S(1)}, f32[15,16,256]{2,1,0:T(8,128)S(1)}, u32[]{:S(2)}, u32[]{:S(2)}) collective-permute-start(f32[15,16,256]{2,1,0:T(8,128)S(1)} %get-tuple-element.62.refs_0_), channel_id=1, source_target_pairs={{1,0},{2,1},{3,2},{5,4},{6,5},{7,6},{9,8},{10,9},{11,10},{13,12},{... | collective-permute-start | bytes 737288 | tf_op jit(solution)/shard_map/ppermute | solution.py:483
  83.7 14.2 %collective-permute-start.17 = (f32[15,16,256]{2,1,0:T(8,128)S(1)}, f32[15,16,256]{2,1,0:T(8,128)S(1)}, u32[]{:S(2)}, u32[]{:S(2)}) collective-permute-start(f32[15,16,256]{2,1,0:T(8,128)S(1)} %get-tuple-element.66.refs_1_), channel_id=1, source_target_pairs={{0,1},{1,2},{2,3},{4,5},{5,6},{6,7},{8,9},{9,10},{10,11},{12,13},{... | collective-permute-start | bytes 737288 | tf_op jit(solution)/shard_map/ppermute | solution.py:482
  88.3 13.5 %collective-permute-start.18 = (f32[15,16,256]{2,1,0:T(8,128)S(1)}, f32[15,16,256]{2,1,0:T(8,128)S(1)}, u32[]{:S(2)}, u32[]{:S(2)}) collective-permute-start(f32[15,16,256]{2,1,0:T(8,128)S(1)} %get-tuple-element.63.refs_4_.refs_0_), channel_id=1, source_target_pairs={{1,0},{2,1},{3,2},{5,4},{6,5},{7,6},{9,8},{10,9},{11,10},{13,12},{... | collective-permute-start | bytes 737288 | tf_op jit(solution)/shard_map/ppermute | solution.py:483
  92.5 15.1 %collective-permute-start.15 = (f32[15,32,256]{2,1,0:T(8,128)S(1)}, f32[15,32,256]{2,1,0:T(8,128)S(1)}, u32[]{:S(2)}, u32[]{:S(2)}) collective-permute-start(f32[15,32,256]{2,1,0:T(8,128)S(1)} %get-tuple-element.65.refs_1_), channel_id=1, source_target_pairs={{0,1},{1,2},{2,3},{4,5},{5,6},{6,7},{8,9},{9,10},{10,11},{12,13},{... | collective-permute-start | bytes 1474568 | tf_op jit(solution)/shard_map/ppermute | solution.py:482
  96.0 16.3 %collective-permute-start.16 = (f32[15,32,256]{2,1,0:T(8,128)S(1)}, f32[15,32,256]{2,1,0:T(8,128)S(1)}, u32[]{:S(2)}, u32[]{:S(2)}) collective-permute-start(f32[15,32,256]{2,1,0:T(8,128)S(1)} %get-tuple-element.64.refs_4_.refs_0_), channel_id=1, source_target_pairs={{1,0},{2,1},{3,2},{5,4},{6,5},{7,6},{9,8},{10,9},{11,10},{13,12},{... | collective-permute-start | bytes 1474568 | tf_op jit(solution)/shard_map/ppermute | solution.py:483
  102.4 12.5 %collective-permute-start.22 = (f32[15,16,256]{2,1,0:T(8,128)S(1)}, f32[15,16,256]{2,1,0:T(8,128)S(1)}, u32[]{:S(2)}, u32[]{:S(2)}) collective-permute-start(f32[15,16,256]{2,1,0:T(8,128)S(1)} %get-tuple-element.69.refs_1_), channel_id=1, source_target_pairs={{0,1},{1,2},{2,3},{4,5},{5,6},{6,7},{8,9},{9,10},{10,11},{12,13},{... | collective-permute-start | bytes 737288 | tf_op jit(solution)/shard_map/ppermute | solution.py:482
  105.9 11.7 %collective-permute-start.23 = (f32[15,16,256]{2,1,0:T(8,128)S(1)}, f32[15,16,256]{2,1,0:T(8,128)S(1)}, u32[]{:S(2)}, u32[]{:S(2)}) collective-permute-start(f32[15,16,256]{2,1,0:T(8,128)S(1)} %get-tuple-element.68.refs_4_.refs_0_), channel_id=1, source_target_pairs={{1,0},{2,1},{3,2},{5,4},{6,5},{7,6},{9,8},{10,9},{11,10},{13,12},{... | collective-permute-start | bytes 737288 | tf_op jit(solution)/shard_map/ppermute | solution.py:483
  114.3 8.9 %collective-permute-start.21 = (f32[16,32,256]{2,1,0:T(8,128)}, f32[16,32,256]{2,1,0:T(8,128)}, u32[]{:S(2)}, u32[]{:S(2)}) collective-permute-start(f32[16,32,256]{2,1,0:T(8,128)} %shard_map.70.refs_4_.refs_2_.refs_3_), channel_id=1, source_target_pairs={{0,4},{4,8},{8,12},{12,0},{1,5},{5,9},{9,13},{13,1},{2,6},{6,10},{... | collective-permute-start | bytes 1572872 | tf_op jit(solution)/shard_map/ppermute | solution.py:489

commit v10 on v8

--- a/solution.py
+++ b/solution.py
@@ -8,6 +8,7 @@
 from jax.sharding import PartitionSpec as P
 
 ITERS = 2
+GROUPS = 4
 F32 = jnp.float32
 BF16 = jnp.bfloat16
 PARAMS = pltpu.CompilerParams(vmem_limit_bytes=16 * 1024 * 1024)
@@ -348,8 +349,10 @@
     )(taps_z, obs, *(x for chunk in chunks for x in chunk), *after)
 
 
-def back_kernel(n, radius, tz_ref, *refs):
+def back_kernel(n, radius, swapped, tz_ref, *refs):
     out_ref = refs[-1]
+    if swapped:
+        refs = (*refs[:2], refs[3], refs[2])
     _, count, columns = out_ref.shape
 
     def body(start, lanes):
@@ -361,10 +364,12 @@
     tiles(count, columns, body)
 
 
-def depth_back(taps_z, chunk, n, after, micro=1.0):
+def depth_back(taps_z, chunk, n, after, micro=1.0, swapped=False):
     radius, count, columns = chunk[0].shape
-    return pl.pallas_call(
-        functools.partial(back_kernel, n, radius),
+    if swapped:
+        chunk = (*chunk[:2], chunk[3], chunk[2])
+    return pl.pallas_call(
+        functools.partial(back_kernel, n, radius, swapped),
         in_specs=[VMEM] * 5 + [ANY],
         out_specs=VMEM,
         out_shape=shape_of(n, count, columns),
@@ -380,28 +385,44 @@
     rows = est_ref.shape[1]
     halo = edge_ref.shape[1]
     used = rows + halo
-    u_ref, refs = refs[-1], refs[:-1]
     if last:
-        (out_ref,) = refs
+        out_ref, u_ref, sems = refs
     else:
-        wx_ref, ah_ref, al_ref, out_ref, w_ref, top_ref, low_ref, high_ref = refs
+        wx_ref, ah_ref, al_ref, out_ref, w_ref, top_ref, low_ref, high_ref, u_ref = refs
     for p in range(n):
         c_hi, c_lo = split(jnp.concatenate([piece[p] for piece in pieces], axis=0))
         u_ref[p] = blur_rows(wa_ref[p, 0, :, :used], wa_ref[p, 1, :, :used], c_hi, c_lo)
+    if last:
+        copies = []
+        group = up(n, GROUPS) // GROUPS
+        for first in range(0, n, group):
+            part = pl.ds(first, min(group, n - first))
+            for p in range(first, min(first + group, n)):
+                u = blur_columns(u_ref[p], bh_ref[p], bl_ref[p])
+                u_ref[p] = est_ref[p] * u * rn_ref[p]
+            copies.append(
+                pltpu.make_async_copy(
+                    u_ref.at[part], out_ref.at[part], sems.at[len(copies)]
+                )
+            )
+            copies[-1].start()
+        for copy in copies:
+            copy.wait()
+        return
     for p in range(n):
         u = blur_columns(u_ref[p], bh_ref[p], bl_ref[p])
         out_ref[p] = est_ref[p] * u * rn_ref[p]
-    if not last:
-        all_columns(lambda p: out_ref[p], (ah_ref, al_ref), w_ref)
-        for p in range(n):
-            top_ref[p] = w_ref[p, :halo]
-        own_rows(w_ref, wx_ref, low_ref, high_ref)
+    all_columns(lambda p: out_ref[p], (ah_ref, al_ref), w_ref)
+    for p in range(n):
+        top_ref[p] = w_ref[p, :halo]
+    own_rows(w_ref, wx_ref, low_ref, high_ref)
 
 
 def update(pieces, est, rn, adjoint, forward, count, radius):
     n, rows, columns = est.shape
     halo = pieces[0].shape[1]
     last = forward is None
+    sems = pltpu.SemaphoreType.DMA((GROUPS,))
     args = [*pieces, est, rn, *adjoint] + ([] if last else [*forward])
     out_shape = [shape_of(*est.shape)]
     if not last:
@@ -410,9 +431,9 @@
     return pl.pallas_call(
         functools.partial(update_kernel, n, last, len(pieces)),
         in_specs=[VMEM] * len(args),
-        out_specs=[VMEM] * len(out_shape),
+        out_specs=[ANY] if last else [VMEM] * len(out_shape),
         out_shape=out_shape,
-        scratch_shapes=[pltpu.VMEM(est.shape, F32)],
+        scratch_shapes=[pltpu.VMEM(est.shape, F32)] + [sems] * last,
         compiler_params=PARAMS,
         cost_estimate=cost(1.0),
     )(*args)
@@ -465,7 +486,7 @@
             adjoint = (wa, bh, bl)
         after = (inner_sends[0],)
         r_edge = depth_exchange(
-            *depth_ratio(taps, shifted, [v_edge], inner, after, 1.0 if step else 1.0)
+            *depth_ratio(taps, shifted, [v_edge], inner, after, 1.0),
         )
         r_sends = depth_ratio(
             taps, shifted, [v_inner], half if step else 0, (r_edge[0],), 1.0
@@ -476,7 +497,7 @@
         if step:
             c_inner.append(depth_back(taps, r_inner[0], n, after, 5.0))
             after = c_inner[0]
-        c_edge = depth_back(taps, r_edge, n, after, 1.0 if step else 1.0)
+        c_edge = depth_back(taps, r_edge, n, after, 1.0, step > 0)
         before = ring(c_edge, 1)
         c_inner.append(depth_back(taps, r_inner[-1], n, c_edge, 100.0))
         last = step == ITERS - 1

time: 125 us -> 125 us (level)
    ppermute x10, waiting for transfers between devices: 13.8 us -> 16.5 us  [depth_exchange(): zhi = lax.ppermute(low, 'slab', backward)]
    ppermute x10, waiting for transfers between devices: 18.5 us -> 15.8 us  [depth_exchange(): zlo = lax.ppermute(high, 'slab', forward)]
where the time goes in v10:
time: 125 us; the launch traced here: 124 us
  starting transfers between devices  59.2 us (47%)
  waiting for transfers between devices  38.9 us (31%)
  Pallas kernels  21.4 us (17%)
  local copies, waits for them, and re-layouts  4.36 us (3%)
    ppermute x10, starting transfers between devices, depth_exchange(): zlo = lax.ppermute(high, 'slab', forward)  42.3 us
    ppermute x10, waiting for transfers between devices, depth_exchange(): zhi = lax.ppermute(low, 'slab', backward)  16.5 us
    ppermute x10, waiting for transfers between devices, depth_exchange(): zlo = lax.ppermute(high, 'slab', forward)  15.8 us
    ppermute x10, starting transfers between devices, depth_exchange(): zhi = lax.ppermute(low, 'slab', backward)  13.1 us
    ppermute x4, waiting for transfers between devices, ring(): lax.ppermute(x, 'row', [(i, (i + step) % count) for i in range(count)])  6.49 us
    pallas_call x5, Pallas kernels, depth_ratio(): pl.pallas_call(functools.partial(ratio_kernel, n, radius, skip), in_specs...  5.19 us
    pallas_call x5, Pallas kernels, depth_back(): pl.pallas_call(functools.partial(back_kernel, n, radius, swapped), in_spe...  4.75 us
    pallas_call x2, Pallas kernels, update(): pl.pallas_call(functools.partial(update_kernel, n, last, len(pieces)), in...  4.26 us
  transfers between devices with their start and end apart: 24, of which 14 were waited for; matrix products, arithmetic and copies ran while one was open for 0% of the time, Pallas kernels for 13%

profile of v10, /device:TPU:0, one launch (start us, length us, event | category | flops | bytes accessed | tf_op | source)
XLA Modules:
  0.0 124.2 jit_solution(13389143737295425589)
XLA Ops:
  0.0 1.1 slice.3
  1.1 2.4 %collective-permute-start = (f32[16,32,256]{2,1,0:T(8,128)S(1)}, f32[16,32,256]{2,1,0:T(8,128)S(1)}, u32[]{:S(2)}, u32[]{:S(2)}) collective-permute-start(f32[16,32,256]{2,1,0:T(8,128)S(1)} %slice.3), channel_id=1, source_target_pairs={{0,12},{4,0},{8,4},{12,8},{1,13},{5,1},{9,5},{13,9},{2,14},{6,2},{... | collective-permute-start | bytes 1572872 | tf_op jit(solution)/shard_map/ppermute | solution.py:453
  3.5 1.2 copy-done
  4.7 0.7 copy-done.2
  5.4 0.7 copy-done.3
  6.1 0.7 copy-done.4
  6.8 2.2 %shard_map.55 = (bf16[16,256,256]{2,1,0:T(8,128)(2,1)S(1)}, bf16[16,256,256]{2,1,0:T(8,128)(2,1)S(1)}, bf16[16,2,64,128]{3,2,1,0:T(8,128)(2,1)S(1)}, f32[16,64,256]{2,1,0:T(8,128)S(1)}) custom-call(s32[16]{0:T(128)S(1)} %copy-done.4, f32[16,31]{1,0:T(8,128)S(1)} %copy-done.2, f32[16,31]{1,0:T(8,128)S(1)} %copy-done.3, f32[16,64,256]{2,1,0:T(8,128)S(1)} %copy-done), custom_call_target="tpu_custom_call" | custom-call | flops 1000000000 | bytes 3500000 | tf_op jit(solution)/shard_map/pallas_call | solution.py:161
  9.0 1.2 collective-permute-done.next_ref
  10.2 1.1 shard_map.56
  11.3 0.0 copy-start.5
  11.3 1.4 %collective-permute-start.2 = (f32[15,32,256]{2,1,0:T(8,128)S(1)}, f32[15,32,256]{2,1,0:T(8,128)S(1)}, u32[]{:S(2)}, u32[]{:S(2)}) collective-permute-start(f32[15,32,256]{2,1,0:T(8,128)S(1)} %get-tuple-element.42.refs_0_), channel_id=1, source_target_pairs={{1,0},{2,1},{3,2},{5,4},{6,5},{7,6},{9,8},{10,9},{11,10},{13,12},{... | collective-permute-start | bytes 1474568 | tf_op jit(solution)/shard_map/ppermute | solution.py:447
  12.8 4.6 %collective-permute-start.1 = (f32[15,32,256]{2,1,0:T(8,128)S(1)}, f32[15,32,256]{2,1,0:T(8,128)S(1)}, u32[]{:S(2)}, u32[]{:S(2)}) collective-permute-start(f32[15,32,256]{2,1,0:T(8,128)S(1)} %get-tuple-element.46.refs_1_), channel_id=1, source_target_pairs={{0,1},{1,2},{2,3},{4,5},{5,6},{6,7},{8,9},{9,10},{10,11},{12,13},{... | collective-permute-start | bytes 1474568 | tf_op jit(solution)/shard_map/ppermute | solution.py:446
  17.3 0.4 shard_map.57
  17.7 1.3 %collective-permute-start.6 = (f32[15,32,256]{2,1,0:T(8,128)S(1)}, f32[15,32,256]{2,1,0:T(8,128)S(1)}, u32[]{:S(2)}, u32[]{:S(2)}) collective-permute-start(f32[15,32,256]{2,1,0:T(8,128)S(1)} %get-tuple-element.43.after_ref.refs_4_.refs_0_), channel_id=1, source_target_pairs={{1,0},{2,1},{3,2},{5,4},{6,5},{7,6},{9,8},{10,9},{11,10},{13,12},{... | collective-permute-start | bytes 1474568 | tf_op jit(solution)/shard_map/ppermute | solution.py:447
  19.0 4.6 %collective-permute-start.5 = (f32[15,32,256]{2,1,0:T(8,128)S(1)}, f32[15,32,256]{2,1,0:T(8,128)S(1)}, u32[]{:S(2)}, u32[]{:S(2)}) collective-permute-start(f32[15,32,256]{2,1,0:T(8,128)S(1)} %get-tuple-element.49.refs_1_), channel_id=1, source_target_pairs={{0,1},{1,2},{2,3},{4,5},{5,6},{6,7},{8,9},{9,10},{10,11},{12,13},{... | collective-permute-start | bytes 1474568 | tf_op jit(solution)/shard_map/ppermute | solution.py:446
  23.6 2.8 %shard_map.58 = (bf16[16,256,256]{2,1,0:T(8,128)(2,1)S(1)}, bf16[16,256,256]{2,1,0:T(8,128)(2,1)S(1)}, bf16[16,2,64,128]{3,2,1,0:T(8,128)(2,1)S(1)}, f32[16,64,2...) custom-call(s32[16]{0:T(128)S(1)} %copy-done.4, f32[16,31]{1,0:T(8,128)S(1)} %copy-done.2, ...), custom_call_target="tpu_custom_call" | custom-call | flops 1000000000 | bytes 3500000 | tf_op jit(solution)/shard_map/pallas_call | solution.py:226
  26.4 1.1 collective-permute-done.2.refs_3_
  27.4 1.4 %collective-permute-done.1.refs_2_ = f32[15,32,256]{2,1,0:T(8,128)S(1)} collective-permute-done((f32[15,32,256]{2,1,0:T(8,128)S(1)}, f32[15,32,256]{2,1,0:T(8,128)S(1)}, u32[]{:S(2)}, u32[]{:S(2)}) %collective-permute-start.1) | collective-permute-done | bytes 491552 | tf_op jit(solution)/shard_map/ppermute | solution.py:446
  28.8 1.3 %shard_map.59 = (f32[15,32,256]{2,1,0:T(8,128)S(1)}, f32[15,32,256]{2,1,0:T(8,128)S(1)}) custom-call(f32[31,8,128]{2,1,0:T(8,128)S(1)} %get-tuple-element.44.tz_ref, f32[16,64,256]{2,1,0:T(8,128)S(1)} %get-tuple-element.45.obs_ref, f32[15,32,256]{2,1,0:T(8,128)S(1)} %get-tuple-element.42.refs_0_, f32[15,32,256]{2,1,0:T(8,128)S(1)} %get-tuple-element.46.refs_1_, ...), custom_call_target="tpu_custom_call" | custom-call | flops 1000000000 | bytes 3500000 | tf_op jit(solution)/shard_map/pallas_call | solution.py:342
  30.1 4.4 %collective-permute-start.3 = (f32[15,32,256]{2,1,0:T(8,128)S(1)}, f32[15,32,256]{2,1,0:T(8,128)S(1)}, u32[]{:S(2)}, u32[]{:S(2)}) collective-permute-start(f32[15,32,256]{2,1,0:T(8,128)S(1)} %get-tuple-element.48.refs_1_), channel_id=1, source_target_pairs={{0,1},{1,2},{2,3},{4,5},{5,6},{6,7},{8,9},{9,10},{10,11},{12,13},{... | collective-permute-start | bytes 1474568 | tf_op jit(solution)/shard_map/ppermute | solution.py:446
  34.6 1.3 %collective-permute-start.4 = (f32[15,32,256]{2,1,0:T(8,128)S(1)}, f32[15,32,256]{2,1,0:T(8,128)S(1)}, u32[]{:S(2)}, u32[]{:S(2)}) collective-permute-start(f32[15,32,256]{2,1,0:T(8,128)S(1)} %get-tuple-element.47.refs_4_.refs_0_), channel_id=1, source_target_pairs={{1,0},{2,1},{3,2},{5,4},{6,5},{7,6},{9,8},{10,9},{11,10},{13,12},{... | collective-permute-start | bytes 1474568 | tf_op jit(solution)/shard_map/ppermute | solution.py:447
  35.9 2.0 %collective-permute-done.6.refs_3_ = f32[15,32,256]{2,1,0:T(8,128)S(1)} collective-permute-done((f32[15,32,256]{2,1,0:T(8,128)S(1)}, f32[15,32,256]{2,1,0:T(8,128)S(1)}, u32[]{:S(2)}, u32[]{:S(2)}) %collective-permute-start.6) | collective-permute-done | bytes 491552 | tf_op jit(solution)/shard_map/ppermute | solution.py:447
  37.9 1.5 %collective-permute-done.5.refs_2_ = f32[15,32,256]{2,1,0:T(8,128)S(1)} collective-permute-done((f32[15,32,256]{2,1,0:T(8,128)S(1)}, f32[15,32,256]{2,1,0:T(8,128)S(1)}, u32[]{:S(2)}, u32[]{:S(2)}) %collective-permute-start.5) | collective-permute-done | bytes 491552 | tf_op jit(solution)/shard_map/ppermute | solution.py:446
  39.4 1.3 %shard_map.60 = (f32[15,32,256]{2,1,0:T(8,128)S(1)}, f32[15,32,256]{2,1,0:T(8,128)S(1)}) custom-call(f32[31,8,128]{2,1,0:T(8,128)S(1)} %get-tuple-element.44.tz_ref, f32[16,64,256]{2,1,0:T(8,128)S(1)} %get-tuple-element.45.obs_ref, f32[15,32,256]{2,1,0:T(8,128)S(1)} %get-tuple-element.43.after_ref.refs_4_.refs_0_, ...), custom_call_target="tpu_custom_call" | custom-call | flops 1000000000 | bytes 3500000 | tf_op jit(solution)/shard_map/pallas_call | solution.py:342
  40.6 4.4 %collective-permute-start.8 = (f32[15,32,256]{2,1,0:T(8,128)S(1)}, f32[15,32,256]{2,1,0:T(8,128)S(1)}, u32[]{:S(2)}, u32[]{:S(2)}) collective-permute-start(f32[15,32,256]{2,1,0:T(8,128)S(1)} %get-tuple-element.51.refs_1_), channel_id=1, source_target_pairs={{0,1},{1,2},{2,3},{4,5},{5,6},{6,7},{8,9},{9,10},{10,11},{12,13},{... | collective-permute-start | bytes 1474568 | tf_op jit(solution)/shard_map/ppermute | solution.py:446
  45.1 1.3 %collective-permute-start.9 = (f32[15,32,256]{2,1,0:T(8,128)S(1)}, f32[15,32,256]{2,1,0:T(8,128)S(1)}, u32[]{:S(2)}, u32[]{:S(2)}) collective-permute-start(f32[15,32,256]{2,1,0:T(8,128)S(1)} %get-tuple-element.50.refs_4_.refs_0_), channel_id=1, source_target_pairs={{1,0},{2,1},{3,2},{5,4},{6,5},{7,6},{9,8},{10,9},{11,10},{13,12},{... | collective-permute-start | bytes 1474568 | tf_op jit(solution)/shard_map/ppermute | solution.py:447
  46.4 3.5 %collective-permute-done.3.refs_2_ = f32[15,32,256]{2,1,0:T(8,128)S(1)} collective-permute-done((f32[15,32,256]{2,1,0:T(8,128)S(1)}, f32[15,32,256]{2,1,0:T(8,128)S(1)}, u32[]{:S(2)}, u32[]{:S(2)}) %collective-permute-start.3) | collective-permute-done | bytes 491552 | tf_op jit(solution)/shard_map/ppermute | solution.py:446
  49.9 1.2 shard_map.61.refs_4_.refs_2_
  51.1 0.1 collective-permute-start.7
  51.1 9.0 %collective-permute-done.8.refs_2_ = f32[15,32,256]{2,1,0:T(8,128)S(1)} collective-permute-done((f32[15,32,256]{2,1,0:T(8,128)S(1)}, f32[15,32,256]{2,1,0:T(8,128)S(1)}, u32[]{:S(2)}, u32[]{:S(2)}) %collective-permute-start.8) | collective-permute-done | bytes 491552 | tf_op jit(solution)/shard_map/ppermute | solution.py:446
  60.1 0.0 collective-permute-done.9.refs_3_
  60.1 1.2 shard_map.62.refs_1_
  61.3 0.0 collective-permute-done.7.refs_0_
  61.3 2.2 %shard_map.63 = (f32[16,64,256]{2,1,0:T(8,128)S(1)}, f32[16,64,256]{2,1,0:T(8,128)S(1)}, f32[16,32,256]{2,1,0:T(8,128)S(1)}, f32[15,16,256]{2,1,0:T(8,128)S(1)}, f32[15,16,256]{2,1,0:T(8,128)S(1)}) custom-call(f32[16,32,256]{2,1,0:T(8,128)S(1)} %collective-permute-done.7.refs_0_, f32[16,32,256]{2,1,0:T(8,128)S(1)} %shard_map.62.refs_1_, ...), custom_call_target="tpu_custom_call" | custom-call | flops 1000000000 | bytes 3500000 | tf_op jit(solution)/shard_map/pallas_call | solution.py:431
  63.5 0.7 collective-permute-start.10
  64.3 4.1 %collective-permute-start.13 = (f32[15,16,256]{2,1,0:T(8,128)S(1)}, f32[15,16,256]{2,1,0:T(8,128)S(1)}, u32[]{:S(2)}, u32[]{:S(2)}) collective-permute-start(f32[15,16,256]{2,1,0:T(8,128)S(1)} %get-tuple-element.61.refs_1_), channel_id=1, source_target_pairs={{0,1},{1,2},{2,3},{4,5},{5,6},{6,7},{8,9},{9,10},{10,11},{12,13},{... | collective-permute-start | bytes 737288 | tf_op jit(solution)/shard_map/ppermute | solution.py:446
  68.4 1.3 %collective-permute-start.14 = (f32[15,16,256]{2,1,0:T(8,128)S(1)}, f32[15,16,256]{2,1,0:T(8,128)S(1)}, u32[]{:S(2)}, u32[]{:S(2)}) collective-permute-start(f32[15,16,256]{2,1,0:T(8,128)S(1)} %get-tuple-element.60.refs_0_), channel_id=1, source_target_pairs={{1,0},{2,1},{3,2},{5,4},{6,5},{7,6},{9,8},{10,9},{11,10},{13,12},{... | collective-permute-start | bytes 737288 | tf_op jit(solution)/shard_map/ppermute | solution.py:447
  69.7 1.3 %collective-permute-done.10.next_ref = f32[16,32,256]{2,1,0:T(8,128)S(1)} collective-permute-done((f32[16,32,256]{2,1,0:T(8,128)S(1)}, f32[16,32,256]{2,1,0:T(8,128)S(1)}, u32[]{:S(2)}, u32[]{:S(2)}) %collective-permute-start.10) | collective-permute-done | bytes 524320 | tf_op jit(solution)/shard_map/ppermute | solution.py:453
  71.0 0.4 shard_map.64
  71.4 4.1 %collective-permute-start.11 = (f32[15,32,256]{2,1,0:T(8,128)S(1)}, f32[15,32,256]{2,1,0:T(8,128)S(1)}, u32[]{:S(2)}, u32[]{:S(2)}) collective-permute-start(f32[15,32,256]{2,1,0:T(8,128)S(1)} %get-tuple-element.59.refs_1_), channel_id=1, source_target_pairs={{0,1},{1,2},{2,3},{4,5},{5,6},{6,7},{8,9},{9,10},{10,11},{12,13},{... | collective-permute-start | bytes 1474568 | tf_op jit(solution)/shard_map/ppermute | solution.py:446
  75.5 1.3 %collective-permute-start.12 = (f32[15,32,256]{2,1,0:T(8,128)S(1)}, f32[15,32,256]{2,1,0:T(8,128)S(1)}, u32[]{:S(2)}, u32[]{:S(2)}) collective-permute-start(f32[15,32,256]{2,1,0:T(8,128)S(1)} %get-tuple-element.58.refs_4_.refs_0_), channel_id=1, source_target_pairs={{1,0},{2,1},{3,2},{5,4},{6,5},{7,6},{9,8},{10,9},{11,10},{13,12},{... | collective-permute-start | bytes 1474568 | tf_op jit(solution)/shard_map/ppermute | solution.py:447
  76.8 1.1 collective-permute-done.14.refs_3_
  77.9 0.6 shard_map.65
  78.6 0.3 shard_map.66
  78.9 3.5 %collective-permute-start.19 = (f32[15,16,256]{2,1,0:T(8,128)S(1)}, f32[15,16,256]{2,1,0:T(8,128)S(1)}, u32[]{:S(2)}, u32[]{:S(2)}) collective-permute-start(f32[15,16,256]{2,1,0:T(8,128)S(1)} %get-tuple-element.67.refs_1_), channel_id=1, source_target_pairs={{0,1},{1,2},{2,3},{4,5},{5,6},{6,7},{8,9},{9,10},{10,11},{12,13},{... | collective-permute-start | bytes 737288 | tf_op jit(solution)/shard_map/ppermute | solution.py:446
  82.4 1.3 %collective-permute-start.20 = (f32[15,16,256]{2,1,0:T(8,128)S(1)}, f32[15,16,256]{2,1,0:T(8,128)S(1)}, u32[]{:S(2)}, u32[]{:S(2)}) collective-permute-start(f32[15,16,256]{2,1,0:T(8,128)S(1)} %get-tuple-element.63.refs_4_.refs_0_), channel_id=1, source_target_pairs={{1,0},{2,1},{3,2},{5,4},{6,5},{7,6},{9,8},{10,9},{11,10},{13,12},{... | collective-permute-start | bytes 737288 | tf_op jit(solution)/shard_map/ppermute | solution.py:447
  83.7 4.6 %collective-permute-start.17 = (f32[15,16,256]{2,1,0:T(8,128)S(1)}, f32[15,16,256]{2,1,0:T(8,128)S(1)}, u32[]{:S(2)}, u32[]{:S(2)}) collective-permute-start(f32[15,16,256]{2,1,0:T(8,128)S(1)} %get-tuple-element.66.refs_1_), channel_id=1, source_target_pairs={{0,1},{1,2},{2,3},{4,5},{5,6},{6,7},{8,9},{9,10},{10,11},{12,13},{... | collective-permute-start | bytes 737288 | tf_op jit(solution)/shard_map/ppermute | solution.py:446
  88.3 1.3 %collective-permute-start.18 = (f32[15,16,256]{2,1,0:T(8,128)S(1)}, f32[15,16,256]{2,1,0:T(8,128)S(1)}, u32[]{:S(2)}, u32[]{:S(2)}) collective-permute-start(f32[15,16,256]{2,1,0:T(8,128)S(1)} %get-tuple-element.62.refs_0_), channel_id=1, source_target_pairs={{1,0},{2,1},{3,2},{5,4},{6,5},{7,6},{9,8},{10,9},{11,10},{13,12},{... | collective-permute-start | bytes 737288 | tf_op jit(solution)/shard_map/ppermute | solution.py:447
  89.6 1.6 %collective-permute-done.12.refs_3_ = f32[15,32,256]{2,1,0:T(8,128)S(1)} collective-permute-done((f32[15,32,256]{2,1,0:T(8,128)S(1)}, f32[15,32,256]{2,1,0:T(8,128)S(1)}, u32[]{:S(2)}, u32[]{:S(2)}) %collective-permute-start.12) | collective-permute-done | bytes 491552 | tf_op jit(solution)/shard_map/ppermute | solution.py:447
  91.2 1.3 %shard_map.67 = (f32[15,32,256]{2,1,0:T(8,128)S(1)}, f32[15,32,256]{2,1,0:T(8,128)S(1)}) custom-call(f32[31,8,128]{2,1,0:T(8,128)S(1)} %get-tuple-element.44.tz_ref, f32[16,64,256]{2,1,0:T(8,128)S(1)} %get-tuple-element.45.obs_ref, f32[15,32,256]{2,1,0:T(8,128)S(1)} %get-tuple-element.58.refs_4_.refs_0_, f32[15,32,256]{2,1,0:T(8,128)S(1)} %get-tuple-element.59.refs_1_, ...), custom_call_target="tpu_custom_call" | custom-call | flops 1000000000 | bytes 3500000 | tf_op jit(solution)/shard_map/pallas_call | solution.py:342
  92.5 1.3 %collective-permute-start.15 = (f32[15,32,256]{2,1,0:T(8,128)S(1)}, f32[15,32,256]{2,1,0:T(8,128)S(1)}, u32[]{:S(2)}, u32[]{:S(2)}) collective-permute-start(f32[15,32,256]{2,1,0:T(8,128)S(1)} %get-tuple-element.64.refs_4_.refs_0_), channel_id=1, source_target_pairs={{1,0},{2,1},{3,2},{5,4},{6,5},{7,6},{9,8},{10,9},{11,10},{13,12},{... | collective-permute-start | bytes 1474568 | tf_op jit(solution)/shard_map/ppermute | solution.py:447
  93.9 4.6 %collective-permute-start.16 = (f32[15,32,256]{2,1,0:T(8,128)S(1)}, f32[15,32,256]{2,1,0:T(8,128)S(1)}, u32[]{:S(2)}, u32[]{:S(2)}) collective-permute-start(f32[15,32,256]{2,1,0:T(8,128)S(1)} %get-tuple-element.65.refs_1_), channel_id=1, source_target_pairs={{0,1},{1,2},{2,3},{4,5},{5,6},{6,7},{8,9},{9,10},{10,11},{12,13},{... | collective-permute-start | bytes 1474568 | tf_op jit(solution)/shard_map/ppermute | solution.py:446
  98.5 0.7 shard_map.68
  99.1 3.5 %collective-permute-start.22 = (f32[15,16,256]{2,1,0:T(8,128)S(1)}, f32[15,16,256]{2,1,0:T(8,128)S(1)}, u32[]{:S(2)}, u32[]{:S(2)}) collective-permute-start(f32[15,16,256]{2,1,0:T(8,128)S(1)} %get-tuple-element.69.refs_1_), channel_id=1, source_target_pairs={{0,1},{1,2},{2,3},{4,5},{5,6},{6,7},{8,9},{9,10},{10,11},{12,13},{... | collective-permute-start | bytes 737288 | tf_op jit(solution)/shard_map/ppermute | solution.py:446
  102.6 1.3 %collective-permute-start.23 = (f32[15,16,256]{2,1,0:T(8,128)S(1)}, f32[15,16,256]{2,1,0:T(8,128)S(1)}, u32[]{:S(2)}, u32[]{:S(2)}) collective-permute-start(f32[15,16,256]{2,1,0:T(8,128)S(1)} %get-tuple-element.68.refs_4_.refs_0_), channel_id=1, source_target_pairs={{1,0},{2,1},{3,2},{5,4},{6,5},{7,6},{9,8},{10,9},{11,10},{13,12},{... | collective-permute-start | bytes 737288 | tf_op jit(solution)/shard_map/ppermute | solution.py:447
  103.9 0.6 shard_map.69.refs_4_.refs_1_
  104.5 7.8 %collective-permute-done.15.refs_2_ = f32[15,32,256]{2,1,0:T(8,128)S(1)} collective-permute-done((f32[15,32,256]{2,1,0:T(8,128)S(1)}, f32[15,32,256]{2,1,0:T(8,128)S(1)}, u32[]{:S(2)}, u32[]{:S(2)}) %collective-permute-start.15) | collective-permute-done | bytes 491552 | tf_op jit(solution)/shard_map/ppermute | solution.py:447
  112.3 1.2 shard_map.70.refs_4_.refs_3_
  113.5 0.7 collective-permute-start.21
  114.2 0.5 collective-permute-done.22.refs_2_
  114.7 2.9 %collective-permute-done.23.refs_3_ = f32[15,16,256]{2,1,0:T(8,128)S(1)} collective-permute-done((f32[15,16,256]{2,1,0:T(8,128)S(1)}, f32[15,16,256]{2,1,0:T(8,128)S(1)}, u32[]{:S(2)}, u32[]{:S(2)}) %collective-permute-start.23) | collective-permute-done | bytes 245792 | tf_op jit(solution)/shard_map/ppermute | solution.py:447
  117.6 0.6 shard_map.71.refs_2_
  118.2 4.0 %collective-permute-done.21.refs_0_ = f32[16,32,256]{2,1,0:T(8,128)S(1)} collective-permute-done((f32[16,32,256]{2,1,0:T(8,128)S(1)}, f32[16,32,256]{2,1,0:T(8,128)S(1)}, u32[]{:S(2)}, u32[]{:S(2)}) %collective-permute-start.21) | collective-permute-done | bytes 524320 | tf_op jit(solution)/shard_map/ppermute | solution.py:453
  122.1 2.0 %shard_map.72 = f32[16,64,256]{2,1,0:T(8,128)} custom-call(f32[16,32,256]{2,1,0:T(8,128)S(1)} %collective-permute-done.21.refs_0_, f32[16,16,256]{2,1,0:T(8,128)S(1)} %shard_map.69.refs_4_.refs_1_, f32[16,16,256]{2,1,0:T(8,128)S(1)} %shard_map.71.refs_2_, f32[16,32,256]{2,1,0:T(8,128)S(1)} %shard_map.70.refs_4_.refs_3_, ...), custom_call_target="tpu_custom_call" | custom-call | flops 1000000000 | bytes 3500000 | tf_op jit(solution)/shard_map/pallas_call | solution.py:431
  (15 shorter events, 0.0 us)
Async XLA Ops:
  1.1 9.1 %collective-permute-start = (f32[16,32,256]{2,1,0:T(8,128)S(1)}, f32[16,32,256]{2,1,0:T(8,128)S(1)}, u32[]{:S(2)}, u32[]{:S(2)}) collective-permute-start(f32[16,32,256]{2,1,0:T(8,128)S(1)} %slice.3), channel_id=1, source_target_pairs={{0,12},{4,0},{8,4},{12,8},{1,13},{5,1},{9,5},{13,9},{2,14},{6,2},{... | collective-permute-start | bytes 1572872 | tf_op jit(solution)/shard_map/ppermute | solution.py:453
  3.5 1.2 copy-start
  4.7 0.7 copy-start.2
  5.4 0.7 copy-start.3
  6.1 0.7 copy-start.4
  11.3 12.3 %copy-start.1 = (f32[16,64,256]{2,1,0:T(8,128)S(1)}, f32[16,64,256]{2,1,0:T(8,128)}, u32[]{:S(2)}) copy-start(f32[16,64,256]{2,1,0:T(8,128)} %refs_3_.1) | copy-start | bytes 3145732
  11.3 12.3 %copy-start.5 = (f32[31]{0:T(128)S(1)}, f32[31]{0:T(128)}, u32[]{:S(2)}) copy-start(f32[31]{0:T(128)} %tz_ref.1) | copy-start | bytes 376
  11.3 16.1 %collective-permute-start.2 = (f32[15,32,256]{2,1,0:T(8,128)S(1)}, f32[15,32,256]{2,1,0:T(8,128)S(1)}, u32[]{:S(2)}, u32[]{:S(2)}) collective-permute-start(f32[15,32,256]{2,1,0:T(8,128)S(1)} %get-tuple-element.42.refs_0_), channel_id=1, source_target_pairs={{1,0},{2,1},{3,2},{5,4},{6,5},{7,6},{9,8},{10,9},{11,10},{13,12},{... | collective-permute-start | bytes 1474568 | tf_op jit(solution)/shard_map/ppermute | solution.py:447
  12.8 16.1 %collective-permute-start.1 = (f32[15,32,256]{2,1,0:T(8,128)S(1)}, f32[15,32,256]{2,1,0:T(8,128)S(1)}, u32[]{:S(2)}, u32[]{:S(2)}) collective-permute-start(f32[15,32,256]{2,1,0:T(8,128)S(1)} %get-tuple-element.46.refs_1_), channel_id=1, source_target_pairs={{0,1},{1,2},{2,3},{4,5},{5,6},{6,7},{8,9},{9,10},{10,11},{12,13},{... | collective-permute-start | bytes 1474568 | tf_op jit(solution)/shard_map/ppermute | solution.py:446
  17.7 20.2 %collective-permute-start.6 = (f32[15,32,256]{2,1,0:T(8,128)S(1)}, f32[15,32,256]{2,1,0:T(8,128)S(1)}, u32[]{:S(2)}, u32[]{:S(2)}) collective-permute-start(f32[15,32,256]{2,1,0:T(8,128)S(1)} %get-tuple-element.43.after_ref.refs_4_.refs_0_), channel_id=1, source_target_pairs={{1,0},{2,1},{3,2},{5,4},{6,5},{7,6},{9,8},{10,9},{11,10},{13,12},{... | collective-permute-start | bytes 1474568 | tf_op jit(solution)/shard_map/ppermute | solution.py:447
  19.0 20.4 %collective-permute-start.5 = (f32[15,32,256]{2,1,0:T(8,128)S(1)}, f32[15,32,256]{2,1,0:T(8,128)S(1)}, u32[]{:S(2)}, u32[]{:S(2)}) collective-permute-start(f32[15,32,256]{2,1,0:T(8,128)S(1)} %get-tuple-element.49.refs_1_), channel_id=1, source_target_pairs={{0,1},{1,2},{2,3},{4,5},{5,6},{6,7},{8,9},{9,10},{10,11},{12,13},{... | collective-permute-start | bytes 1474568 | tf_op jit(solution)/shard_map/ppermute | solution.py:446
  30.1 19.8 %collective-permute-start.3 = (f32[15,32,256]{2,1,0:T(8,128)S(1)}, f32[15,32,256]{2,1,0:T(8,128)S(1)}, u32[]{:S(2)}, u32[]{:S(2)}) collective-permute-start(f32[15,32,256]{2,1,0:T(8,128)S(1)} %get-tuple-element.48.refs_1_), channel_id=1, source_target_pairs={{0,1},{1,2},{2,3},{4,5},{5,6},{6,7},{8,9},{9,10},{10,11},{12,13},{... | collective-permute-start | bytes 1474568 | tf_op jit(solution)/shard_map/ppermute | solution.py:446
  34.6 15.3 %collective-permute-start.4 = (f32[15,32,256]{2,1,0:T(8,128)S(1)}, f32[15,32,256]{2,1,0:T(8,128)S(1)}, u32[]{:S(2)}, u32[]{:S(2)}) collective-permute-start(f32[15,32,256]{2,1,0:T(8,128)S(1)} %get-tuple-element.47.refs_4_.refs_0_), channel_id=1, source_target_pairs={{1,0},{2,1},{3,2},{5,4},{6,5},{7,6},{9,8},{10,9},{11,10},{13,12},{... | collective-permute-start | bytes 1474568 | tf_op jit(solution)/shard_map/ppermute | solution.py:447
  40.6 19.5 %collective-permute-start.8 = (f32[15,32,256]{2,1,0:T(8,128)S(1)}, f32[15,32,256]{2,1,0:T(8,128)S(1)}, u32[]{:S(2)}, u32[]{:S(2)}) collective-permute-start(f32[15,32,256]{2,1,0:T(8,128)S(1)} %get-tuple-element.51.refs_1_), channel_id=1, source_target_pairs={{0,1},{1,2},{2,3},{4,5},{5,6},{6,7},{8,9},{9,10},{10,11},{12,13},{... | collective-permute-start | bytes 1474568 | tf_op jit(solution)/shard_map/ppermute | solution.py:446
  45.1 15.0 %collective-permute-start.9 = (f32[15,32,256]{2,1,0:T(8,128)S(1)}, f32[15,32,256]{2,1,0:T(8,128)S(1)}, u32[]{:S(2)}, u32[]{:S(2)}) collective-permute-start(f32[15,32,256]{2,1,0:T(8,128)S(1)} %get-tuple-element.50.refs_4_.refs_0_), channel_id=1, source_target_pairs={{1,0},{2,1},{3,2},{5,4},{6,5},{7,6},{9,8},{10,9},{11,10},{13,12},{... | collective-permute-start | bytes 1474568 | tf_op jit(solution)/shard_map/ppermute | solution.py:447
  51.1 10.2 %collective-permute-start.7 = (f32[16,32,256]{2,1,0:T(8,128)S(1)}, f32[16,32,256]{2,1,0:T(8,128)S(1)}, u32[]{:S(2)}, u32[]{:S(2)}) collective-permute-start(f32[16,32,256]{2,1,0:T(8,128)S(1)} %shard_map.61.refs_4_.refs_2_), channel_id=1, source_target_pairs={{0,4},{4,8},{8,12},{12,0},{1,5},{5,9},{9,13},{13,1},{2,6},{6,10},{... | collective-permute-start | bytes 1572872 | tf_op jit(solution)/shard_map/ppermute | solution.py:453
  63.5 7.4 %collective-permute-start.10 = (f32[16,32,256]{2,1,0:T(8,128)S(1)}, f32[16,32,256]{2,1,0:T(8,128)S(1)}, u32[]{:S(2)}, u32[]{:S(2)}) collective-permute-start(f32[16,32,256]{2,1,0:T(8,128)S(1)} %get-tuple-element.57), channel_id=1, source_target_pairs={{0,12},{4,0},{8,4},{12,8},{1,13},{5,1},{9,5},{13,9},{2,14},{6,2},{... | collective-permute-start | bytes 1572872 | tf_op jit(solution)/shard_map/ppermute | solution.py:453
  64.3 12.5 %collective-permute-start.13 = (f32[15,16,256]{2,1,0:T(8,128)S(1)}, f32[15,16,256]{2,1,0:T(8,128)S(1)}, u32[]{:S(2)}, u32[]{:S(2)}) collective-permute-start(f32[15,16,256]{2,1,0:T(8,128)S(1)} %get-tuple-element.61.refs_1_), channel_id=1, source_target_pairs={{0,1},{1,2},{2,3},{4,5},{5,6},{6,7},{8,9},{9,10},{10,11},{12,13},{... | collective-permute-start | bytes 737288 | tf_op jit(solution)/shard_map/ppermute | solution.py:446
  68.4 9.6 %collective-permute-start.14 = (f32[15,16,256]{2,1,0:T(8,128)S(1)}, f32[15,16,256]{2,1,0:T(8,128)S(1)}, u32[]{:S(2)}, u32[]{:S(2)}) collective-permute-start(f32[15,16,256]{2,1,0:T(8,128)S(1)} %get-tuple-element.60.refs_0_), channel_id=1, source_target_pairs={{1,0},{2,1},{3,2},{5,4},{6,5},{7,6},{9,8},{10,9},{11,10},{13,12},{... | collective-permute-start | bytes 737288 | tf_op jit(solution)/shard_map/ppermute | solution.py:447
  71.4 16.9 %collective-permute-start.11 = (f32[15,32,256]{2,1,0:T(8,128)S(1)}, f32[15,32,256]{2,1,0:T(8,128)S(1)}, u32[]{:S(2)}, u32[]{:S(2)}) collective-permute-start(f32[15,32,256]{2,1,0:T(8,128)S(1)} %get-tuple-element.59.refs_1_), channel_id=1, source_target_pairs={{0,1},{1,2},{2,3},{4,5},{5,6},{6,7},{8,9},{9,10},{10,11},{12,13},{... | collective-permute-start | bytes 1474568 | tf_op jit(solution)/shard_map/ppermute | solution.py:446
  75.5 15.7 %collective-permute-start.12 = (f32[15,32,256]{2,1,0:T(8,128)S(1)}, f32[15,32,256]{2,1,0:T(8,128)S(1)}, u32[]{:S(2)}, u32[]{:S(2)}) collective-permute-start(f32[15,32,256]{2,1,0:T(8,128)S(1)} %get-tuple-element.58.refs_4_.refs_0_), channel_id=1, source_target_pairs={{1,0},{2,1},{3,2},{5,4},{6,5},{7,6},{9,8},{10,9},{11,10},{13,12},{... | collective-permute-start | bytes 1474568 | tf_op jit(solution)/shard_map/ppermute | solution.py:447
  78.9 14.9 %collective-permute-start.19 = (f32[15,16,256]{2,1,0:T(8,128)S(1)}, f32[15,16,256]{2,1,0:T(8,128)S(1)}, u32[]{:S(2)}, u32[]{:S(2)}) collective-permute-start(f32[15,16,256]{2,1,0:T(8,128)S(1)} %get-tuple-element.67.refs_1_), channel_id=1, source_target_pairs={{0,1},{1,2},{2,3},{4,5},{5,6},{6,7},{8,9},{9,10},{10,11},{12,13},{... | collective-permute-start | bytes 737288 | tf_op jit(solution)/shard_map/ppermute | solution.py:446
  82.4 16.1 %collective-permute-start.20 = (f32[15,16,256]{2,1,0:T(8,128)S(1)}, f32[15,16,256]{2,1,0:T(8,128)S(1)}, u32[]{:S(2)}, u32[]{:S(2)}) collective-permute-start(f32[15,16,256]{2,1,0:T(8,128)S(1)} %get-tuple-element.63.refs_4_.refs_0_), channel_id=1, source_target_pairs={{1,0},{2,1},{3,2},{5,4},{6,5},{7,6},{9,8},{10,9},{11,10},{13,12},{... | collective-permute-start | bytes 737288 | tf_op jit(solution)/shard_map/ppermute | solution.py:447
  83.7 18.9 %collective-permute-start.17 = (f32[15,16,256]{2,1,0:T(8,128)S(1)}, f32[15,16,256]{2,1,0:T(8,128)S(1)}, u32[]{:S(2)}, u32[]{:S(2)}) collective-permute-start(f32[15,16,256]{2,1,0:T(8,128)S(1)} %get-tuple-element.66.refs_1_), channel_id=1, source_target_pairs={{0,1},{1,2},{2,3},{4,5},{5,6},{6,7},{8,9},{9,10},{10,11},{12,13},{... | collective-permute-start | bytes 737288 | tf_op jit(solution)/shard_map/ppermute | solution.py:446
  88.3 15.6 %collective-permute-start.18 = (f32[15,16,256]{2,1,0:T(8,128)S(1)}, f32[15,16,256]{2,1,0:T(8,128)S(1)}, u32[]{:S(2)}, u32[]{:S(2)}) collective-permute-start(f32[15,16,256]{2,1,0:T(8,128)S(1)} %get-tuple-element.62.refs_0_), channel_id=1, source_target_pairs={{1,0},{2,1},{3,2},{5,4},{6,5},{7,6},{9,8},{10,9},{11,10},{13,12},{... | collective-permute-start | bytes 737288 | tf_op jit(solution)/shard_map/ppermute | solution.py:447
  92.5 19.8 %collective-permute-start.15 = (f32[15,32,256]{2,1,0:T(8,128)S(1)}, f32[15,32,256]{2,1,0:T(8,128)S(1)}, u32[]{:S(2)}, u32[]{:S(2)}) collective-permute-start(f32[15,32,256]{2,1,0:T(8,128)S(1)} %get-tuple-element.64.refs_4_.refs_0_), channel_id=1, source_target_pairs={{1,0},{2,1},{3,2},{5,4},{6,5},{7,6},{9,8},{10,9},{11,10},{13,12},{... | collective-permute-start | bytes 1474568 | tf_op jit(solution)/shard_map/ppermute | solution.py:447
  93.9 18.4 %collective-permute-start.16 = (f32[15,32,256]{2,1,0:T(8,128)S(1)}, f32[15,32,256]{2,1,0:T(8,128)S(1)}, u32[]{:S(2)}, u32[]{:S(2)}) collective-permute-start(f32[15,32,256]{2,1,0:T(8,128)S(1)} %get-tuple-element.65.refs_1_), channel_id=1, source_target_pairs={{0,1},{1,2},{2,3},{4,5},{5,6},{6,7},{8,9},{9,10},{10,11},{12,13},{... | collective-permute-start | bytes 1474568 | tf_op jit(solution)/shard_map/ppermute | solution.py:446
  99.1 15.5 %collective-permute-start.22 = (f32[15,16,256]{2,1,0:T(8,128)S(1)}, f32[15,16,256]{2,1,0:T(8,128)S(1)}, u32[]{:S(2)}, u32[]{:S(2)}) collective-permute-start(f32[15,16,256]{2,1,0:T(8,128)S(1)} %get-tuple-element.69.refs_1_), channel_id=1, source_target_pairs={{0,1},{1,2},{2,3},{4,5},{5,6},{6,7},{8,9},{9,10},{10,11},{12,13},{... | collective-permute-start | bytes 737288 | tf_op jit(solution)/shard_map/ppermute | solution.py:446
  102.6 15.0 %collective-permute-start.23 = (f32[15,16,256]{2,1,0:T(8,128)S(1)}, f32[15,16,256]{2,1,0:T(8,128)S(1)}, u32[]{:S(2)}, u32[]{:S(2)}) collective-permute-start(f32[15,16,256]{2,1,0:T(8,128)S(1)} %get-tuple-element.68.refs_4_.refs_0_), channel_id=1, source_target_pairs={{1,0},{2,1},{3,2},{5,4},{6,5},{7,6},{9,8},{10,9},{11,10},{13,12},{... | collective-permute-start | bytes 737288 | tf_op jit(solution)/shard_map/ppermute | solution.py:447
  113.5 8.7 %collective-permute-start.21 = (f32[16,32,256]{2,1,0:T(8,128)S(1)}, f32[16,32,256]{2,1,0:T(8,128)S(1)}, u32[]{:S(2)}, u32[]{:S(2)}) collective-permute-start(f32[16,32,256]{2,1,0:T(8,128)S(1)} %shard_map.70.refs_4_.refs_3_), channel_id=1, source_target_pairs={{0,4},{4,8},{8,12},{12,0},{1,5},{5,9},{9,13},{13,1},{2,6},{6,10},{... | collective-permute-start | bytes 1572872 | tf_op jit(solution)/shard_map/ppermute | solution.py:453

commit v11 on v10

--- a/solution.py
+++ b/solution.py
@@ -439,13 +439,18 @@
     )(*args)
 
 
+def send_up(x):
+    steps = range(lax.axis_size("slab") - 1)
+    return lax.ppermute(x, "slab", [(i, i + 1) for i in steps])
+
+
+def send_down(x):
+    steps = range(lax.axis_size("slab") - 1)
+    return lax.ppermute(x, "slab", [(i + 1, i) for i in steps])
+
+
 def depth_exchange(low, high):
-    count = lax.axis_size("slab")
-    forward = [(i, i + 1) for i in range(count - 1)]
-    backward = [(i + 1, i) for i in range(count - 1)]
-    zlo = lax.ppermute(high, "slab", forward)
-    zhi = lax.ppermute(low, "slab", backward)
-    return low, high, zlo, zhi
+    return low, high, send_up(high), send_down(low)
 
 
 def ring(x, step):
@@ -468,8 +473,9 @@
             v_first = depth_exchange(*first_sends)
             edge_sends = edge_blur(w, beyond, wx, (), radius)
             v_edge = depth_exchange(*edge_sends)
-            r_sends = depth_ratio(taps, shifted, [v_first], 0, (edge_sends[0],), 1.0)
-            r_inner = [depth_exchange(*r_sends)]
+            r_sends = depth_ratio(taps, shifted, [v_first], 0, (edge_sends[0],), 20.0)
+            first_low = send_up(r_sends[1])
+            r_inner = []
             after = (r_sends[0],)
             inner_sends = inner_blur(w, wx, half, inner - half, radius, after, 1.0)
             v_inner = depth_exchange(*inner_sends)
@@ -488,18 +494,23 @@
         r_edge = depth_exchange(
             *depth_ratio(taps, shifted, [v_edge], inner, after, 1.0),
         )
+        after = (r_edge[0],)
+        if step:
+            again = depth_ratio(taps, shifted, [v_first], 0, after, 20.0)
+            r_inner.append((*again, first_low, send_down(again[0])))
+            after = (again[0],)
         r_sends = depth_ratio(
-            taps, shifted, [v_inner], half if step else 0, (r_edge[0],), 1.0
+            taps, shifted, [v_inner], half if step else 0, after, 1.0
         )
         r_inner.append(depth_exchange(*r_sends))
         after = r_sends[0]
-        c_inner = []
-        if step:
-            c_inner.append(depth_back(taps, r_inner[0], n, after, 5.0))
-            after = c_inner[0]
         c_edge = depth_back(taps, r_edge, n, after, 1.0, step > 0)
         before = ring(c_edge, 1)
-        c_inner.append(depth_back(taps, r_inner[-1], n, c_edge, 100.0))
+        after, c_inner = c_edge, []
+        if step:
+            after = depth_back(taps, r_inner[0], n, after, 1.0)
+            c_inner.append(after)
+        c_inner.append(depth_back(taps, r_inner[-1], n, after, 100.0))
         last = step == ITERS - 1
         out = update(
             (before, *c_inner, c_edge), est, rn, adjoint,

time: 125 us -> 123 us (0.984)
  waiting for transfers between devices: 38.9 us -> 35.2 us
    ppermute x4, waiting for transfers between devices: 6.49 us -> 2.76 us  [ring(): lax.ppermute(x, 'row', [(i, (i + step) % count) for i in range(count)])]
    pallas_call x5 -> x6, Pallas kernels: 5.19 us -> 5.89 us  [depth_ratio(): pl.pallas_call(functools.partial(ratio_kernel, n, radius, skip), in_specs...]
    unnamed x12 -> x20, local copies, waits for them, and re-layouts: 3.28 us -> 3.3 us
  transfers between devices with their start and end apart: 24 -> 24, of which waited for: 14 -> 16; matrix products, arithmetic and copies ran while one was open for 0% -> 0% of each run, Pallas kernels for 13% -> 14%
where the time goes in v11:
time: 123 us; the launch traced here: 122 us
  starting transfers between devices  59.7 us (49%)
  waiting for transfers between devices  35.2 us (29%)
  Pallas kernels  22.1 us (18%)
  local copies, waits for them, and re-layouts  4.38 us (4%)
    ppermute x10, starting transfers between devices, send_up(): return lax.ppermute(x, 'slab', [(i, i + 1) for i in steps])  43.4 us
    ppermute x10, waiting for transfers between devices, send_down(): return lax.ppermute(x, 'slab', [(i + 1, i) for i in steps])  16.6 us
    ppermute x10, waiting for transfers between devices, send_up(): return lax.ppermute(x, 'slab', [(i, i + 1) for i in steps])  15.8 us
    ppermute x10, starting transfers between devices, send_down(): return lax.ppermute(x, 'slab', [(i + 1, i) for i in steps])  13 us
    pallas_call x6, Pallas kernels, depth_ratio(): pl.pallas_call(functools.partial(ratio_kernel, n, radius, skip), in_specs...  5.89 us
    pallas_call x5, Pallas kernels, depth_back(): pl.pallas_call(functools.partial(back_kernel, n, radius, swapped), in_spe...  4.77 us
    pallas_call x2, Pallas kernels, update(): pl.pallas_call(functools.partial(update_kernel, n, last, len(pieces)), in...  4.26 us
    unnamed x20, local copies, waits for them, and re-layouts  3.3 us
  transfers between devices with their start and end apart: 24, of which 16 were waited for; matrix products, arithmetic and copies ran while one was open for 0% of the time, Pallas kernels for 14%

profile of v11, /device:TPU:0, one launch (start us, length us, event | category | flops | bytes accessed | tf_op | source)
XLA Modules:
  0.0 121.8 jit_solution(12618096385590625315)
XLA Ops:
  0.0 1.1 slice.3
  1.1 2.4 %collective-permute-start = (f32[16,32,256]{2,1,0:T(8,128)S(1)}, f32[16,32,256]{2,1,0:T(8,128)S(1)}, u32[]{:S(2)}, u32[]{:S(2)}) collective-permute-start(f32[16,32,256]{2,1,0:T(8,128)S(1)} %slice.3), channel_id=1, source_target_pairs={{0,12},{4,0},{8,4},{12,8},{1,13},{5,1},{9,5},{13,9},{2,14},{6,2},{... | collective-permute-start | bytes 1572872 | tf_op jit(solution)/shard_map/ppermute | solution.py:458
  3.5 1.2 %copy-done.2 = f32[16,64,256]{2,1,0:T(8,128)S(1)} copy-done((f32[16,64,256]{2,1,0:T(8,128)S(1)}, f32[16,64,256]{2,1,0:T(8,128)}, u32[]{:S(2)}) %copy-start.2) | copy-done | bytes 1048600
  4.7 0.7 copy-done.6
  5.4 0.7 copy-done.7
  6.1 0.7 copy-done.8
  6.8 2.2 %shard_map.55 = (bf16[16,256,256]{2,1,0:T(8,128)(2,1)S(1)}, bf16[16,256,256]{2,1,0:T(8,128)(2,1)S(1)}, bf16[16,2,64,128]{3,2,1,0:T(8,128)(2,1)S(1)}, f32[16,64,256]{2,1,0:T(8,128)S(1)}) custom-call(s32[16]{0:T(128)S(1)} %copy-done.8, f32[16,31]{1,0:T(8,128)S(1)} %copy-done.6, f32[16,31]{1,0:T(8,128)S(1)} %copy-done.7, f32[16,64,256]{2,1,0:T(8,128)S(1)} %copy-done.2), custom_call_target="tpu_custom_call" | custom-call | flops 1000000000 | bytes 3500000 | tf_op jit(solution)/shard_map/pallas_call | solution.py:161
  9.0 1.2 collective-permute-done.next_ref
  10.2 1.1 shard_map.56
  11.3 1.4 %collective-permute-start.2 = (f32[15,32,256]{2,1,0:T(8,128)S(1)}, f32[15,32,256]{2,1,0:T(8,128)S(1)}, u32[]{:S(2)}, u32[]{:S(2)}) collective-permute-start(f32[15,32,256]{2,1,0:T(8,128)S(1)} %get-tuple-element.44.refs_0_), channel_id=1, source_target_pairs={{1,0},{2,1},{3,2},{5,4},{6,5},{7,6},{9,8},{10,9},{11,10},{13,12},{... | collective-permute-start | bytes 1474568 | tf_op jit(solution)/shard_map/ppermute | solution.py:449
  12.8 4.6 %collective-permute-start.1 = (f32[15,32,256]{2,1,0:T(8,128)S(1)}, f32[15,32,256]{2,1,0:T(8,128)S(1)}, u32[]{:S(2)}, u32[]{:S(2)}) collective-permute-start(f32[15,32,256]{2,1,0:T(8,128)S(1)} %get-tuple-element.48.refs_1_), channel_id=1, source_target_pairs={{0,1},{1,2},{2,3},{4,5},{5,6},{6,7},{8,9},{9,10},{10,11},{12,13},{... | collective-permute-start | bytes 1474568 | tf_op jit(solution)/shard_map/ppermute | solution.py:444
  17.3 0.4 shard_map.57
  17.7 1.3 %collective-permute-start.6 = (f32[15,32,256]{2,1,0:T(8,128)S(1)}, f32[15,32,256]{2,1,0:T(8,128)S(1)}, u32[]{:S(2)}, u32[]{:S(2)}) collective-permute-start(f32[15,32,256]{2,1,0:T(8,128)S(1)} %get-tuple-element.45.after_ref.refs_4_.refs_0_), channel_id=1, source_target_pairs={{1,0},{2,1},{3,2},{5,4},{6,5},{7,6},{9,8},{10,9},{11,10},{13,12},{... | collective-permute-start | bytes 1474568 | tf_op jit(solution)/shard_map/ppermute | solution.py:449
  19.0 4.6 %collective-permute-start.5 = (f32[15,32,256]{2,1,0:T(8,128)S(1)}, f32[15,32,256]{2,1,0:T(8,128)S(1)}, u32[]{:S(2)}, u32[]{:S(2)}) collective-permute-start(f32[15,32,256]{2,1,0:T(8,128)S(1)} %get-tuple-element.51.refs_1_), channel_id=1, source_target_pairs={{0,1},{1,2},{2,3},{4,5},{5,6},{6,7},{8,9},{9,10},{10,11},{12,13},{... | collective-permute-start | bytes 1474568 | tf_op jit(solution)/shard_map/ppermute | solution.py:444
  23.6 2.8 %shard_map.58 = (bf16[16,256,256]{2,1,0:T(8,128)(2,1)S(1)}, bf16[16,256,256]{2,1,0:T(8,128)(2,1)S(1)}, bf16[16,2,64,128]{3,2,1,0:T(8,128)(2,1)S(1)}, f32[16,64,2...) custom-call(s32[16]{0:T(128)S(1)} %copy-done.8, f32[16,31]{1,0:T(8,128)S(1)} %copy-done.6, ...), custom_call_target="tpu_custom_call" | custom-call | flops 1000000000 | bytes 3500000 | tf_op jit(solution)/shard_map/pallas_call | solution.py:226
  26.4 1.0 collective-permute-done.2.refs_3_
  27.4 1.4 %collective-permute-done.1.refs_2_ = f32[15,32,256]{2,1,0:T(8,128)S(1)} collective-permute-done((f32[15,32,256]{2,1,0:T(8,128)S(1)}, f32[15,32,256]{2,1,0:T(8,128)S(1)}, u32[]{:S(2)}, u32[]{:S(2)}) %collective-permute-start.1) | collective-permute-done | bytes 491552 | tf_op jit(solution)/shard_map/ppermute | solution.py:444
  28.8 1.3 %shard_map.59 = (f32[15,32,256]{2,1,0:T(8,128)S(1)}, f32[15,32,256]{2,1,0:T(8,128)S(1)}) custom-call(f32[31,8,128]{2,1,0:T(8,128)S(1)} %get-tuple-element.46.tz_ref, f32[16,64,256]{2,1,0:T(8,128)S(1)} %get-tuple-element.47.obs_ref, f32[15,32,256]{2,1,0:T(8,128)S(1)} %get-tuple-element.44.refs_0_, f32[15,32,256]{2,1,0:T(8,128)S(1)} %get-tuple-element.48.refs_1_, ...), custom_call_target="tpu_custom_call" | custom-call | flops 1000000000 | bytes 3500000 | tf_op jit(solution)/shard_map/pallas_call | solution.py:342
  30.1 4.4 %collective-permute-start.3 = (f32[15,32,256]{2,1,0:T(8,128)S(1)}, f32[15,32,256]{2,1,0:T(8,128)S(1)}, u32[]{:S(2)}, u32[]{:S(2)}) collective-permute-start(f32[15,32,256]{2,1,0:T(8,128)S(1)} %get-tuple-element.50.refs_1_), channel_id=1, source_target_pairs={{0,1},{1,2},{2,3},{4,5},{5,6},{6,7},{8,9},{9,10},{10,11},{12,13},{... | collective-permute-start | bytes 1474568 | tf_op jit(solution)/shard_map/ppermute | solution.py:444
  34.6 1.3 %collective-permute-start.4 = (f32[15,32,256]{2,1,0:T(8,128)S(1)}, f32[15,32,256]{2,1,0:T(8,128)S(1)}, u32[]{:S(2)}, u32[]{:S(2)}) collective-permute-start(f32[15,32,256]{2,1,0:T(8,128)S(1)} %get-tuple-element.49.refs_4_.refs_0_), channel_id=1, source_target_pairs={{1,0},{2,1},{3,2},{5,4},{6,5},{7,6},{9,8},{10,9},{11,10},{13,12},{... | collective-permute-start | bytes 1474568 | tf_op jit(solution)/shard_map/ppermute | solution.py:449
  35.9 2.0 %collective-permute-done.6.refs_3_ = f32[15,32,256]{2,1,0:T(8,128)S(1)} collective-permute-done((f32[15,32,256]{2,1,0:T(8,128)S(1)}, f32[15,32,256]{2,1,0:T(8,128)S(1)}, u32[]{:S(2)}, u32[]{:S(2)}) %collective-permute-start.6) | collective-permute-done | bytes 491552 | tf_op jit(solution)/shard_map/ppermute | solution.py:449
  37.8 1.5 %collective-permute-done.5.refs_2_ = f32[15,32,256]{2,1,0:T(8,128)S(1)} collective-permute-done((f32[15,32,256]{2,1,0:T(8,128)S(1)}, f32[15,32,256]{2,1,0:T(8,128)S(1)}, u32[]{:S(2)}, u32[]{:S(2)}) %collective-permute-start.5) | collective-permute-done | bytes 491552 | tf_op jit(solution)/shard_map/ppermute | solution.py:444
  39.3 1.3 %shard_map.60 = (f32[15,32,256]{2,1,0:T(8,128)S(1)}, f32[15,32,256]{2,1,0:T(8,128)S(1)}) custom-call(f32[31,8,128]{2,1,0:T(8,128)S(1)} %get-tuple-element.46.tz_ref, f32[16,64,256]{2,1,0:T(8,128)S(1)} %get-tuple-element.47.obs_ref, f32[15,32,256]{2,1,0:T(8,128)S(1)} %get-tuple-element.45.after_ref.refs_4_.refs_0_, ...), custom_call_target="tpu_custom_call" | custom-call | flops 1000000000 | bytes 3500000 | tf_op jit(solution)/shard_map/pallas_call | solution.py:342
  40.6 4.4 %collective-permute-start.8 = (f32[15,32,256]{2,1,0:T(8,128)S(1)}, f32[15,32,256]{2,1,0:T(8,128)S(1)}, u32[]{:S(2)}, u32[]{:S(2)}) collective-permute-start(f32[15,32,256]{2,1,0:T(8,128)S(1)} %get-tuple-element.53.refs_1_), channel_id=1, source_target_pairs={{0,1},{1,2},{2,3},{4,5},{5,6},{6,7},{8,9},{9,10},{10,11},{12,13},{... | collective-permute-start | bytes 1474568 | tf_op jit(solution)/shard_map/ppermute | solution.py:444
  45.1 1.3 %collective-permute-start.9 = (f32[15,32,256]{2,1,0:T(8,128)S(1)}, f32[15,32,256]{2,1,0:T(8,128)S(1)}, u32[]{:S(2)}, u32[]{:S(2)}) collective-permute-start(f32[15,32,256]{2,1,0:T(8,128)S(1)} %get-tuple-element.52.refs_4_.refs_0_), channel_id=1, source_target_pairs={{1,0},{2,1},{3,2},{5,4},{6,5},{7,6},{9,8},{10,9},{11,10},{13,12},{... | collective-permute-start | bytes 1474568 | tf_op jit(solution)/shard_map/ppermute | solution.py:449
  46.4 3.5 %collective-permute-done.3.refs_2_ = f32[15,32,256]{2,1,0:T(8,128)S(1)} collective-permute-done((f32[15,32,256]{2,1,0:T(8,128)S(1)}, f32[15,32,256]{2,1,0:T(8,128)S(1)}, u32[]{:S(2)}, u32[]{:S(2)}) %collective-permute-start.3) | collective-permute-done | bytes 491552 | tf_op jit(solution)/shard_map/ppermute | solution.py:444
  49.9 1.2 shard_map.61.refs_4_.refs_2_
  51.1 0.1 collective-permute-start.7
  51.1 9.0 %collective-permute-done.8.refs_2_ = f32[15,32,256]{2,1,0:T(8,128)S(1)} collective-permute-done((f32[15,32,256]{2,1,0:T(8,128)S(1)}, f32[15,32,256]{2,1,0:T(8,128)S(1)}, u32[]{:S(2)}, u32[]{:S(2)}) %collective-permute-start.8) | collective-permute-done | bytes 491552 | tf_op jit(solution)/shard_map/ppermute | solution.py:444
  60.1 1.2 shard_map.62.refs_1_
  61.3 2.2 %shard_map.63 = (f32[16,64,256]{2,1,0:T(8,128)S(1)}, f32[16,64,256]{2,1,0:T(8,128)S(1)}, f32[16,32,256]{2,1,0:T(8,128)S(1)}, f32[15,16,256]{2,1,0:T(8,128)S(1)}, f32[15,16,256]{2,1,0:T(8,128)S(1)}) custom-call(f32[16,32,256]{2,1,0:T(8,128)S(1)} %collective-permute-done.7.refs_0_, f32[16,32,256]{2,1,0:T(8,128)S(1)} %shard_map.62.refs_1_, ...), custom_call_target="tpu_custom_call" | custom-call | flops 1000000000 | bytes 3500000 | tf_op jit(solution)/shard_map/pallas_call | solution.py:431
  63.6 0.7 collective-permute-start.10
  64.3 4.1 %collective-permute-start.13 = (f32[15,16,256]{2,1,0:T(8,128)S(1)}, f32[15,16,256]{2,1,0:T(8,128)S(1)}, u32[]{:S(2)}, u32[]{:S(2)}) collective-permute-start(f32[15,16,256]{2,1,0:T(8,128)S(1)} %get-tuple-element.63.refs_1_), channel_id=1, source_target_pairs={{0,1},{1,2},{2,3},{4,5},{5,6},{6,7},{8,9},{9,10},{10,11},{12,13},{... | collective-permute-start | bytes 737288 | tf_op jit(solution)/shard_map/ppermute | solution.py:444
  68.4 1.3 %collective-permute-start.14 = (f32[15,16,256]{2,1,0:T(8,128)S(1)}, f32[15,16,256]{2,1,0:T(8,128)S(1)}, u32[]{:S(2)}, u32[]{:S(2)}) collective-permute-start(f32[15,16,256]{2,1,0:T(8,128)S(1)} %get-tuple-element.62.refs_0_), channel_id=1, source_target_pairs={{1,0},{2,1},{3,2},{5,4},{6,5},{7,6},{9,8},{10,9},{11,10},{13,12},{... | collective-permute-start | bytes 737288 | tf_op jit(solution)/shard_map/ppermute | solution.py:449
  69.7 1.3 %collective-permute-done.10.next_ref = f32[16,32,256]{2,1,0:T(8,128)S(1)} collective-permute-done((f32[16,32,256]{2,1,0:T(8,128)S(1)}, f32[16,32,256]{2,1,0:T(8,128)S(1)}, u32[]{:S(2)}, u32[]{:S(2)}) %collective-permute-start.10) | collective-permute-done | bytes 524320 | tf_op jit(solution)/shard_map/ppermute | solution.py:458
  71.0 0.4 shard_map.64
  71.4 4.1 %collective-permute-start.11 = (f32[15,32,256]{2,1,0:T(8,128)S(1)}, f32[15,32,256]{2,1,0:T(8,128)S(1)}, u32[]{:S(2)}, u32[]{:S(2)}) collective-permute-start(f32[15,32,256]{2,1,0:T(8,128)S(1)} %get-tuple-element.61.refs_1_), channel_id=1, source_target_pairs={{0,1},{1,2},{2,3},{4,5},{5,6},{6,7},{8,9},{9,10},{10,11},{12,13},{... | collective-permute-start | bytes 1474568 | tf_op jit(solution)/shard_map/ppermute | solution.py:444
  75.5 1.3 %collective-permute-start.12 = (f32[15,32,256]{2,1,0:T(8,128)S(1)}, f32[15,32,256]{2,1,0:T(8,128)S(1)}, u32[]{:S(2)}, u32[]{:S(2)}) collective-permute-start(f32[15,32,256]{2,1,0:T(8,128)S(1)} %get-tuple-element.60.refs_4_.refs_0_), channel_id=1, source_target_pairs={{1,0},{2,1},{3,2},{5,4},{6,5},{7,6},{9,8},{10,9},{11,10},{13,12},{... | collective-permute-start | bytes 1474568 | tf_op jit(solution)/shard_map/ppermute | solution.py:449
  76.8 1.1 collective-permute-done.14.refs_3_
  78.0 0.7 shard_map.65
  78.6 0.3 shard_map.66
  78.9 3.5 %collective-permute-start.17 = (f32[15,16,256]{2,1,0:T(8,128)S(1)}, f32[15,16,256]{2,1,0:T(8,128)S(1)}, u32[]{:S(2)}, u32[]{:S(2)}) collective-permute-start(f32[15,16,256]{2,1,0:T(8,128)S(1)} %get-tuple-element.68.refs_1_), channel_id=1, source_target_pairs={{0,1},{1,2},{2,3},{4,5},{5,6},{6,7},{8,9},{9,10},{10,11},{12,13},{... | collective-permute-start | bytes 737288 | tf_op jit(solution)/shard_map/ppermute | solution.py:444
  82.4 1.3 %collective-permute-start.18 = (f32[15,16,256]{2,1,0:T(8,128)S(1)}, f32[15,16,256]{2,1,0:T(8,128)S(1)}, u32[]{:S(2)}, u32[]{:S(2)}) collective-permute-start(f32[15,16,256]{2,1,0:T(8,128)S(1)} %get-tuple-element.65.refs_4_.refs_0_), channel_id=1, source_target_pairs={{1,0},{2,1},{3,2},{5,4},{6,5},{7,6},{9,8},{10,9},{11,10},{13,12},{... | collective-permute-start | bytes 737288 | tf_op jit(solution)/shard_map/ppermute | solution.py:449
  83.7 4.6 %collective-permute-start.20 = (f32[15,16,256]{2,1,0:T(8,128)S(1)}, f32[15,16,256]{2,1,0:T(8,128)S(1)}, u32[]{:S(2)}, u32[]{:S(2)}) collective-permute-start(f32[15,16,256]{2,1,0:T(8,128)S(1)} %get-tuple-element.72), channel_id=1, source_target_pairs={{0,1},{1,2},{2,3},{4,5},{5,6},{6,7},{8,9},{9,10},{10,11},{12,13},{... | collective-permute-start | bytes 737288 | tf_op jit(solution)/shard_map/ppermute | solution.py:444
  88.3 2.9 %collective-permute-done.12.refs_3_ = f32[15,32,256]{2,1,0:T(8,128)S(1)} collective-permute-done((f32[15,32,256]{2,1,0:T(8,128)S(1)}, f32[15,32,256]{2,1,0:T(8,128)S(1)}, u32[]{:S(2)}, u32[]{:S(2)}) %collective-permute-start.12) | collective-permute-done | bytes 491552 | tf_op jit(solution)/shard_map/ppermute | solution.py:449
  91.2 1.3 %shard_map.67 = (f32[15,32,256]{2,1,0:T(8,128)S(1)}, f32[15,32,256]{2,1,0:T(8,128)S(1)}) custom-call(f32[31,8,128]{2,1,0:T(8,128)S(1)} %get-tuple-element.46.tz_ref, f32[16,64,256]{2,1,0:T(8,128)S(1)} %get-tuple-element.47.obs_ref, f32[15,32,256]{2,1,0:T(8,128)S(1)} %get-tuple-element.60.refs_4_.refs_0_, f32[15,32,256]{2,1,0:T(8,128)S(1)} %get-tuple-element.61.refs_1_, ...), custom_call_target="tpu_custom_call" | custom-call | flops 1000000000 | bytes 3500000 | tf_op jit(solution)/shard_map/pallas_call | solution.py:342
  92.5 1.3 %collective-permute-start.15 = (f32[15,32,256]{2,1,0:T(8,128)S(1)}, f32[15,32,256]{2,1,0:T(8,128)S(1)}, u32[]{:S(2)}, u32[]{:S(2)}) collective-permute-start(f32[15,32,256]{2,1,0:T(8,128)S(1)} %get-tuple-element.66.refs_4_.refs_0_), channel_id=1, source_target_pairs={{1,0},{2,1},{3,2},{5,4},{6,5},{7,6},{9,8},{10,9},{11,10},{13,12},{... | collective-permute-start | bytes 1474568 | tf_op jit(solution)/shard_map/ppermute | solution.py:449
  93.8 4.6 %collective-permute-start.16 = (f32[15,32,256]{2,1,0:T(8,128)S(1)}, f32[15,32,256]{2,1,0:T(8,128)S(1)}, u32[]{:S(2)}, u32[]{:S(2)}) collective-permute-start(f32[15,32,256]{2,1,0:T(8,128)S(1)} %get-tuple-element.67.refs_1_), channel_id=1, source_target_pairs={{0,1},{1,2},{2,3},{4,5},{5,6},{6,7},{8,9},{9,10},{10,11},{12,13},{... | collective-permute-start | bytes 1474568 | tf_op jit(solution)/shard_map/ppermute | solution.py:444
  98.4 0.7 shard_map.68
  99.1 1.3 %collective-permute-start.21 = (f32[15,16,256]{2,1,0:T(8,128)S(1)}, f32[15,16,256]{2,1,0:T(8,128)S(1)}, u32[]{:S(2)}, u32[]{:S(2)}) collective-permute-start(f32[15,16,256]{2,1,0:T(8,128)S(1)} %get-tuple-element.69.refs_4_.refs_0_), channel_id=1, source_target_pairs={{1,0},{2,1},{3,2},{5,4},{6,5},{7,6},{9,8},{10,9},{11,10},{13,12},{... | collective-permute-start | bytes 737288 | tf_op jit(solution)/shard_map/ppermute | solution.py:449
  100.4 0.7 shard_map.69
  101.0 4.6 %collective-permute-start.22 = (f32[15,16,256]{2,1,0:T(8,128)S(1)}, f32[15,16,256]{2,1,0:T(8,128)S(1)}, u32[]{:S(2)}, u32[]{:S(2)}) collective-permute-start(f32[15,16,256]{2,1,0:T(8,128)S(1)} %get-tuple-element.73.refs_1_), channel_id=1, source_target_pairs={{0,1},{1,2},{2,3},{4,5},{5,6},{6,7},{8,9},{9,10},{10,11},{12,13},{... | collective-permute-start | bytes 737288 | tf_op jit(solution)/shard_map/ppermute | solution.py:444
  105.6 2.9 %collective-permute-done.15.refs_2_ = f32[15,32,256]{2,1,0:T(8,128)S(1)} collective-permute-done((f32[15,32,256]{2,1,0:T(8,128)S(1)}, f32[15,32,256]{2,1,0:T(8,128)S(1)}, u32[]{:S(2)}, u32[]{:S(2)}) %collective-permute-start.15) | collective-permute-done | bytes 491552 | tf_op jit(solution)/shard_map/ppermute | solution.py:449
  108.5 1.3 %collective-permute-start.23 = (f32[15,16,256]{2,1,0:T(8,128)S(1)}, f32[15,16,256]{2,1,0:T(8,128)S(1)}, u32[]{:S(2)}, u32[]{:S(2)}) collective-permute-start(f32[15,16,256]{2,1,0:T(8,128)S(1)} %get-tuple-element.70.refs_4_.refs_0_), channel_id=1, source_target_pairs={{1,0},{2,1},{3,2},{5,4},{6,5},{7,6},{9,8},{10,9},{11,10},{13,12},{... | collective-permute-start | bytes 737288 | tf_op jit(solution)/shard_map/ppermute | solution.py:449
  109.8 0.1 collective-permute-done.16.refs_3_
  109.9 1.2 shard_map.70.refs_4_.refs_3_
  111.1 0.1 collective-permute-start.19
  111.2 2.6 %collective-permute-done.21.refs_3_ = f32[15,16,256]{2,1,0:T(8,128)S(1)} collective-permute-done((f32[15,16,256]{2,1,0:T(8,128)S(1)}, f32[15,16,256]{2,1,0:T(8,128)S(1)}, u32[]{:S(2)}, u32[]{:S(2)}) %collective-permute-start.21) | collective-permute-done | bytes 245792 | tf_op jit(solution)/shard_map/ppermute | solution.py:449
  113.8 0.6 shard_map.71.refs_4_.refs_1_
  114.4 0.4 collective-permute-done.22.refs_2_
  114.8 4.1 %collective-permute-done.23.refs_3_ = f32[15,16,256]{2,1,0:T(8,128)S(1)} collective-permute-done((f32[15,16,256]{2,1,0:T(8,128)S(1)}, f32[15,16,256]{2,1,0:T(8,128)S(1)}, u32[]{:S(2)}, u32[]{:S(2)}) %collective-permute-start.23) | collective-permute-done | bytes 245792 | tf_op jit(solution)/shard_map/ppermute | solution.py:449
  118.9 0.6 shard_map.72.refs_2_
  119.5 0.3 collective-permute-done.19.refs_0_
  119.8 2.0 %shard_map.73 = f32[16,64,256]{2,1,0:T(8,128)} custom-call(f32[16,32,256]{2,1,0:T(8,128)S(1)} %collective-permute-done.19.refs_0_, f32[16,16,256]{2,1,0:T(8,128)S(1)} %shard_map.71.refs_4_.refs_1_, f32[16,16,256]{2,1,0:T(8,128)S(1)} %shard_map.72.refs_2_, f32[16,32,256]{2,1,0:T(8,128)S(1)} %shard_map.70.refs_4_.refs_3_, ...), custom_call_target="tpu_custom_call" | custom-call | flops 1000000000 | bytes 3500000 | tf_op jit(solution)/shard_map/pallas_call | solution.py:431
  (24 shorter events, 0.1 us)
Async XLA Ops:
  1.1 9.1 %collective-permute-start = (f32[16,32,256]{2,1,0:T(8,128)S(1)}, f32[16,32,256]{2,1,0:T(8,128)S(1)}, u32[]{:S(2)}, u32[]{:S(2)}) collective-permute-start(f32[16,32,256]{2,1,0:T(8,128)S(1)} %slice.3), channel_id=1, source_target_pairs={{0,12},{4,0},{8,4},{12,8},{1,13},{5,1},{9,5},{13,9},{2,14},{6,2},{... | collective-permute-start | bytes 1572872 | tf_op jit(solution)/shard_map/ppermute | solution.py:458
  3.5 1.2 %copy-start.2 = (f32[16,64,256]{2,1,0:T(8,128)S(1)}, f32[16,64,256]{2,1,0:T(8,128)}, u32[]{:S(2)}) copy-start(f32[16,64,256]{2,1,0:T(8,128)} %refs_3_.1) | copy-start | bytes 3145732
  4.7 0.7 copy-start.6
  5.4 0.7 copy-start.7
  6.1 0.7 copy-start.8
  11.3 12.3 %copy-start.3 = (f32[16,64,256]{2,1,0:T(8,128)S(1)}, f32[16,64,256]{2,1,0:T(8,128)}, u32[]{:S(2)}) copy-start(f32[16,64,256]{2,1,0:T(8,128)} %refs_3_.1) | copy-start | bytes 3145732
  11.3 12.3 %copy-start.9 = (f32[31]{0:T(128)S(1)}, f32[31]{0:T(128)}, u32[]{:S(2)}) copy-start(f32[31]{0:T(128)} %tz_ref.1) | copy-start | bytes 376
  11.3 16.1 %collective-permute-start.2 = (f32[15,32,256]{2,1,0:T(8,128)S(1)}, f32[15,32,256]{2,1,0:T(8,128)S(1)}, u32[]{:S(2)}, u32[]{:S(2)}) collective-permute-start(f32[15,32,256]{2,1,0:T(8,128)S(1)} %get-tuple-element.44.refs_0_), channel_id=1, source_target_pairs={{1,0},{2,1},{3,2},{5,4},{6,5},{7,6},{9,8},{10,9},{11,10},{13,12},{... | collective-permute-start | bytes 1474568 | tf_op jit(solution)/shard_map/ppermute | solution.py:449
  12.8 16.1 %collective-permute-start.1 = (f32[15,32,256]{2,1,0:T(8,128)S(1)}, f32[15,32,256]{2,1,0:T(8,128)S(1)}, u32[]{:S(2)}, u32[]{:S(2)}) collective-permute-start(f32[15,32,256]{2,1,0:T(8,128)S(1)} %get-tuple-element.48.refs_1_), channel_id=1, source_target_pairs={{0,1},{1,2},{2,3},{4,5},{5,6},{6,7},{8,9},{9,10},{10,11},{12,13},{... | collective-permute-start | bytes 1474568 | tf_op jit(solution)/shard_map/ppermute | solution.py:444
  17.7 20.2 %collective-permute-start.6 = (f32[15,32,256]{2,1,0:T(8,128)S(1)}, f32[15,32,256]{2,1,0:T(8,128)S(1)}, u32[]{:S(2)}, u32[]{:S(2)}) collective-permute-start(f32[15,32,256]{2,1,0:T(8,128)S(1)} %get-tuple-element.45.after_ref.refs_4_.refs_0_), channel_id=1, source_target_pairs={{1,0},{2,1},{3,2},{5,4},{6,5},{7,6},{9,8},{10,9},{11,10},{13,12},{... | collective-permute-start | bytes 1474568 | tf_op jit(solution)/shard_map/ppermute | solution.py:449
  19.0 20.4 %collective-permute-start.5 = (f32[15,32,256]{2,1,0:T(8,128)S(1)}, f32[15,32,256]{2,1,0:T(8,128)S(1)}, u32[]{:S(2)}, u32[]{:S(2)}) collective-permute-start(f32[15,32,256]{2,1,0:T(8,128)S(1)} %get-tuple-element.51.refs_1_), channel_id=1, source_target_pairs={{0,1},{1,2},{2,3},{4,5},{5,6},{6,7},{8,9},{9,10},{10,11},{12,13},{... | collective-permute-start | bytes 1474568 | tf_op jit(solution)/shard_map/ppermute | solution.py:444
  26.4 34.9 %copy-start = (f32[16,64,256]{2,1,0:T(8,128)}, f32[16,64,256]{2,1,0:T(8,128)S(1)}, u32[]{:S(2)}) copy-start(f32[16,64,256]{2,1,0:T(8,128)S(1)} %get-tuple-element.54.refs_4_.refs_5_) | copy-start | bytes 3145732
  26.4 34.9 %copy-start.4 = (bf16[16,2,64,128]{3,2,1,0:T(8,128)(2,1)}, bf16[16,2,64,128]{3,2,1,0:T(8,128)(2,1)S(1)}, u32[]{:S(2)}) copy-start(bf16[16,2,64,128]{3,2,1,0:T(8,128)(2,1)S(1)} %get-tuple-element.55.refs_5_.refs_6_) | copy-start | bytes 1572868
  30.1 19.7 %collective-permute-start.3 = (f32[15,32,256]{2,1,0:T(8,128)S(1)}, f32[15,32,256]{2,1,0:T(8,128)S(1)}, u32[]{:S(2)}, u32[]{:S(2)}) collective-permute-start(f32[15,32,256]{2,1,0:T(8,128)S(1)} %get-tuple-element.50.refs_1_), channel_id=1, source_target_pairs={{0,1},{1,2},{2,3},{4,5},{5,6},{6,7},{8,9},{9,10},{10,11},{12,13},{... | collective-permute-start | bytes 1474568 | tf_op jit(solution)/shard_map/ppermute | solution.py:444
  34.6 15.3 %collective-permute-start.4 = (f32[15,32,256]{2,1,0:T(8,128)S(1)}, f32[15,32,256]{2,1,0:T(8,128)S(1)}, u32[]{:S(2)}, u32[]{:S(2)}) collective-permute-start(f32[15,32,256]{2,1,0:T(8,128)S(1)} %get-tuple-element.49.refs_4_.refs_0_), channel_id=1, source_target_pairs={{1,0},{2,1},{3,2},{5,4},{6,5},{7,6},{9,8},{10,9},{11,10},{13,12},{... | collective-permute-start | bytes 1474568 | tf_op jit(solution)/shard_map/ppermute | solution.py:449
  40.6 19.4 %collective-permute-start.8 = (f32[15,32,256]{2,1,0:T(8,128)S(1)}, f32[15,32,256]{2,1,0:T(8,128)S(1)}, u32[]{:S(2)}, u32[]{:S(2)}) collective-permute-start(f32[15,32,256]{2,1,0:T(8,128)S(1)} %get-tuple-element.53.refs_1_), channel_id=1, source_target_pairs={{0,1},{1,2},{2,3},{4,5},{5,6},{6,7},{8,9},{9,10},{10,11},{12,13},{... | collective-permute-start | bytes 1474568 | tf_op jit(solution)/shard_map/ppermute | solution.py:444
  45.1 15.0 %collective-permute-start.9 = (f32[15,32,256]{2,1,0:T(8,128)S(1)}, f32[15,32,256]{2,1,0:T(8,128)S(1)}, u32[]{:S(2)}, u32[]{:S(2)}) collective-permute-start(f32[15,32,256]{2,1,0:T(8,128)S(1)} %get-tuple-element.52.refs_4_.refs_0_), channel_id=1, source_target_pairs={{1,0},{2,1},{3,2},{5,4},{6,5},{7,6},{9,8},{10,9},{11,10},{13,12},{... | collective-permute-start | bytes 1474568 | tf_op jit(solution)/shard_map/ppermute | solution.py:449
  51.1 10.2 %collective-permute-start.7 = (f32[16,32,256]{2,1,0:T(8,128)S(1)}, f32[16,32,256]{2,1,0:T(8,128)S(1)}, u32[]{:S(2)}, u32[]{:S(2)}) collective-permute-start(f32[16,32,256]{2,1,0:T(8,128)S(1)} %shard_map.61.refs_4_.refs_2_), channel_id=1, source_target_pairs={{0,4},{4,8},{8,12},{12,0},{1,5},{5,9},{9,13},{13,1},{2,6},{6,10},{... | collective-permute-start | bytes 1572872 | tf_op jit(solution)/shard_map/ppermute | solution.py:458
  63.6 7.4 %collective-permute-start.10 = (f32[16,32,256]{2,1,0:T(8,128)S(1)}, f32[16,32,256]{2,1,0:T(8,128)S(1)}, u32[]{:S(2)}, u32[]{:S(2)}) collective-permute-start(f32[16,32,256]{2,1,0:T(8,128)S(1)} %get-tuple-element.59), channel_id=1, source_target_pairs={{0,12},{4,0},{8,4},{12,8},{1,13},{5,1},{9,5},{13,9},{2,14},{6,2},{... | collective-permute-start | bytes 1572872 | tf_op jit(solution)/shard_map/ppermute | solution.py:458
  64.3 12.5 %collective-permute-start.13 = (f32[15,16,256]{2,1,0:T(8,128)S(1)}, f32[15,16,256]{2,1,0:T(8,128)S(1)}, u32[]{:S(2)}, u32[]{:S(2)}) collective-permute-start(f32[15,16,256]{2,1,0:T(8,128)S(1)} %get-tuple-element.63.refs_1_), channel_id=1, source_target_pairs={{0,1},{1,2},{2,3},{4,5},{5,6},{6,7},{8,9},{9,10},{10,11},{12,13},{... | collective-permute-start | bytes 737288 | tf_op jit(solution)/shard_map/ppermute | solution.py:444
  68.4 9.6 %collective-permute-start.14 = (f32[15,16,256]{2,1,0:T(8,128)S(1)}, f32[15,16,256]{2,1,0:T(8,128)S(1)}, u32[]{:S(2)}, u32[]{:S(2)}) collective-permute-start(f32[15,16,256]{2,1,0:T(8,128)S(1)} %get-tuple-element.62.refs_0_), channel_id=1, source_target_pairs={{1,0},{2,1},{3,2},{5,4},{6,5},{7,6},{9,8},{10,9},{11,10},{13,12},{... | collective-permute-start | bytes 737288 | tf_op jit(solution)/shard_map/ppermute | solution.py:449
  71.4 16.9 %collective-permute-start.11 = (f32[15,32,256]{2,1,0:T(8,128)S(1)}, f32[15,32,256]{2,1,0:T(8,128)S(1)}, u32[]{:S(2)}, u32[]{:S(2)}) collective-permute-start(f32[15,32,256]{2,1,0:T(8,128)S(1)} %get-tuple-element.61.refs_1_), channel_id=1, source_target_pairs={{0,1},{1,2},{2,3},{4,5},{5,6},{6,7},{8,9},{9,10},{10,11},{12,13},{... | collective-permute-start | bytes 1474568 | tf_op jit(solution)/shard_map/ppermute | solution.py:444
  75.5 15.6 %collective-permute-start.12 = (f32[15,32,256]{2,1,0:T(8,128)S(1)}, f32[15,32,256]{2,1,0:T(8,128)S(1)}, u32[]{:S(2)}, u32[]{:S(2)}) collective-permute-start(f32[15,32,256]{2,1,0:T(8,128)S(1)} %get-tuple-element.60.refs_4_.refs_0_), channel_id=1, source_target_pairs={{1,0},{2,1},{3,2},{5,4},{6,5},{7,6},{9,8},{10,9},{11,10},{13,12},{... | collective-permute-start | bytes 1474568 | tf_op jit(solution)/shard_map/ppermute | solution.py:449
  78.9 20.1 %collective-permute-start.17 = (f32[15,16,256]{2,1,0:T(8,128)S(1)}, f32[15,16,256]{2,1,0:T(8,128)S(1)}, u32[]{:S(2)}, u32[]{:S(2)}) collective-permute-start(f32[15,16,256]{2,1,0:T(8,128)S(1)} %get-tuple-element.68.refs_1_), channel_id=1, source_target_pairs={{0,1},{1,2},{2,3},{4,5},{5,6},{6,7},{8,9},{9,10},{10,11},{12,13},{... | collective-permute-start | bytes 737288 | tf_op jit(solution)/shard_map/ppermute | solution.py:444
  82.4 17.9 %collective-permute-start.18 = (f32[15,16,256]{2,1,0:T(8,128)S(1)}, f32[15,16,256]{2,1,0:T(8,128)S(1)}, u32[]{:S(2)}, u32[]{:S(2)}) collective-permute-start(f32[15,16,256]{2,1,0:T(8,128)S(1)} %get-tuple-element.65.refs_4_.refs_0_), channel_id=1, source_target_pairs={{1,0},{2,1},{3,2},{5,4},{6,5},{7,6},{9,8},{10,9},{11,10},{13,12},{... | collective-permute-start | bytes 737288 | tf_op jit(solution)/shard_map/ppermute | solution.py:449
  83.7 27.4 %collective-permute-start.20 = (f32[15,16,256]{2,1,0:T(8,128)S(1)}, f32[15,16,256]{2,1,0:T(8,128)S(1)}, u32[]{:S(2)}, u32[]{:S(2)}) collective-permute-start(f32[15,16,256]{2,1,0:T(8,128)S(1)} %get-tuple-element.72), channel_id=1, source_target_pairs={{0,1},{1,2},{2,3},{4,5},{5,6},{6,7},{8,9},{9,10},{10,11},{12,13},{... | collective-permute-start | bytes 737288 | tf_op jit(solution)/shard_map/ppermute | solution.py:444
  92.5 16.0 %collective-permute-start.15 = (f32[15,32,256]{2,1,0:T(8,128)S(1)}, f32[15,32,256]{2,1,0:T(8,128)S(1)}, u32[]{:S(2)}, u32[]{:S(2)}) collective-permute-start(f32[15,32,256]{2,1,0:T(8,128)S(1)} %get-tuple-element.66.refs_4_.refs_0_), channel_id=1, source_target_pairs={{1,0},{2,1},{3,2},{5,4},{6,5},{7,6},{9,8},{10,9},{11,10},{13,12},{... | collective-permute-start | bytes 1474568 | tf_op jit(solution)/shard_map/ppermute | solution.py:449
  93.8 16.1 %collective-permute-start.16 = (f32[15,32,256]{2,1,0:T(8,128)S(1)}, f32[15,32,256]{2,1,0:T(8,128)S(1)}, u32[]{:S(2)}, u32[]{:S(2)}) collective-permute-start(f32[15,32,256]{2,1,0:T(8,128)S(1)} %get-tuple-element.67.refs_1_), channel_id=1, source_target_pairs={{0,1},{1,2},{2,3},{4,5},{5,6},{6,7},{8,9},{9,10},{10,11},{12,13},{... | collective-permute-start | bytes 1474568 | tf_op jit(solution)/shard_map/ppermute | solution.py:444
  99.1 14.7 %collective-permute-start.21 = (f32[15,16,256]{2,1,0:T(8,128)S(1)}, f32[15,16,256]{2,1,0:T(8,128)S(1)}, u32[]{:S(2)}, u32[]{:S(2)}) collective-permute-start(f32[15,16,256]{2,1,0:T(8,128)S(1)} %get-tuple-element.69.refs_4_.refs_0_), channel_id=1, source_target_pairs={{1,0},{2,1},{3,2},{5,4},{6,5},{7,6},{9,8},{10,9},{11,10},{13,12},{... | collective-permute-start | bytes 737288 | tf_op jit(solution)/shard_map/ppermute | solution.py:449
  101.0 13.7 %collective-permute-start.22 = (f32[15,16,256]{2,1,0:T(8,128)S(1)}, f32[15,16,256]{2,1,0:T(8,128)S(1)}, u32[]{:S(2)}, u32[]{:S(2)}) collective-permute-start(f32[15,16,256]{2,1,0:T(8,128)S(1)} %get-tuple-element.73.refs_1_), channel_id=1, source_target_pairs={{0,1},{1,2},{2,3},{4,5},{5,6},{6,7},{8,9},{9,10},{10,11},{12,13},{... | collective-permute-start | bytes 737288 | tf_op jit(solution)/shard_map/ppermute | solution.py:444
  108.5 10.4 %collective-permute-start.23 = (f32[15,16,256]{2,1,0:T(8,128)S(1)}, f32[15,16,256]{2,1,0:T(8,128)S(1)}, u32[]{:S(2)}, u32[]{:S(2)}) collective-permute-start(f32[15,16,256]{2,1,0:T(8,128)S(1)} %get-tuple-element.70.refs_4_.refs_0_), channel_id=1, source_target_pairs={{1,0},{2,1},{3,2},{5,4},{6,5},{7,6},{9,8},{10,9},{11,10},{13,12},{... | collective-permute-start | bytes 737288 | tf_op jit(solution)/shard_map/ppermute | solution.py:449
  111.1 8.7 %collective-permute-start.19 = (f32[16,32,256]{2,1,0:T(8,128)S(1)}, f32[16,32,256]{2,1,0:T(8,128)S(1)}, u32[]{:S(2)}, u32[]{:S(2)}) collective-permute-start(f32[16,32,256]{2,1,0:T(8,128)S(1)} %shard_map.70.refs_4_.refs_3_), channel_id=1, source_target_pairs={{0,4},{4,8},{8,12},{12,0},{1,5},{5,9},{9,13},{13,1},{2,6},{6,10},{... | collective-permute-start | bytes 1572872 | tf_op jit(solution)/shard_map/ppermute | solution.py:458
  114.4 5.4 %copy-start.1 = (f32[16,64,256]{2,1,0:T(8,128)S(1)}, f32[16,64,256]{2,1,0:T(8,128)}, u32[]{:S(2)}) copy-start(f32[16,64,256]{2,1,0:T(8,128)} %copy-done) | copy-start | bytes 3145732
  114.4 5.4 %copy-start.5 = (bf16[16,2,64,128]{3,2,1,0:T(8,128)(2,1)S(1)}, bf16[16,2,64,128]{3,2,1,0:T(8,128)(2,1)}, u32[]{:S(2)}) copy-start(bf16[16,2,64,128]{3,2,1,0:T(8,128)(2,1)} %copy-done.4) | copy-start | bytes 1572868

commit v12 on v11

--- a/solution.py
+++ b/solution.py
@@ -8,7 +8,7 @@
 from jax.sharding import PartitionSpec as P
 
 ITERS = 2
-GROUPS = 4
+GROUPS = 2
 F32 = jnp.float32
 BF16 = jnp.bfloat16
 PARAMS = pltpu.CompilerParams(vmem_limit_bytes=16 * 1024 * 1024)

time: 123 us -> 123 us (level)
  no operation moved by 1% of the time
where the time goes in v12:
time: 123 us; the launch traced here: 122 us
  starting transfers between devices  59.7 us (49%)
  waiting for transfers between devices  35.2 us (29%)
  Pallas kernels  22.2 us (18%)
  local copies, waits for them, and re-layouts  4.38 us (4%)
    ppermute x10, starting transfers between devices, send_up(): return lax.ppermute(x, 'slab', [(i, i + 1) for i in steps])  43.4 us
    ppermute x10, waiting for transfers between devices, send_down(): return lax.ppermute(x, 'slab', [(i + 1, i) for i in steps])  16.6 us
    ppermute x10, waiting for transfers between devices, send_up(): return lax.ppermute(x, 'slab', [(i, i + 1) for i in steps])  15.8 us
    ppermute x10, starting transfers between devices, send_down(): return lax.ppermute(x, 'slab', [(i + 1, i) for i in steps])  13 us
    pallas_call x6, Pallas kernels, depth_ratio(): pl.pallas_call(functools.partial(ratio_kernel, n, radius, skip), in_specs...  5.89 us
    pallas_call x5, Pallas kernels, depth_back(): pl.pallas_call(functools.partial(back_kernel, n, radius, swapped), in_spe...  4.77 us
    pallas_call x2, Pallas kernels, update(): pl.pallas_call(functools.partial(update_kernel, n, last, len(pieces)), in...  4.33 us
    unnamed x20, local copies, waits for them, and re-layouts  3.3 us
  transfers between devices with their start and end apart: 24, of which 16 were waited for; matrix products, arithmetic and copies ran while one was open for 0% of the time, Pallas kernels for 14%

profile of v12, /device:TPU:0, one launch (start us, length us, event | category | flops | bytes accessed | tf_op | source)
XLA Modules:
  0.0 121.8 jit_solution(932221975664366126)
XLA Ops:
  0.0 1.1 slice.3
  1.1 2.4 %collective-permute-start = (f32[16,32,256]{2,1,0:T(8,128)S(1)}, f32[16,32,256]{2,1,0:T(8,128)S(1)}, u32[]{:S(2)}, u32[]{:S(2)}) collective-permute-start(f32[16,32,256]{2,1,0:T(8,128)S(1)} %slice.3), channel_id=1, source_target_pairs={{0,12},{4,0},{8,4},{12,8},{1,13},{5,1},{9,5},{13,9},{2,14},{6,2},{... | collective-permute-start | bytes 1572872 | tf_op jit(solution)/shard_map/ppermute | solution.py:458
  3.5 1.2 %copy-done.2 = f32[16,64,256]{2,1,0:T(8,128)S(1)} copy-done((f32[16,64,256]{2,1,0:T(8,128)S(1)}, f32[16,64,256]{2,1,0:T(8,128)}, u32[]{:S(2)}) %copy-start.2) | copy-done | bytes 1048600
  4.7 0.7 copy-done.6
  5.4 0.7 copy-done.7
  6.1 0.7 copy-done.8
  6.8 2.2 %shard_map.55 = (bf16[16,256,256]{2,1,0:T(8,128)(2,1)S(1)}, bf16[16,256,256]{2,1,0:T(8,128)(2,1)S(1)}, bf16[16,2,64,128]{3,2,1,0:T(8,128)(2,1)S(1)}, f32[16,64,256]{2,1,0:T(8,128)S(1)}) custom-call(s32[16]{0:T(128)S(1)} %copy-done.8, f32[16,31]{1,0:T(8,128)S(1)} %copy-done.6, f32[16,31]{1,0:T(8,128)S(1)} %copy-done.7, f32[16,64,256]{2,1,0:T(8,128)S(1)} %copy-done.2), custom_call_target="tpu_custom_call" | custom-call | flops 1000000000 | bytes 3500000 | tf_op jit(solution)/shard_map/pallas_call | solution.py:161
  9.0 1.2 collective-permute-done.next_ref
  10.2 1.1 shard_map.56
  11.3 1.4 %collective-permute-start.2 = (f32[15,32,256]{2,1,0:T(8,128)S(1)}, f32[15,32,256]{2,1,0:T(8,128)S(1)}, u32[]{:S(2)}, u32[]{:S(2)}) collective-permute-start(f32[15,32,256]{2,1,0:T(8,128)S(1)} %get-tuple-element.44.refs_0_), channel_id=1, source_target_pairs={{1,0},{2,1},{3,2},{5,4},{6,5},{7,6},{9,8},{10,9},{11,10},{13,12},{... | collective-permute-start | bytes 1474568 | tf_op jit(solution)/shard_map/ppermute | solution.py:449
  12.8 4.6 %collective-permute-start.1 = (f32[15,32,256]{2,1,0:T(8,128)S(1)}, f32[15,32,256]{2,1,0:T(8,128)S(1)}, u32[]{:S(2)}, u32[]{:S(2)}) collective-permute-start(f32[15,32,256]{2,1,0:T(8,128)S(1)} %get-tuple-element.48.refs_1_), channel_id=1, source_target_pairs={{0,1},{1,2},{2,3},{4,5},{5,6},{6,7},{8,9},{9,10},{10,11},{12,13},{... | collective-permute-start | bytes 1474568 | tf_op jit(solution)/shard_map/ppermute | solution.py:444
  17.3 0.4 shard_map.57
  17.7 1.3 %collective-permute-start.6 = (f32[15,32,256]{2,1,0:T(8,128)S(1)}, f32[15,32,256]{2,1,0:T(8,128)S(1)}, u32[]{:S(2)}, u32[]{:S(2)}) collective-permute-start(f32[15,32,256]{2,1,0:T(8,128)S(1)} %get-tuple-element.45.after_ref.refs_4_.refs_0_), channel_id=1, source_target_pairs={{1,0},{2,1},{3,2},{5,4},{6,5},{7,6},{9,8},{10,9},{11,10},{13,12},{... | collective-permute-start | bytes 1474568 | tf_op jit(solution)/shard_map/ppermute | solution.py:449
  19.0 4.6 %collective-permute-start.5 = (f32[15,32,256]{2,1,0:T(8,128)S(1)}, f32[15,32,256]{2,1,0:T(8,128)S(1)}, u32[]{:S(2)}, u32[]{:S(2)}) collective-permute-start(f32[15,32,256]{2,1,0:T(8,128)S(1)} %get-tuple-element.51.refs_1_), channel_id=1, source_target_pairs={{0,1},{1,2},{2,3},{4,5},{5,6},{6,7},{8,9},{9,10},{10,11},{12,13},{... | collective-permute-start | bytes 1474568 | tf_op jit(solution)/shard_map/ppermute | solution.py:444
  23.6 2.8 %shard_map.58 = (bf16[16,256,256]{2,1,0:T(8,128)(2,1)S(1)}, bf16[16,256,256]{2,1,0:T(8,128)(2,1)S(1)}, bf16[16,2,64,128]{3,2,1,0:T(8,128)(2,1)S(1)}, f32[16,64,2...) custom-call(s32[16]{0:T(128)S(1)} %copy-done.8, f32[16,31]{1,0:T(8,128)S(1)} %copy-done.6, ...), custom_call_target="tpu_custom_call" | custom-call | flops 1000000000 | bytes 3500000 | tf_op jit(solution)/shard_map/pallas_call | solution.py:226
  26.4 1.0 collective-permute-done.2.refs_3_
  27.4 1.4 %collective-permute-done.1.refs_2_ = f32[15,32,256]{2,1,0:T(8,128)S(1)} collective-permute-done((f32[15,32,256]{2,1,0:T(8,128)S(1)}, f32[15,32,256]{2,1,0:T(8,128)S(1)}, u32[]{:S(2)}, u32[]{:S(2)}) %collective-permute-start.1) | collective-permute-done | bytes 491552 | tf_op jit(solution)/shard_map/ppermute | solution.py:444
  28.8 1.3 %shard_map.59 = (f32[15,32,256]{2,1,0:T(8,128)S(1)}, f32[15,32,256]{2,1,0:T(8,128)S(1)}) custom-call(f32[31,8,128]{2,1,0:T(8,128)S(1)} %get-tuple-element.46.tz_ref, f32[16,64,256]{2,1,0:T(8,128)S(1)} %get-tuple-element.47.obs_ref, f32[15,32,256]{2,1,0:T(8,128)S(1)} %get-tuple-element.44.refs_0_, f32[15,32,256]{2,1,0:T(8,128)S(1)} %get-tuple-element.48.refs_1_, ...), custom_call_target="tpu_custom_call" | custom-call | flops 1000000000 | bytes 3500000 | tf_op jit(solution)/shard_map/pallas_call | solution.py:342
  30.1 4.4 %collective-permute-start.3 = (f32[15,32,256]{2,1,0:T(8,128)S(1)}, f32[15,32,256]{2,1,0:T(8,128)S(1)}, u32[]{:S(2)}, u32[]{:S(2)}) collective-permute-start(f32[15,32,256]{2,1,0:T(8,128)S(1)} %get-tuple-element.50.refs_1_), channel_id=1, source_target_pairs={{0,1},{1,2},{2,3},{4,5},{5,6},{6,7},{8,9},{9,10},{10,11},{12,13},{... | collective-permute-start | bytes 1474568 | tf_op jit(solution)/shard_map/ppermute | solution.py:444
  34.6 1.3 %collective-permute-start.4 = (f32[15,32,256]{2,1,0:T(8,128)S(1)}, f32[15,32,256]{2,1,0:T(8,128)S(1)}, u32[]{:S(2)}, u32[]{:S(2)}) collective-permute-start(f32[15,32,256]{2,1,0:T(8,128)S(1)} %get-tuple-element.49.refs_4_.refs_0_), channel_id=1, source_target_pairs={{1,0},{2,1},{3,2},{5,4},{6,5},{7,6},{9,8},{10,9},{11,10},{13,12},{... | collective-permute-start | bytes 1474568 | tf_op jit(solution)/shard_map/ppermute | solution.py:449
  35.9 2.0 %collective-permute-done.6.refs_3_ = f32[15,32,256]{2,1,0:T(8,128)S(1)} collective-permute-done((f32[15,32,256]{2,1,0:T(8,128)S(1)}, f32[15,32,256]{2,1,0:T(8,128)S(1)}, u32[]{:S(2)}, u32[]{:S(2)}) %collective-permute-start.6) | collective-permute-done | bytes 491552 | tf_op jit(solution)/shard_map/ppermute | solution.py:449
  37.8 1.5 %collective-permute-done.5.refs_2_ = f32[15,32,256]{2,1,0:T(8,128)S(1)} collective-permute-done((f32[15,32,256]{2,1,0:T(8,128)S(1)}, f32[15,32,256]{2,1,0:T(8,128)S(1)}, u32[]{:S(2)}, u32[]{:S(2)}) %collective-permute-start.5) | collective-permute-done | bytes 491552 | tf_op jit(solution)/shard_map/ppermute | solution.py:444
  39.3 1.3 %shard_map.60 = (f32[15,32,256]{2,1,0:T(8,128)S(1)}, f32[15,32,256]{2,1,0:T(8,128)S(1)}) custom-call(f32[31,8,128]{2,1,0:T(8,128)S(1)} %get-tuple-element.46.tz_ref, f32[16,64,256]{2,1,0:T(8,128)S(1)} %get-tuple-element.47.obs_ref, f32[15,32,256]{2,1,0:T(8,128)S(1)} %get-tuple-element.45.after_ref.refs_4_.refs_0_, ...), custom_call_target="tpu_custom_call" | custom-call | flops 1000000000 | bytes 3500000 | tf_op jit(solution)/shard_map/pallas_call | solution.py:342
  40.6 4.4 %collective-permute-start.8 = (f32[15,32,256]{2,1,0:T(8,128)S(1)}, f32[15,32,256]{2,1,0:T(8,128)S(1)}, u32[]{:S(2)}, u32[]{:S(2)}) collective-permute-start(f32[15,32,256]{2,1,0:T(8,128)S(1)} %get-tuple-element.53.refs_1_), channel_id=1, source_target_pairs={{0,1},{1,2},{2,3},{4,5},{5,6},{6,7},{8,9},{9,10},{10,11},{12,13},{... | collective-permute-start | bytes 1474568 | tf_op jit(solution)/shard_map/ppermute | solution.py:444
  45.1 1.3 %collective-permute-start.9 = (f32[15,32,256]{2,1,0:T(8,128)S(1)}, f32[15,32,256]{2,1,0:T(8,128)S(1)}, u32[]{:S(2)}, u32[]{:S(2)}) collective-permute-start(f32[15,32,256]{2,1,0:T(8,128)S(1)} %get-tuple-element.52.refs_4_.refs_0_), channel_id=1, source_target_pairs={{1,0},{2,1},{3,2},{5,4},{6,5},{7,6},{9,8},{10,9},{11,10},{13,12},{... | collective-permute-start | bytes 1474568 | tf_op jit(solution)/shard_map/ppermute | solution.py:449
  46.4 3.5 %collective-permute-done.3.refs_2_ = f32[15,32,256]{2,1,0:T(8,128)S(1)} collective-permute-done((f32[15,32,256]{2,1,0:T(8,128)S(1)}, f32[15,32,256]{2,1,0:T(8,128)S(1)}, u32[]{:S(2)}, u32[]{:S(2)}) %collective-permute-start.3) | collective-permute-done | bytes 491552 | tf_op jit(solution)/shard_map/ppermute | solution.py:444
  49.9 1.2 shard_map.61.refs_4_.refs_2_
  51.1 0.1 collective-permute-start.7
  51.1 9.0 %collective-permute-done.8.refs_2_ = f32[15,32,256]{2,1,0:T(8,128)S(1)} collective-permute-done((f32[15,32,256]{2,1,0:T(8,128)S(1)}, f32[15,32,256]{2,1,0:T(8,128)S(1)}, u32[]{:S(2)}, u32[]{:S(2)}) %collective-permute-start.8) | collective-permute-done | bytes 491552 | tf_op jit(solution)/shard_map/ppermute | solution.py:444
  60.1 1.2 shard_map.62.refs_1_
  61.3 2.2 %shard_map.63 = (f32[16,64,256]{2,1,0:T(8,128)S(1)}, f32[16,64,256]{2,1,0:T(8,128)S(1)}, f32[16,32,256]{2,1,0:T(8,128)S(1)}, f32[15,16,256]{2,1,0:T(8,128)S(1)}, f32[15,16,256]{2,1,0:T(8,128)S(1)}) custom-call(f32[16,32,256]{2,1,0:T(8,128)S(1)} %collective-permute-done.7.refs_0_, f32[16,32,256]{2,1,0:T(8,128)S(1)} %shard_map.62.refs_1_, ...), custom_call_target="tpu_custom_call" | custom-call | flops 1000000000 | bytes 3500000 | tf_op jit(solution)/shard_map/pallas_call | solution.py:431
  63.6 0.7 collective-permute-start.10
  64.3 4.1 %collective-permute-start.13 = (f32[15,16,256]{2,1,0:T(8,128)S(1)}, f32[15,16,256]{2,1,0:T(8,128)S(1)}, u32[]{:S(2)}, u32[]{:S(2)}) collective-permute-start(f32[15,16,256]{2,1,0:T(8,128)S(1)} %get-tuple-element.63.refs_1_), channel_id=1, source_target_pairs={{0,1},{1,2},{2,3},{4,5},{5,6},{6,7},{8,9},{9,10},{10,11},{12,13},{... | collective-permute-start | bytes 737288 | tf_op jit(solution)/shard_map/ppermute | solution.py:444
  68.4 1.3 %collective-permute-start.14 = (f32[15,16,256]{2,1,0:T(8,128)S(1)}, f32[15,16,256]{2,1,0:T(8,128)S(1)}, u32[]{:S(2)}, u32[]{:S(2)}) collective-permute-start(f32[15,16,256]{2,1,0:T(8,128)S(1)} %get-tuple-element.62.refs_0_), channel_id=1, source_target_pairs={{1,0},{2,1},{3,2},{5,4},{6,5},{7,6},{9,8},{10,9},{11,10},{13,12},{... | collective-permute-start | bytes 737288 | tf_op jit(solution)/shard_map/ppermute | solution.py:449
  69.7 1.3 %collective-permute-done.10.next_ref = f32[16,32,256]{2,1,0:T(8,128)S(1)} collective-permute-done((f32[16,32,256]{2,1,0:T(8,128)S(1)}, f32[16,32,256]{2,1,0:T(8,128)S(1)}, u32[]{:S(2)}, u32[]{:S(2)}) %collective-permute-start.10) | collective-permute-done | bytes 524320 | tf_op jit(solution)/shard_map/ppermute | solution.py:458
  71.0 0.4 shard_map.64
  71.4 4.1 %collective-permute-start.11 = (f32[15,32,256]{2,1,0:T(8,128)S(1)}, f32[15,32,256]{2,1,0:T(8,128)S(1)}, u32[]{:S(2)}, u32[]{:S(2)}) collective-permute-start(f32[15,32,256]{2,1,0:T(8,128)S(1)} %get-tuple-element.61.refs_1_), channel_id=1, source_target_pairs={{0,1},{1,2},{2,3},{4,5},{5,6},{6,7},{8,9},{9,10},{10,11},{12,13},{... | collective-permute-start | bytes 1474568 | tf_op jit(solution)/shard_map/ppermute | solution.py:444
  75.5 1.3 %collective-permute-start.12 = (f32[15,32,256]{2,1,0:T(8,128)S(1)}, f32[15,32,256]{2,1,0:T(8,128)S(1)}, u32[]{:S(2)}, u32[]{:S(2)}) collective-permute-start(f32[15,32,256]{2,1,0:T(8,128)S(1)} %get-tuple-element.60.refs_4_.refs_0_), channel_id=1, source_target_pairs={{1,0},{2,1},{3,2},{5,4},{6,5},{7,6},{9,8},{10,9},{11,10},{13,12},{... | collective-permute-start | bytes 1474568 | tf_op jit(solution)/shard_map/ppermute | solution.py:449
  76.8 1.1 collective-permute-done.14.refs_3_
  78.0 0.7 shard_map.65
  78.6 0.3 shard_map.66
  78.9 3.5 %collective-permute-start.17 = (f32[15,16,256]{2,1,0:T(8,128)S(1)}, f32[15,16,256]{2,1,0:T(8,128)S(1)}, u32[]{:S(2)}, u32[]{:S(2)}) collective-permute-start(f32[15,16,256]{2,1,0:T(8,128)S(1)} %get-tuple-element.68.refs_1_), channel_id=1, source_target_pairs={{0,1},{1,2},{2,3},{4,5},{5,6},{6,7},{8,9},{9,10},{10,11},{12,13},{... | collective-permute-start | bytes 737288 | tf_op jit(solution)/shard_map/ppermute | solution.py:444
  82.4 1.3 %collective-permute-start.18 = (f32[15,16,256]{2,1,0:T(8,128)S(1)}, f32[15,16,256]{2,1,0:T(8,128)S(1)}, u32[]{:S(2)}, u32[]{:S(2)}) collective-permute-start(f32[15,16,256]{2,1,0:T(8,128)S(1)} %get-tuple-element.65.refs_4_.refs_0_), channel_id=1, source_target_pairs={{1,0},{2,1},{3,2},{5,4},{6,5},{7,6},{9,8},{10,9},{11,10},{13,12},{... | collective-permute-start | bytes 737288 | tf_op jit(solution)/shard_map/ppermute | solution.py:449
  83.7 4.6 %collective-permute-start.20 = (f32[15,16,256]{2,1,0:T(8,128)S(1)}, f32[15,16,256]{2,1,0:T(8,128)S(1)}, u32[]{:S(2)}, u32[]{:S(2)}) collective-permute-start(f32[15,16,256]{2,1,0:T(8,128)S(1)} %get-tuple-element.72), channel_id=1, source_target_pairs={{0,1},{1,2},{2,3},{4,5},{5,6},{6,7},{8,9},{9,10},{10,11},{12,13},{... | collective-permute-start | bytes 737288 | tf_op jit(solution)/shard_map/ppermute | solution.py:444
  88.3 2.9 %collective-permute-done.12.refs_3_ = f32[15,32,256]{2,1,0:T(8,128)S(1)} collective-permute-done((f32[15,32,256]{2,1,0:T(8,128)S(1)}, f32[15,32,256]{2,1,0:T(8,128)S(1)}, u32[]{:S(2)}, u32[]{:S(2)}) %collective-permute-start.12) | collective-permute-done | bytes 491552 | tf_op jit(solution)/shard_map/ppermute | solution.py:449
  91.2 1.3 %shard_map.67 = (f32[15,32,256]{2,1,0:T(8,128)S(1)}, f32[15,32,256]{2,1,0:T(8,128)S(1)}) custom-call(f32[31,8,128]{2,1,0:T(8,128)S(1)} %get-tuple-element.46.tz_ref, f32[16,64,256]{2,1,0:T(8,128)S(1)} %get-tuple-element.47.obs_ref, f32[15,32,256]{2,1,0:T(8,128)S(1)} %get-tuple-element.60.refs_4_.refs_0_, f32[15,32,256]{2,1,0:T(8,128)S(1)} %get-tuple-element.61.refs_1_, ...), custom_call_target="tpu_custom_call" | custom-call | flops 1000000000 | bytes 3500000 | tf_op jit(solution)/shard_map/pallas_call | solution.py:342
  92.5 1.3 %collective-permute-start.15 = (f32[15,32,256]{2,1,0:T(8,128)S(1)}, f32[15,32,256]{2,1,0:T(8,128)S(1)}, u32[]{:S(2)}, u32[]{:S(2)}) collective-permute-start(f32[15,32,256]{2,1,0:T(8,128)S(1)} %get-tuple-element.66.refs_4_.refs_0_), channel_id=1, source_target_pairs={{1,0},{2,1},{3,2},{5,4},{6,5},{7,6},{9,8},{10,9},{11,10},{13,12},{... | collective-permute-start | bytes 1474568 | tf_op jit(solution)/shard_map/ppermute | solution.py:449
  93.8 4.6 %collective-permute-start.16 = (f32[15,32,256]{2,1,0:T(8,128)S(1)}, f32[15,32,256]{2,1,0:T(8,128)S(1)}, u32[]{:S(2)}, u32[]{:S(2)}) collective-permute-start(f32[15,32,256]{2,1,0:T(8,128)S(1)} %get-tuple-element.67.refs_1_), channel_id=1, source_target_pairs={{0,1},{1,2},{2,3},{4,5},{5,6},{6,7},{8,9},{9,10},{10,11},{12,13},{... | collective-permute-start | bytes 1474568 | tf_op jit(solution)/shard_map/ppermute | solution.py:444
  98.4 0.7 shard_map.68
  99.1 1.3 %collective-permute-start.21 = (f32[15,16,256]{2,1,0:T(8,128)S(1)}, f32[15,16,256]{2,1,0:T(8,128)S(1)}, u32[]{:S(2)}, u32[]{:S(2)}) collective-permute-start(f32[15,16,256]{2,1,0:T(8,128)S(1)} %get-tuple-element.69.refs_4_.refs_0_), channel_id=1, source_target_pairs={{1,0},{2,1},{3,2},{5,4},{6,5},{7,6},{9,8},{10,9},{11,10},{13,12},{... | collective-permute-start | bytes 737288 | tf_op jit(solution)/shard_map/ppermute | solution.py:449
  100.4 0.7 shard_map.69
  101.0 4.6 %collective-permute-start.22 = (f32[15,16,256]{2,1,0:T(8,128)S(1)}, f32[15,16,256]{2,1,0:T(8,128)S(1)}, u32[]{:S(2)}, u32[]{:S(2)}) collective-permute-start(f32[15,16,256]{2,1,0:T(8,128)S(1)} %get-tuple-element.73.refs_1_), channel_id=1, source_target_pairs={{0,1},{1,2},{2,3},{4,5},{5,6},{6,7},{8,9},{9,10},{10,11},{12,13},{... | collective-permute-start | bytes 737288 | tf_op jit(solution)/shard_map/ppermute | solution.py:444
  105.6 2.9 %collective-permute-done.15.refs_2_ = f32[15,32,256]{2,1,0:T(8,128)S(1)} collective-permute-done((f32[15,32,256]{2,1,0:T(8,128)S(1)}, f32[15,32,256]{2,1,0:T(8,128)S(1)}, u32[]{:S(2)}, u32[]{:S(2)}) %collective-permute-start.15) | collective-permute-done | bytes 491552 | tf_op jit(solution)/shard_map/ppermute | solution.py:449
  108.5 1.3 %collective-permute-start.23 = (f32[15,16,256]{2,1,0:T(8,128)S(1)}, f32[15,16,256]{2,1,0:T(8,128)S(1)}, u32[]{:S(2)}, u32[]{:S(2)}) collective-permute-start(f32[15,16,256]{2,1,0:T(8,128)S(1)} %get-tuple-element.70.refs_4_.refs_0_), channel_id=1, source_target_pairs={{1,0},{2,1},{3,2},{5,4},{6,5},{7,6},{9,8},{10,9},{11,10},{13,12},{... | collective-permute-start | bytes 737288 | tf_op jit(solution)/shard_map/ppermute | solution.py:449
  109.8 0.1 collective-permute-done.16.refs_3_
  109.9 1.2 shard_map.70.refs_4_.refs_3_
  111.1 0.1 collective-permute-start.19
  111.2 2.6 %collective-permute-done.21.refs_3_ = f32[15,16,256]{2,1,0:T(8,128)S(1)} collective-permute-done((f32[15,16,256]{2,1,0:T(8,128)S(1)}, f32[15,16,256]{2,1,0:T(8,128)S(1)}, u32[]{:S(2)}, u32[]{:S(2)}) %collective-permute-start.21) | collective-permute-done | bytes 245792 | tf_op jit(solution)/shard_map/ppermute | solution.py:449
  113.8 0.6 shard_map.71.refs_4_.refs_1_
  114.4 0.4 collective-permute-done.22.refs_2_
  114.8 4.1 %collective-permute-done.23.refs_3_ = f32[15,16,256]{2,1,0:T(8,128)S(1)} collective-permute-done((f32[15,16,256]{2,1,0:T(8,128)S(1)}, f32[15,16,256]{2,1,0:T(8,128)S(1)}, u32[]{:S(2)}, u32[]{:S(2)}) %collective-permute-start.23) | collective-permute-done | bytes 245792 | tf_op jit(solution)/shard_map/ppermute | solution.py:449
  118.9 0.6 shard_map.72.refs_2_
  119.5 0.3 collective-permute-done.19.refs_0_
  119.8 2.1 %shard_map.73 = f32[16,64,256]{2,1,0:T(8,128)} custom-call(f32[16,32,256]{2,1,0:T(8,128)S(1)} %collective-permute-done.19.refs_0_, f32[16,16,256]{2,1,0:T(8,128)S(1)} %shard_map.71.refs_4_.refs_1_, f32[16,16,256]{2,1,0:T(8,128)S(1)} %shard_map.72.refs_2_, f32[16,32,256]{2,1,0:T(8,128)S(1)} %shard_map.70.refs_4_.refs_3_, ...), custom_call_target="tpu_custom_call" | custom-call | flops 1000000000 | bytes 3500000 | tf_op jit(solution)/shard_map/pallas_call | solution.py:431
  (24 shorter events, 0.1 us)
Async XLA Ops:
  1.1 9.1 %collective-permute-start = (f32[16,32,256]{2,1,0:T(8,128)S(1)}, f32[16,32,256]{2,1,0:T(8,128)S(1)}, u32[]{:S(2)}, u32[]{:S(2)}) collective-permute-start(f32[16,32,256]{2,1,0:T(8,128)S(1)} %slice.3), channel_id=1, source_target_pairs={{0,12},{4,0},{8,4},{12,8},{1,13},{5,1},{9,5},{13,9},{2,14},{6,2},{... | collective-permute-start | bytes 1572872 | tf_op jit(solution)/shard_map/ppermute | solution.py:458
  3.5 1.2 %copy-start.2 = (f32[16,64,256]{2,1,0:T(8,128)S(1)}, f32[16,64,256]{2,1,0:T(8,128)}, u32[]{:S(2)}) copy-start(f32[16,64,256]{2,1,0:T(8,128)} %refs_3_.1) | copy-start | bytes 3145732
  4.7 0.7 copy-start.6
  5.4 0.7 copy-start.7
  6.1 0.7 copy-start.8
  11.3 12.3 %copy-start.3 = (f32[16,64,256]{2,1,0:T(8,128)S(1)}, f32[16,64,256]{2,1,0:T(8,128)}, u32[]{:S(2)}) copy-start(f32[16,64,256]{2,1,0:T(8,128)} %refs_3_.1) | copy-start | bytes 3145732
  11.3 12.3 %copy-start.9 = (f32[31]{0:T(128)S(1)}, f32[31]{0:T(128)}, u32[]{:S(2)}) copy-start(f32[31]{0:T(128)} %tz_ref.1) | copy-start | bytes 376
  11.3 16.1 %collective-permute-start.2 = (f32[15,32,256]{2,1,0:T(8,128)S(1)}, f32[15,32,256]{2,1,0:T(8,128)S(1)}, u32[]{:S(2)}, u32[]{:S(2)}) collective-permute-start(f32[15,32,256]{2,1,0:T(8,128)S(1)} %get-tuple-element.44.refs_0_), channel_id=1, source_target_pairs={{1,0},{2,1},{3,2},{5,4},{6,5},{7,6},{9,8},{10,9},{11,10},{13,12},{... | collective-permute-start | bytes 1474568 | tf_op jit(solution)/shard_map/ppermute | solution.py:449
  12.8 16.1 %collective-permute-start.1 = (f32[15,32,256]{2,1,0:T(8,128)S(1)}, f32[15,32,256]{2,1,0:T(8,128)S(1)}, u32[]{:S(2)}, u32[]{:S(2)}) collective-permute-start(f32[15,32,256]{2,1,0:T(8,128)S(1)} %get-tuple-element.48.refs_1_), channel_id=1, source_target_pairs={{0,1},{1,2},{2,3},{4,5},{5,6},{6,7},{8,9},{9,10},{10,11},{12,13},{... | collective-permute-start | bytes 1474568 | tf_op jit(solution)/shard_map/ppermute | solution.py:444
  17.7 20.2 %collective-permute-start.6 = (f32[15,32,256]{2,1,0:T(8,128)S(1)}, f32[15,32,256]{2,1,0:T(8,128)S(1)}, u32[]{:S(2)}, u32[]{:S(2)}) collective-permute-start(f32[15,32,256]{2,1,0:T(8,128)S(1)} %get-tuple-element.45.after_ref.refs_4_.refs_0_), channel_id=1, source_target_pairs={{1,0},{2,1},{3,2},{5,4},{6,5},{7,6},{9,8},{10,9},{11,10},{13,12},{... | collective-permute-start | bytes 1474568 | tf_op jit(solution)/shard_map/ppermute | solution.py:449
  19.0 20.4 %collective-permute-start.5 = (f32[15,32,256]{2,1,0:T(8,128)S(1)}, f32[15,32,256]{2,1,0:T(8,128)S(1)}, u32[]{:S(2)}, u32[]{:S(2)}) collective-permute-start(f32[15,32,256]{2,1,0:T(8,128)S(1)} %get-tuple-element.51.refs_1_), channel_id=1, source_target_pairs={{0,1},{1,2},{2,3},{4,5},{5,6},{6,7},{8,9},{9,10},{10,11},{12,13},{... | collective-permute-start | bytes 1474568 | tf_op jit(solution)/shard_map/ppermute | solution.py:444
  26.4 34.9 %copy-start = (f32[16,64,256]{2,1,0:T(8,128)}, f32[16,64,256]{2,1,0:T(8,128)S(1)}, u32[]{:S(2)}) copy-start(f32[16,64,256]{2,1,0:T(8,128)S(1)} %get-tuple-element.54.refs_4_.refs_5_) | copy-start | bytes 3145732
  26.4 34.9 %copy-start.4 = (bf16[16,2,64,128]{3,2,1,0:T(8,128)(2,1)}, bf16[16,2,64,128]{3,2,1,0:T(8,128)(2,1)S(1)}, u32[]{:S(2)}) copy-start(bf16[16,2,64,128]{3,2,1,0:T(8,128)(2,1)S(1)} %get-tuple-element.55.refs_5_.refs_6_) | copy-start | bytes 1572868
  30.1 19.7 %collective-permute-start.3 = (f32[15,32,256]{2,1,0:T(8,128)S(1)}, f32[15,32,256]{2,1,0:T(8,128)S(1)}, u32[]{:S(2)}, u32[]{:S(2)}) collective-permute-start(f32[15,32,256]{2,1,0:T(8,128)S(1)} %get-tuple-element.50.refs_1_), channel_id=1, source_target_pairs={{0,1},{1,2},{2,3},{4,5},{5,6},{6,7},{8,9},{9,10},{10,11},{12,13},{... | collective-permute-start | bytes 1474568 | tf_op jit(solution)/shard_map/ppermute | solution.py:444
  34.6 15.3 %collective-permute-start.4 = (f32[15,32,256]{2,1,0:T(8,128)S(1)}, f32[15,32,256]{2,1,0:T(8,128)S(1)}, u32[]{:S(2)}, u32[]{:S(2)}) collective-permute-start(f32[15,32,256]{2,1,0:T(8,128)S(1)} %get-tuple-element.49.refs_4_.refs_0_), channel_id=1, source_target_pairs={{1,0},{2,1},{3,2},{5,4},{6,5},{7,6},{9,8},{10,9},{11,10},{13,12},{... | collective-permute-start | bytes 1474568 | tf_op jit(solution)/shard_map/ppermute | solution.py:449
  40.6 19.4 %collective-permute-start.8 = (f32[15,32,256]{2,1,0:T(8,128)S(1)}, f32[15,32,256]{2,1,0:T(8,128)S(1)}, u32[]{:S(2)}, u32[]{:S(2)}) collective-permute-start(f32[15,32,256]{2,1,0:T(8,128)S(1)} %get-tuple-element.53.refs_1_), channel_id=1, source_target_pairs={{0,1},{1,2},{2,3},{4,5},{5,6},{6,7},{8,9},{9,10},{10,11},{12,13},{... | collective-permute-start | bytes 1474568 | tf_op jit(solution)/shard_map/ppermute | solution.py:444
  45.1 15.0 %collective-permute-start.9 = (f32[15,32,256]{2,1,0:T(8,128)S(1)}, f32[15,32,256]{2,1,0:T(8,128)S(1)}, u32[]{:S(2)}, u32[]{:S(2)}) collective-permute-start(f32[15,32,256]{2,1,0:T(8,128)S(1)} %get-tuple-element.52.refs_4_.refs_0_), channel_id=1, source_target_pairs={{1,0},{2,1},{3,2},{5,4},{6,5},{7,6},{9,8},{10,9},{11,10},{13,12},{... | collective-permute-start | bytes 1474568 | tf_op jit(solution)/shard_map/ppermute | solution.py:449
  51.1 10.2 %collective-permute-start.7 = (f32[16,32,256]{2,1,0:T(8,128)S(1)}, f32[16,32,256]{2,1,0:T(8,128)S(1)}, u32[]{:S(2)}, u32[]{:S(2)}) collective-permute-start(f32[16,32,256]{2,1,0:T(8,128)S(1)} %shard_map.61.refs_4_.refs_2_), channel_id=1, source_target_pairs={{0,4},{4,8},{8,12},{12,0},{1,5},{5,9},{9,13},{13,1},{2,6},{6,10},{... | collective-permute-start | bytes 1572872 | tf_op jit(solution)/shard_map/ppermute | solution.py:458
  63.6 7.4 %collective-permute-start.10 = (f32[16,32,256]{2,1,0:T(8,128)S(1)}, f32[16,32,256]{2,1,0:T(8,128)S(1)}, u32[]{:S(2)}, u32[]{:S(2)}) collective-permute-start(f32[16,32,256]{2,1,0:T(8,128)S(1)} %get-tuple-element.59), channel_id=1, source_target_pairs={{0,12},{4,0},{8,4},{12,8},{1,13},{5,1},{9,5},{13,9},{2,14},{6,2},{... | collective-permute-start | bytes 1572872 | tf_op jit(solution)/shard_map/ppermute | solution.py:458
  64.3 12.5 %collective-permute-start.13 = (f32[15,16,256]{2,1,0:T(8,128)S(1)}, f32[15,16,256]{2,1,0:T(8,128)S(1)}, u32[]{:S(2)}, u32[]{:S(2)}) collective-permute-start(f32[15,16,256]{2,1,0:T(8,128)S(1)} %get-tuple-element.63.refs_1_), channel_id=1, source_target_pairs={{0,1},{1,2},{2,3},{4,5},{5,6},{6,7},{8,9},{9,10},{10,11},{12,13},{... | collective-permute-start | bytes 737288 | tf_op jit(solution)/shard_map/ppermute | solution.py:444
  68.4 9.6 %collective-permute-start.14 = (f32[15,16,256]{2,1,0:T(8,128)S(1)}, f32[15,16,256]{2,1,0:T(8,128)S(1)}, u32[]{:S(2)}, u32[]{:S(2)}) collective-permute-start(f32[15,16,256]{2,1,0:T(8,128)S(1)} %get-tuple-element.62.refs_0_), channel_id=1, source_target_pairs={{1,0},{2,1},{3,2},{5,4},{6,5},{7,6},{9,8},{10,9},{11,10},{13,12},{... | collective-permute-start | bytes 737288 | tf_op jit(solution)/shard_map/ppermute | solution.py:449
  71.4 16.9 %collective-permute-start.11 = (f32[15,32,256]{2,1,0:T(8,128)S(1)}, f32[15,32,256]{2,1,0:T(8,128)S(1)}, u32[]{:S(2)}, u32[]{:S(2)}) collective-permute-start(f32[15,32,256]{2,1,0:T(8,128)S(1)} %get-tuple-element.61.refs_1_), channel_id=1, source_target_pairs={{0,1},{1,2},{2,3},{4,5},{5,6},{6,7},{8,9},{9,10},{10,11},{12,13},{... | collective-permute-start | bytes 1474568 | tf_op jit(solution)/shard_map/ppermute | solution.py:444
  75.5 15.6 %collective-permute-start.12 = (f32[15,32,256]{2,1,0:T(8,128)S(1)}, f32[15,32,256]{2,1,0:T(8,128)S(1)}, u32[]{:S(2)}, u32[]{:S(2)}) collective-permute-start(f32[15,32,256]{2,1,0:T(8,128)S(1)} %get-tuple-element.60.refs_4_.refs_0_), channel_id=1, source_target_pairs={{1,0},{2,1},{3,2},{5,4},{6,5},{7,6},{9,8},{10,9},{11,10},{13,12},{... | collective-permute-start | bytes 1474568 | tf_op jit(solution)/shard_map/ppermute | solution.py:449
  78.9 20.1 %collective-permute-start.17 = (f32[15,16,256]{2,1,0:T(8,128)S(1)}, f32[15,16,256]{2,1,0:T(8,128)S(1)}, u32[]{:S(2)}, u32[]{:S(2)}) collective-permute-start(f32[15,16,256]{2,1,0:T(8,128)S(1)} %get-tuple-element.68.refs_1_), channel_id=1, source_target_pairs={{0,1},{1,2},{2,3},{4,5},{5,6},{6,7},{8,9},{9,10},{10,11},{12,13},{... | collective-permute-start | bytes 737288 | tf_op jit(solution)/shard_map/ppermute | solution.py:444
  82.4 17.9 %collective-permute-start.18 = (f32[15,16,256]{2,1,0:T(8,128)S(1)}, f32[15,16,256]{2,1,0:T(8,128)S(1)}, u32[]{:S(2)}, u32[]{:S(2)}) collective-permute-start(f32[15,16,256]{2,1,0:T(8,128)S(1)} %get-tuple-element.65.refs_4_.refs_0_), channel_id=1, source_target_pairs={{1,0},{2,1},{3,2},{5,4},{6,5},{7,6},{9,8},{10,9},{11,10},{13,12},{... | collective-permute-start | bytes 737288 | tf_op jit(solution)/shard_map/ppermute | solution.py:449
  83.7 27.4 %collective-permute-start.20 = (f32[15,16,256]{2,1,0:T(8,128)S(1)}, f32[15,16,256]{2,1,0:T(8,128)S(1)}, u32[]{:S(2)}, u32[]{:S(2)}) collective-permute-start(f32[15,16,256]{2,1,0:T(8,128)S(1)} %get-tuple-element.72), channel_id=1, source_target_pairs={{0,1},{1,2},{2,3},{4,5},{5,6},{6,7},{8,9},{9,10},{10,11},{12,13},{... | collective-permute-start | bytes 737288 | tf_op jit(solution)/shard_map/ppermute | solution.py:444
  92.5 16.0 %collective-permute-start.15 = (f32[15,32,256]{2,1,0:T(8,128)S(1)}, f32[15,32,256]{2,1,0:T(8,128)S(1)}, u32[]{:S(2)}, u32[]{:S(2)}) collective-permute-start(f32[15,32,256]{2,1,0:T(8,128)S(1)} %get-tuple-element.66.refs_4_.refs_0_), channel_id=1, source_target_pairs={{1,0},{2,1},{3,2},{5,4},{6,5},{7,6},{9,8},{10,9},{11,10},{13,12},{... | collective-permute-start | bytes 1474568 | tf_op jit(solution)/shard_map/ppermute | solution.py:449
  93.8 16.1 %collective-permute-start.16 = (f32[15,32,256]{2,1,0:T(8,128)S(1)}, f32[15,32,256]{2,1,0:T(8,128)S(1)}, u32[]{:S(2)}, u32[]{:S(2)}) collective-permute-start(f32[15,32,256]{2,1,0:T(8,128)S(1)} %get-tuple-element.67.refs_1_), channel_id=1, source_target_pairs={{0,1},{1,2},{2,3},{4,5},{5,6},{6,7},{8,9},{9,10},{10,11},{12,13},{... | collective-permute-start | bytes 1474568 | tf_op jit(solution)/shard_map/ppermute | solution.py:444
  99.1 14.7 %collective-permute-start.21 = (f32[15,16,256]{2,1,0:T(8,128)S(1)}, f32[15,16,256]{2,1,0:T(8,128)S(1)}, u32[]{:S(2)}, u32[]{:S(2)}) collective-permute-start(f32[15,16,256]{2,1,0:T(8,128)S(1)} %get-tuple-element.69.refs_4_.refs_0_), channel_id=1, source_target_pairs={{1,0},{2,1},{3,2},{5,4},{6,5},{7,6},{9,8},{10,9},{11,10},{13,12},{... | collective-permute-start | bytes 737288 | tf_op jit(solution)/shard_map/ppermute | solution.py:449
  101.0 13.7 %collective-permute-start.22 = (f32[15,16,256]{2,1,0:T(8,128)S(1)}, f32[15,16,256]{2,1,0:T(8,128)S(1)}, u32[]{:S(2)}, u32[]{:S(2)}) collective-permute-start(f32[15,16,256]{2,1,0:T(8,128)S(1)} %get-tuple-element.73.refs_1_), channel_id=1, source_target_pairs={{0,1},{1,2},{2,3},{4,5},{5,6},{6,7},{8,9},{9,10},{10,11},{12,13},{... | collective-permute-start | bytes 737288 | tf_op jit(solution)/shard_map/ppermute | solution.py:444
  108.5 10.4 %collective-permute-start.23 = (f32[15,16,256]{2,1,0:T(8,128)S(1)}, f32[15,16,256]{2,1,0:T(8,128)S(1)}, u32[]{:S(2)}, u32[]{:S(2)}) collective-permute-start(f32[15,16,256]{2,1,0:T(8,128)S(1)} %get-tuple-element.70.refs_4_.refs_0_), channel_id=1, source_target_pairs={{1,0},{2,1},{3,2},{5,4},{6,5},{7,6},{9,8},{10,9},{11,10},{13,12},{... | collective-permute-start | bytes 737288 | tf_op jit(solution)/shard_map/ppermute | solution.py:449
  111.1 8.7 %collective-permute-start.19 = (f32[16,32,256]{2,1,0:T(8,128)S(1)}, f32[16,32,256]{2,1,0:T(8,128)S(1)}, u32[]{:S(2)}, u32[]{:S(2)}) collective-permute-start(f32[16,32,256]{2,1,0:T(8,128)S(1)} %shard_map.70.refs_4_.refs_3_), channel_id=1, source_target_pairs={{0,4},{4,8},{8,12},{12,0},{1,5},{5,9},{9,13},{13,1},{2,6},{6,10},{... | collective-permute-start | bytes 1572872 | tf_op jit(solution)/shard_map/ppermute | solution.py:458
  114.4 5.4 %copy-start.1 = (f32[16,64,256]{2,1,0:T(8,128)S(1)}, f32[16,64,256]{2,1,0:T(8,128)}, u32[]{:S(2)}) copy-start(f32[16,64,256]{2,1,0:T(8,128)} %copy-done) | copy-start | bytes 3145732
  114.4 5.4 %copy-start.5 = (bf16[16,2,64,128]{3,2,1,0:T(8,128)(2,1)S(1)}, bf16[16,2,64,128]{3,2,1,0:T(8,128)(2,1)}, u32[]{:S(2)}) copy-start(bf16[16,2,64,128]{3,2,1,0:T(8,128)(2,1)} %copy-done.4) | copy-start | bytes 1572868
